TPU v7x, 32 devices: a whole 2x2x4 slice. The times are simulated.
32 devices in a mesh: dp: 8 (over z, x), ctx: 4 (over y, core).
Axes of the slice: x: 2, y: 2, z: 4, core: 2. Of those that a mesh axis runs over, the one named last changes fastest.
Arguments:
- hidden: bfloat16 [16384, 1024], P(('dp', 'ctx')), may hold values from -6 to 6
- memory: bfloat16 [8192, 1024], P(('dp', 'ctx')), may hold values from -6 to 6
- cotangent: bfloat16 [16384, 1024], P(('dp', 'ctx')), may hold values from -6 to 6
- dec_segment: int32 [32, 512], P(('dp', 'ctx')), may hold values from 0 to 31, as said below
- pad_length: int32 [32], P(('dp', 'ctx')), may hold values from 0 to 127
- mem_segment: int32 [8192], P(('dp', 'ctx')), may hold values from -1 to 31, as said below
- self_query: bfloat16 [1024, 1024], P(('dp', 'ctx')), may hold values from -0.1875 to 0.1875
- self_key: bfloat16 [1024, 1024], P(('dp', 'ctx')), may hold values from -0.1875 to 0.1875
- self_value: bfloat16 [1024, 1024], P(('dp', 'ctx')), may hold values from -0.1875 to 0.1875
- self_output: bfloat16 [1024, 1024], P(('dp', 'ctx')), may hold values from -3 to 3
- norm1_gain: float32 [1024], P(('dp', 'ctx')), may hold values from 0.5 to 1.5
- norm1_bias: float32 [1024], P(('dp', 'ctx')), may hold values from -1.2 to 1.2
- cross_query: bfloat16 [1024, 1024], P(('dp', 'ctx')), may hold values from -0.1875 to 0.1875
- cross_key: bfloat16 [1024, 1024], P(('dp', 'ctx')), may hold values from -0.1875 to 0.1875
- cross_value: bfloat16 [1024, 1024], P(('dp', 'ctx')), may hold values from -0.1875 to 0.1875
- cross_output: bfloat16 [1024, 1024], P(('dp', 'ctx')), may hold values from -3 to 3
- norm2_gain: float32 [1024], P(('dp', 'ctx')), may hold values from 0.5 to 1.5
- norm2_bias: float32 [1024], P(('dp', 'ctx')), may hold values from -1.2 to 1.2
- ffn_up: bfloat16 [1024, 4096], P(('dp', 'ctx')), may hold values from -0.1875 to 0.1875
- ffn_down: bfloat16 [4096, 1024], P(('dp', 'ctx')), may hold values from -0.75 to 0.75
- norm3_gain: float32 [1024], P(('dp', 'ctx')), may hold values from 0.5 to 1.5
- norm3_bias: float32 [1024], P(('dp', 'ctx')), may hold values from -1.2 to 1.2
Outputs:
- output: bfloat16 [16384, 1024], P(('dp', 'ctx'))
- grad_input: float32 [16384, 1024], P(('dp', 'ctx'))
- grad_memory: float32 [8192, 1024], P(('dp', 'ctx'))
- grad_self_query: float32 [1024, 1024], P(('dp', 'ctx'))
- grad_self_key: float32 [1024, 1024], P(('dp', 'ctx'))
- grad_self_value: float32 [1024, 1024], P(('dp', 'ctx'))
- grad_self_output: float32 [1024, 1024], P(('dp', 'ctx'))
- grad_norm1_gain: float32 [1024], P(('dp', 'ctx'))
- grad_norm1_bias: float32 [1024], P(('dp', 'ctx'))
- grad_cross_query: float32 [1024, 1024], P(('dp', 'ctx'))
- grad_cross_key: float32 [1024, 1024], P(('dp', 'ctx'))
- grad_cross_value: float32 [1024, 1024], P(('dp', 'ctx'))
- grad_cross_output: float32 [1024, 1024], P(('dp', 'ctx'))
- grad_norm2_gain: float32 [1024], P(('dp', 'ctx'))
- grad_norm2_bias: float32 [1024], P(('dp', 'ctx'))
- grad_ffn_up: float32 [1024, 4096], P(('dp', 'ctx'))
- grad_ffn_down: float32 [4096, 1024], P(('dp', 'ctx'))
- grad_norm3_gain: float32 [1024], P(('dp', 'ctx'))
- grad_norm3_bias: float32 [1024], P(('dp', 'ctx'))
Inputs may be any that keep to these rules, and one draw needn't show every extreme that they name: `dec_segment`: ids count the sentence pairs of a group (4 rows of one index of dp): row j of a group holds pairs j * 8 to j * 8 + 7 in order, each on one or more positions. `mem_segment`: within each group's 1024 memory tokens the ids never fall; every pair of the group has one or more tokens; -1 marks one or more padding tokens at the group's end.
All inputs are finite; a program needn't handle non-finite values.
Results may differ from a plain program's by a relative error of at most 0.02.
Values may be sent and summed in bfloat16 or wider, within the bound.
No kernel may reach another device: no remote copies, remote signals or barrier semaphores. Data moves between devices by JAX's collectives and lax.ppermute only.
A program may use at most 256 MiB of HBM per device.

v0:
```python
import math

import jax
import jax.numpy as jnp
from jax import lax
from jax.sharding import PartitionSpec as P

HD = 64


ALPHA_RES = 4.16
EPSILON = 1e-05
MASKED = -1e30
SCORE_SCALE = 0.125


def combined_all(array, axis, combine):
    everything = jax.tree.map(lambda part: lax.all_gather(part, axis), array)
    initial = jax.tree.map(lambda part: part[0], everything)

    def hop(k, so_far):
        return combine(so_far, jax.tree.map(lambda part: part[k], everything))

    return lax.fori_loop(1, lax.axis_size(axis), hop, initial)


def matmul(left, right):
    return jnp.dot(left, right, preferred_element_type=jnp.float32)


def inner_left_part(left, right):
    return lax.dot_general(
        left, right, (((0,), (0,)), ((), ())), preferred_element_type=jnp.float32
    )


def outer_right(left, right):
    return lax.dot_general(
        left, right, (((1,), (1,)), ((), ())), preferred_element_type=jnp.float32
    )


def normalize(resid, gain, bias):
    center = resid - jnp.mean(resid, axis=-1, keepdims=True)
    spread = jnp.mean(center * center, axis=-1, keepdims=True)
    return center * lax.rsqrt(spread + EPSILON) * gain + bias


def smooth_gate(values):
    return jax.nn.gelu(values, approximate=False)


def self_mask(segment, padding):
    length = segment.shape[1]
    positions = jnp.arange(length)
    same_pair = segment[:, :, None] == segment[:, None, :]
    causal = positions[None, :, None] >= positions[None, None, :]
    live_key = positions[None, None, :] < (length - padding)[:, None, None]
    diagonal = positions[:, None] == positions[None, :]
    return same_pair & causal & (live_key | diagonal[None])


def self_scores(queries, key_rows, live):
    attention_scores = (
        jnp.einsum("rqhd,rkhd->rhqk", queries, key_rows, preferred_element_type=jnp.float32)
        * SCORE_SCALE
    )
    return jnp.where(live[:, None], attention_scores, MASKED)


def cross_scores(query_block, id_block, key_heads, key_ids):
    attention_scores = (
        jnp.einsum("qhd,khd->hqk", query_block, key_heads, preferred_element_type=jnp.float32)
        * SCORE_SCALE
    )
    live = id_block[:, None] == key_ids[None, :]
    return (jnp.where(live[None], attention_scores, MASKED), live)


def combine_stats(left_pair, right_pair):
    left_peak, left_total = left_pair
    right_peak, right_total = right_pair
    maxima = jnp.maximum(left_peak, right_peak)
    return (
        maxima,
        left_total * jnp.exp(left_peak - maxima) + right_total * jnp.exp(right_peak - maxima),
    )


def body(
    hidden,
    memory,
    cotangent,
    dec_segment,
    pad_length,
    mem_segment,
    self_query,
    self_key,
    self_value,
    self_output,
    norm1_gain,
    norm1_bias,
    cross_query,
    cross_key,
    cross_value,
    cross_output,
    norm2_gain,
    norm2_bias,
    ffn_up,
    ffn_down,
    norm3_gain,
    norm3_bias,
):
    gain_one_low = norm1_gain.astype(jnp.bfloat16)
    bias_one_low = norm1_bias.astype(jnp.bfloat16)
    gain_two_low = norm2_gain.astype(jnp.bfloat16)
    bias_two_low = norm2_bias.astype(jnp.bfloat16)
    gain_three_low = norm3_gain.astype(jnp.bfloat16)
    bias_three_low = norm3_bias.astype(jnp.bfloat16)

    def self_weights():
        return (
            lax.all_gather(self_query, ("dp", "ctx"), axis=0, tiled=True),
            lax.all_gather(self_key, ("dp", "ctx"), axis=0, tiled=True),
            lax.all_gather(self_value, ("dp", "ctx"), axis=0, tiled=True),
            lax.all_gather(self_output, ("dp", "ctx"), axis=0, tiled=True),
            lax.all_gather(gain_one_low, ("dp", "ctx"), axis=0, tiled=True),
            lax.all_gather(bias_one_low, ("dp", "ctx"), axis=0, tiled=True),
        )

    def cross_weights():
        return (
            lax.all_gather(cross_query, ("dp", "ctx"), axis=0, tiled=True),
            lax.all_gather(cross_key, ("dp", "ctx"), axis=0, tiled=True),
            lax.all_gather(cross_value, ("dp", "ctx"), axis=0, tiled=True),
            lax.all_gather(cross_output, ("dp", "ctx"), axis=0, tiled=True),
            lax.all_gather(gain_two_low, ("dp", "ctx"), axis=0, tiled=True),
            lax.all_gather(bias_two_low, ("dp", "ctx"), axis=0, tiled=True),
        )

    def ffn_weights():
        return (
            lax.all_gather(ffn_up, ("dp", "ctx"), axis=0, tiled=True),
            lax.all_gather(ffn_down, ("dp", "ctx"), axis=0, tiled=True),
            lax.all_gather(gain_three_low, ("dp", "ctx"), axis=0, tiled=True),
            lax.all_gather(bias_three_low, ("dp", "ctx"), axis=0, tiled=True),
        )

    tok_rows, model_width = hidden.shape
    row_count, length = dec_segment.shape
    head_count = model_width // HD
    mem_rows = memory.shape[0]
    hidden_f = hidden.astype(jnp.float32)
    self_set = self_weights()
    queries = matmul(hidden, self_set[0]).astype(jnp.bfloat16)
    key_rows = matmul(hidden, self_set[1]).astype(jnp.bfloat16)
    value_rows = matmul(hidden, self_set[2]).astype(jnp.bfloat16)
    query_heads = queries.reshape(row_count, length, head_count, HD)
    key_heads = key_rows.reshape(row_count, length, head_count, HD)
    value_heads = value_rows.reshape(row_count, length, head_count, HD)
    live_self = self_mask(dec_segment, pad_length)
    attention_scores = self_scores(query_heads, key_heads, live_self)
    maxima = jnp.max(attention_scores, axis=-1, keepdims=True)
    exponent = jnp.exp(attention_scores - maxima)
    totals = jnp.sum(exponent, axis=-1, keepdims=True)
    self_probs = exponent / totals
    self_lse = maxima + jnp.log(totals)
    self_att = (
        jnp.einsum(
            "rhqk,rkhd->rqhd",
            self_probs.astype(jnp.bfloat16),
            value_heads,
            preferred_element_type=jnp.float32,
        )
        .astype(jnp.bfloat16)
        .reshape(tok_rows, model_width)
    )
    branch = matmul(self_att, self_set[3])
    first_out, norm_one_back = jax.vjp(
        normalize,
        ALPHA_RES * hidden_f + branch,
        self_set[4].astype(jnp.float32),
        self_set[5].astype(jnp.float32),
    )
    first_low = first_out.astype(jnp.bfloat16)
    cross_set = cross_weights()
    cross_rows = matmul(first_low, cross_set[0]).astype(jnp.bfloat16)
    mem_keys = matmul(memory, cross_set[1]).astype(jnp.bfloat16)
    mem_values = matmul(memory, cross_set[2]).astype(jnp.bfloat16)
    own_ids = dec_segment.reshape(-1)
    queries_all, ids_low = (
        lax.all_gather(cross_rows, "ctx", axis=0, tiled=True),
        lax.all_gather(own_ids.astype(jnp.bfloat16), "ctx", axis=0, tiled=True),
    )
    ids_all = ids_low.astype(jnp.int32)
    total_rows = queries_all.shape[0]
    block_rows = math.gcd(total_rows, 1024)
    block_count = total_rows // block_rows
    mem_key_heads = mem_keys.reshape(mem_rows, head_count, HD)
    mem_value_heads = mem_values.reshape(mem_rows, head_count, HD)
    query_blocks = queries_all.reshape(block_count, block_rows, head_count, HD)
    id_blocks = ids_all.reshape(block_count, block_rows)

    def local_stats(inputs):
        query_block, id_block = inputs
        block_scores, live = cross_scores(query_block, id_block, mem_key_heads, mem_segment)
        peaks = jnp.max(block_scores, axis=-1)
        sums = jnp.sum(
            jnp.where(live[None], jnp.exp(block_scores - peaks[..., None]), 0.0), axis=-1
        )
        return (peaks, sums)

    peaks, sums = lax.map(local_stats, (query_blocks, id_blocks))
    peaks, sums = combined_all((peaks, sums), "ctx", combine_stats)
    cross_lse = peaks + jnp.log(sums)

    def partial_out(inputs):
        query_block, id_block, lse_block = inputs
        block_scores, live = cross_scores(query_block, id_block, mem_key_heads, mem_segment)
        block_probs = jnp.where(live[None], jnp.exp(block_scores - lse_block[..., None]), 0.0)
        return jnp.einsum(
            "hqk,khd->qhd",
            block_probs.astype(jnp.bfloat16),
            mem_value_heads,
            preferred_element_type=jnp.float32,
        )

    partial_value = lax.map(partial_out, (query_blocks, id_blocks, cross_lse)).reshape(
        total_rows, model_width
    )
    cross_att = lax.psum_scatter(partial_value, "ctx", scatter_dimension=0, tiled=True).astype(
        jnp.bfloat16
    )
    cross_branch = matmul(cross_att, cross_set[3])
    second, norm_two_back = jax.vjp(
        normalize,
        ALPHA_RES * first_out + cross_branch,
        cross_set[4].astype(jnp.float32),
        cross_set[5].astype(jnp.float32),
    )
    second_low = second.astype(jnp.bfloat16)
    ffn_set = ffn_weights()
    pre_act = matmul(second_low, ffn_set[0])
    gated, gate_back = jax.vjp(smooth_gate, pre_act)
    activated = gated.astype(jnp.bfloat16)
    ffn_branch = matmul(activated, ffn_set[1])
    output, norm_three_back = jax.vjp(
        normalize,
        ALPHA_RES * second + ffn_branch,
        ffn_set[2].astype(jnp.float32),
        ffn_set[3].astype(jnp.float32),
    )
    grad_third, grad_gain_three, gradient_third_bias = norm_three_back(
        cotangent.astype(jnp.float32)
    )
    ffn_set = ffn_weights()
    ffn_low = grad_third.astype(jnp.bfloat16)
    grad_down = inner_left_part(activated, ffn_low)
    grad_act = outer_right(ffn_low, ffn_set[1])
    grad_pre = gate_back(grad_act)[0].astype(jnp.bfloat16)
    grad_up = inner_left_part(second_low, grad_pre)
    grad_second = ALPHA_RES * grad_third + outer_right(grad_pre, ffn_set[0])
    ffn_shards = (
        lax.psum_scatter(grad_up, ("dp", "ctx"), scatter_dimension=0, tiled=True),
        lax.psum_scatter(grad_down, ("dp", "ctx"), scatter_dimension=0, tiled=True),
        lax.psum_scatter(grad_gain_three, ("dp", "ctx"), scatter_dimension=0, tiled=True),
        lax.psum_scatter(gradient_third_bias, ("dp", "ctx"), scatter_dimension=0, tiled=True),
    )
    grad_mid, grad_gain_two, grad_bias_two = norm_two_back(grad_second)
    cross_set = cross_weights()
    cross_low = grad_mid.astype(jnp.bfloat16)
    grad_cout = inner_left_part(cross_att, cross_low)
    grad_catt = outer_right(cross_low, cross_set[3]).astype(jnp.bfloat16)
    grads_all = lax.all_gather(grad_catt, "ctx", axis=0, tiled=True)
    grad_blocks = grads_all.reshape(block_count, block_rows, head_count, HD)

    def delta_part(inputs):
        query_block, id_block, lse_block, grad_block = inputs
        block_scores, live = cross_scores(query_block, id_block, mem_key_heads, mem_segment)
        block_probs = jnp.where(live[None], jnp.exp(block_scores - lse_block[..., None]), 0.0)
        block_dprob = jnp.einsum(
            "qhd,khd->hqk", grad_block, mem_value_heads, preferred_element_type=jnp.float32
        )
        return jnp.sum(block_probs * block_dprob, axis=-1)

    deltas = lax.map(delta_part, (query_blocks, id_blocks, cross_lse, grad_blocks))
    deltas = lax.psum(deltas.astype(jnp.bfloat16), "ctx").astype(jnp.float32)

    def grad_step(running, inputs):
        key_acc, value_acc = running
        query_block, id_block, lse_block, grad_block, delta_block = inputs
        block_scores, live = cross_scores(query_block, id_block, mem_key_heads, mem_segment)
        block_probs = jnp.where(live[None], jnp.exp(block_scores - lse_block[..., None]), 0.0)
        block_dprob = jnp.einsum(
            "qhd,khd->hqk", grad_block, mem_value_heads, preferred_element_type=jnp.float32
        )
        block_dscore = (block_probs * (block_dprob - delta_block[..., None])).astype(jnp.bfloat16)
        grad_query_block = (
            jnp.einsum(
                "hqk,khd->qhd", block_dscore, mem_key_heads, preferred_element_type=jnp.float32
            )
            * SCORE_SCALE
        )
        key_acc = (
            key_acc
            + jnp.einsum(
                "hqk,qhd->khd", block_dscore, query_block, preferred_element_type=jnp.float32
            )
            * SCORE_SCALE
        )
        value_acc = value_acc + jnp.einsum(
            "hqk,qhd->khd",
            block_probs.astype(jnp.bfloat16),
            grad_block,
            preferred_element_type=jnp.float32,
        )
        return ((key_acc, value_acc), grad_query_block)

    zeros_kv = jnp.zeros((mem_rows, head_count, HD), jnp.float32)
    (key_acc, value_acc), dq_blocks = lax.scan(
        grad_step, (zeros_kv, zeros_kv), (query_blocks, id_blocks, cross_lse, grad_blocks, deltas)
    )
    grad_cq = lax.psum_scatter(
        dq_blocks.reshape(total_rows, model_width).astype(jnp.bfloat16),
        "ctx",
        scatter_dimension=0,
        tiled=True,
    )
    grad_mk = key_acc.reshape(mem_rows, model_width)
    grad_mv = value_acc.reshape(mem_rows, model_width)
    mk_low = grad_mk.astype(jnp.bfloat16)
    mv_low = grad_mv.astype(jnp.bfloat16)
    grad_cquery = inner_left_part(first_low, grad_cq)
    grad_ckey = inner_left_part(memory, mk_low)
    grad_cvalue = inner_left_part(memory, mv_low)
    grad_memory = outer_right(mk_low, cross_set[1]) + outer_right(mv_low, cross_set[2])
    grad_first = ALPHA_RES * grad_mid + outer_right(grad_cq, cross_set[0])
    cross_shards = (
        lax.psum_scatter(grad_cquery, ("dp", "ctx"), scatter_dimension=0, tiled=True),
        lax.psum_scatter(grad_ckey, ("dp", "ctx"), scatter_dimension=0, tiled=True),
        lax.psum_scatter(grad_cvalue, ("dp", "ctx"), scatter_dimension=0, tiled=True),
        lax.psum_scatter(grad_cout, ("dp", "ctx"), scatter_dimension=0, tiled=True),
        lax.psum_scatter(grad_gain_two, ("dp", "ctx"), scatter_dimension=0, tiled=True),
        lax.psum_scatter(grad_bias_two, ("dp", "ctx"), scatter_dimension=0, tiled=True),
    )
    grad_res, grad_gain_one, grad_bias_one = norm_one_back(grad_first)
    self_set = self_weights()
    self_low = grad_res.astype(jnp.bfloat16)
    gradient_self_outputs = inner_left_part(self_att, self_low)
    gradient_self_attention = (
        outer_right(self_low, self_set[3])
        .astype(jnp.bfloat16)
        .reshape(row_count, length, head_count, HD)
    )
    attention_scores = self_scores(query_heads, key_heads, live_self)
    probs_again = jnp.exp(attention_scores - self_lse)
    self_dprob = jnp.einsum(
        "rqhd,rkhd->rhqk", gradient_self_attention, value_heads, preferred_element_type=jnp.float32
    )
    self_delta = jnp.sum(probs_again * self_dprob, axis=-1, keepdims=True)
    self_dscore = (probs_again * (self_dprob - self_delta)).astype(jnp.bfloat16)
    grad_q = (
        (
            jnp.einsum(
                "rhqk,rkhd->rqhd", self_dscore, key_heads, preferred_element_type=jnp.float32
            )
            * SCORE_SCALE
        )
        .astype(jnp.bfloat16)
        .reshape(tok_rows, model_width)
    )
    gradient_key_rows = (
        (
            jnp.einsum(
                "rhqk,rqhd->rkhd", self_dscore, query_heads, preferred_element_type=jnp.float32
            )
            * SCORE_SCALE
        )
        .astype(jnp.bfloat16)
        .reshape(tok_rows, model_width)
    )
    grad_v = (
        jnp.einsum(
            "rhqk,rqhd->rkhd",
            probs_again.astype(jnp.bfloat16),
            gradient_self_attention,
            preferred_element_type=jnp.float32,
        )
        .astype(jnp.bfloat16)
        .reshape(tok_rows, model_width)
    )
    grad_squery = inner_left_part(hidden, grad_q)
    gradient_self_keys = inner_left_part(hidden, gradient_key_rows)
    grad_svalue = inner_left_part(hidden, grad_v)
    grad_hidden = (
        ALPHA_RES * grad_res
        + outer_right(grad_q, self_set[0])
        + outer_right(gradient_key_rows, self_set[1])
        + outer_right(grad_v, self_set[2])
    )
    self_shards = (
        lax.psum_scatter(grad_squery, ("dp", "ctx"), scatter_dimension=0, tiled=True),
        lax.psum_scatter(gradient_self_keys, ("dp", "ctx"), scatter_dimension=0, tiled=True),
        lax.psum_scatter(grad_svalue, ("dp", "ctx"), scatter_dimension=0, tiled=True),
        lax.psum_scatter(gradient_self_outputs, ("dp", "ctx"), scatter_dimension=0, tiled=True),
        lax.psum_scatter(grad_gain_one, ("dp", "ctx"), scatter_dimension=0, tiled=True),
        lax.psum_scatter(grad_bias_one, ("dp", "ctx"), scatter_dimension=0, tiled=True),
    )
    return (
        output.astype(jnp.bfloat16),
        grad_hidden,
        grad_memory,
        self_shards[0],
        self_shards[1],
        self_shards[2],
        self_shards[3],
        self_shards[4],
        self_shards[5],
        cross_shards[0],
        cross_shards[1],
        cross_shards[2],
        cross_shards[3],
        cross_shards[4],
        cross_shards[5],
        ffn_shards[0],
        ffn_shards[1],
        ffn_shards[2],
        ffn_shards[3],
    )


def solution(mesh):
    return jax.shard_map(
        body,
        mesh=mesh,
        in_specs=(
            P(("dp", "ctx"), None),
            P(("dp", "ctx"), None),
            P(("dp", "ctx"), None),
            P(("dp", "ctx"), None),
            P(("dp", "ctx")),
            P(("dp", "ctx")),
            P(("dp", "ctx"), None),
            P(("dp", "ctx"), None),
            P(("dp", "ctx"), None),
            P(("dp", "ctx"), None),
            P(("dp", "ctx")),
            P(("dp", "ctx")),
            P(("dp", "ctx"), None),
            P(("dp", "ctx"), None),
            P(("dp", "ctx"), None),
            P(("dp", "ctx"), None),
            P(("dp", "ctx")),
            P(("dp", "ctx")),
            P(("dp", "ctx"), None),
            P(("dp", "ctx"), None),
            P(("dp", "ctx")),
            P(("dp", "ctx")),
        ),
        out_specs=(
            P(("dp", "ctx"), None),
            P(("dp", "ctx"), None),
            P(("dp", "ctx"), None),
            P(("dp", "ctx"), None),
            P(("dp", "ctx"), None),
            P(("dp", "ctx"), None),
            P(("dp", "ctx"), None),
            P(("dp", "ctx")),
            P(("dp", "ctx")),
            P(("dp", "ctx"), None),
            P(("dp", "ctx"), None),
            P(("dp", "ctx"), None),
            P(("dp", "ctx"), None),
            P(("dp", "ctx")),
            P(("dp", "ctx")),
            P(("dp", "ctx"), None),
            P(("dp", "ctx"), None),
            P(("dp", "ctx")),
            P(("dp", "ctx")),
        ),
        check_vma=False,
    )
```

profile of v0, /device:TPU:8, one launch (start us, length us, event | category | flops | bytes accessed | tf_op | source)
XLA Modules:
  0.0 2718.7 jit_solution(11820734082618544147)
XLA Ops:
  17.8 40.8 %all-reduce.13 = (bf16[1024]{0:T(1024)(128)(2,1)S(1)}, bf16[1024]{0:T(1024)(128)(2,1)S(1)}, bf16[1024]{0:T(1024)(128)(2,1)}, bf16[1024]{0:T(1024)(128)(2,1)}, bf...) all-reduce(bf16[1024]{0:T(1024)(128)(2,1)S(1)} %dynamic-update-slice.1,, ...), channel_id=1, replica_groups=mesh['dp'=8,'ctx'=4] {'dp','ctx'}, use_global_device_ids=true, to_apply=%add.1 | all-reduce | flops 6144 | bytes 24576
  59.6 8.3 all-gather.18.cloned.1.call-done
  71.6 54.3 %all-gather.20.cloned.1.call-done = bf16[1024,1024]{1,0:T(8,128)(2,1)} async-done(((bf16[32,1024]{1,0:T(8,128)(2,1)}), bf16[1024,1024]{1,0:T(8,128)(2,1)}) %all-gather.20.cloned.1.call-update) | async-done | bytes 2097168 | tf_op jit(solution)/shard_map/all_gather | solution.py:124
  131.6 7.5 fusion.110
  139.0 8.4 fusion.65
  147.4 36.6 %all-gather.16.cloned.1.call-done = bf16[1024,1024]{1,0:T(8,128)(2,1)} async-done(((bf16[32,1024]{1,0:T(8,128)(2,1)}), bf16[1024,1024]{1,0:T(8,128)(2,1)}) %all-gather.16.cloned.1.call-update) | async-done | bytes 2097168 | tf_op jit(solution)/shard_map/all_gather | solution.py:125
  187.5 9.0 fusion.83
  196.5 45.5 %all-gather.22.cloned.1.call-done = bf16[1024,1024]{1,0:T(8,128)(2,1)} async-done(((bf16[32,1024]{1,0:T(8,128)(2,1)}), bf16[1024,1024]{1,0:T(8,128)(2,1)}) %all-gather.22.cloned.1.call-update) | async-done | bytes 2097168 | tf_op jit(solution)/shard_map/all_gather | solution.py:126
  246.0 54.1 %all-gather.24.cloned.1.call-done = bf16[1024,1024]{1,0:T(8,128)(2,1)} async-done(((bf16[32,1024]{1,0:T(8,128)(2,1)}), bf16[1024,1024]{1,0:T(8,128)(2,1)}) %all-gather.24.cloned.1.call-update) | async-done | bytes 2097168 | tf_op jit(solution)/shard_map/all_gather | solution.py:133
  310.0 48.0 %all-gather.28.cloned.1.call-done = bf16[1024,1024]{1,0:T(8,128)(2,1)} async-done(((bf16[32,1024]{1,0:T(8,128)(2,1)}), bf16[1024,1024]{1,0:T(8,128)(2,1)}) %all-gather.28.cloned.1.call-update) | async-done | bytes 2097168 | tf_op jit(solution)/shard_map/all_gather | solution.py:134
  362.4 53.8 %all-gather.30.cloned.1.call-done = bf16[1024,1024]{1,0:T(8,128)(2,1)} async-done(((bf16[32,1024]{1,0:T(8,128)(2,1)}), bf16[1024,1024]{1,0:T(8,128)(2,1)}) %all-gather.30.cloned.1.call-update) | async-done | bytes 2097168 | tf_op jit(solution)/shard_map/all_gather | solution.py:135
  421.4 31.2 %all-gather.26.cloned.1.call-done = bf16[2048,1024]{1,0:T(8,128)(2,1)} async-done(((bf16[512,1024]{1,0:T(8,128)(2,1)}), bf16[2048,1024]{1,0:T(8,128)(2,1)}) %all-gather.26.cloned.1.call-update) | async-done | bytes 4194320 | tf_op jit(solution)/shard_map/all_gather | solution.py:192
  452.6 11.6 reshape.560
  464.2 9.8 copy.103
  474.0 17.0 while.64
  491.0 7.2 all-gather
  498.2 8.2 all-gather.1
  510.9 182.7 %while.66 = (s32[]{:T(128)}, f32[2,1024,16,64]{1,0,3,2:T(2,128)}, s32[2,1024]{1,0:T(2,128)S(1)}, s32[256]{0:T(256)S(1)}, bf16[2,1024,16,64]{1,3,2,0:T(8,128)(2,1...) while((s32[]{:T(128)}, f32[2,1024,16,64]{1,0,3,2:T(2,128)}, ...), condition=%wide.region_11.12_spmd, body=%wide.region_10.11_spmd.sunk | while | flops 1094975488 | bytes 24851580 | solution.py:228
  511.8 9.8 fusion.216
  521.6 8.8 copy.163
  530.4 71.8 %dynamic_update_slice.27 = f32[2,1024,16,64]{1,0,3,2:T(2,128)} dynamic-update-slice(f32[2,1024,16,64]{1,0,3,2:T(2,128)} %get-tuple-element.1015, f32[1,1024,16,64]{1,0,3,2:T(1,128)} %copy.163, s32[]{:T(128)S(6)} %copy.195, s32[]{:T(128)} %constant.173.clone.1..sunk.1, s32[]{:T(128)} %constant.173.clone.1..sunk.1, s32[]{:T(128)} %constant.173.clone.1..sunk.1) | dynamic-update-slice | bytes 8388612 | tf_op jit(solution)/shard_map/while/body/jit(dynamic_update_index_in_dim)/dynamic_update_slice | solution.py:228
  603.0 9.8 fusion.216
  612.8 8.8 copy.163
  621.6 71.8 %dynamic_update_slice.27 = f32[2,1024,16,64]{1,0,3,2:T(2,128)} dynamic-update-slice(f32[2,1024,16,64]{1,0,3,2:T(2,128)} %get-tuple-element.1015, f32[1,1024,16,64]{1,0,3,2:T(1,128)} %copy.163, s32[]{:T(128)S(6)} %copy.195, s32[]{:T(128)} %constant.173.clone.1..sunk.1, s32[]{:T(128)} %constant.173.clone.1..sunk.1, s32[]{:T(128)} %constant.173.clone.1..sunk.1) | dynamic-update-slice | bytes 8388612 | tf_op jit(solution)/shard_map/while/body/jit(dynamic_update_index_in_dim)/dynamic_update_slice | solution.py:228
  693.6 10.8 copy.160
  705.9 70.4 %reduce-scatter.23.cloned.1.call-done = f32[512,1024]{0,1:T(8,128)} async-done(((f32[2048,1024]{0,1:T(8,128)}), f32[512,1024]{0,1:T(8,128)}) %reduce-scatter.23.cloned.1.call-update) | async-done | bytes 2097168 | tf_op jit(solution)/shard_map/reduce_scatter | solution.py:231
  781.8 75.4 %all-gather.34.cloned.1.call-done = bf16[1024,4096]{1,0:T(8,128)(2,1)} async-done(((bf16[32,4096]{1,0:T(8,128)(2,1)}), bf16[1024,4096]{1,0:T(8,128)(2,1)}) %all-gather.34.cloned.1.call-update) | async-done | bytes 8388624 | tf_op jit(solution)/shard_map/all_gather | solution.py:143
  857.3 26.9 multiply_convert_fusion.2
  884.1 52.4 %all-gather.36.cloned.1.call-done = bf16[4096,1024]{1,0:T(8,128)(2,1)} async-done(((bf16[128,1024]{1,0:T(8,128)(2,1)}), bf16[4096,1024]{1,0:T(8,128)(2,1)}) %all-gather.36.cloned.1.call-update) | async-done | bytes 8388624 | tf_op jit(solution)/shard_map/all_gather | solution.py:144
  936.6 8.5 fusion.113
  948.7 15.2 add_convert_fusion
  963.9 9.6 multiply_reduce_fusion.2
  978.1 33.1 %all-gather.38.cloned.1.call-done = bf16[2048,1024]{1,0:T(8,128)(2,1)} async-done(((bf16[512,1024]{1,0:T(8,128)(2,1)}), bf16[2048,1024]{1,0:T(8,128)(2,1)}) %all-gather.38.cloned.1.call-update) | async-done | bytes 4194320 | tf_op jit(solution)/shard_map/all_gather | solution.py:274
  1011.2 12.1 reshape.561
  1023.3 9.8 copy.109
  1033.1 25.7 while.67
  1037.3 8.6 multiply_reduce_fusion.10
  1050.2 8.6 multiply_reduce_fusion.10
  1059.6 31.1 %all-reduce.16.cloned.1.call-done = bf16[2,16,1024]{2,1,0:T(8,128)(2,1)} async-done(((bf16[2,16,1024]{2,1,0:T(8,128)(2,1)}), bf16[2,16,1024]{2,1,0:T(8,128)(2,1)}) %all-reduce.16.cloned.1.call-update) | async-done | bytes 65552 | tf_op jit(solution)/shard_map/psum | solution.py:287
  1091.5 69.4 %while.68 = (s32[]{:T(128)}, f32[256,16,64]{0,2,1:T(8,128)S(1)}, f32[256,16,64]{0,2,1:T(8,128)}, bf16[2,1024,16,64]{1,3,2,0:T(8,128)(2,1)}, bf16[2,1024,16,64]{1...) while((s32[]{:T(128)}, f32[256,16,64]{0,2,1:T(8,128)S(1)}, ...), condition=%wide.region_26.27_spmd.clone, body=%wide.region_25.26_spmd.clone.sunk | while | flops 2737307648 | bytes 229324160 | solution.py:320
  1096.1 10.7 multiply_convert_fusion.6
  1106.9 5.8 fusion.233
  1112.7 8.6 fusion.234
  1130.6 10.7 multiply_convert_fusion.6
  1141.4 5.8 fusion.233
  1147.2 8.6 fusion.234
  1160.9 8.5 copy.110
  1201.8 17.9 reduce-scatter.25.cloned.1.call-done
  1229.7 16.7 multiply_reduce_fusion.1
  1246.5 8.1 multiply_convert_fusion.1
  1268.9 6.1 multiply_convert_fusion.3
  1284.9 8.6 fusion.84
  1316.3 10.5 fusion.99
  1328.5 10.5 fusion.96
  1343.5 40.1 %all-reduce.12 = (f32[1024]{0:T(1024)S(1)}, f32[1024]{0:T(1024)S(1)}, f32[1024]{0:T(1024)S(1)}, f32[1024]{0:T(1024)S(1)}, f32[1024]{0:T(1024)S(1)}, /*index=5*/f32[1024]{0:T(1024)S(1)}) all-reduce(f32[1024]{0:T(1024)S(1)} %copy-done.81, f32[1024]{0:T(1024)S(1)} %copy-done.82, ...), channel_id=10, replica_groups=mesh['dp'=8,'ctx'=4] {'dp','ctx'}, use_global_device_ids=true, to_apply=%region_36.37.clone | all-reduce | flops 6144 | bytes 49152
  1395.6 88.9 %reduce-scatter.43.cloned.1.call-done = f32[32,1024]{1,0:T(8,128)} async-done(((f32[1024,1024]{1,0:T(8,128)}), f32[32,1024]{1,0:T(8,128)}) %reduce-scatter.43.cloned.1.call-update) | async-done | bytes 131088
  1484.5 140.1 %reduce-scatter.45.cloned.1.call-done = f32[32,1024]{1,0:T(8,128)} async-done(((f32[1024,1024]{1,0:T(8,128)}), f32[32,1024]{1,0:T(8,128)}) %reduce-scatter.45.cloned.1.call-update) | async-done | bytes 131088
  1624.6 139.6 %reduce-scatter.37.cloned.1.call-done = f32[32,1024]{1,0:T(8,128)} async-done(((f32[1024,1024]{1,0:T(8,128)}), f32[32,1024]{1,0:T(8,128)}) %reduce-scatter.37.cloned.1.call-update) | async-done | bytes 131088
  1764.2 140.0 %reduce-scatter.39.cloned.1.call-done = f32[32,1024]{1,0:T(8,128)} async-done(((f32[1024,1024]{1,0:T(8,128)}), f32[32,1024]{1,0:T(8,128)}) %reduce-scatter.39.cloned.1.call-update) | async-done | bytes 131088
  1904.1 139.8 %reduce-scatter.41.cloned.1.call-done = f32[32,1024]{1,0:T(8,128)} async-done(((f32[1024,1024]{1,0:T(8,128)}), f32[32,1024]{1,0:T(8,128)}) %reduce-scatter.41.cloned.1.call-update) | async-done | bytes 131088
  2043.9 140.1 %reduce-scatter.27.cloned.1.call-done = f32[32,1024]{1,0:T(8,128)} async-done(((f32[1024,1024]{1,0:T(8,128)}), f32[32,1024]{1,0:T(8,128)}) %reduce-scatter.27.cloned.1.call-update) | async-done | bytes 131088 | tf_op jit(solution)/shard_map/reduce_scatter | solution.py:405
  2184.0 140.2 %reduce-scatter.29.cloned.1.call-done = f32[32,1024]{1,0:T(8,128)} async-done(((f32[1024,1024]{1,0:T(8,128)}), f32[32,1024]{1,0:T(8,128)}) %reduce-scatter.29.cloned.1.call-update) | async-done | bytes 131088 | tf_op jit(solution)/shard_map/reduce_scatter | solution.py:339
  2324.2 200.2 %reduce-scatter.33.cloned.1.call-done = f32[32,4096]{1,0:T(8,128)} async-done(((f32[1024,4096]{1,0:T(8,128)}), f32[32,4096]{1,0:T(8,128)}) %reduce-scatter.33.cloned.1.call-update) | async-done | bytes 524304 | tf_op jit(solution)/shard_map/reduce_scatter | solution.py:264
  2524.4 187.6 %reduce-scatter.35.cloned.1.call-done = f32[128,1024]{1,0:T(8,128)} async-done(((f32[4096,1024]{1,0:T(8,128)}), f32[128,1024]{1,0:T(8,128)}) %reduce-scatter.35.cloned.1.call-update) | async-done | bytes 524304 | tf_op jit(solution)/shard_map/reduce_scatter | solution.py:265
  (410 shorter events, 223.8 us)
Async XLA Ops:
  7.2 350.9 %copy-start = (bf16[256,1024]{1,0:T(8,128)(2,1)S(1)}, bf16[256,1024]{1,0:T(8,128)(2,1)}, u32[]{:S(2)}) copy-start(bf16[256,1024]{1,0:T(8,128)(2,1)} %param.33) | copy-start | bytes 1572868
  7.2 60.7 %all-gather.18.cloned.1.call-start = ((), (), s32[]{:S(2)}) async-start(), calls=%async_computation.13 | async-start | bytes 2162688 | tf_op jit(solution)/shard_map/all_gather | solution.py:123
  7.9 118.0 %all-gather.20.cloned.1.call-start = ((), (), s32[]{:S(2)}) async-start(), calls=%async_computation.14 | async-start | bytes 2162688 | tf_op jit(solution)/shard_map/all_gather | solution.py:124
  8.7 175.4 %all-gather.16.cloned.1.call-start = ((), (), s32[]{:S(2)}) async-start(), calls=%async_computation.12 | async-start | bytes 2162688 | tf_op jit(solution)/shard_map/all_gather | solution.py:125
  9.4 232.7 %all-gather.22.cloned.1.call-start = ((), (), s32[]{:S(2)}) async-start(), calls=%async_computation.15 | async-start | bytes 2162688 | tf_op jit(solution)/shard_map/all_gather | solution.py:126
  10.0 290.1 %all-gather.24.cloned.1.call-start = ((), (), s32[]{:S(2)}) async-start(), calls=%async_computation.16 | async-start | bytes 2162688 | tf_op jit(solution)/shard_map/all_gather | solution.py:133
  10.6 347.5 %all-gather.28.cloned.1.call-start = ((), (), s32[]{:S(2)}) async-start(), calls=%async_computation.18 | async-start | bytes 2162688 | tf_op jit(solution)/shard_map/all_gather | solution.py:134
  11.2 405.0 %all-gather.30.cloned.1.call-start = ((), (), s32[]{:S(2)}) async-start(), calls=%async_computation.19 | async-start | bytes 2162688 | tf_op jit(solution)/shard_map/all_gather | solution.py:135
  11.9 440.7 %all-gather.26.cloned.1.call-start = ((), (), s32[]{:S(2)}) async-start(), calls=%async_computation.17 | async-start | bytes 5242880 | tf_op jit(solution)/shard_map/all_gather | solution.py:192
  58.5 241.5 %copy-start.74 = (f32[1024]{0:T(1024)}, f32[1024]{0:T(1024)S(1)}, u32[]{:S(2)}) copy-start(f32[1024]{0:T(1024)S(1)} %convert_element_type.189) | copy-start | bytes 12292
  58.6 241.5 %copy-start.61 = (f32[1024]{0:T(1024)}, f32[1024]{0:T(1024)S(1)}, u32[]{:S(2)}) copy-start(f32[1024]{0:T(1024)S(1)} %convert_element_type.187) | copy-start | bytes 12292
  71.6 60.0 %copy-start.11 = (bf16[512,1024]{0,1:T(8,128)(2,1)}, bf16[512,1024]{0,1:T(8,128)(2,1)S(1)}, u32[]{:S(2)}) copy-start(bf16[512,1024]{0,1:T(8,128)(2,1)S(1)} %copy.96) | copy-start | bytes 3145732
  139.0 48.4 %copy-start.47 = (f32[16,512]{1,0:T(8,128)}, f32[16,512]{1,0:T(8,128)S(1)}, u32[]{:S(2)}) copy-start(f32[16,512]{1,0:T(8,128)S(1)} %get-tuple-element.676) | copy-start | bytes 98308
  139.0 45.0 %copy-start.40 = (bf16[512,1024]{1,0:T(8,128)(2,1)S(1)}, bf16[512,1024]{1,0:T(8,128)(2,1)}, u32[]{:S(2)}) copy-start(bf16[512,1024]{1,0:T(8,128)(2,1)} %param.32) | copy-start | bytes 3145732
  147.4 40.1 %copy-start.50 = (f32[16,512]{1,0:T(8,128)}, f32[16,512]{1,0:T(8,128)S(1)}, u32[]{:S(2)}) copy-start(f32[16,512]{1,0:T(8,128)S(1)} %fusion.65) | copy-start | bytes 98308
  245.6 530.8 %copy-start.3 = (f32[512,1024]{1,0:T(8,128)}, f32[512,1024]{1,0:T(8,128)S(1)}, u32[]{:S(2)}) copy-start(f32[512,1024]{1,0:T(8,128)S(1)} %get-tuple-element.679) | copy-start | bytes 6291460
  245.6 530.7 %copy-start.53 = (f32[512]{0:T(512)}, f32[512]{0:T(512)S(1)}, u32[]{:S(2)}) copy-start(f32[512]{0:T(512)S(1)} %broadcast_multiply_fusion.2) | copy-start | bytes 6148
  246.0 58.0 %copy-start.57 = (f32[512]{0:T(512)}, f32[512]{0:T(512)S(1)}, u32[]{:S(2)}) copy-start(f32[512]{0:T(512)S(1)} %multiply_reduce_fusion.8) | copy-start | bytes 6148
  246.0 58.0 %copy-start.66 = (f32[512]{0:T(512)}, f32[512]{0:T(512)S(1)}, u32[]{:S(2)}) copy-start(f32[512]{0:T(512)S(1)} %fusion.93) | copy-start | bytes 6148
  246.0 58.8 %copy-start.52 = (s32[1,512]{1,0:T(1,128)S(1)}, s32[1,512]{1,0:T(1,128)}, u32[]{:S(2)}) copy-start(s32[1,512]{1,0:T(1,128)} %param.35) | copy-start | bytes 6148
  304.0 402.0 %all-gather.32.cloned.1.call-start = ((), (), s32[]{:S(2)}) async-start(), calls=%async_computation.21 | async-start | bytes 2162688 | tf_op jit(solution)/shard_map/all_gather | solution.py:136
  304.7 471.6 %reduce-scatter.23.cloned.1.call-start = ((), (), s32[]{:S(2)}) async-start(), calls=%async_computation.20 | async-start | bytes 10485760 | tf_op jit(solution)/shard_map/reduce_scatter | solution.py:231
  464.2 9.8 copy-start.46
  704.4 72.0 %copy-start.62 = (f32[1024]{0:T(1024)S(1)}, f32[1024]{0:T(1024)}, u32[]{:S(2)}) copy-start(f32[1024]{0:T(1024)} %copy-done.61) | copy-start | bytes 12292
  704.4 72.0 %copy-start.67 = (f32[512]{0:T(512)S(1)}, f32[512]{0:T(512)}, u32[]{:S(2)}) copy-start(f32[512]{0:T(512)} %copy-done.66) | copy-start | bytes 6148
  704.4 72.0 %copy-start.75 = (f32[1024]{0:T(1024)S(1)}, f32[1024]{0:T(1024)}, u32[]{:S(2)}) copy-start(f32[1024]{0:T(1024)} %copy-done.74) | copy-start | bytes 12292
  704.4 152.8 %all-gather.34.cloned.1.call-start = ((), (), s32[]{:S(2)}) async-start(), calls=%async_computation.22 | async-start | bytes 8650752 | tf_op jit(solution)/shard_map/all_gather | solution.py:143
  705.2 231.4 %all-gather.36.cloned.1.call-start = ((), (), s32[]{:S(2)}) async-start(), calls=%async_computation.23 | async-start | bytes 8650752 | tf_op jit(solution)/shard_map/all_gather | solution.py:144
  705.8 305.4 %all-gather.38.cloned.1.call-start = ((), (), s32[]{:S(2)}) async-start(), calls=%async_computation.24 | async-start | bytes 5242880 | tf_op jit(solution)/shard_map/all_gather | solution.py:274
  705.8 230.7 %copy-start.77 = (f32[1024]{0:T(1024)}, f32[1024]{0:T(1024)S(1)}, u32[]{:S(2)}) copy-start(f32[1024]{0:T(1024)S(1)} %convert_element_type.199) | copy-start | bytes 12292
  705.9 267.6 %copy-start.64 = (f32[1024]{0:T(1024)}, f32[1024]{0:T(1024)S(1)}, u32[]{:S(2)}) copy-start(f32[1024]{0:T(1024)S(1)} %convert_element_type.197) | copy-start | bytes 12292
  780.2 193.4 %copy-start.55 = (f32[512]{0:T(512)}, f32[512]{0:T(512)S(1)}, u32[]{:S(2)}) copy-start(f32[512]{0:T(512)S(1)} %broadcast_multiply_fusion.1) | copy-start | bytes 6148
  781.8 191.7 %copy-start.70 = (f32[512]{0:T(512)}, f32[512]{0:T(512)S(1)}, u32[]{:S(2)}) copy-start(f32[512]{0:T(512)S(1)} %fusion.94) | copy-start | bytes 6148
  781.8 154.7 %copy-start.15 = (f32[512,1024]{1,0:T(8,128)S(1)}, f32[512,1024]{1,0:T(8,128)}, u32[]{:S(2)}) copy-start(f32[512,1024]{1,0:T(8,128)} %copy-done.14) | copy-start | bytes 6291460
  948.7 15.2 copy-start.30
  948.7 15.2 copy-start.87
  978.0 112.7 %all-reduce.16.cloned.1.call-start = ((), (), s32[]{:S(2)}) async-start(), calls=%async_computation.25 | async-start | bytes 131072 | tf_op jit(solution)/shard_map/psum | solution.py:287
  1023.3 9.8 copy-start.44
  1059.5 160.2 %reduce-scatter.25.cloned.1.call-start = ((), (), s32[]{:S(2)}) async-start(), calls=%async_computation.26 | async-start | bytes 5242880 | tf_op jit(solution)/shard_map/reduce_scatter | solution.py:323
  1095.9 11.0 copy-start.1
  1106.9 15.4 slice-start
  1112.7 9.6 slice-start.1
  1130.4 11.0 copy-start.1
  1141.4 15.4 slice-start
  1175.0 220.6 %reduce-scatter.31.cloned.1.call-start = ((), (), s32[]{:S(2)}) async-start(), calls=%async_computation.29 | async-start | bytes 4325376 | tf_op jit(solution)/shard_map/reduce_scatter | solution.py:342
  1181.3 303.2 %reduce-scatter.43.cloned.1.call-start = ((), (), s32[]{:S(2)}) async-start(), calls=%async_computation.35 | async-start | bytes 4325376
  1190.1 434.5 %reduce-scatter.45.cloned.1.call-start = ((), (), s32[]{:S(2)}) async-start(), calls=%async_computation.36 | async-start | bytes 4325376
  1200.4 19.3 copy-start.4
  1200.4 19.3 copy-start.54
  1200.4 19.3 copy-start.63
  1200.4 19.2 copy-start.68
  1200.5 563.7 %reduce-scatter.37.cloned.1.call-start = ((), (), s32[]{:S(2)}) async-start(), calls=%async_computation.32 | async-start | bytes 4325376
  1201.8 23.2 copy-start.58
  1229.7 16.8 slice-start.2
  1229.7 16.8 slice-start.3
  1229.7 16.8 slice-start.4
  1229.7 16.8 slice-start.5
  1267.7 636.4 %reduce-scatter.39.cloned.1.call-start = ((), (), s32[]{:S(2)}) async-start(), calls=%async_computation.33 | async-start | bytes 4325376
  1283.7 760.2 %reduce-scatter.41.cloned.1.call-start = ((), (), s32[]{:S(2)}) async-start(), calls=%async_computation.34 | async-start | bytes 4325376
  1302.2 881.8 %reduce-scatter.27.cloned.1.call-start = ((), (), s32[]{:S(2)}) async-start(), calls=%async_computation.27 | async-start | bytes 4325376 | tf_op jit(solution)/shard_map/reduce_scatter | solution.py:405
  1308.4 1015.8 %reduce-scatter.29.cloned.1.call-start = ((), (), s32[]{:S(2)}) async-start(), calls=%async_computation.28 | async-start | bytes 4325376 | tf_op jit(solution)/shard_map/reduce_scatter | solution.py:339
  1314.8 1209.6 %reduce-scatter.33.cloned.1.call-start = ((), (), s32[]{:S(2)}) async-start(), calls=%async_computation.30 | async-start | bytes 17301504 | tf_op jit(solution)/shard_map/reduce_scatter | solution.py:264
  1326.9 1385.1 %reduce-scatter.35.cloned.1.call-start = ((), (), s32[]{:S(2)}) async-start(), calls=%async_computation.31 | async-start | bytes 17301504 | tf_op jit(solution)/shard_map/reduce_scatter | solution.py:265
  1341.7 45.4 %copy-start.36 = (bf16[16,64,512]{2,1,0:T(8,128)(2,1)S(1)}, bf16[16,64,512]{2,1,0:T(8,128)(2,1)}, u32[]{:S(2)}) copy-start(bf16[16,64,512]{2,1,0:T(8,128)(2,1)} %copy-done.35) | copy-start | bytes 3145732
  (65 other events, 193.4 us)
Sparse Core Ops, SparseCore 0:
  10.9 56.9 all-gather.17
  70.8 55.1 all-gather.19
  128.8 55.2 all-gather.15
  186.8 55.2 all-gather.21
  244.8 55.2 all-gather.23
  302.8 55.2 all-gather.27
  360.9 55.2 all-gather.29
  418.3 34.2 all-gather.25
  455.5 55.3 all-gather.31
  704.6 71.7 reduce-scatter.22
  779.6 77.5 all-gather.33
  860.4 76.1 all-gather.35
  978.1 33.0 all-gather.37
  1059.6 31.0 all-reduce.15
  1175.1 44.4 reduce-scatter.24
  1222.5 122.1 reduce-scatter.30
  1347.5 136.9 reduce-scatter.42
  1487.3 137.2 reduce-scatter.44
  1627.5 136.5 reduce-scatter.36
  1767.0 137.1 reduce-scatter.38
  1907.1 136.7 reduce-scatter.40
  2046.8 137.1 reduce-scatter.26
  2186.9 137.1 reduce-scatter.28
  2327.0 197.3 reduce-scatter.32
  2527.4 184.5 reduce-scatter.34
where the time goes:
time: 2740 us; the launch traced here: 2720 us
  waiting for transfers between devices  1940 us (71%)
  matrix products  329 us (12%)
  local copies, waits for them, and re-layouts  292 us (11%)
  blocking collectives  101 us (4%)
  other arithmetic  42 us (2%)
    unnamed x30, waiting for transfers between devices  655 us
    reduce_scatter x1, waiting for transfers between devices, body(): lax.psum_scatter(grad_up, ('dp', 'ctx'), scatter_dimension=0, tiled=True)  200 us
    reduce_scatter x1, waiting for transfers between devices, body(): lax.psum_scatter(grad_down, ('dp', 'ctx'), scatter_dimension=0, tiled=True)  188 us
    dynamic_update_slice x4, local copies, waits for them, and re-layouts, body(): lax.map(partial_out, (query_blocks, id_blocks, cross_lse))  161 us
    reduce_scatter x1, waiting for transfers between devices, body(): lax.psum_scatter(grad_cquery, ('dp', 'ctx'), scatter_dimension=0, tiled=T...  140 us
    reduce_scatter x1, waiting for transfers between devices, body(): lax.psum_scatter(gradient_self_outputs, ('dp', 'ctx'), scatter_dimension=...  140 us
    unnamed x2, blocking collectives  80.9 us
    unnamed x207, local copies, waits for them, and re-layouts  78.4 us
  transfers between devices with their start and end apart: 25, of which 23 were waited for; matrix products, arithmetic and copies ran while one was open for 17% of the time, Pallas kernels for 0%

commit v1 on v0

v1 whole, which is shorter than its diff:
```python
import functools

import jax
import jax.numpy as jnp
from jax import lax
from jax.experimental import pallas as pl
from jax.experimental.pallas import tpu as pltpu
from jax.sharding import PartitionSpec as P

HD = 64
ALPHA_RES = 4.16
EPSILON = 1e-05
MASKED = -1e30
SCORE_SCALE = 0.125
BF = jnp.bfloat16
F32 = jnp.float32
BOTH = ("dp", "ctx")


class Grid:
    def __init__(self, dp, ctx):
        cores = 2
        y = ctx // cores
        x = y
        z = dp // x
        self.size = {"z": z, "x": x, "y": y, "c": cores}
        self.order = ("z", "x", "y", "c")
        self.total = dp * ctx

    def index(self, coords):
        value = 0
        for name in self.order:
            value = value * self.size[name] + coords[name]
        return value

    def coords(self, index):
        out = {}
        for name in reversed(self.order):
            out[name] = index % self.size[name]
            index = index // self.size[name]
        return out

    def here(self):
        dp, ctx = lax.axis_index("dp"), lax.axis_index("ctx")
        return {
            "z": dp // self.size["x"],
            "x": dp % self.size["x"],
            "y": ctx // self.size["c"],
            "c": ctx % self.size["c"],
        }

    def exchange(self, array, name, bit):
        pairs = []
        for source in range(self.total):
            coords = self.coords(source)
            coords[name] ^= bit
            pairs.append((source, self.index(coords)))
        return lax.ppermute(array, BOTH, pairs)

    def gather(self, array, name):
        return [array] + [self.exchange(array, name, k) for k in range(1, self.size[name])]

    def scatter(self, chunks, name):
        total = chunks[0].astype(F32)
        for k in range(1, self.size[name]):
            total = total + self.exchange(chunks[k].astype(BF), name, k).astype(F32)
        return total

    def blocks(self):
        return [
            (i, j, k)
            for i in range(self.size["x"])
            for j in range(self.size["y"])
            for k in range(self.size["c"])
        ]

    def positions(self):
        here = self.here()
        return jnp.stack(
            [
                ((i ^ here["x"]) * self.size["y"] + (j ^ here["y"])) * self.size["c"]
                + (k ^ here["c"])
                for i, j, k in self.blocks()
            ]
            + [k ^ here["z"] for k in range(self.size["z"])]
        ).astype(jnp.int32)

    def gather_weights(self, array, split):
        line = jnp.stack(self.gather(array, "z"))
        out = []
        for part, first, then in ((line[:, :, :split], "x", "y"), (line[:, :, split:], "y", "x")):
            part = jnp.stack(self.gather(part, first))
            part = jnp.stack(self.gather(part, then))
            out.append(self.gather(part, "c"))
        return out


def assemble(grid, positions, pieces, widths):
    nx, ny, nz, nc = (grid.size[name] for name in "xyzc")
    count = nx * ny * nc
    rows = pieces[0][0].shape[3]
    copies = []
    at = 0
    for which in range(2):
        half = pieces[which][0].shape[4]
        start = 0
        for matrix, width in enumerate(widths):
            low, high = max(at, start), min(at + half, start + width)
            if low < high:
                copies.append((which, low - at, matrix, low - start, high - low))
            start += width
        at += half

    def kernel(where, *refs):
        sources = refs[: 2 * nc]
        targets = refs[2 * nc : 2 * nc + len(widths)]
        sems = refs[-1]
        started = []
        for which, source_at, matrix, target_at, width in copies:
            for number, (i, j, k) in enumerate(grid.blocks()):
                for z in range(nz):
                    a, b = (j, i) if which == 0 else (i, j)
                    started.append(
                        pltpu.make_async_copy(
                            sources[which * nc + k].at[a, b, z, :, pl.ds(source_at, width)],
                            targets[matrix].at[
                                where[count + z], where[number], :, pl.ds(target_at, width)
                            ],
                            sems.at[len(started)],
                        )
                    )
        for copy in started:
            copy.start()
        for copy in started:
            copy.wait()

    out = pl.pallas_call(
        kernel,
        out_shape=[jax.ShapeDtypeStruct((nz, count, rows, width), BF) for width in widths],
        in_specs=[pl.BlockSpec(memory_space=pltpu.SMEM)]
        + [pl.BlockSpec(memory_space=pl.ANY)] * (2 * nc),
        out_specs=[pl.BlockSpec(memory_space=pltpu.VMEM)] * len(widths),
        scratch_shapes=[pltpu.SemaphoreType.DMA((len(copies) * count * nz,))],
        compiler_params=pltpu.CompilerParams(vmem_limit_bytes=40 * 2**20),
    )(positions, *pieces[0], *pieces[1])
    return [a.reshape(nz * count * rows, a.shape[3]) for a in out]


def matmul(left, right):
    return jnp.dot(left, right, preferred_element_type=F32)


def outer_right(left, right):
    return lax.dot_general(left, right, (((1,), (1,)), ((), ())), preferred_element_type=F32)


def norm_forward(resid, gain, bias):
    center = resid - jnp.mean(resid, axis=-1, keepdims=True)
    scale = lax.rsqrt(jnp.mean(center * center, axis=-1, keepdims=True) + EPSILON)
    normal = center * scale
    return normal * gain + bias, normal, scale


def norm_backward(dy, normal, scale, gain):
    dn = dy * gain
    grad = (
        dn
        - jnp.mean(dn, axis=-1, keepdims=True)
        - normal * jnp.mean(dn * normal, axis=-1, keepdims=True)
    ) * scale
    return grad, jnp.sum(dy * normal, axis=0), jnp.sum(dy, axis=0)


def turn(grid, positions, left):
    z, count = grid.size["z"], len(grid.blocks())
    rows = left.shape[1] // grid.total
    turned = left.T.reshape(z, count, rows, left.shape[0])
    out = {}
    for n, key in enumerate(grid.blocks()):
        for k in range(z):
            out[key + (k,)] = lax.dynamic_slice(
                turned, (positions[count + k], positions[n], 0, 0), (1, 1, rows, left.shape[0])
            )[0]
    return out


def weight_grad(grid, products):
    x, y, z, c = (grid.size[name] for name in "xyzc")

    def product(part, keys):
        outs = []
        for left, right in part:
            rows = jnp.concatenate([left[key] for key in keys], axis=0)
            tokens = rows.shape[2]
            got = matmul(rows.reshape(-1, tokens), right)
            outs.append(got.reshape(len(keys), rows.shape[1], right.shape[1]))
        return outs[0] if len(outs) == 1 else jnp.concatenate(outs, axis=-1)

    def group(part, first, then):
        def keys(one, core):
            out = []
            for two in range(grid.size[then]):
                i, j = (one, two) if first == "x" else (two, one)
                out += [(i, j, core, k) for k in range(z)]
            return out

        away = [product(part, [b for one in range(grid.size[first]) for b in keys(one, k)]) for k in range(1, c)]
        kept = [product(part, keys(one, 0)) for one in range(grid.size[first])]
        for k in range(1, c):
            got = grid.exchange(away[k - 1].astype(BF), "c", k)
            got = got.reshape((grid.size[first],) + kept[0].shape).astype(F32)
            kept = [a + got[n] for n, a in enumerate(kept)]
        kept = grid.scatter(kept, first)
        kept = kept.reshape((grid.size[then], z) + kept.shape[1:])
        return grid.scatter([kept[n] for n in range(grid.size[then])], then)

    one = group(products[0], "x", "y")
    two = group(products[1], "y", "x")
    both = jnp.concatenate([one, two], axis=-1)
    return grid.scatter([both[k] for k in range(z)], "z")


PAIR = 2 * HD
BLOCK = 128
DIMS_NT = (((1,), (1,)), ((), ()))
DIMS_TN = (((0,), (0,)), ((), ()))


def head_of(array, which, scale=None):
    lane = lax.broadcasted_iota(jnp.int32, array.shape, 1)
    mine = (lane < HD) if which == 0 else (lane >= HD)
    out = jnp.where(mine, array.astype(F32), 0.0)
    return (out if scale is None else out * scale).astype(BF)


def probabilities(q, k, bias):
    scores = lax.dot_general(q, k, DIMS_NT, preferred_element_type=F32) + bias
    exponent = jnp.exp(scores - jnp.max(scores, axis=-1, keepdims=True))
    return exponent * (1.0 / jnp.sum(exponent, axis=-1, keepdims=True))


def pair_forward(q, k, v, bias):
    lane = lax.broadcasted_iota(jnp.int32, q.shape, 1)
    outs = []
    for which in range(2):
        probs = probabilities(head_of(q, which, SCORE_SCALE), k, bias)
        outs.append(matmul(probs.astype(BF), v))
    return jnp.where(lane < HD, outs[0], outs[1]).astype(BF)


def pair_backward(q, k, v, grad, bias):
    gq, gk, gv = 0.0, 0.0, 0.0
    for which in range(2):
        q_one = head_of(q, which, SCORE_SCALE)
        g_one = head_of(grad, which)
        probs = probabilities(q_one, k, bias)
        dprob = lax.dot_general(g_one, v, DIMS_NT, preferred_element_type=F32)
        delta = jnp.sum(probs * dprob, axis=-1, keepdims=True)
        dscore = (probs * (dprob - delta)).astype(BF)
        gq = gq + matmul(dscore, head_of(k, which, SCORE_SCALE))
        gk = gk + lax.dot_general(dscore, q_one, DIMS_TN, preferred_element_type=F32)
        gv = gv + lax.dot_general(probs.astype(BF), g_one, DIMS_TN, preferred_element_type=F32)
    return gq, gk, gv


def self_bias(column, row, pad):
    length = column.shape[0]
    at_q = lax.broadcasted_iota(jnp.int32, (length, length), 0)
    at_k = lax.broadcasted_iota(jnp.int32, (length, length), 1)
    live = (column == row) & (at_q >= at_k) & ((at_k < length - pad) | (at_q == at_k))
    return jnp.where(live, 0.0, MASKED)


def pair_spec(array):
    return pl.BlockSpec((array.shape[0], PAIR), lambda n: (0, n))


def whole_spec(array):
    return pl.BlockSpec(array.shape, lambda n: (0,) * array.ndim)


def self_forward(pad, column, row, q, k, v):
    length, width = q.shape

    def kernel(pad_ref, column_ref, row_ref, q_ref, k_ref, v_ref, out_ref, bias_ref):
        @pl.when(pl.program_id(0) == 0)
        def _():
            bias_ref[...] = self_bias(column_ref[...], row_ref[...], pad_ref[0])

        for start in range(0, length, BLOCK):
            mine, seen = pl.ds(start, BLOCK), pl.ds(0, start + BLOCK)
            out_ref[mine, :] = pair_forward(
                q_ref[mine, :], k_ref[seen, :], v_ref[seen, :], bias_ref[mine, seen]
            )

    return pl.pallas_call(
        kernel,
        grid=(width // PAIR,),
        out_shape=jax.ShapeDtypeStruct(q.shape, BF),
        in_specs=[pl.BlockSpec(memory_space=pltpu.SMEM), whole_spec(column), whole_spec(row)]
        + [pair_spec(q)] * 3,
        out_specs=pair_spec(q),
        scratch_shapes=[pltpu.VMEM((length, length), F32)],
        compiler_params=pltpu.CompilerParams(vmem_limit_bytes=40 * 2**20),
    )(pad, column, row, q, k, v)


def self_backward(pad, column, row, q, k, v, grad):
    length, width = q.shape

    def kernel(pad_ref, column_ref, row_ref, q_ref, k_ref, v_ref, g_ref, gq_ref, gk_ref, gv_ref, bias_ref, k_sum, v_sum):
        @pl.when(pl.program_id(0) == 0)
        def _():
            bias_ref[...] = self_bias(column_ref[...], row_ref[...], pad_ref[0])

        for start in reversed(range(0, length, BLOCK)):
            mine, seen = pl.ds(start, BLOCK), pl.ds(0, start + BLOCK)
            gq, gk, gv = pair_backward(
                q_ref[mine, :], k_ref[seen, :], v_ref[seen, :], g_ref[mine, :], bias_ref[mine, seen]
            )
            gq_ref[mine, :] = gq.astype(BF)
            if start + BLOCK == length:
                k_sum[...] = gk
                v_sum[...] = gv
            else:
                k_sum[seen, :] += gk
                v_sum[seen, :] += gv
        gk_ref[...] = k_sum[...].astype(BF)
        gv_ref[...] = v_sum[...].astype(BF)

    return pl.pallas_call(
        kernel,
        grid=(width // PAIR,),
        out_shape=[jax.ShapeDtypeStruct(q.shape, BF)] * 3,
        in_specs=[pl.BlockSpec(memory_space=pltpu.SMEM), whole_spec(column), whole_spec(row)]
        + [pair_spec(q)] * 4,
        out_specs=[pair_spec(q)] * 3,
        scratch_shapes=[pltpu.VMEM((length, length), F32)] + [pltpu.VMEM((length, PAIR), F32)] * 2,
        compiler_params=pltpu.CompilerParams(vmem_limit_bytes=40 * 2**20),
    )(pad, column, row, q, k, v, grad)


def windows(total):
    return sorted({min(512, total), min(640, total), total})


def choose_window(segment, ids):
    total = ids.shape[0]
    at = jnp.arange(total, dtype=jnp.int32)
    live = (ids >= segment[0]) & (ids <= segment[-1])
    low = jnp.min(jnp.where(live, at, total))
    high = jnp.max(jnp.where(live, at + 1, 0))
    choice, starts, rows = jnp.int32(0), [], []
    for size in windows(total):
        start = jnp.clip(low // 16 * 16, 0, total - size)
        starts.append(start)
        rows.append(lax.dynamic_slice(ids, (start,), (size,)).reshape(1, size))
        choice = choice + (high - start > size).astype(jnp.int32)
    return jnp.stack([choice] + starts), rows


def on_window(window_ref, total, run):
    for n, size in enumerate(windows(total)):
        @pl.when(window_ref[0] == n)
        def _():
            run(n, size, pl.ds(pl.multiple_of(window_ref[1 + n], 16), size))


def cross_forward(window, column, rows, q, k, v):
    length, width = q.shape
    total = k.shape[0]

    def kernel(window_ref, column_ref, *refs):
        row_refs = refs[: len(rows)]
        q_ref, k_ref, v_ref, out_ref, bias_ref = refs[len(rows) :]

        def run(n, size, seen):
            @pl.when(pl.program_id(0) == 0)
            def _():
                bias_ref[:, :size] = jnp.where(column_ref[...] == row_refs[n][...], 0.0, MASKED)

            for start in range(0, length, BLOCK):
                mine = pl.ds(start, BLOCK)
                out_ref[mine, :] = pair_forward(
                    q_ref[mine, :], k_ref[seen, :], v_ref[seen, :], bias_ref[mine, :size]
                )

        on_window(window_ref, total, run)

    return pl.pallas_call(
        kernel,
        grid=(width // PAIR,),
        out_shape=jax.ShapeDtypeStruct(q.shape, BF),
        in_specs=[pl.BlockSpec(memory_space=pltpu.SMEM), whole_spec(column)]
        + [whole_spec(row) for row in rows]
        + [pair_spec(q), pair_spec(k), pair_spec(v)],
        out_specs=pair_spec(q),
        scratch_shapes=[pltpu.VMEM((length, total), F32)],
        compiler_params=pltpu.CompilerParams(vmem_limit_bytes=40 * 2**20),
    )(window, column, *rows, q, k, v)


def cross_backward(window, column, rows, q, k, v, grad):
    length, width = q.shape
    total = k.shape[0]

    def kernel(window_ref, column_ref, *refs):
        row_refs = refs[: len(rows)]
        q_ref, k_ref, v_ref, g_ref, gq_ref, gk_ref, gv_ref, bias_ref, k_sum, v_sum = refs[len(rows) :]

        def run(n, size, seen):
            @pl.when(pl.program_id(0) == 0)
            def _():
                bias_ref[:, :size] = jnp.where(column_ref[...] == row_refs[n][...], 0.0, MASKED)

            if size < total:
                gk_ref[...] = jnp.zeros_like(gk_ref)
                gv_ref[...] = jnp.zeros_like(gv_ref)
            for start in range(0, length, BLOCK):
                mine = pl.ds(start, BLOCK)
                gq, gk, gv = pair_backward(
                    q_ref[mine, :], k_ref[seen, :], v_ref[seen, :], g_ref[mine, :], bias_ref[mine, :size]
                )
                gq_ref[mine, :] = gq.astype(BF)
                if start == 0:
                    k_sum[:size, :] = gk
                    v_sum[:size, :] = gv
                else:
                    k_sum[:size, :] += gk
                    v_sum[:size, :] += gv
            gk_ref[seen, :] = k_sum[:size, :].astype(BF)
            gv_ref[seen, :] = v_sum[:size, :].astype(BF)

        on_window(window_ref, total, run)

    return pl.pallas_call(
        kernel,
        grid=(width // PAIR,),
        out_shape=[jax.ShapeDtypeStruct(a.shape, BF) for a in (q, k, v)],
        in_specs=[pl.BlockSpec(memory_space=pltpu.SMEM), whole_spec(column)]
        + [whole_spec(row) for row in rows]
        + [pair_spec(q), pair_spec(k), pair_spec(v), pair_spec(q)],
        out_specs=[pair_spec(q), pair_spec(k), pair_spec(v)],
        scratch_shapes=[pltpu.VMEM((length, total), F32)] + [pltpu.VMEM((total, PAIR), F32)] * 2,
        compiler_params=pltpu.CompilerParams(vmem_limit_bytes=40 * 2**20),
    )(window, column, *rows, q, k, v, grad)


def body(
    grid,
    hidden,
    memory,
    cotangent,
    dec_segment,
    pad_length,
    mem_segment,
    self_query,
    self_key,
    self_value,
    self_output,
    norm1_gain,
    norm1_bias,
    cross_query,
    cross_key,
    cross_value,
    cross_output,
    norm2_gain,
    norm2_bias,
    ffn_up,
    ffn_down,
    norm3_gain,
    norm3_bias,
):
    width = hidden.shape[1]
    mem_rows = memory.shape[0]
    own_rows = self_query.shape[0]
    positions = grid.positions()
    me = lax.axis_index("dp") * lax.axis_size("ctx") + lax.axis_index("ctx")
    own_width = norm1_gain.shape[0]

    vectors = [norm1_gain, norm1_bias, norm2_gain, norm2_bias, norm3_gain, norm3_bias]
    vectors = jnp.pad(jnp.stack(vectors, axis=1).astype(BF), ((0, 0), (0, 122)))
    pieces = grid.gather_weights(
        jnp.concatenate([self_query, self_key, self_value, self_output, vectors], axis=1), 2 * width
    )
    w_sq, w_sk, w_sv, w_so, vectors = assemble(grid, positions, pieces, [width] * 4 + [128])
    vectors = vectors[:, :6].T.astype(F32)
    gain1, bias1, gain2, bias2, gain3, bias3 = [vectors[n] for n in range(6)]

    ny, nc = grid.size["y"], grid.size["c"]
    here = grid.here()

    def group_all(array):
        found = jnp.stack(
            [jnp.stack(grid.gather(a, "c")) for a in grid.gather(array, "y")]
        )
        rows = [
            lax.dynamic_index_in_dim(
                lax.dynamic_index_in_dim(found, n ^ here["y"], 0, keepdims=False),
                m ^ here["c"],
                0,
                keepdims=False,
            )
            for n in range(ny)
            for m in range(nc)
        ]
        return jnp.concatenate(rows, axis=0)

    mem_all = group_all(memory)
    ids_all = group_all(mem_segment)

    pieces = grid.gather_weights(
        jnp.concatenate([cross_query, cross_key, cross_value, cross_output], axis=1), 2 * width
    )
    w_cq, w_ck, w_cv, w_co = assemble(grid, positions, pieces, [width] * 4)
    ffn = ffn_up.shape[1]
    (w_up,) = assemble(grid, positions, grid.gather_weights(ffn_up, ffn // 2), [ffn])
    (w_down,) = assemble(grid, positions, grid.gather_weights(ffn_down, width // 2), [width])

    segment = dec_segment.reshape(-1)
    column, row = segment.reshape(-1, 1), segment.reshape(1, -1)
    q = matmul(hidden, w_sq).astype(BF)
    k = matmul(hidden, w_sk).astype(BF)
    v = matmul(hidden, w_sv).astype(BF)
    self_att = self_forward(pad_length, column, row, q, k, v)
    first, normal1, scale1 = norm_forward(
        ALPHA_RES * hidden.astype(F32) + matmul(self_att, w_so), gain1, bias1
    )
    first_low = first.astype(BF)
    window, rows = choose_window(segment, ids_all)
    cq = matmul(first_low, w_cq).astype(BF)
    mk = matmul(mem_all, w_ck).astype(BF)
    mv = matmul(mem_all, w_cv).astype(BF)
    cross_att = cross_forward(window, column, rows, cq, mk, mv)
    second, normal2, scale2 = norm_forward(
        ALPHA_RES * first + matmul(cross_att, w_co), gain2, bias2
    )
    second_low = second.astype(BF)
    pre = matmul(second_low, w_up)
    erf = 1.0 + lax.erf(pre * (0.5**0.5))
    act = (0.5 * pre * erf).astype(BF)
    slope = 0.5 * erf + pre * jnp.exp(-0.5 * pre * pre) * 0.3989422804014327
    third, normal3, scale3 = norm_forward(ALPHA_RES * second + matmul(act, w_down), gain3, bias3)

    def turned(left):
        return turn(grid, positions, left)

    grad_third, g_gain3, g_bias3 = norm_backward(cotangent.astype(F32), normal3, scale3, gain3)
    third_low = grad_third.astype(BF)
    grad_pre = (slope * outer_right(third_low, w_down)).astype(BF)
    act_t = turned(act)
    out_down = weight_grad(
        grid, ([(act_t, third_low[:, : width // 2])], [(act_t, third_low[:, width // 2 :])])
    )
    grad_second = ALPHA_RES * grad_third + outer_right(grad_pre, w_up)
    second_t = turned(second_low)
    out_up = weight_grad(
        grid, ([(second_t, grad_pre[:, : ffn // 2])], [(second_t, grad_pre[:, ffn // 2 :])])
    )
    grad_mid, g_gain2, g_bias2 = norm_backward(grad_second, normal2, scale2, gain2)
    mid_low = grad_mid.astype(BF)
    grad_catt = outer_right(mid_low, w_co).astype(BF)
    grad_cq, grad_mk, grad_mv = cross_backward(window, column, rows, cq, mk, mv, grad_catt)
    mem_t = turned(mem_all)
    out_cross = weight_grad(
        grid,
        (
            [(turned(cross_att), mid_low), (turned(first_low), grad_cq)],
            [(mem_t, grad_mk), (mem_t, grad_mv)],
        ),
    )
    grad_mem = outer_right(grad_mk, w_ck) + outer_right(grad_mv, w_cv)
    grad_mem = grad_mem.reshape(ny, nc, mem_rows, width)
    grad_mem = grid.scatter(
        [lax.dynamic_index_in_dim(grad_mem, n ^ here["c"], 1, keepdims=False) for n in range(nc)], "c"
    )
    grad_mem = grid.scatter(
        [lax.dynamic_index_in_dim(grad_mem, n ^ here["y"], 0, keepdims=False) for n in range(ny)], "y"
    )
    grad_first = ALPHA_RES * grad_mid + outer_right(grad_cq, w_cq)
    grad_res, g_gain1, g_bias1 = norm_backward(grad_first, normal1, scale1, gain1)
    res_low = grad_res.astype(BF)
    grad_satt = outer_right(res_low, w_so).astype(BF)
    grad_q, grad_k, grad_v = self_backward(pad_length, column, row, q, k, v, grad_satt)
    hidden_t = turned(hidden)
    out_self = weight_grad(
        grid,
        (
            [(turned(self_att), res_low), (hidden_t, grad_q)],
            [(hidden_t, grad_k), (hidden_t, grad_v)],
        ),
    )
    grad_in = (
        ALPHA_RES * grad_res
        + outer_right(grad_q, w_sq)
        + outer_right(grad_k, w_sk)
        + outer_right(grad_v, w_sv)
    )
    out_so, out_sq, out_sk, out_sv = [out_self[:, n * width : (n + 1) * width] for n in range(4)]
    out_co, out_cq, out_ck, out_cv = [out_cross[:, n * width : (n + 1) * width] for n in range(4)]

    def own_part(vectors):
        total = lax.psum(jnp.stack(vectors), BOTH).reshape(-1, grid.total, own_width)
        return lax.dynamic_index_in_dim(total, me, 1, keepdims=False)

    late = own_part([g_gain2, g_bias2, g_gain3, g_bias3])
    last = own_part([g_gain1, g_bias1])
    return (
        third.astype(BF),
        grad_in,
        grad_mem,
        out_sq,
        out_sk,
        out_sv,
        out_so,
        last[0],
        last[1],
        out_cq,
        out_ck,
        out_cv,
        out_co,
        late[0],
        late[1],
        out_up,
        out_down,
        late[2],
        late[3],
    )


def solution(mesh):
    grid = Grid(mesh.shape["dp"], mesh.shape["ctx"])
    row, flat = P(BOTH, None), P(BOTH)
    block = (row,) * 4 + (flat,) * 2
    return jax.shard_map(
        functools.partial(body, grid),
        mesh=mesh,
        in_specs=(row, row, row, row, flat, flat) + block + block + (row, row, flat, flat),
        out_specs=(row, row, row) + block + block + (row, row, flat, flat),
        check_vma=False,
    )
```

time: 2740 us -> 1010 us (0.37)
  waiting for transfers between devices: 1940 us -> 299 us
  matrix products: 329 us -> 142 us
  Pallas kernels: 0 us -> 129 us
  local copies, waits for them, and re-layouts: 292 us -> 204 us
  starting transfers between devices: 1.79 us -> 75.7 us
  blocking collectives: 101 us -> 41.3 us
  other arithmetic: 42 us -> 89 us
    reduce_scatter x7 -> x0, waiting for transfers between devices: 756 us -> none  [the longest x1 200 us: body(): lax.psum_scatter(grad_up, ('dp', 'ctx'), scatter_dimension=0, tiled=True)]
    unnamed x30 -> x0, waiting for transfers between devices: 655 us -> none
    all_gather x12 -> x0, waiting for transfers between devices: 493 us -> none  [the longest x1 75.4 us: ffn_weights(): lax.all_gather(ffn_up, ('dp', 'ctx'), axis=0, tiled=True)]
    ppermute x0 -> x80, waiting for transfers between devices: none -> 299 us  [exchange(): return lax.ppermute(array, BOTH, pairs)]
    dot_general x44 -> x46, matrix products: 283 us -> 103 us  [matmul(): return jnp.dot(left, right, preferred_element_type=F32)]
    dynamic_update_slice x8 -> x0, local copies, waits for them, and re-layouts: 161 us -> none  [the longest x4 161 us: body(): lax.map(partial_out, (query_blocks, id_blocks, cross_lse))]
    pallas_call x0 -> x8, Pallas kernels: none -> 129 us  [the longest x1 29.5 us: cross_backward(): pl.pallas_call(kernel, grid=(width // PAIR,), out_shape=[jax.ShapeDtypeSt...]
    unnamed x2 -> x0, blocking collectives: 80.9 us -> none
  transfers between devices with their start and end apart: 25 -> 80, of which waited for: 23 -> 32; matrix products, arithmetic and copies ran while one was open for 17% -> 32% of each run, Pallas kernels for 0% -> 2%
where the time goes in v1:
time: 1010 us; the launch traced here: 989 us
  waiting for transfers between devices  299 us (30%)
  local copies, waits for them, and re-layouts  204 us (20%)
  matrix products  142 us (14%)
  Pallas kernels  129 us (13%)
  other arithmetic  89 us (9%)
  starting transfers between devices  75.7 us (7%)
  blocking collectives  41.3 us (4%)
    ppermute x80, waiting for transfers between devices, exchange(): return lax.ppermute(array, BOTH, pairs)  299 us
    unnamed x431, local copies, waits for them, and re-layouts  119 us
    dot_general x46, matrix products, matmul(): return jnp.dot(left, right, preferred_element_type=F32)  103 us
    ppermute x80, starting transfers between devices, exchange(): return lax.ppermute(array, BOTH, pairs)  75.7 us
    dynamic_slice x33, local copies, waits for them, and re-layouts, turn(): lax.dynamic_slice(turned, (positions[count + k], positions[n], 0, 0), (1,...  52.9 us
    psum x1, blocking collectives, own_part(): lax.psum(jnp.stack(vectors), BOTH).reshape(-1, grid.total, own_width)  41.3 us
    dot_general x10, matrix products, outer_right(): lax.dot_general(left, right, (((1,), (1,)), ((), ())), preferred_element_...  39.9 us
    pallas_call x1, Pallas kernels, cross_backward(): pl.pallas_call(kernel, grid=(width // PAIR,), out_shape=[jax.ShapeDtypeSt...  29.5 us
  transfers between devices with their start and end apart: 80, of which 32 were waited for; matrix products, arithmetic and copies ran while one was open for 32% of the time, Pallas kernels for 2%

profile of v1, /device:TPU:8, one launch (start us, length us, event | category | flops | bytes accessed | tf_op | source)
XLA Modules:
  0.0 988.9 jit_solution(7389091263671070286)
XLA Ops:
  42.6 2.6 collective-permute-done.14
  46.6 20.5 %collective-permute-done.13 = bf16[32,4096]{1,0:T(8,128)(2,1)} collective-permute-done((bf16[32,4096]{1,0:T(8,128)(2,1)}, bf16[32,4096]{1,0:T(8,128)(2,1)}, u32[]{:S(2)}, u32[]{:S(2)}) %collective-permute-start.13) | collective-permute-done | bytes 262176 | tf_op jit(solution)/shard_map/ppermute | solution.py:58
  67.1 3.4 collective-permute-start.34
  71.8 19.1 %collective-permute-done.35 = bf16[128,1024]{1,0:T(8,128)(2,1)S(1)} collective-permute-done((bf16[128,1024]{1,0:T(8,128)(2,1)S(1)}, bf16[128,1024]{1,0:T(8,128)(2,1)S(1)}, u32[]{:S(2)}, u32[]{:S(2)}) %collective-permute-start.35) | collective-permute-done | bytes 262176 | tf_op jit(solution)/shard_map/ppermute | solution.py:58
  90.8 4.3 collective-permute-done.34
  103.2 7.6 collective-permute-done.27
  112.4 8.7 collective-permute-done.30
  123.7 8.7 collective-permute-done.18
  137.8 28.3 %collective-permute-done.39 = bf16[4,128,512]{2,1,0:T(8,128)(2,1)S(1)} collective-permute-done((bf16[4,128,512]{2,1,0:T(8,128)(2,1)S(1)}, bf16[4,128,512]{2,1,0:T(8,128)(2,1)S(1)}, u32[]{:S(2)}, u32[]{:S(2)}) %collective-permute-start.39) | collective-permute-done | bytes 524320 | tf_op jit(solution)/shard_map/ppermute | solution.py:58
  170.6 7.5 collective-permute-done.6
  184.2 16.3 %collective-permute-done.16 = bf16[2,4,32,2048]{3,2,1,0:T(8,128)(2,1)S(1)} collective-permute-done((bf16[2,4,32,2048]{3,2,1,0:T(8,128)(2,1)S(1)}, bf16[2,4,32,2048]{3,2,1,0:T(8,128)(2,1)S(1)}, u32[]{:S(2)}, u32[]{:S(2)}) %collective-permute-start.16) | collective-permute-done | bytes 1048608 | tf_op jit(solution)/shard_map/ppermute | solution.py:58
  202.6 20.3 %collective-permute-done.37 = bf16[2,4,128,512]{3,2,1,0:T(8,128)(2,1)S(1)} collective-permute-done((bf16[2,4,128,512]{3,2,1,0:T(8,128)(2,1)S(1)}, bf16[2,4,128,512]{3,2,1,0:T(8,128)(2,1)S(1)}, u32[]{:S(2)}, u32[]{:S(2)}) %collective-permute-start.37) | collective-permute-done | bytes 1048608 | tf_op jit(solution)/shard_map/ppermute | solution.py:58
  227.0 3.9 copy.396
  239.3 5.8 collective-permute-done.4
  245.1 3.9 collective-permute-done.7
  252.0 2.8 pad_maximum_fusion.4.refs_2_
  262.6 7.6 shard_map.361
  270.2 5.1 shard_map.359
  275.5 9.0 shard_map.362
  286.8 3.7 convolution_convert_fusion.2.refs_5_
  290.5 5.2 shard_map.357
  306.5 23.6 %shard_map.358 = bf16[512,1024]{1,0:T(8,128)(2,1)S(1)} custom-call(s32[1]{0:T(128)S(6)} %copy.715.pad_ref, s32[512,1]{1,0:T(8,128)S(1)} %copy.386.column_ref, s32[1,512]{1,0:T(1,128)S(1)} %copy-done.12, bf16[512,1024]{1,0:T(8,128)(2,1)S(1)} %fusion.53.q_ref, bf16[512,1024]{1,0:T(8,128)(2,1)S(1)} %copy-done.5, bf16[512,1024]{1,0:T(8,128)(2,1)S(1)} %copy-done.7), custom_call_target="tpu_custom_call" | custom-call | tf_op jit(solution)/shard_map/pallas_call | solution.py:296
  334.7 25.9 %shard_map.360 = bf16[512,1024]{1,0:T(8,128)(2,1)S(1)} custom-call(s32[4]{0:T(128)S(1)} %pad_add_fusion.1.window_ref, s32[512,1]{1,0:T(8,128)S(1)} %copy.386.column_ref, s32[1,512]{1,0:T(1,128)S(1)} %bitcast.1356, s32[1,640]{1,0:T(1,128)S(1)} %reshape.455.refs_1_, s32[1,1024]{1,0:T(1,128)S(1)} %bitcast.1353, ...), custom_call_target="tpu_custom_call" | custom-call | tf_op jit(solution)/shard_map/pallas_call | solution.py:390
  362.5 10.5 %multiply_convert_fusion = (bf16[512,4096]{1,0:T(8,128)(2,1)}, f32[512,4096]{1,0:T(8,128)}) fusion(bf16[1024,4096]{1,0:T(8,128)(2,1)} %bitcast.1373, f32[512,1024]{1,0:T(8,128)S(1)} %get-tuple-element.387, f32[1024]{0:T(1024)S(1)} %bitcast.1558, f32[1024]{0:T(1024)S(1)} %bitcast.1548, f32[512]{0:T(512)S(1)} %add_rsqrt_fusion.1, ...), kind=kOutput, calls=%fused_computation.7 | convolution fusion | flops 4308074496 | bytes 23080960 | tf_op jit(solution)/shard_map/dot_general | solution.py:150
  373.0 7.2 fusion.317
  384.2 11.9 %fusion.5 = bf16[512,4096]{1,0:T(8,128)(2,1)} fusion(f32[512,4096]{1,0:T(8,128)} %get-tuple-element.389, bf16[512,1024]{1,0:T(8,128)(2,1)S(1)} %get-tuple-element.103, bf16[4096,1024]{1,0:T(8,128)(2,1)} %bitcast.1375), kind=kOutput, calls=%fused_computation.6 | convolution fusion | flops 4315938816 | bytes 22020096 | tf_op jit(solution)/shard_map/dot_general | solution.py:154
  396.1 11.0 %multiply_add_fusion.1 = f32[512,1024]{1,0:T(8,128)} fusion(bf16[512,4096]{1,0:T(8,128)(2,1)} %fusion.5, bf16[1024,4096]{1,0:T(8,128)(2,1)} %bitcast.1374, f32[512]{0:T(512)S(1)} %broadcast_multiply_fusion.4, f32[512]{0:T(512)S(1)} %add_rsqrt_fusion, f32[512,1024]{1,0:T(8,128)S(1)} %get-tuple-element.391, f32[512]{0:T(512)S(1)} %broadcast_multiply_fusion.6, ...), kind=kOutput, calls=%fused_computation.114 | convolution fusion | flops 4300210176 | bytes 17838080 | tf_op jit(solution)/shard_map/dot_general | solution.py:154
  407.1 4.1 multiply_reduce_fusion
  415.5 29.5 %shard_map.363 = (bf16[512,1024]{1,0:T(8,128)(2,1)S(1)}, bf16[1024,1024]{1,0:T(8,128)(2,1)S(1)}, bf16[1024,1024]{1,0:T(8,128)(2,1)S(1)}) custom-call(s32[4]{0:T(128)S(1)} %pad_add_fusion.1.window_ref, s32[512,1]{1,0:T(8,128)S(1)} %copy.386.column_ref, s32[1,512]{1,0:T(1,128)S(1)} %bitcast.1357, s32[1,640]{1,0:T(1,128)S(1)} %reshape.455.refs_1_, ...), custom_call_target="tpu_custom_call" | custom-call | tf_op jit(solution)/shard_map/pallas_call | solution.py:436
  453.0 23.0 %shard_map.364 = (bf16[512,1024]{1,0:T(8,128)(2,1)S(1)}, bf16[512,1024]{1,0:T(8,128)(2,1)S(1)}, bf16[512,1024]{1,0:T(8,128)(2,1)S(1)}) custom-call(s32[1]{0:T(128)S(6)} %copy.715.pad_ref, s32[512,1]{1,0:T(8,128)S(1)} %copy.386.column_ref, s32[1,512]{1,0:T(1,128)S(1)} %copy-done.12, bf16[512,1024]{1,0:T(8,128)(2,1)S(1)} %copy-done.4, ...), custom_call_target="tpu_custom_call" | custom-call | tf_op jit(solution)/shard_map/pallas_call | solution.py:331
  476.0 2.6 fusion.319
  487.8 2.4 fusion.320
  490.1 3.4 fusion.50
  493.6 3.5 fusion.47
  503.9 2.4 convolution_add_fusion
  509.6 2.4 copy.392
  583.6 2.6 convolution_convert_fusion.1
  586.4 2.5 convolution_convert_fusion
  590.2 11.2 %constant_dynamic-slice_fusion.6 = (bf16[1,1,128,512]{2,1,0,3:T(2,128)(2,1)}, bf16[1,1,128,512]{2,1,0,3:T(2,128)(2,1)}, bf16[1,1,128,512]{2,1,0,3:T(2,128)(2,1)}...) fusion(bf16[4,8,128,512]{2,1,0,3:T(8,128)(2,1)S(1)} %bitcast.13, ...), kind=kLoop, calls=%fused_computation.605 | loop fusion | bytes 8388656 | tf_op jit(solution)/shard_map/dynamic_slice | solution.py:181
  622.0 3.3 fusion.121
  635.4 3.1 copy.681
  670.2 4.2 convolution_convert_fusion.5
  689.9 3.4 fusion.123
  698.4 41.3 %all-reduce.1 = (f32[2,32,32]{2,1,0:T(8,128)}, f32[4,32,32]{2,1,0:T(8,128)S(1)}) all-reduce(f32[2,32,32]{2,1,0:T(8,128)} %reshape.466, f32[4,32,32]{2,1,0:T(8,128)} %reshape.470), channel_id=1, replica_groups=mesh['dp'=8,'ctx'=4] {'dp','ctx'}, use_global_device_ids=true, to_apply=%region_16.17 | all-reduce | flops 6144 | bytes 49152 | tf_op jit(solution)/shard_map/psum | solution.py:603
  740.5 3.0 fusion.318
  746.9 2.3 collective-permute-start.43
  749.2 2.7 add_add_fusion
  751.9 8.6 collective-permute-done.43
  761.3 2.6 convolution_convert_fusion.4
  796.8 3.0 fusion.17
  812.0 36.5 %collective-permute-done.63 = bf16[8,32,2048]{2,1,0:T(8,128)(2,1)} collective-permute-done((bf16[8,32,2048]{2,1,0:T(8,128)(2,1)}, bf16[8,32,2048]{2,1,0:T(8,128)(2,1)}, u32[]{:S(2)}, u32[]{:S(2)}) %collective-permute-start.63) | collective-permute-done | bytes 1048608 | tf_op jit(solution)/shard_map/ppermute | solution.py:58
  860.8 10.0 %collective-permute-done.72 = bf16[8,128,512]{2,1,0:T(8,128)(2,1)} collective-permute-done((bf16[8,128,512]{2,1,0:T(8,128)(2,1)}, bf16[8,128,512]{2,1,0:T(8,128)(2,1)}, u32[]{:S(2)}, u32[]{:S(2)}) %collective-permute-start.72) | collective-permute-done | bytes 1048608 | tf_op jit(solution)/shard_map/ppermute | solution.py:58
  878.7 8.4 collective-permute-done.46
  889.7 8.7 collective-permute-done.55
  901.0 8.7 collective-permute-done.64
  909.8 2.9 collective-permute-start.50
  913.0 6.9 collective-permute-done.73
  927.4 22.3 %collective-permute-done.61 = bf16[32,4096]{1,0:T(8,128)(2,1)S(1)} collective-permute-done((bf16[32,4096]{1,0:T(8,128)(2,1)S(1)}, bf16[32,4096]{1,0:T(8,128)(2,1)S(1)}, u32[]{:S(2)}, u32[]{:S(2)}) %collective-permute-start.61) | collective-permute-done | bytes 262176 | tf_op jit(solution)/shard_map/ppermute | solution.py:58
  949.7 5.3 collective-permute-done.60
  956.0 4.3 collective-permute-start.78
  960.5 12.9 %collective-permute-done.70 = bf16[32,4096]{1,0:T(8,128)(2,1)S(1)} collective-permute-done((bf16[32,4096]{1,0:T(8,128)(2,1)S(1)}, bf16[32,4096]{1,0:T(8,128)(2,1)S(1)}, u32[]{:S(2)}, u32[]{:S(2)}) %collective-permute-start.70) | collective-permute-done | bytes 262176 | tf_op jit(solution)/shard_map/ppermute | solution.py:58
  973.4 4.2 collective-permute-done.69
  980.0 4.6 collective-permute-done.79
  984.6 3.1 collective-permute-done.78
  (780 shorter events, 390.3 us)
Async XLA Ops:
  0.7 36.0 %collective-permute-start.26 = (bf16[32,4096]{1,0:T(8,128)(2,1)}, bf16[32,4096]{1,0:T(8,128)(2,1)}, u32[]{:S(2)}, u32[]{:S(2)}) collective-permute-start(bf16[32,4096]{1,0:T(8,128)(2,1)} %param.40), channel_id=1, source_target_pairs={{0,24},{1,25},{2,26},{3,27},{4,28},{5,29},{6,30},{7,31},{8,16},{9,... | collective-permute-start | bytes 786440 | tf_op jit(solution)/shard_map/ppermute | solution.py:58
  2.3 35.5 %collective-permute-start.25 = (bf16[32,4096]{1,0:T(8,128)(2,1)}, bf16[32,4096]{1,0:T(8,128)(2,1)}, u32[]{:S(2)}, u32[]{:S(2)}) collective-permute-start(bf16[32,4096]{1,0:T(8,128)(2,1)} %param.40), channel_id=1, source_target_pairs={{0,16},{1,17},{2,18},{3,19},{4,20},{5,21},{6,22},{7,23},{8,24},{9,... | collective-permute-start | bytes 786440 | tf_op jit(solution)/shard_map/ppermute | solution.py:58
  3.4 36.0 %collective-permute-start.24 = (bf16[32,4096]{1,0:T(8,128)(2,1)}, bf16[32,4096]{1,0:T(8,128)(2,1)}, u32[]{:S(2)}, u32[]{:S(2)}) collective-permute-start(bf16[32,4096]{1,0:T(8,128)(2,1)} %param.40), channel_id=1, source_target_pairs={{0,8},{1,9},{2,10},{3,11},{4,12},{5,13},{6,14},{7,15},{8,0},{9,1},... | collective-permute-start | bytes 786440 | tf_op jit(solution)/shard_map/ppermute | solution.py:58
  27.4 39.7 %collective-permute-start.13 = (bf16[32,4096]{1,0:T(8,128)(2,1)}, bf16[32,4096]{1,0:T(8,128)(2,1)}, u32[]{:S(2)}, u32[]{:S(2)}) collective-permute-start(bf16[32,4096]{1,0:T(8,128)(2,1)} %constant_dynamic-update-slice_fusion.5), channel_id=1, source_target_pairs={{0,16},{1,17},{2,18},{3,19},{4,20},{5,21},{6,22},{7,23},{8,24},{9,... | collective-permute-start | bytes 786440 | tf_op jit(solution)/shard_map/ppermute | solution.py:58
  36.6 33.9 %collective-permute-start.12 = (bf16[32,4096]{1,0:T(8,128)(2,1)}, bf16[32,4096]{1,0:T(8,128)(2,1)S(1)}, u32[]{:S(2)}, u32[]{:S(2)}) collective-permute-start(bf16[32,4096]{1,0:T(8,128)(2,1)} %constant_dynamic-update-slice_fusion.5), channel_id=1, source_target_pairs={{0,8},{1,9},{2,10},{3,11},{4,12},{5,13},{6,14},{7,15},{8,0},{9,1},... | collective-permute-start | bytes 786440 | tf_op jit(solution)/shard_map/ppermute | solution.py:58
  37.8 58.1 %collective-permute-start.2 = (bf16[32,4224]{1,0:T(8,128)(2,1)S(1)}, bf16[32,4224]{1,0:T(8,128)(2,1)S(1)}, u32[]{:S(2)}, u32[]{:S(2)}) collective-permute-start(bf16[32,4224]{1,0:T(8,128)(2,1)S(1)} %constant_dynamic-update-slice_fusion), channel_id=1, source_target_pairs={{0,24},{1,25},{2,26},{3,27},{4,28},{5,29},{6,30},{7,31},{8,16},{9,... | collective-permute-start | bytes 811016 | tf_op jit(solution)/shard_map/ppermute | solution.py:58
  39.4 58.1 %collective-permute-start.1 = (bf16[32,4224]{1,0:T(8,128)(2,1)S(1)}, bf16[32,4224]{1,0:T(8,128)(2,1)S(1)}, u32[]{:S(2)}, u32[]{:S(2)}) collective-permute-start(bf16[32,4224]{1,0:T(8,128)(2,1)S(1)} %constant_dynamic-update-slice_fusion), channel_id=1, source_target_pairs={{0,16},{1,17},{2,18},{3,19},{4,20},{5,21},{6,22},{7,23},{8,24},{9,... | collective-permute-start | bytes 811016 | tf_op jit(solution)/shard_map/ppermute | solution.py:58
  45.2 45.7 %collective-permute-start.35 = (bf16[128,1024]{1,0:T(8,128)(2,1)S(1)}, bf16[128,1024]{1,0:T(8,128)(2,1)S(1)}, u32[]{:S(2)}, u32[]{:S(2)}) collective-permute-start(bf16[128,1024]{1,0:T(8,128)(2,1)S(1)} %copy-done.127), channel_id=1, source_target_pairs={{0,24},{1,25},{2,26},{3,27},{4,28},{5,29},{6,30},{7,31},{8,16},{9,... | collective-permute-start | bytes 786440 | tf_op jit(solution)/shard_map/ppermute | solution.py:58
  67.1 28.0 %collective-permute-start.34 = (bf16[128,1024]{1,0:T(8,128)(2,1)S(1)}, bf16[128,1024]{1,0:T(8,128)(2,1)S(1)}, u32[]{:S(2)}, u32[]{:S(2)}) collective-permute-start(bf16[128,1024]{1,0:T(8,128)(2,1)S(1)} %copy-done.127), channel_id=1, source_target_pairs={{0,16},{1,17},{2,18},{3,19},{4,20},{5,21},{6,22},{7,23},{8,24},{9,... | collective-permute-start | bytes 786440 | tf_op jit(solution)/shard_map/ppermute | solution.py:58
  70.5 24.6 %collective-permute-start.33 = (bf16[128,1024]{1,0:T(8,128)(2,1)S(1)}, bf16[128,1024]{1,0:T(8,128)(2,1)S(1)}, u32[]{:S(2)}, u32[]{:S(2)}) collective-permute-start(bf16[128,1024]{1,0:T(8,128)(2,1)S(1)} %copy-done.127), channel_id=1, source_target_pairs={{0,8},{1,9},{2,10},{3,11},{4,12},{5,13},{6,14},{7,15},{8,0},{9,1},... | collective-permute-start | bytes 786440 | tf_op jit(solution)/shard_map/ppermute | solution.py:58
  95.1 41.6 %collective-permute-start.22 = (bf16[256,1024]{1,0:T(8,128)(2,1)S(1)}, bf16[256,1024]{1,0:T(8,128)(2,1)S(1)}, u32[]{:S(2)}, u32[]{:S(2)}) collective-permute-start(bf16[256,1024]{1,0:T(8,128)(2,1)S(1)} %copy-done.116), channel_id=1, source_target_pairs={{0,2},{1,3},{2,0},{3,1},{4,6},{5,7},{6,4},{7,5},{8,10},{9,11},{10,... | collective-permute-start | bytes 1572872 | tf_op jit(solution)/shard_map/ppermute | solution.py:58
  97.5 23.6 %collective-permute-start.30 = (bf16[4,32,2048]{2,1,0:T(8,128)(2,1)S(1)}, bf16[4,32,2048]{2,1,0:T(8,128)(2,1)S(1)}, u32[]{:S(2)}, u32[]{:S(2)}) collective-permute-start(bf16[4,32,2048]{2,1,0:T(8,128)(2,1)S(1)} %get-tuple-element.315), channel_id=1, source_target_pairs={{0,2},{1,3},{2,0},{3,1},{4,6},{5,7},{6,4},{7,5},{8,10},{9,11},{10,... | collective-permute-start | bytes 1572872 | tf_op jit(solution)/shard_map/ppermute | solution.py:58
  102.5 29.8 %collective-permute-start.18 = (bf16[4,32,2048]{2,1,0:T(8,128)(2,1)S(1)}, bf16[4,32,2048]{2,1,0:T(8,128)(2,1)S(1)}, u32[]{:S(2)}, u32[]{:S(2)}) collective-permute-start(bf16[4,32,2048]{2,1,0:T(8,128)(2,1)S(1)} %get-tuple-element.307), channel_id=1, source_target_pairs={{0,2},{1,3},{2,0},{3,1},{4,6},{5,7},{6,4},{7,5},{8,10},{9,11},{10,... | collective-permute-start | bytes 1572872 | tf_op jit(solution)/shard_map/ppermute | solution.py:58
  110.8 23.1 %collective-permute-start.36 = (bf16[4,128,512]{2,1,0:T(8,128)(2,1)S(1)}, bf16[4,128,512]{2,1,0:T(8,128)(2,1)S(1)}, u32[]{:S(2)}, u32[]{:S(2)}) collective-permute-start(bf16[4,128,512]{2,1,0:T(8,128)(2,1)S(1)} %get-tuple-element.298), channel_id=1, source_target_pairs={{0,4},{1,5},{2,6},{3,7},{4,0},{5,1},{6,2},{7,3},{8,12},{9,13},{10,... | collective-permute-start | bytes 1572872 | tf_op jit(solution)/shard_map/ppermute | solution.py:58
  121.1 47.7 %collective-permute-start.28 = (bf16[2,4,32,2048]{3,2,1,0:T(8,128)(2,1)S(1)}, bf16[2,4,32,2048]{3,2,1,0:T(8,128)(2,1)S(1)}, u32[]{:S(2)}, u32[]{:S(2)}) collective-permute-start(bf16[2,4,32,2048]{3,2,1,0:T(8,128)(2,1)S(1)} %get-tuple-element.318), channel_id=1, source_target_pairs={{0,2},{1,3},{2,0},{3,1},{4,6},{5,7},{6,4},{7,5},{8,10},{9,11},{10,... | collective-permute-start | bytes 3145736 | tf_op jit(solution)/shard_map/ppermute | solution.py:58
  122.0 44.0 %collective-permute-start.39 = (bf16[4,128,512]{2,1,0:T(8,128)(2,1)S(1)}, bf16[4,128,512]{2,1,0:T(8,128)(2,1)S(1)}, u32[]{:S(2)}, u32[]{:S(2)}) collective-permute-start(bf16[4,128,512]{2,1,0:T(8,128)(2,1)S(1)} %get-tuple-element.297), channel_id=1, source_target_pairs={{0,2},{1,3},{2,0},{3,1},{4,6},{5,7},{6,4},{7,5},{8,10},{9,11},{10,... | collective-permute-start | bytes 1572872 | tf_op jit(solution)/shard_map/ppermute | solution.py:58
  132.4 34.8 %collective-permute-start.3 = (bf16[4,32,2048]{2,1,0:T(8,128)(2,1)S(1)}, bf16[4,32,2048]{2,1,0:T(8,128)(2,1)S(1)}, u32[]{:S(2)}, u32[]{:S(2)}) collective-permute-start(bf16[4,32,2048]{2,1,0:T(8,128)(2,1)S(1)} %pad_maximum_fusion.31), channel_id=1, source_target_pairs={{0,4},{1,5},{2,6},{3,7},{4,0},{5,1},{6,2},{7,3},{8,12},{9,13},{10,... | collective-permute-start | bytes 1572872 | tf_op jit(solution)/shard_map/ppermute | solution.py:58
  133.9 46.2 %collective-permute-start.31 = (bf16[2,4,32,2048]{3,2,1,0:T(8,128)(2,1)S(1)}, bf16[2,4,32,2048]{3,2,1,0:T(8,128)(2,1)S(1)}, u32[]{:S(2)}, u32[]{:S(2)}) collective-permute-start(bf16[2,4,32,2048]{3,2,1,0:T(8,128)(2,1)S(1)} %get-tuple-element.312), channel_id=1, source_target_pairs={{0,4},{1,5},{2,6},{3,7},{4,0},{5,1},{6,2},{7,3},{8,12},{9,13},{10,... | collective-permute-start | bytes 3145736 | tf_op jit(solution)/shard_map/ppermute | solution.py:58
  136.7 41.3 %collective-permute-start.6 = (bf16[4,32,2176]{2,1,0:T(8,128)(2,1)S(1)}, bf16[4,32,2176]{2,1,0:T(8,128)(2,1)S(1)}, u32[]{:S(2)}, u32[]{:S(2)}) collective-permute-start(bf16[4,32,2176]{2,1,0:T(8,128)(2,1)S(1)} %pad_maximum_fusion.28), channel_id=1, source_target_pairs={{0,2},{1,3},{2,0},{3,1},{4,6},{5,7},{6,4},{7,5},{8,10},{9,11},{10,... | collective-permute-start | bytes 1671176 | tf_op jit(solution)/shard_map/ppermute | solution.py:58
  167.2 33.3 %collective-permute-start.16 = (bf16[2,4,32,2048]{3,2,1,0:T(8,128)(2,1)S(1)}, bf16[2,4,32,2048]{3,2,1,0:T(8,128)(2,1)S(1)}, u32[]{:S(2)}, u32[]{:S(2)}) collective-permute-start(bf16[2,4,32,2048]{3,2,1,0:T(8,128)(2,1)S(1)} %get-tuple-element.310), channel_id=1, source_target_pairs={{0,2},{1,3},{2,0},{3,1},{4,6},{5,7},{6,4},{7,5},{8,10},{9,11},{10,... | collective-permute-start | bytes 3145736 | tf_op jit(solution)/shard_map/ppermute | solution.py:58
  168.9 33.3 %collective-permute-start.19 = (bf16[2,4,32,2048]{3,2,1,0:T(8,128)(2,1)S(1)}, bf16[2,4,32,2048]{3,2,1,0:T(8,128)(2,1)S(1)}, u32[]{:S(2)}, u32[]{:S(2)}) collective-permute-start(bf16[2,4,32,2048]{3,2,1,0:T(8,128)(2,1)S(1)} %get-tuple-element.304), channel_id=1, source_target_pairs={{0,4},{1,5},{2,6},{3,7},{4,0},{5,1},{6,2},{7,3},{8,12},{9,13},{10,... | collective-permute-start | bytes 3145736 | tf_op jit(solution)/shard_map/ppermute | solution.py:58
  178.0 44.9 %collective-permute-start.37 = (bf16[2,4,128,512]{3,2,1,0:T(8,128)(2,1)S(1)}, bf16[2,4,128,512]{3,2,1,0:T(8,128)(2,1)S(1)}, u32[]{:S(2)}, u32[]{:S(2)}) collective-permute-start(bf16[2,4,128,512]{3,2,1,0:T(8,128)(2,1)S(1)} %get-tuple-element.300), channel_id=1, source_target_pairs={{0,2},{1,3},{2,0},{3,1},{4,6},{5,7},{6,4},{7,5},{8,10},{9,11},{10,... | collective-permute-start | bytes 3145736 | tf_op jit(solution)/shard_map/ppermute | solution.py:58
  178.5 45.9 %collective-permute-start.40 = (bf16[2,4,128,512]{3,2,1,0:T(8,128)(2,1)S(1)}, bf16[2,4,128,512]{3,2,1,0:T(8,128)(2,1)S(1)}, u32[]{:S(2)}, u32[]{:S(2)}) collective-permute-start(bf16[2,4,128,512]{3,2,1,0:T(8,128)(2,1)S(1)} %get-tuple-element.294), channel_id=1, source_target_pairs={{0,4},{1,5},{2,6},{3,7},{4,0},{5,1},{6,2},{7,3},{8,12},{9,13},{10,... | collective-permute-start | bytes 3145736 | tf_op jit(solution)/shard_map/ppermute | solution.py:58
  180.0 68.9 %collective-permute-start.29 = (bf16[2,2,4,32,2048]{4,3,2,1,0:T(8,128)(2,1)S(1)}, bf16[2,2,4,32,2048]{4,3,2,1,0:T(8,128)(2,1)}, u32[]{:S(2)}, u32[]{:S(2)}) collective-permute-start(bf16[2,2,4,32,2048]{4,3,2,1,0:T(8,128)(2,1)S(1)} %pad_maximum_fusion.9.refs_0_), channel_id=1, source_target_pairs={{0,1},{1,0},{2,3},{3,2},{4,5},{5,4},{6,7},{7,6},{8,9},{9,8},{10,11... | collective-permute-start | bytes 6291464 | tf_op jit(solution)/shard_map/ppermute | solution.py:58
  200.5 54.3 %collective-permute-start.32 = (bf16[2,2,4,32,2048]{4,3,2,1,0:T(8,128)(2,1)}, bf16[2,2,4,32,2048]{4,3,2,1,0:T(8,128)(2,1)}, u32[]{:S(2)}, u32[]{:S(2)}) collective-permute-start(bf16[2,2,4,32,2048]{4,3,2,1,0:T(8,128)(2,1)} %pad_maximum_fusion.10.refs_2_), channel_id=1, source_target_pairs={{0,1},{1,0},{2,3},{3,2},{4,5},{5,4},{6,7},{7,6},{8,9},{9,8},{10,11... | collective-permute-start | bytes 6291464 | tf_op jit(solution)/shard_map/ppermute | solution.py:58
  202.1 42.9 %collective-permute-start.4 = (bf16[2,4,32,2048]{3,2,1,0:T(8,128)(2,1)}, bf16[2,4,32,2048]{3,2,1,0:T(8,128)(2,1)}, u32[]{:S(2)}, u32[]{:S(2)}) collective-permute-start(bf16[2,4,32,2048]{3,2,1,0:T(8,128)(2,1)} %get-tuple-element.302), channel_id=1, source_target_pairs={{0,2},{1,3},{2,0},{3,1},{4,6},{5,7},{6,4},{7,5},{8,10},{9,11},{10,... | collective-permute-start | bytes 3145736 | tf_op jit(solution)/shard_map/ppermute | solution.py:58
  223.0 26.0 %collective-permute-start.7 = (bf16[2,4,32,2176]{3,2,1,0:T(8,128)(2,1)}, bf16[2,4,32,2176]{3,2,1,0:T(8,128)(2,1)}, u32[]{:S(2)}, u32[]{:S(2)}) collective-permute-start(bf16[2,4,32,2176]{3,2,1,0:T(8,128)(2,1)} %get-tuple-element.134), channel_id=1, source_target_pairs={{0,4},{1,5},{2,6},{3,7},{4,0},{5,1},{6,2},{7,3},{8,12},{9,13},{10,... | collective-permute-start | bytes 3342344 | tf_op jit(solution)/shard_map/ppermute | solution.py:58
  224.5 31.8 %collective-permute-start.17 = (bf16[2,2,4,32,2048]{4,3,2,1,0:T(8,128)(2,1)}, bf16[2,2,4,32,2048]{4,3,2,1,0:T(8,128)(2,1)}, u32[]{:S(2)}, u32[]{:S(2)}) collective-permute-start(bf16[2,2,4,32,2048]{4,3,2,1,0:T(8,128)(2,1)} %pad_maximum_fusion.6.refs_0_), channel_id=1, source_target_pairs={{0,1},{1,0},{2,3},{3,2},{4,5},{5,4},{6,7},{7,6},{8,9},{9,8},{10,11... | collective-permute-start | bytes 6291464 | tf_op jit(solution)/shard_map/ppermute | solution.py:58
  245.1 25.2 %collective-permute-start.20 = (bf16[2,2,4,32,2048]{4,3,2,1,0:T(8,128)(2,1)S(1)}, bf16[2,2,4,32,2048]{4,3,2,1,0:T(8,128)(2,1)}, u32[]{:S(2)}, u32[]{:S(2)}) collective-permute-start(bf16[2,2,4,32,2048]{4,3,2,1,0:T(8,128)(2,1)S(1)} %pad_maximum_fusion.7.refs_2_), channel_id=1, source_target_pairs={{0,1},{1,0},{2,3},{3,2},{4,5},{5,4},{6,7},{7,6},{8,9},{9,8},{10,11... | collective-permute-start | bytes 6291464 | tf_op jit(solution)/shard_map/ppermute | solution.py:58
  248.9 26.5 %collective-permute-start.38 = (bf16[2,2,4,128,512]{4,3,2,1,0:T(8,128)(2,1)S(1)}, bf16[2,2,4,128,512]{4,3,2,1,0:T(8,128)(2,1)S(1)}, u32[]{:S(2)}, u32[]{:S(2)}) collective-permute-start(bf16[2,2,4,128,512]{4,3,2,1,0:T(8,128)(2,1)S(1)} %pad_maximum_fusion.11.refs_0_), channel_id=1, source_target_pairs={{0,1},{1,0},{2,3},{3,2},{4,5},{5,4},{6,7},{7,6},{8,9},{9,8},{10,11... | collective-permute-start | bytes 6291464 | tf_op jit(solution)/shard_map/ppermute | solution.py:58
  248.9 26.5 %collective-permute-start.41 = (bf16[2,2,4,128,512]{4,3,2,1,0:T(8,128)(2,1)S(1)}, bf16[2,2,4,128,512]{4,3,2,1,0:T(8,128)(2,1)}, u32[]{:S(2)}, u32[]{:S(2)}) collective-permute-start(bf16[2,2,4,128,512]{4,3,2,1,0:T(8,128)(2,1)S(1)} %pad_maximum_fusion.12.refs_2_), channel_id=1, source_target_pairs={{0,1},{1,0},{2,3},{3,2},{4,5},{5,4},{6,7},{7,6},{8,9},{9,8},{10,11... | collective-permute-start | bytes 6291464 | tf_op jit(solution)/shard_map/ppermute | solution.py:58
  254.8 35.7 %collective-permute-start.8 = (bf16[2,2,4,32,2176]{4,3,2,1,0:T(8,128)(2,1)}, bf16[2,2,4,32,2176]{4,3,2,1,0:T(8,128)(2,1)}, u32[]{:S(2)}, u32[]{:S(2)}) collective-permute-start(bf16[2,2,4,32,2176]{4,3,2,1,0:T(8,128)(2,1)} %pad_maximum_fusion.4.refs_2_), channel_id=1, source_target_pairs={{0,1},{1,0},{2,3},{3,2},{4,5},{5,4},{6,7},{7,6},{8,9},{9,8},{10,11... | collective-permute-start | bytes 6684680 | tf_op jit(solution)/shard_map/ppermute | solution.py:58
  256.3 34.2 %collective-permute-start.5 = (bf16[2,2,4,32,2048]{4,3,2,1,0:T(8,128)(2,1)S(1)}, bf16[2,2,4,32,2048]{4,3,2,1,0:T(8,128)(2,1)}, u32[]{:S(2)}, u32[]{:S(2)}) collective-permute-start(bf16[2,2,4,32,2048]{4,3,2,1,0:T(8,128)(2,1)S(1)} %pad_maximum_fusion.5.refs_0_), channel_id=1, source_target_pairs={{0,1},{1,0},{2,3},{3,2},{4,5},{5,4},{6,7},{7,6},{8,9},{9,8},{10,11... | collective-permute-start | bytes 6291464 | tf_op jit(solution)/shard_map/ppermute | solution.py:58
  509.4 234.2 %collective-permute-start.42 = (bf16[2,256,1024]{2,1,0:T(8,128)(2,1)}, bf16[2,256,1024]{2,1,0:T(8,128)(2,1)}, u32[]{:S(2)}, u32[]{:S(2)}) collective-permute-start(bf16[2,256,1024]{2,1,0:T(8,128)(2,1)} %fusion.60), channel_id=1, source_target_pairs={{0,1},{1,0},{2,3},{3,2},{4,5},{5,4},{6,7},{7,6},{8,9},{9,8},{10,11... | collective-permute-start | bytes 3145736 | tf_op jit(solution)/shard_map/ppermute | solution.py:58
  527.7 236.2 %collective-permute-start.44 = (bf16[16,32,2048]{2,1,0:T(8,128)(2,1)}, bf16[16,32,2048]{2,1,0:T(8,128)(2,1)}, u32[]{:S(2)}, u32[]{:S(2)}) collective-permute-start(bf16[16,32,2048]{2,1,0:T(8,128)(2,1)} %pad_maximum_fusion.13), channel_id=1, source_target_pairs={{0,1},{1,0},{2,3},{3,2},{4,5},{5,4},{6,7},{7,6},{8,9},{9,8},{10,11... | collective-permute-start | bytes 6291464 | tf_op jit(solution)/shard_map/ppermute | solution.py:58
  535.3 235.3 %collective-permute-start.47 = (bf16[16,32,2048]{2,1,0:T(8,128)(2,1)}, bf16[16,32,2048]{2,1,0:T(8,128)(2,1)}, u32[]{:S(2)}, u32[]{:S(2)}) collective-permute-start(bf16[16,32,2048]{2,1,0:T(8,128)(2,1)} %pad_maximum_fusion.14), channel_id=1, source_target_pairs={{0,1},{1,0},{2,3},{3,2},{4,5},{5,4},{6,7},{7,6},{8,9},{9,8},{10,11... | collective-permute-start | bytes 6291464 | tf_op jit(solution)/shard_map/ppermute | solution.py:58
  569.8 203.5 %collective-permute-start.53 = (bf16[16,32,2048]{2,1,0:T(8,128)(2,1)}, bf16[16,32,2048]{2,1,0:T(8,128)(2,1)}, u32[]{:S(2)}, u32[]{:S(2)}) collective-permute-start(bf16[16,32,2048]{2,1,0:T(8,128)(2,1)} %pad_maximum_fusion.15), channel_id=1, source_target_pairs={{0,1},{1,0},{2,3},{3,2},{4,5},{5,4},{6,7},{7,6},{8,9},{9,8},{10,11... | collective-permute-start | bytes 6291464 | tf_op jit(solution)/shard_map/ppermute | solution.py:58
  577.4 199.8 %collective-permute-start.56 = (bf16[16,32,2048]{2,1,0:T(8,128)(2,1)}, bf16[16,32,2048]{2,1,0:T(8,128)(2,1)}, u32[]{:S(2)}, u32[]{:S(2)}) collective-permute-start(bf16[16,32,2048]{2,1,0:T(8,128)(2,1)} %pad_maximum_fusion.16), channel_id=1, source_target_pairs={{0,1},{1,0},{2,3},{3,2},{4,5},{5,4},{6,7},{7,6},{8,9},{9,8},{10,11... | collective-permute-start | bytes 6291464 | tf_op jit(solution)/shard_map/ppermute | solution.py:58
  770.6 29.2 %collective-permute-start.65 = (bf16[16,32,2048]{2,1,0:T(8,128)(2,1)S(1)}, bf16[16,32,2048]{2,1,0:T(8,128)(2,1)S(1)}, u32[]{:S(2)}, u32[]{:S(2)}) collective-permute-start(bf16[16,32,2048]{2,1,0:T(8,128)(2,1)S(1)} %copy-done.132), channel_id=1, source_target_pairs={{0,1},{1,0},{2,3},{3,2},{4,5},{5,4},{6,7},{7,6},{8,9},{9,8},{10,11... | collective-permute-start | bytes 6291464 | tf_op jit(solution)/shard_map/ppermute | solution.py:58
  777.2 26.3 %collective-permute-start.45 = (bf16[8,32,2048]{2,1,0:T(8,128)(2,1)}, bf16[8,32,2048]{2,1,0:T(8,128)(2,1)}, u32[]{:S(2)}, u32[]{:S(2)}) collective-permute-start(bf16[8,32,2048]{2,1,0:T(8,128)(2,1)} %fusion.31), channel_id=1, source_target_pairs={{0,4},{1,5},{2,6},{3,7},{4,0},{5,1},{6,2},{7,3},{8,12},{9,13},{10,... | collective-permute-start | bytes 3145736 | tf_op jit(solution)/shard_map/ppermute | solution.py:58
  782.3 26.3 %collective-permute-start.48 = (bf16[8,32,2048]{2,1,0:T(8,128)(2,1)}, bf16[8,32,2048]{2,1,0:T(8,128)(2,1)}, u32[]{:S(2)}, u32[]{:S(2)}) collective-permute-start(bf16[8,32,2048]{2,1,0:T(8,128)(2,1)} %fusion.29), channel_id=1, source_target_pairs={{0,2},{1,3},{2,0},{3,1},{4,6},{5,7},{6,4},{7,5},{8,10},{9,11},{10,... | collective-permute-start | bytes 3145736 | tf_op jit(solution)/shard_map/ppermute | solution.py:58
  786.3 65.9 %collective-permute-start.54 = (bf16[8,32,2048]{2,1,0:T(8,128)(2,1)}, bf16[8,32,2048]{2,1,0:T(8,128)(2,1)}, u32[]{:S(2)}, u32[]{:S(2)}) collective-permute-start(bf16[8,32,2048]{2,1,0:T(8,128)(2,1)} %fusion.27), channel_id=1, source_target_pairs={{0,4},{1,5},{2,6},{3,7},{4,0},{5,1},{6,2},{7,3},{8,12},{9,13},{10,... | collective-permute-start | bytes 3145736 | tf_op jit(solution)/shard_map/ppermute | solution.py:58
  791.2 63.4 %collective-permute-start.57 = (bf16[8,32,2048]{2,1,0:T(8,128)(2,1)}, bf16[8,32,2048]{2,1,0:T(8,128)(2,1)}, u32[]{:S(2)}, u32[]{:S(2)}) collective-permute-start(bf16[8,32,2048]{2,1,0:T(8,128)(2,1)} %fusion.25), channel_id=1, source_target_pairs={{0,2},{1,3},{2,0},{3,1},{4,6},{5,7},{6,4},{7,5},{8,10},{9,11},{10,... | collective-permute-start | bytes 3145736 | tf_op jit(solution)/shard_map/ppermute | solution.py:58
  799.8 48.6 %collective-permute-start.63 = (bf16[8,32,2048]{2,1,0:T(8,128)(2,1)}, bf16[8,32,2048]{2,1,0:T(8,128)(2,1)}, u32[]{:S(2)}, u32[]{:S(2)}) collective-permute-start(bf16[8,32,2048]{2,1,0:T(8,128)(2,1)} %fusion.23), channel_id=1, source_target_pairs={{0,4},{1,5},{2,6},{3,7},{4,0},{5,1},{6,2},{7,3},{8,12},{9,13},{10,... | collective-permute-start | bytes 3145736 | tf_op jit(solution)/shard_map/ppermute | solution.py:58
  803.5 54.9 %collective-permute-start.66 = (bf16[8,32,2048]{2,1,0:T(8,128)(2,1)}, bf16[8,32,2048]{2,1,0:T(8,128)(2,1)}, u32[]{:S(2)}, u32[]{:S(2)}) collective-permute-start(bf16[8,32,2048]{2,1,0:T(8,128)(2,1)} %fusion.21), channel_id=1, source_target_pairs={{0,2},{1,3},{2,0},{3,1},{4,6},{5,7},{6,4},{7,5},{8,10},{9,11},{10,... | collective-permute-start | bytes 3145736 | tf_op jit(solution)/shard_map/ppermute | solution.py:58
  808.6 62.3 %collective-permute-start.72 = (bf16[8,128,512]{2,1,0:T(8,128)(2,1)}, bf16[8,128,512]{2,1,0:T(8,128)(2,1)}, u32[]{:S(2)}, u32[]{:S(2)}) collective-permute-start(bf16[8,128,512]{2,1,0:T(8,128)(2,1)} %fusion.19), channel_id=1, source_target_pairs={{0,4},{1,5},{2,6},{3,7},{4,0},{5,1},{6,2},{7,3},{8,12},{9,13},{10,... | collective-permute-start | bytes 3145736 | tf_op jit(solution)/shard_map/ppermute | solution.py:58
  848.4 27.6 %collective-permute-start.75 = (bf16[8,128,512]{2,1,0:T(8,128)(2,1)}, bf16[8,128,512]{2,1,0:T(8,128)(2,1)}, u32[]{:S(2)}, u32[]{:S(2)}) collective-permute-start(bf16[8,128,512]{2,1,0:T(8,128)(2,1)} %fusion.17), channel_id=1, source_target_pairs={{0,2},{1,3},{2,0},{3,1},{4,6},{5,7},{6,4},{7,5},{8,10},{9,11},{10,... | collective-permute-start | bytes 3145736 | tf_op jit(solution)/shard_map/ppermute | solution.py:58
  852.2 35.0 %collective-permute-start.46 = (bf16[4,32,2048]{2,1,0:T(8,128)(2,1)}, bf16[4,32,2048]{2,1,0:T(8,128)(2,1)S(1)}, u32[]{:S(2)}, u32[]{:S(2)}) collective-permute-start(bf16[4,32,2048]{2,1,0:T(8,128)(2,1)} %slice.638), channel_id=1, source_target_pairs={{0,2},{1,3},{2,0},{3,1},{4,6},{5,7},{6,4},{7,5},{8,10},{9,11},{10,... | collective-permute-start | bytes 1572872 | tf_op jit(solution)/shard_map/ppermute | solution.py:58
  854.6 33.3 %collective-permute-start.49 = (bf16[4,32,2048]{2,1,0:T(8,128)(2,1)S(1)}, bf16[4,32,2048]{2,1,0:T(8,128)(2,1)S(1)}, u32[]{:S(2)}, u32[]{:S(2)}) collective-permute-start(bf16[4,32,2048]{2,1,0:T(8,128)(2,1)S(1)} %copy-done.115), channel_id=1, source_target_pairs={{0,4},{1,5},{2,6},{3,7},{4,0},{5,1},{6,2},{7,3},{8,12},{9,13},{10,... | collective-permute-start | bytes 1572872 | tf_op jit(solution)/shard_map/ppermute | solution.py:58
  858.4 40.0 %collective-permute-start.55 = (bf16[4,32,2048]{2,1,0:T(8,128)(2,1)S(1)}, bf16[4,32,2048]{2,1,0:T(8,128)(2,1)S(1)}, u32[]{:S(2)}, u32[]{:S(2)}) collective-permute-start(bf16[4,32,2048]{2,1,0:T(8,128)(2,1)S(1)} %slice.636), channel_id=1, source_target_pairs={{0,2},{1,3},{2,0},{3,1},{4,6},{5,7},{6,4},{7,5},{8,10},{9,11},{10,... | collective-permute-start | bytes 1572872 | tf_op jit(solution)/shard_map/ppermute | solution.py:58
  870.9 28.3 %collective-permute-start.58 = (bf16[4,32,2048]{2,1,0:T(8,128)(2,1)S(1)}, bf16[4,32,2048]{2,1,0:T(8,128)(2,1)S(1)}, u32[]{:S(2)}, u32[]{:S(2)}) collective-permute-start(bf16[4,32,2048]{2,1,0:T(8,128)(2,1)S(1)} %slice.635), channel_id=1, source_target_pairs={{0,4},{1,5},{2,6},{3,7},{4,0},{5,1},{6,2},{7,3},{8,12},{9,13},{10,... | collective-permute-start | bytes 1572872 | tf_op jit(solution)/shard_map/ppermute | solution.py:58
  876.0 33.6 %collective-permute-start.64 = (bf16[4,32,2048]{2,1,0:T(8,128)(2,1)S(1)}, bf16[4,32,2048]{2,1,0:T(8,128)(2,1)S(1)}, u32[]{:S(2)}, u32[]{:S(2)}) collective-permute-start(bf16[4,32,2048]{2,1,0:T(8,128)(2,1)S(1)} %slice.634), channel_id=1, source_target_pairs={{0,2},{1,3},{2,0},{3,1},{4,6},{5,7},{6,4},{7,5},{8,10},{9,11},{10,... | collective-permute-start | bytes 1572872 | tf_op jit(solution)/shard_map/ppermute | solution.py:58
  887.2 22.6 %collective-permute-start.67 = (bf16[4,32,2048]{2,1,0:T(8,128)(2,1)S(1)}, bf16[4,32,2048]{2,1,0:T(8,128)(2,1)S(1)}, u32[]{:S(2)}, u32[]{:S(2)}) collective-permute-start(bf16[4,32,2048]{2,1,0:T(8,128)(2,1)S(1)} %slice.633), channel_id=1, source_target_pairs={{0,4},{1,5},{2,6},{3,7},{4,0},{5,1},{6,2},{7,3},{8,12},{9,13},{10,... | collective-permute-start | bytes 1572872 | tf_op jit(solution)/shard_map/ppermute | solution.py:58
  888.0 32.0 %collective-permute-start.73 = (bf16[4,128,512]{2,1,0:T(8,128)(2,1)S(1)}, bf16[4,128,512]{2,1,0:T(8,128)(2,1)S(1)}, u32[]{:S(2)}, u32[]{:S(2)}) collective-permute-start(bf16[4,128,512]{2,1,0:T(8,128)(2,1)S(1)} %slice.632), channel_id=1, source_target_pairs={{0,2},{1,3},{2,0},{3,1},{4,6},{5,7},{6,4},{7,5},{8,10},{9,11},{10,... | collective-permute-start | bytes 1572872 | tf_op jit(solution)/shard_map/ppermute | solution.py:58
  898.4 23.1 %collective-permute-start.76 = (bf16[4,128,512]{2,1,0:T(8,128)(2,1)S(1)}, bf16[4,128,512]{2,1,0:T(8,128)(2,1)S(1)}, u32[]{:S(2)}, u32[]{:S(2)}) collective-permute-start(bf16[4,128,512]{2,1,0:T(8,128)(2,1)S(1)} %slice.631), channel_id=1, source_target_pairs={{0,4},{1,5},{2,6},{3,7},{4,0},{5,1},{6,2},{7,3},{8,12},{9,13},{10,... | collective-permute-start | bytes 1572872 | tf_op jit(solution)/shard_map/ppermute | solution.py:58
  899.2 23.6 %collective-permute-start.52 = (bf16[32,4096]{1,0:T(8,128)(2,1)S(1)}, bf16[32,4096]{1,0:T(8,128)(2,1)S(1)}, u32[]{:S(2)}, u32[]{:S(2)}) collective-permute-start(bf16[32,4096]{1,0:T(8,128)(2,1)S(1)} %get-tuple-element.230), channel_id=1, source_target_pairs={{0,24},{1,25},{2,26},{3,27},{4,28},{5,29},{6,30},{7,31},{8,16},{9,... | collective-permute-start | bytes 786440 | tf_op jit(solution)/shard_map/ppermute | solution.py:58
  919.9 29.8 %collective-permute-start.61 = (bf16[32,4096]{1,0:T(8,128)(2,1)S(1)}, bf16[32,4096]{1,0:T(8,128)(2,1)S(1)}, u32[]{:S(2)}, u32[]{:S(2)}) collective-permute-start(bf16[32,4096]{1,0:T(8,128)(2,1)S(1)} %get-tuple-element.179), channel_id=1, source_target_pairs={{0,24},{1,25},{2,26},{3,27},{4,28},{5,29},{6,30},{7,31},{8,16},{9,... | collective-permute-start | bytes 786440 | tf_op jit(solution)/shard_map/ppermute | solution.py:58
  921.5 33.5 %collective-permute-start.60 = (bf16[32,4096]{1,0:T(8,128)(2,1)S(1)}, bf16[32,4096]{1,0:T(8,128)(2,1)S(1)}, u32[]{:S(2)}, u32[]{:S(2)}) collective-permute-start(bf16[32,4096]{1,0:T(8,128)(2,1)S(1)} %get-tuple-element.180), channel_id=1, source_target_pairs={{0,16},{1,17},{2,18},{3,19},{4,20},{5,21},{6,22},{7,23},{8,24},{9,... | collective-permute-start | bytes 786440 | tf_op jit(solution)/shard_map/ppermute | solution.py:58
  922.8 33.2 %collective-permute-start.59 = (bf16[32,4096]{1,0:T(8,128)(2,1)S(1)}, bf16[32,4096]{1,0:T(8,128)(2,1)S(1)}, u32[]{:S(2)}, u32[]{:S(2)}) collective-permute-start(bf16[32,4096]{1,0:T(8,128)(2,1)S(1)} %get-tuple-element.178), channel_id=1, source_target_pairs={{0,8},{1,9},{2,10},{3,11},{4,12},{5,13},{6,14},{7,15},{8,0},{9,1},... | collective-permute-start | bytes 786440 | tf_op jit(solution)/shard_map/ppermute | solution.py:58
  924.1 49.2 %collective-permute-start.70 = (bf16[32,4096]{1,0:T(8,128)(2,1)S(1)}, bf16[32,4096]{1,0:T(8,128)(2,1)S(1)}, u32[]{:S(2)}, u32[]{:S(2)}) collective-permute-start(bf16[32,4096]{1,0:T(8,128)(2,1)S(1)} %get-tuple-element.139), channel_id=1, source_target_pairs={{0,24},{1,25},{2,26},{3,27},{4,28},{5,29},{6,30},{7,31},{8,16},{9,... | collective-permute-start | bytes 786440 | tf_op jit(solution)/shard_map/ppermute | solution.py:58
  925.5 52.0 %collective-permute-start.69 = (bf16[32,4096]{1,0:T(8,128)(2,1)S(1)}, bf16[32,4096]{1,0:T(8,128)(2,1)S(1)}, u32[]{:S(2)}, u32[]{:S(2)}) collective-permute-start(bf16[32,4096]{1,0:T(8,128)(2,1)S(1)} %get-tuple-element.140), channel_id=1, source_target_pairs={{0,16},{1,17},{2,18},{3,19},{4,20},{5,21},{6,22},{7,23},{8,24},{9,... | collective-permute-start | bytes 786440 | tf_op jit(solution)/shard_map/ppermute | solution.py:58
  949.7 27.8 %collective-permute-start.68 = (bf16[32,4096]{1,0:T(8,128)(2,1)S(1)}, bf16[32,4096]{1,0:T(8,128)(2,1)S(1)}, u32[]{:S(2)}, u32[]{:S(2)}) collective-permute-start(bf16[32,4096]{1,0:T(8,128)(2,1)S(1)} %get-tuple-element.138), channel_id=1, source_target_pairs={{0,8},{1,9},{2,10},{3,11},{4,12},{5,13},{6,14},{7,15},{8,0},{9,1},... | collective-permute-start | bytes 786440 | tf_op jit(solution)/shard_map/ppermute | solution.py:58
  955.0 29.6 %collective-permute-start.79 = (bf16[128,1024]{1,0:T(8,128)(2,1)S(1)}, bf16[128,1024]{1,0:T(8,128)(2,1)S(1)}, u32[]{:S(2)}, u32[]{:S(2)}) collective-permute-start(bf16[128,1024]{1,0:T(8,128)(2,1)S(1)} %get-tuple-element.136), channel_id=1, source_target_pairs={{0,24},{1,25},{2,26},{3,27},{4,28},{5,29},{6,30},{7,31},{8,16},{9,... | collective-permute-start | bytes 786440 | tf_op jit(solution)/shard_map/ppermute | solution.py:58
  956.0 31.7 %collective-permute-start.78 = (bf16[128,1024]{1,0:T(8,128)(2,1)S(1)}, bf16[128,1024]{1,0:T(8,128)(2,1)S(1)}, u32[]{:S(2)}, u32[]{:S(2)}) collective-permute-start(bf16[128,1024]{1,0:T(8,128)(2,1)S(1)} %get-tuple-element.137), channel_id=1, source_target_pairs={{0,16},{1,17},{2,18},{3,19},{4,20},{5,21},{6,22},{7,23},{8,24},{9,... | collective-permute-start | bytes 786440 | tf_op jit(solution)/shard_map/ppermute | solution.py:58
  (152 other events, 1362.5 us)

commit v2 on v1

v2 whole, which is shorter than its diff:
```python
import functools

import jax
import jax.numpy as jnp
from jax import lax
from jax.experimental import pallas as pl
from jax.experimental.pallas import tpu as pltpu
from jax.sharding import PartitionSpec as P

HD = 64
ALPHA_RES = 4.16
EPSILON = 1e-05
MASKED = -1e30
SCORE_SCALE = 0.125
BF = jnp.bfloat16
F32 = jnp.float32
BOTH = ("dp", "ctx")


class Grid:
    def __init__(self, dp, ctx):
        y = ctx // 2
        x = y
        self.size = {"z": dp // x, "x": x, "y": y, "c": 2}
        self.total = dp * ctx

    def index(self, coords):
        value = 0
        for name in "zxyc":
            value = value * self.size[name] + coords[name]
        return value

    def coords(self, index):
        out = {}
        for name in "cyxz":
            out[name] = index % self.size[name]
            index = index // self.size[name]
        return out

    def here(self):
        dp, ctx = lax.axis_index("dp"), lax.axis_index("ctx")
        nx = self.size["x"]
        return {"z": dp // nx, "x": dp % nx, "y": ctx // 2, "c": ctx % 2}

    def exchange(self, array, name, bit):
        pairs = []
        for source in range(self.total):
            coords = self.coords(source)
            coords[name] ^= bit
            pairs.append((source, self.index(coords)))
        return lax.ppermute(array, BOTH, pairs)

    def others(self, array, name):
        return [self.exchange(array, name, k) for k in range(1, self.size[name])]

    def blocks(self):
        nz, nx, ny = self.size["z"], self.size["x"], self.size["y"]
        out = []
        for c in range(2):
            out += [(z, x, y, c) for x in range(nx) for y in range(ny) for z in range(nz // 2)]
            out += [(z, x, y, c) for y in range(ny) for x in range(nx) for z in range(nz // 2, nz)]
        return out

    def positions(self):
        here = self.here()
        return jnp.stack(
            [
                self.index({name: k ^ here[name] for name, k in zip("zxyc", block)})
                for block in self.blocks()
            ]
        ).astype(jnp.int32)


def after(value, *before):
    return lax.optimization_barrier((value,) + before)[0]


SHORT = pl.CostEstimate(flops=1, bytes_accessed=1, transcendentals=0)
call = functools.partial(pl.pallas_call, cost_estimate=SHORT)


def params(mib=48):
    return pltpu.CompilerParams(vmem_limit_bytes=mib * 2**20)


def full(shape):
    return pl.BlockSpec(shape, lambda *_: (0,) * len(shape))


SCALARS = pl.BlockSpec(memory_space=pltpu.SMEM)
ANYWHERE = pl.BlockSpec(memory_space=pl.ANY)


def side_by_side(arrays):
    widths = [a.shape[1] for a in arrays]

    def kernel(*refs):
        at = 0
        for ref, width in zip(refs, widths):
            refs[-1][:, at : at + width] = ref[...]
            at += width

    return call(
        kernel, out_shape=jax.ShapeDtypeStruct((arrays[0].shape[0], sum(widths)), BF)
    )(*arrays)


def stack(groups):
    flat = [a for group in groups for a in group]

    def kernel(*refs):
        outs, sems = refs[len(flat) : -1], refs[-1]
        started = []
        for group, out in zip(groups, outs):
            for n in range(len(group)):
                at = len(started)
                started.append(pltpu.make_async_copy(refs[at], out.at[n], sems.at[at]))
        for copy in started:
            copy.start()
        for copy in started:
            copy.wait()

    return list(call(
        kernel,
        out_shape=[
            jax.ShapeDtypeStruct((len(group),) + group[0].shape, group[0].dtype) for group in groups
        ],
        in_specs=[ANYWHERE] * len(flat),
        out_specs=[pl.BlockSpec(memory_space=pltpu.VMEM)] * len(groups),
        scratch_shapes=[pltpu.SemaphoreType.DMA((len(flat),))],
        compiler_params=params(),
    )(*flat))


def assemble(grid, positions, part_a, part_b, parts, shapes):
    blocks = grid.blocks()
    nx, ny, nz = (grid.size[name] for name in "xyz")
    rows = part_a[0][0].shape[2]
    arrays = [a for part in part_a + part_b for a in part]

    def kernel(where, *refs):
        sources = refs[: len(arrays)]
        targets = refs[len(arrays) : -1]
        sems = refs[-1]
        started = []
        for column, width, result, at in parts:
            for n, (z, x, y, c) in enumerate(blocks):
                if z < nz // 2:
                    source = sources[c * ny + y].at[x, z]
                else:
                    source = sources[2 * ny + c * nx + x].at[y, z - nz // 2]
                started.append(
                    pltpu.make_async_copy(
                        source.at[:, pl.ds(column, width)],
                        targets[result].at[where[n], pl.ds(at, rows), :],
                        sems.at[len(started)],
                    )
                )
        for copy in started:
            copy.start()
        for copy in started:
            copy.wait()

    out = call(
        kernel,
        out_shape=[jax.ShapeDtypeStruct((len(blocks),) + shape, BF) for shape in shapes],
        in_specs=[SCALARS] + [ANYWHERE] * len(arrays),
        out_specs=[pl.BlockSpec(memory_space=pltpu.VMEM)] * len(shapes),
        scratch_shapes=[pltpu.SemaphoreType.DMA((len(parts) * len(blocks),))],
        compiler_params=params(),
    )(positions, *arrays)
    return [a.reshape(-1, a.shape[2]) for a in out]


def turn(grid, positions, left):
    tokens, width = left.shape
    rows = width // grid.total

    def kernel(where, left_ref, out_ref, turned):
        turned[...] = left_ref[...].T
        for n in range(grid.total):
            at = pl.multiple_of(where[n] * rows, rows)
            out_ref[n * rows : (n + 1) * rows, :] = turned[pl.ds(at, rows), :]

    return call(
        kernel,
        out_shape=jax.ShapeDtypeStruct((width, tokens), BF),
        in_specs=[SCALARS, pl.BlockSpec(memory_space=pltpu.VMEM)],
        out_specs=pl.BlockSpec(memory_space=pltpu.VMEM),
        scratch_shapes=[pltpu.VMEM((width, tokens), BF)],
        compiler_params=params(),
    )(positions, left)


def products(pairs, core, groups, got=None):
    rows = pairs[0][0].shape[0] // 2
    if len(pairs) == 1:
        width = pairs[0][1].shape[1]
        block = min(width, 1024)
        if width == block:
            block = width // 2
        steps = width // block
    else:
        block = pairs[0][1].shape[1]
        steps = len(pairs)
        width = sum(b.shape[1] for _, b in pairs)
    starts = [sum(groups[:n]) for n in range(len(groups))]

    def kernel(*refs):
        lefts, rights = refs[: len(pairs)], refs[len(pairs) : 2 * len(pairs)]
        rest = refs[2 * len(pairs) :]
        got_ref, outs = (None, rest) if got is None else (rest[0], rest[1:])

        def run(left, right):
            for start, size, out in zip(starts, groups, outs):
                value = matmul(left[start : start + size, :], right[...])
                cols = slice(0, right.shape[1])
                if got_ref is not None:
                    value = value + got_ref[start : start + size, cols].astype(F32)
                out[:, cols] = value.astype(BF)

        if len(pairs) == 1:
            run(lefts[0], rights[0])
        else:
            for n in range(len(pairs)):
                @pl.when(pl.program_id(0) == n)
                def _():
                    run(lefts[n], rights[n])

    left_specs = [pl.BlockSpec((rows, a.shape[1]), lambda n: (core, 0)) for a, _ in pairs]
    if len(pairs) == 1:
        right_specs = [pl.BlockSpec((pairs[0][1].shape[0], block), lambda n: (0, n))]
    else:
        right_specs = [full(b.shape) for _, b in pairs]
    operands = [a for a, _ in pairs] + [b for _, b in pairs]
    got_specs = []
    if got is not None:
        operands.append(got)
        got_specs = [pl.BlockSpec((rows, block), lambda n: (0, n))]
    return call(
        kernel,
        grid=(steps,),
        out_shape=[jax.ShapeDtypeStruct((size, width), BF) for size in groups],
        in_specs=left_specs + right_specs + got_specs,
        out_specs=[pl.BlockSpec((size, block), lambda n: (0, n)) for size in groups],
        compiler_params=params(),
    )(*operands)


def add_split(sums, counts):
    rows = [arrays[0].shape[0] for arrays in sums]
    width = sums[0][0].shape[1]
    steps = next(n for n in (2, 3, 1) if width % (n * 128) == 0)

    def kernel(*refs):
        at = 0
        out = sum(len(arrays) for arrays in sums)
        for arrays, count, total in zip(sums, counts, rows):
            each = total // count
            for n in range(count):
                value = refs[at][n * each : (n + 1) * each, :].astype(F32)
                for m in range(1, len(arrays)):
                    value = value + refs[at + m][n * each : (n + 1) * each, :].astype(F32)
                refs[out + n][...] = value.astype(BF)
            at += len(arrays)
            out += count

    block = width // steps
    out = call(
        kernel,
        grid=(steps,),
        out_shape=[
            jax.ShapeDtypeStruct((total // count, width), BF)
            for count, total in zip(counts, rows)
            for _ in range(count)
        ],
        in_specs=[
            pl.BlockSpec((total, block), lambda n: (0, n))
            for arrays, total in zip(sums, rows)
            for _ in arrays
        ],
        out_specs=[
            pl.BlockSpec((total // count, block), lambda n: (0, n))
            for count, total in zip(counts, rows)
            for _ in range(count)
        ],
        compiler_params=params(),
    )(*[a for arrays in sums for a in arrays])
    split, at = [], 0
    for count in counts:
        split.append(list(out[at : at + count]))
        at += count
    return split


class Reduction:
    def __init__(self, grid, pairs):
        self.grid = grid
        self.pairs = pairs
        self.rows = pairs[0][0].shape[0]
        self.got, self.got_a, self.got_b = None, [], []

    def start(self):
        (self.away,) = products(self.pairs, 1, [self.rows // 2])
        return self.away

    def wait(self, *before):
        if self.got is not None:
            self.got = after(self.got, *before)
        self.got_a = [after(a, *before) for a in self.got_a]
        self.got_b = [after(b, *before) for b in self.got_b]

    def cores(self, *before):
        away = after(self.away, *before) if before else self.away
        self.got = self.grid.exchange(away, "c", 1)

    def keep(self):
        nx, ny = self.grid.size["x"], self.grid.size["y"]
        quarter = self.rows // 4
        outs = products(
            self.pairs, 0, [quarter // nx] * nx + [quarter // ny] * ny, self.got
        )
        self.got = None
        self.a, self.b = list(outs[:nx]), list(outs[nx:])
        return self.a + self.b

    def hold(self, *before):
        self.a = list(lax.optimization_barrier(tuple(self.a) + before)[: len(self.a)])
        self.b = list(lax.optimization_barrier(tuple(self.b) + before)[: len(self.b)])

    def send(self, name_a, name_b):
        self.got_a = [self.grid.exchange(a, name_a, k + 1) for k, a in enumerate(self.a[1:])]
        self.got_b = [self.grid.exchange(b, name_b, k + 1) for k, b in enumerate(self.b[1:])]
        return self.got_a + self.got_b

    def first(self):
        return self.send("x", "y")

    def add_first(self):
        counts = [self.grid.size["y"], self.grid.size["x"]]
        self.a, self.b = add_split([[self.a[0]] + self.got_a, [self.b[0]] + self.got_b], counts)
        return self.a + self.b

    def second(self):
        return self.send("y", "x")

    def add_second(self):
        half = self.grid.size["z"] // 2
        low, high = add_split([[self.a[0]] + self.got_a, [self.b[0]] + self.got_b], [half, half])
        self.a = low + high
        return self.a

    def last(self):
        self.got_a = [self.grid.exchange(a, "z", k + 1) for k, a in enumerate(self.a[1:])]
        self.got_b = []
        return self.got_a

    def finish(self, widths):
        arrays = [self.a[0]] + self.got_a

        def kernel(*refs):
            at = 0
            for width, out in zip(widths, refs[len(arrays) :]):
                value = refs[0][:, at : at + width].astype(F32)
                for ref in refs[1 : len(arrays)]:
                    value = value + ref[:, at : at + width].astype(F32)
                out[...] = value
                at += width

        return call(
            kernel,
            out_shape=[jax.ShapeDtypeStruct((self.a[0].shape[0], width), F32) for width in widths],
            compiler_params=params(),
        )(*arrays)


def matmul(left, right):
    return jnp.dot(left, right, preferred_element_type=F32)


def outer_right(left, right):
    return lax.dot_general(left, right, (((1,), (1,)), ((), ())), preferred_element_type=F32)


def norm_forward(resid, gain, bias):
    center = resid - jnp.mean(resid, axis=-1, keepdims=True)
    scale = lax.rsqrt(jnp.mean(center * center, axis=-1, keepdims=True) + EPSILON)
    normal = center * scale
    return normal * gain + bias, normal, scale


def norm_backward(dy, normal, scale, gain):
    dn = dy * gain
    grad = (
        dn
        - jnp.mean(dn, axis=-1, keepdims=True)
        - normal * jnp.mean(dn * normal, axis=-1, keepdims=True)
    ) * scale
    return grad, jnp.sum(dy * normal, axis=0), jnp.sum(dy, axis=0)


PAIR = 2 * HD
BLOCK = 128
DIMS_NT = (((1,), (1,)), ((), ()))
DIMS_TN = (((0,), (0,)), ((), ()))


def head_of(array, which, scale=None):
    lane = lax.broadcasted_iota(jnp.int32, array.shape, 1)
    mine = (lane < HD) if which == 0 else (lane >= HD)
    out = jnp.where(mine, array.astype(F32), 0.0)
    return (out if scale is None else out * scale).astype(BF)


def probabilities(q, k, bias):
    scores = lax.dot_general(q, k, DIMS_NT, preferred_element_type=F32) + bias
    exponent = jnp.exp(scores - jnp.max(scores, axis=-1, keepdims=True))
    return exponent * (1.0 / jnp.sum(exponent, axis=-1, keepdims=True))


def pair_forward(q, k, v, bias):
    lane = lax.broadcasted_iota(jnp.int32, q.shape, 1)
    outs = []
    for which in range(2):
        probs = probabilities(head_of(q, which, SCORE_SCALE), k, bias)
        outs.append(matmul(probs.astype(BF), v))
    return jnp.where(lane < HD, outs[0], outs[1]).astype(BF)


def pair_backward(q, k, v, grad, bias):
    gq, gk, gv = 0.0, 0.0, 0.0
    for which in range(2):
        q_one = head_of(q, which, SCORE_SCALE)
        g_one = head_of(grad, which)
        probs = probabilities(q_one, k, bias)
        dprob = lax.dot_general(g_one, v, DIMS_NT, preferred_element_type=F32)
        delta = jnp.sum(probs * dprob, axis=-1, keepdims=True)
        dscore = (probs * (dprob - delta)).astype(BF)
        gq = gq + matmul(dscore, head_of(k, which, SCORE_SCALE))
        gk = gk + lax.dot_general(dscore, q_one, DIMS_TN, preferred_element_type=F32)
        gv = gv + lax.dot_general(probs.astype(BF), g_one, DIMS_TN, preferred_element_type=F32)
    return gq, gk, gv


def self_bias(column, row, pad):
    length = column.shape[0]
    at_q = lax.broadcasted_iota(jnp.int32, (length, length), 0)
    at_k = lax.broadcasted_iota(jnp.int32, (length, length), 1)
    live = (column == row) & (at_q >= at_k) & ((at_k < length - pad) | (at_q == at_k))
    return jnp.where(live, 0.0, MASKED)


def pair_spec(array):
    return pl.BlockSpec((array.shape[0], PAIR), lambda n: (0, n))


def whole_spec(array):
    return pl.BlockSpec(array.shape, lambda n: (0,) * array.ndim)


def self_forward(pad, column, row, q, k, v):
    length, width = q.shape

    def kernel(pad_ref, column_ref, row_ref, q_ref, k_ref, v_ref, out_ref, bias_ref):
        @pl.when(pl.program_id(0) == 0)
        def _():
            bias_ref[...] = self_bias(column_ref[...], row_ref[...], pad_ref[0])

        for start in range(0, length, BLOCK):
            mine, seen = pl.ds(start, BLOCK), pl.ds(0, start + BLOCK)
            out_ref[mine, :] = pair_forward(
                q_ref[mine, :], k_ref[seen, :], v_ref[seen, :], bias_ref[mine, seen]
            )

    return call(
        kernel,
        grid=(width // PAIR,),
        out_shape=jax.ShapeDtypeStruct(q.shape, BF),
        in_specs=[pl.BlockSpec(memory_space=pltpu.SMEM), whole_spec(column), whole_spec(row)]
        + [pair_spec(q)] * 3,
        out_specs=pair_spec(q),
        scratch_shapes=[pltpu.VMEM((length, length), F32)],
        compiler_params=pltpu.CompilerParams(vmem_limit_bytes=40 * 2**20),
    )(pad, column, row, q, k, v)


def self_backward(pad, column, row, q, k, v, grad):
    length, width = q.shape

    def kernel(pad_ref, column_ref, row_ref, q_ref, k_ref, v_ref, g_ref, gq_ref, gk_ref, gv_ref, bias_ref, k_sum, v_sum):
        @pl.when(pl.program_id(0) == 0)
        def _():
            bias_ref[...] = self_bias(column_ref[...], row_ref[...], pad_ref[0])

        for start in reversed(range(0, length, BLOCK)):
            mine, seen = pl.ds(start, BLOCK), pl.ds(0, start + BLOCK)
            gq, gk, gv = pair_backward(
                q_ref[mine, :], k_ref[seen, :], v_ref[seen, :], g_ref[mine, :], bias_ref[mine, seen]
            )
            gq_ref[mine, :] = gq.astype(BF)
            if start + BLOCK == length:
                k_sum[...] = gk
                v_sum[...] = gv
            else:
                k_sum[seen, :] += gk
                v_sum[seen, :] += gv
        gk_ref[...] = k_sum[...].astype(BF)
        gv_ref[...] = v_sum[...].astype(BF)

    return call(
        kernel,
        grid=(width // PAIR,),
        out_shape=[jax.ShapeDtypeStruct(q.shape, BF)] * 3,
        in_specs=[pl.BlockSpec(memory_space=pltpu.SMEM), whole_spec(column), whole_spec(row)]
        + [pair_spec(q)] * 4,
        out_specs=[pair_spec(q)] * 3,
        scratch_shapes=[pltpu.VMEM((length, length), F32)] + [pltpu.VMEM((length, PAIR), F32)] * 2,
        compiler_params=pltpu.CompilerParams(vmem_limit_bytes=40 * 2**20),
    )(pad, column, row, q, k, v, grad)


def windows(total):
    return sorted({min(512, total), min(640, total), total})


def choose_window(segment, ids):
    total = ids.shape[0]
    at = jnp.arange(total, dtype=jnp.int32)
    live = (ids >= segment[0]) & (ids <= segment[-1])
    low = jnp.min(jnp.where(live, at, total))
    high = jnp.max(jnp.where(live, at + 1, 0))
    choice, starts, rows = jnp.int32(0), [], []
    for size in windows(total):
        start = jnp.clip(low // 16 * 16, 0, total - size)
        starts.append(start)
        rows.append(lax.dynamic_slice(ids, (start,), (size,)).reshape(1, size))
        choice = choice + (high - start > size).astype(jnp.int32)
    return jnp.stack([choice] + starts), rows


def on_window(window_ref, total, run):
    for n, size in enumerate(windows(total)):
        @pl.when(window_ref[0] == n)
        def _():
            run(n, size, pl.ds(pl.multiple_of(window_ref[1 + n], 16), size))


def cross_forward(window, column, rows, q, k, v):
    length, width = q.shape
    total = k.shape[0]

    def kernel(window_ref, column_ref, *refs):
        row_refs = refs[: len(rows)]
        q_ref, k_ref, v_ref, out_ref, bias_ref = refs[len(rows) :]

        def run(n, size, seen):
            @pl.when(pl.program_id(0) == 0)
            def _():
                bias_ref[:, :size] = jnp.where(column_ref[...] == row_refs[n][...], 0.0, MASKED)

            for start in range(0, length, BLOCK):
                mine = pl.ds(start, BLOCK)
                out_ref[mine, :] = pair_forward(
                    q_ref[mine, :], k_ref[seen, :], v_ref[seen, :], bias_ref[mine, :size]
                )

        on_window(window_ref, total, run)

    return call(
        kernel,
        grid=(width // PAIR,),
        out_shape=jax.ShapeDtypeStruct(q.shape, BF),
        in_specs=[pl.BlockSpec(memory_space=pltpu.SMEM), whole_spec(column)]
        + [whole_spec(row) for row in rows]
        + [pair_spec(q), pair_spec(k), pair_spec(v)],
        out_specs=pair_spec(q),
        scratch_shapes=[pltpu.VMEM((length, total), F32)],
        compiler_params=pltpu.CompilerParams(vmem_limit_bytes=40 * 2**20),
    )(window, column, *rows, q, k, v)


def cross_backward(window, column, rows, q, k, v, grad):
    length, width = q.shape
    total = k.shape[0]

    def kernel(window_ref, column_ref, *refs):
        row_refs = refs[: len(rows)]
        q_ref, k_ref, v_ref, g_ref, gq_ref, gk_ref, gv_ref, bias_ref, k_sum, v_sum = refs[len(rows) :]

        def run(n, size, seen):
            @pl.when(pl.program_id(0) == 0)
            def _():
                bias_ref[:, :size] = jnp.where(column_ref[...] == row_refs[n][...], 0.0, MASKED)

            if size < total:
                gk_ref[...] = jnp.zeros_like(gk_ref)
                gv_ref[...] = jnp.zeros_like(gv_ref)
            for start in range(0, length, BLOCK):
                mine = pl.ds(start, BLOCK)
                gq, gk, gv = pair_backward(
                    q_ref[mine, :], k_ref[seen, :], v_ref[seen, :], g_ref[mine, :], bias_ref[mine, :size]
                )
                gq_ref[mine, :] = gq.astype(BF)
                if start == 0:
                    k_sum[:size, :] = gk
                    v_sum[:size, :] = gv
                else:
                    k_sum[:size, :] += gk
                    v_sum[:size, :] += gv
            gk_ref[seen, :] = k_sum[:size, :].astype(BF)
            gv_ref[seen, :] = v_sum[:size, :].astype(BF)

        on_window(window_ref, total, run)

    return call(
        kernel,
        grid=(width // PAIR,),
        out_shape=[jax.ShapeDtypeStruct(a.shape, BF) for a in (q, k, v)],
        in_specs=[pl.BlockSpec(memory_space=pltpu.SMEM), whole_spec(column)]
        + [whole_spec(row) for row in rows]
        + [pair_spec(q), pair_spec(k), pair_spec(v), pair_spec(q)],
        out_specs=[pair_spec(q), pair_spec(k), pair_spec(v)],
        scratch_shapes=[pltpu.VMEM((length, total), F32)] + [pltpu.VMEM((total, PAIR), F32)] * 2,
        compiler_params=pltpu.CompilerParams(vmem_limit_bytes=40 * 2**20),
    )(window, column, *rows, q, k, v, grad)


def body(
    grid,
    hidden,
    memory,
    cotangent,
    dec_segment,
    pad_length,
    mem_segment,
    self_query,
    self_key,
    self_value,
    self_output,
    norm1_gain,
    norm1_bias,
    cross_query,
    cross_key,
    cross_value,
    cross_output,
    norm2_gain,
    norm2_bias,
    ffn_up,
    ffn_down,
    norm3_gain,
    norm3_bias,
):
    width = hidden.shape[1]
    ffn = ffn_up.shape[1]
    mem_rows = memory.shape[0]
    own_rows = self_query.shape[0]
    nx, ny, nz = grid.size["x"], grid.size["y"], grid.size["z"]
    here = grid.here()
    positions = grid.positions()

    def gather_z(piece):
        return [piece] + grid.others(piece, "z")

    def stacked(line, *before):
        line = [after(a, *before) for a in line] if before else line
        return stack([line[: nz // 2], line[nz // 2 :]])

    def hold(pair, *before):
        return after(pair[0], *before), after(pair[1], *before)

    class Gather:
        def first(self, pair):
            self.pair = pair
            self.got = grid.others(pair[0], "x"), grid.others(pair[1], "y")
            return self.got[0] + self.got[1]

        def second(self, *before):
            got = [[after(a, *before) for a in part] if before else part for part in self.got]
            self.pair = stack([[a] + part for a, part in zip(self.pair, got)])
            self.got = grid.others(self.pair[0], "y"), grid.others(self.pair[1], "x")
            self.core = [[grid.exchange(a, "c", 1)] for a in self.pair]
            return self.pair

        def cores(self, *before):
            got = [[after(a, *before) for a in part] if before else part for part in self.got]
            out = []
            for a, part, core in zip(self.pair, got, self.core):
                out.append([[a] + part, core + [grid.exchange(b, "c", 1) for b in part]])
            return out

    vectors = [norm1_gain, norm1_bias, norm2_gain, norm2_bias, norm3_gain, norm3_bias]
    vectors = jnp.pad(jnp.stack(vectors, axis=1).astype(BF), ((0, 0), (0, 122)))
    self_piece = side_by_side([self_query, self_key, self_value, self_output, vectors])
    self_z = gather_z(self_piece)
    cross_piece = side_by_side([cross_query, cross_key, cross_value, cross_output])
    many = ffn_down.shape[0] // own_rows
    ffn_piece = side_by_side(
        [ffn_up] + [ffn_down[n * own_rows : (n + 1) * own_rows] for n in range(many)]
    )

    self_z = self_z[:1] + [after(a, cross_piece, ffn_piece) for a in self_z[1:]]

    self_ag, cross_ag, ffn_ag = Gather(), Gather(), Gather()
    mem_y = [memory] + grid.others(memory, "y")
    ids_y = [mem_segment] + grid.others(mem_segment, "y")
    self_pair = stacked(self_z, cross_piece, ffn_piece, *mem_y[1:], *ids_y[1:])
    self_ag.first(self_pair)
    cross_z = gather_z(after(cross_piece, *self_pair))
    mem_c = stack([[after(a, *self_z) for a in mem_y]])
    mem_c += grid.others(mem_c[0], "c")
    ids_c = [jnp.stack(ids_y)]
    ids_c += grid.others(ids_c[0], "c")
    self_pair = self_ag.second(*mem_c[1:], *ids_c[1:])
    cross_pair = stacked(cross_z, *self_pair)
    ffn_z = gather_z(after(ffn_piece, *cross_pair))
    self_a, self_b = self_ag.cores(*cross_pair)
    cross_ag.first(hold(cross_pair, *self_ag.got[0], *self_ag.got[1]))

    mem_blocks = jnp.stack(
        [(y ^ here["y"]) * 2 + (c ^ here["c"]) for c in range(2) for y in range(ny)]
    ).astype(jnp.int32)

    def place_kernel(where, *refs):
        target, sems = refs[2], refs[3]
        started = []
        for c in range(2):
            for y in range(ny):
                n = c * ny + y
                started.append(
                    pltpu.make_async_copy(refs[c].at[y], target.at[where[n]], sems.at[n])
                )
        for copy in started:
            copy.start()
        for copy in started:
            copy.wait()

    mem_all = call(
        place_kernel,
        out_shape=jax.ShapeDtypeStruct((2 * ny, mem_rows, width), BF),
        in_specs=[SCALARS, ANYWHERE, ANYWHERE],
        out_specs=pl.BlockSpec(memory_space=pltpu.VMEM),
        scratch_shapes=[pltpu.SemaphoreType.DMA((2 * ny,))],
        compiler_params=params(),
    )(mem_blocks, *mem_c).reshape(-1, width)
    ids_all = jnp.zeros((2 * ny, mem_rows), jnp.int32)
    for c in range(2):
        for y in range(ny):
            ids_all = lax.dynamic_update_slice(
                ids_all, ids_c[c][y][None], (mem_blocks[c * ny + y], 0)
            )
    ids_all = ids_all.reshape(-1)

    w_sq, w_sk, w_sv, w_so, vectors = assemble(
        grid,
        positions,
        self_a,
        self_b,
        [(n * width, width, n, 0) for n in range(4)] + [(4 * width, 128, 4, 0)],
        [(own_rows, width)] * 4 + [(own_rows, 128)],
    )
    vectors = vectors[:, :6].T.astype(F32)
    gain1, bias1, gain2, bias2, gain3, bias3 = [vectors[n] for n in range(6)]

    segment = dec_segment.reshape(-1)
    column, row = segment.reshape(-1, 1), segment.reshape(1, -1)
    window, rows = choose_window(segment, ids_all)
    hidden_t = turn(grid, positions, hidden)
    mem_t = turn(grid, positions, mem_all)
    q = matmul(hidden, w_sq).astype(BF)
    k = matmul(hidden, w_sk).astype(BF)
    v = matmul(hidden, w_sv).astype(BF)
    cross_pair = cross_ag.second(q, k, v)
    self_att = self_forward(pad_length, column, row, after(q, *cross_pair), k, v)
    ffn_pair = stacked(ffn_z, self_att)
    cross_a, cross_b = cross_ag.cores(self_att)
    cross_got = cross_a[0][1:] + cross_b[0][1:]
    ffn_ag.first(hold(ffn_pair, *cross_got))
    first, normal1, scale1 = norm_forward(
        ALPHA_RES * hidden.astype(F32) + matmul(after(self_att, *cross_got), w_so), gain1, bias1
    )
    first_low = first.astype(BF)
    w_cq, w_ck, w_cv, w_co = assemble(
        grid,
        positions,
        cross_a,
        cross_b,
        [(n * width, width, n, 0) for n in range(4)],
        [(own_rows, width)] * 4,
    )
    cq = matmul(first_low, w_cq).astype(BF)
    mk = matmul(mem_all, w_ck).astype(BF)
    mv = matmul(mem_all, w_cv).astype(BF)
    ffn_pair = ffn_ag.second(cq, mk, mv)
    cross_att = cross_forward(window, column, rows, after(cq, *ffn_pair), mk, mv)
    second, normal2, scale2 = norm_forward(
        ALPHA_RES * first + matmul(cross_att, w_co), gain2, bias2
    )
    second_low = second.astype(BF)
    second_t = turn(grid, positions, second_low)
    self_att_t = turn(grid, positions, self_att)
    first_t = turn(grid, positions, first_low)
    cross_att_t = turn(grid, positions, cross_att)
    turned = (hidden_t, mem_t, second_t, self_att_t, first_t, cross_att_t)
    ffn_a, ffn_b = ffn_ag.cores(*turned)
    w_up, w_down = assemble(
        grid,
        positions,
        ffn_a,
        ffn_b,
        [(0, ffn, 0, 0)] + [(ffn + n * width, width, 1, n * own_rows) for n in range(many)],
        [(own_rows, ffn), (own_rows * many, width)],
    )
    pre = matmul(second_low, w_up)
    erf = 1.0 + lax.erf(pre * (0.5**0.5))
    act = (0.5 * pre * erf).astype(BF)
    slope = 0.5 * erf + pre * jnp.exp(-0.5 * pre * pre) * 0.3989422804014327
    third, normal3, scale3 = norm_forward(ALPHA_RES * second + matmul(act, w_down), gain3, bias3)

    grad_third, g_gain3, g_bias3 = norm_backward(cotangent.astype(F32), normal3, scale3, gain3)
    third_low = grad_third.astype(BF)
    down = Reduction(grid, [(turn(grid, positions, act), third_low)])
    down.start()
    down.cores()
    grad_pre = (slope * outer_right(after(third_low, down.away), w_down)).astype(BF)
    down.wait(grad_pre)
    down_kept = down.keep()
    down.first()
    up = Reduction(grid, [(second_t, after(grad_pre, *down_kept))])
    up.start()
    up.cores()
    grad_second = ALPHA_RES * grad_third + outer_right(after(grad_pre, up.away), w_up)
    up.wait(grad_second)
    up_kept = up.keep()
    grad_mid, g_gain2, g_bias2 = norm_backward(
        after(grad_second, *up_kept), normal2, scale2, gain2
    )
    mid_low = grad_mid.astype(BF)
    grad_catt = outer_right(mid_low, w_co).astype(BF)
    down.wait(grad_catt)
    down_kept = down.add_first()
    down.second()
    up.hold(*down_kept)
    up.first()
    unit = jnp.eye(128, dtype=BF)

    def spread(vectors):
        vectors = jnp.pad(jnp.stack(vectors).astype(BF), ((0, 128 - len(vectors)), (0, 0)))
        return turn(grid, positions, vectors), unit

    cross_norms = spread([g_gain2, g_bias2, g_gain3, g_bias3])
    grad_cq, grad_mk, grad_mv = cross_backward(
        window, column, rows, cq, mk, mv, after(grad_catt, *down_kept, cross_norms[0])
    )
    cross = Reduction(
        grid,
        [(cross_att_t, mid_low), (first_t, grad_cq), (mem_t, grad_mk), (mem_t, grad_mv), cross_norms],
    )
    cross.start()
    cross.cores(*down.got_a, *down.got_b, *up.got_a, *up.got_b)
    down.wait(cross.away)
    down_kept = down.add_second()
    down.last()
    up.wait(*down_kept)
    up_kept = up.add_first()
    up.second()
    grad_first = ALPHA_RES * grad_mid + outer_right(after(grad_cq, cross.away, *up_kept), w_cq)
    grad_res, g_gain1, g_bias1 = norm_backward(grad_first, normal1, scale1, gain1)
    res_low = grad_res.astype(BF)
    grad_satt = outer_right(res_low, w_so).astype(BF)
    own_norms = spread([g_gain1, g_bias1])
    cross.wait(grad_satt, own_norms[0])
    cross_kept = cross.keep()
    up.wait(*cross_kept)
    up_kept = up.add_second()
    cross.hold(*up_kept)
    cross.first()
    up.a = [after(a, *down.got_a) for a in up.a]
    up.last()
    grad_q, grad_k, grad_v = self_backward(
        pad_length, column, row, q, k, v, after(grad_satt, *cross_kept, *up_kept, *down.got_a)
    )
    own = Reduction(
        grid,
        [(self_att_t, res_low), (hidden_t, grad_q), (hidden_t, grad_k), (hidden_t, grad_v), own_norms],
    )
    own.start()
    own.cores(*cross.got_a, *cross.got_b, *up.got_a)
    cross.wait(own.away)
    cross_kept = cross.add_first()
    cross.second()
    grad_in = (
        ALPHA_RES * grad_res
        + outer_right(after(grad_q, own.away, *cross_kept), w_sq)
        + outer_right(grad_k, w_sk)
        + outer_right(grad_v, w_sv)
    )
    own.wait(grad_in)
    own_kept = own.keep()
    own.hold(*cross.got_a, *cross.got_b)
    own.first()
    cross.wait(*own_kept)
    cross_kept = cross.add_second()
    cross.last()
    grad_mem = outer_right(after(grad_mk, *cross_kept), w_ck) + outer_right(grad_mv, w_cv)
    grad_mem = grad_mem.reshape(ny, 2, mem_rows, width)
    mem_own = [lax.dynamic_index_in_dim(grad_mem, n ^ here["c"], 1, keepdims=False) for n in range(2)]
    mem_own = mem_own[0] + grid.exchange(mem_own[1].astype(BF), "c", 1).astype(F32)
    mem_own = [lax.dynamic_index_in_dim(mem_own, n ^ here["y"], 0, keepdims=False) for n in range(ny)]
    (out_down,) = down.finish([width])
    (out_up,) = up.finish([ffn])
    own.wait(out_down, out_up, *mem_own)
    own_kept = own.add_first()
    own.second()
    out_mem = mem_own[0]
    mem_own = [after(a, *own.got_a, *own.got_b) for a in mem_own]
    for n in range(1, ny):
        out_mem = out_mem + grid.exchange(mem_own[n].astype(BF), "y", n).astype(F32)
    own.wait(*cross.got_a)
    out_co, out_cq, out_ck, out_cv, late = cross.finish([width] * 4 + [128])
    own.wait(out_co)
    own.add_second()
    own.last()
    out_so, out_sq, out_sk, out_sv, last = own.finish([width] * 4 + [128])
    norms = [last[:, 0], last[:, 1]] + [late[:, n] for n in range(4)]
    return (
        third.astype(BF),
        grad_in,
        out_mem,
        out_sq,
        out_sk,
        out_sv,
        out_so,
        norms[0],
        norms[1],
        out_cq,
        out_ck,
        out_cv,
        out_co,
        norms[2],
        norms[3],
        out_up,
        out_down,
        norms[4],
        norms[5],
    )


def solution(mesh):
    grid = Grid(mesh.shape["dp"], mesh.shape["ctx"])
    row, flat = P(BOTH, None), P(BOTH)
    block = (row,) * 4 + (flat,) * 2
    return jax.shard_map(
        functools.partial(body, grid),
        mesh=mesh,
        in_specs=(row, row, row, row, flat, flat) + block + block + (row, row, flat, flat),
        out_specs=(row, row, row) + block + block + (row, row, flat, flat),
        check_vma=False,
    )
```

time: 1010 us -> 632 us (0.63); the launches traced: 989 us -> 622 us
  local copies, waits for them, and re-layouts: 204 us -> 44.7 us
  waiting for transfers between devices: 299 us -> 168 us
  Pallas kernels: 129 us -> 224 us
  other arithmetic: 89 us -> 20.9 us
  matrix products: 142 us -> 98.3 us
  blocking collectives: 41.3 us -> 0 us
  starting transfers between devices: 75.7 us -> 58.7 us
    ppermute x80 -> x71, waiting for transfers between devices: 299 us -> 168 us  [exchange(): return lax.ppermute(array, BOTH, pairs)]
    pallas_call x8 -> x47, Pallas kernels: 129 us -> 224 us  [the longest x8 52.3 us: products(): call(kernel, grid=(steps,), out_shape=[jax.ShapeDtypeStruct((size, width)...]
    unnamed x431 -> x229, local copies, waits for them, and re-layouts: 119 us -> 38.4 us
    dot_general x46 -> x10, matrix products: 103 us -> 46.2 us  [matmul(): return jnp.dot(left, right, preferred_element_type=F32)]
    dynamic_slice x33 -> x0, local copies, waits for them, and re-layouts: 52.9 us -> none  [turn(): lax.dynamic_slice(turned, (positions[count + k], positions[n], 0, 0), (1,...]
    psum x1 -> x0, blocking collectives: 41.3 us -> none  [own_part(): lax.psum(jnp.stack(vectors), BOTH).reshape(-1, grid.total, own_width)]
    another operation x34 -> x4, other arithmetic: 21.4 us -> 0.15 us  [the longest x1 0.08 us: body(): jnp.stack([(y ^ here['y']) * 2 + (c ^ here['c']) for c in range(2) for y...]
    add x22 -> x2, other arithmetic: 22.3 us -> 3.46 us  [the longest x1 2.36 us: body(): mem_own[0] + grid.exchange(mem_own[1].astype(BF), 'c', 1).astype(F32)]
  transfers between devices with their start and end apart: 80 -> 71, of which waited for: 32 -> 31; matrix products, arithmetic and copies ran while one was open for 32% -> 16% of each run, Pallas kernels for 2% -> 29%
where the time goes in v2:
time: 632 us; the launch traced here: 622 us
  Pallas kernels  224 us (35%)
  waiting for transfers between devices  168 us (27%)
  matrix products  98.3 us (16%)
  starting transfers between devices  58.7 us (9%)
  local copies, waits for them, and re-layouts  44.7 us (7%)
  other arithmetic  20.9 us (3%)
  between operations  7.79 us (1%)
    ppermute x71, waiting for transfers between devices, exchange(): return lax.ppermute(array, BOTH, pairs)  168 us
    ppermute x71, starting transfers between devices, exchange(): return lax.ppermute(array, BOTH, pairs)  58.7 us
    pallas_call x8, Pallas kernels, products(): call(kernel, grid=(steps,), out_shape=[jax.ShapeDtypeStruct((size, width)...  52.3 us
    dot_general x10, matrix products, outer_right(): lax.dot_general(left, right, (((1,), (1,)), ((), ())), preferred_element_...  52.1 us
    dot_general x10, matrix products, matmul(): return jnp.dot(left, right, preferred_element_type=F32)  46.2 us
    unnamed x229, local copies, waits for them, and re-layouts  38.4 us
    pallas_call x3, Pallas kernels, assemble(): call(kernel, out_shape=[jax.ShapeDtypeStruct((len(blocks),) + shape, BF)...  29.8 us
    pallas_call x1, Pallas kernels, cross_backward(): call(kernel, grid=(width // PAIR,), out_shape=[jax.ShapeDtypeStruct(a.sha...  29.7 us
  transfers between devices with their start and end apart: 71, of which 31 were waited for; matrix products, arithmetic and copies ran while one was open for 16% of the time, Pallas kernels for 29%

profile of v2, /device:TPU:8, one launch (start us, length us, event | category | flops | bytes accessed | tf_op | source)
XLA Modules:
  0.0 622.1 jit_solution(180115500728468418)
XLA Ops:
  7.1 2.6 collective-permute-start.3
  17.8 10.8 %collective-permute-done.3.refs_2_ = bf16[32,4224]{1,0:T(8,128)(2,1)S(1)} collective-permute-done((bf16[32,4224]{1,0:T(8,128)(2,1)}, bf16[32,4224]{1,0:T(8,128)(2,1)S(1)}, u32[]{:S(2)}, u32[]{:S(2)}) %collective-permute-start.3) | collective-permute-done | bytes 270368 | tf_op jit(solution)/shard_map/ppermute | solution.py:51
  28.6 4.9 collective-permute-done.4.refs_3_
  34.2 3.1 collective-permute-done.1
  40.7 10.3 %collective-permute-done.5.refs_1_ = bf16[2,32,4224]{2,1,0:T(8,128)(2,1)S(1)} collective-permute-done((bf16[2,32,4224]{2,1,0:T(8,128)(2,1)S(1)}, bf16[2,32,4224]{2,1,0:T(8,128)(2,1)S(1)}, u32[]{:S(2)}, u32[]{:S(2)}) %collective-permute-start.5) | collective-permute-done | bytes 540704 | tf_op jit(solution)/shard_map/ppermute | solution.py:51
  54.3 3.0 collective-permute-start.11
  57.8 5.8 collective-permute-done.10.refs_1_
  63.6 10.6 %collective-permute-done.11.refs_2_ = bf16[32,4096]{1,0:T(8,128)(2,1)S(1)} collective-permute-done((bf16[32,4096]{1,0:T(8,128)(2,1)S(1)}, bf16[32,4096]{1,0:T(8,128)(2,1)S(1)}, u32[]{:S(2)}, u32[]{:S(2)}) %collective-permute-start.11) | collective-permute-done | bytes 262176 | tf_op jit(solution)/shard_map/ppermute | solution.py:51
  74.2 4.2 collective-permute-done.12.refs_3_
  84.7 8.4 %shard_map.364 = (bf16[32,32,1024]{2,1,0:T(8,128)(2,1)}, bf16[32,32,1024]{2,1,0:T(8,128)(2,1)}, bf16[32,32,1024]{2,1,0:T(8,128)(2,1)}, bf16[32,32,1024]{2,1,0:T(8,128)(2,1)}, bf16[32,32,128]{2,1,0:T(8,128)(2,1)S(1)}) custom-call(s32[32]{0:T(128)S(1)} %stack.230.where, bf16[2,2,32,4224]{3,2,1,0:T(8,128)(2,1)S(1)} %get-tuple-element.207.refs_0_, ...), custom_call_target="tpu_custom_call" | custom-call | flops 1 | bytes 1 | tf_op jit(solution)/shard_map/pallas_call | solution.py:164
  93.2 4.0 fusion.15.q_ref
  105.3 3.0 collective-permute-start.27
  112.8 23.5 %shard_map.366.left_ref = bf16[512,1024]{1,0:T(8,128)(2,1)S(1)} custom-call(s32[1]{0:T(128)S(6)} %copy.83.pad_ref, s32[512,1]{1,0:T(8,128)S(1)} %copy.68.column_ref, s32[1,512]{1,0:T(1,128)S(1)} %copy-done.82, bf16[512,1024]{1,0:T(8,128)(2,1)S(1)} %copy-done.23, bf16[512,1024]{1,0:T(8,128)(2,1)S(1)} %copy-done.25, bf16[512,1024]{1,0:T(8,128)(2,1)S(1)} %copy-done.27), custom_call_target="tpu_custom_call" | custom-call | flops 1 | bytes 1 | tf_op jit(solution)/shard_map/pallas_call | solution.py:475
  136.5 7.1 %collective-permute-done.27.refs_2_ = bf16[32,8192]{1,0:T(8,128)(2,1)} collective-permute-done((bf16[32,8192]{1,0:T(8,128)(2,1)}, bf16[32,8192]{1,0:T(8,128)(2,1)}, u32[]{:S(2)}, u32[]{:S(2)}) %collective-permute-start.27) | collective-permute-done | bytes 524320 | tf_op jit(solution)/shard_map/ppermute | solution.py:51
  143.5 10.5 %collective-permute-done.28.refs_3_ = bf16[32,8192]{1,0:T(8,128)(2,1)} collective-permute-done((bf16[32,8192]{1,0:T(8,128)(2,1)}, bf16[32,8192]{1,0:T(8,128)(2,1)}, u32[]{:S(2)}, u32[]{:S(2)}) %collective-permute-start.28) | collective-permute-done | bytes 524320 | tf_op jit(solution)/shard_map/ppermute | solution.py:51
  160.7 3.2 fusion.37
  167.4 8.3 %shard_map.367 = (bf16[32,32,1024]{2,1,0:T(8,128)(2,1)}, bf16[32,32,1024]{2,1,0:T(8,128)(2,1)}, bf16[32,32,1024]{2,1,0:T(8,128)(2,1)}, bf16[32,32,1024]{2,1,0:T(8,128)(2,1)}) custom-call(s32[32]{0:T(128)S(1)} %stack.230.where, bf16[2,2,32,4096]{3,2,1,0:T(8,128)(2,1)} %get-tuple-element.225.refs_0_, bf16[2,2,32,4096]{3,2,1,0:T(8,128)(2,1)} %collective-permute-done.20.refs_1_, ...), custom_call_target="tpu_custom_call" | custom-call | flops 1 | bytes 1 | tf_op jit(solution)/shard_map/pallas_call | solution.py:164
  175.7 4.0 convolution_convert_fusion.7.refs_3_
  179.7 3.7 convolution_convert_fusion.1.refs_4_
  183.4 3.7 convolution_convert_fusion.refs_5_
  187.1 3.7 collective-permute-done.30.refs_3_
  207.2 26.1 %shard_map.371.left_ref = bf16[512,1024]{1,0:T(8,128)(2,1)S(1)} custom-call(s32[4]{0:T(128)S(1)} %pad_add_fusion.1.window_ref, s32[512,1]{1,0:T(8,128)S(1)} %copy.68.column_ref, s32[1,512]{1,0:T(1,128)S(1)} %bitcast.148, s32[1,640]{1,0:T(1,128)S(1)} %reshape.165.refs_1_, s32[1,1024]{1,0:T(1,128)S(1)} %bitcast.145, bf16[512,1024]{1,0:T(8,128)(2,1)S(1)} %copy-done.29, ...), custom_call_target="tpu_custom_call" | custom-call | flops 1 | bytes 1 | tf_op jit(solution)/shard_map/pallas_call | solution.py:569
  234.9 3.1 fusion.38
  245.4 4.9 collective-permute-done.33.refs_3_
  251.7 13.1 %shard_map.378 = (bf16[32,32,4096]{2,1,0:T(8,128)(2,1)}, bf16[32,128,1024]{2,1,0:T(8,128)(2,1)}) custom-call(s32[32]{0:T(128)S(1)} %stack.230.where, bf16[2,2,32,8192]{3,2,1,0:T(8,128)(2,1)S(1)} %copy-done.33, bf16[2,2,32,8192]{3,2,1,0:T(8,128)(2,1)} %collective-permute-done.31.refs_1_, bf16[2,2,32,8192]{3,2,1,0:T(8,128)(2,1)} %copy-done.99, ...), custom_call_target="tpu_custom_call" | custom-call | flops 1 | bytes 1 | tf_op jit(solution)/shard_map/pallas_call | solution.py:164
  264.8 10.1 %multiply_convert_fusion = (bf16[512,4096]{1,0:T(8,128)(2,1)}, f32[512,4096]{1,0:T(8,128)}) fusion(bf16[512,1024]{1,0:T(8,128)(2,1)S(1)} %fusion.14.left_ref, bf16[1024,4096]{1,0:T(8,128)(2,1)} %bitcast.178), kind=kOutput, calls=%fused_computation.7 | convolution fusion | flops 4305453056 | bytes 22020096 | tf_op jit(solution)/shard_map/dot_general | solution.py:378
  274.9 3.6 shard_map.379.refs_0_
  278.5 10.0 %fusion.39 = (f32[512]{0:T(512)S(1)}, f32[512,1024]{1,0:T(8,128)S(1)}) fusion(bf16[512,4096]{1,0:T(8,128)(2,1)} %get-tuple-element.412.left_ref, bf16[4096,1024]{1,0:T(8,128)(2,1)} %bitcast.180, f32[1024]{0:T(1024)S(1)} %bitcast.171, f32[1024]{0:T(1024)S(1)} %bitcast.157, f32[512]{0:T(512)S(1)} %add_rsqrt_fusion.1, ...), kind=kOutput, calls=%fused_computation.116 | convolution fusion | flops 4298636800 | bytes 16791552 | tf_op jit(solution)/shard_map/dot_general | solution.py:378
  293.2 4.5 shard_map.380
  298.1 11.4 %fusion.5.refs_1_ = bf16[512,4096]{1,0:T(8,128)(2,1)} fusion(f32[512,4096]{1,0:T(8,128)} %get-tuple-element.413, bf16[512,1024]{1,0:T(8,128)(2,1)S(1)} %get-tuple-element.255.refs_1_, bf16[4096,1024]{1,0:T(8,128)(2,1)} %bitcast.181), kind=kOutput, calls=%fused_computation.6 | convolution fusion | flops 4315938816 | bytes 22020096 | tf_op jit(solution)/shard_map/dot_general | solution.py:382
  309.5 5.3 shard_map.381
  314.8 4.9 shard_map.382
  323.0 11.5 %multiply_add_fusion.1 = f32[512,1024]{1,0:T(8,128)} fusion(bf16[512,4096]{1,0:T(8,128)(2,1)} %fusion.5.refs_1_, bf16[1024,4096]{1,0:T(8,128)(2,1)} %bitcast.179, f32[512]{0:T(512)S(1)} %broadcast_multiply_fusion.4, f32[512]{0:T(512)S(1)} %add_rsqrt_fusion, f32[512,1024]{1,0:T(8,128)} %copy-done.89, f32[512]{0:T(512)S(1)} %broadcast_multiply_fusion.6, ...), kind=kOutput, calls=%fused_computation.28 | convolution fusion | flops 4300210176 | bytes 17838080 | tf_op jit(solution)/shard_map/dot_general | solution.py:382
  334.5 6.6 %shard_map.383 = (bf16[128,4096]{1,0:T(8,128)(2,1)S(1)}, bf16[128,4096]{1,0:T(8,128)(2,1)}, bf16[128,4096]{1,0:T(8,128)(2,1)S(1)}, bf16[128,4096]{1,0:T(8,128)(2,1)}) custom-call(bf16[1024,512]{1,0:T(8,128)(2,1)S(1)} %shard_map.374.refs_0_, bf16[512,4096]{1,0:T(8,128)(2,1)} %fusion.5.refs_1_, bf16[512,4096]{1,0:T(8,128)(2,1)} %collective-permute-done.38.refs_2_), custom_call_target="tpu_custom_call" | custom-call | flops 1 | bytes 1 | tf_op jit(solution)/shard_map/pallas_call | solution.py:240
  341.1 3.3 multiply_reduce_fusion.2
  348.8 2.5 shard_map.384
  364.8 29.7 %shard_map.386 = (bf16[512,1024]{1,0:T(8,128)(2,1)S(1)}, bf16[1024,1024]{1,0:T(8,128)(2,1)S(1)}, bf16[1024,1024]{1,0:T(8,128)(2,1)S(1)}) custom-call(s32[4]{0:T(128)S(1)} %pad_add_fusion.1.window_ref, s32[512,1]{1,0:T(8,128)S(1)} %copy.68.column_ref, s32[1,512]{1,0:T(1,128)S(1)} %bitcast.149, s32[1,640]{1,0:T(1,128)S(1)} %reshape.165.refs_1_, ...), custom_call_target="tpu_custom_call" | custom-call | flops 1 | bytes 1 | tf_op jit(solution)/shard_map/pallas_call | solution.py:615
  397.2 8.6 %shard_map.387 = bf16[512,4224]{1,0:T(8,128)(2,1)} custom-call(bf16[1024,512]{1,0:T(8,128)(2,1)S(1)} %copy-done.3, bf16[1024,512]{1,0:T(8,128)(2,1)S(1)} %shard_map.376.refs_1_, bf16[1024,1024]{1,0:T(8,128)(2,1)} %copy-done, bf16[1024,1024]{1,0:T(8,128)(2,1)} %copy-done, bf16[1024,128]{1,0:T(8,128)(2,1)S(1)} %shard_map.385.refs_4_, ...), custom_call_target="tpu_custom_call" | custom-call | flops 1 | bytes 1 | tf_op jit(solution)/shard_map/pallas_call | solution.py:240
  411.3 4.3 multiply_reduce_fusion
  418.3 3.0 convolution_convert_fusion.5.g_ref
  421.3 9.3 %shard_map.391 = (bf16[128,4224]{1,0:T(8,128)(2,1)S(1)}, bf16[128,4224]{1,0:T(8,128)(2,1)}, bf16[128,4224]{1,0:T(8,128)(2,1)}, bf16[128,4224]{1,0:T(8,128)(2,1)}) custom-call(bf16[1024,512]{1,0:T(8,128)(2,1)S(1)} %copy-done.3, bf16[1024,512]{1,0:T(8,128)(2,1)S(1)} %shard_map.376.refs_1_, bf16[1024,1024]{1,0:T(8,128)(2,1)} %copy-done, ...), custom_call_target="tpu_custom_call" | custom-call | flops 1 | bytes 1 | tf_op jit(solution)/shard_map/pallas_call | solution.py:240
  435.9 3.1 collective-permute-start.49
  439.4 6.4 %collective-permute-done.48.refs_1_ = bf16[128,1024]{1,0:T(8,128)(2,1)S(1)} collective-permute-done((bf16[128,1024]{1,0:T(8,128)(2,1)S(1)}, bf16[128,1024]{1,0:T(8,128)(2,1)S(1)}, u32[]{:S(2)}, u32[]{:S(2)}) %collective-permute-start.48) | collective-permute-done | bytes 262176 | tf_op jit(solution)/shard_map/ppermute | solution.py:51
  446.5 10.6 %collective-permute-done.49.refs_2_ = bf16[128,1024]{1,0:T(8,128)(2,1)S(1)} collective-permute-done((bf16[128,1024]{1,0:T(8,128)(2,1)S(1)}, bf16[128,1024]{1,0:T(8,128)(2,1)S(1)}, u32[]{:S(2)}, u32[]{:S(2)}) %collective-permute-start.49) | collective-permute-done | bytes 262176 | tf_op jit(solution)/shard_map/ppermute | solution.py:51
  457.7 3.7 collective-permute-done.50.refs_3_
  462.1 3.2 collective-permute-start.55
  465.6 22.8 %shard_map.393 = (bf16[512,1024]{1,0:T(8,128)(2,1)S(1)}, bf16[512,1024]{1,0:T(8,128)(2,1)S(1)}, bf16[512,1024]{1,0:T(8,128)(2,1)S(1)}) custom-call(s32[1]{0:T(128)S(6)} %copy.83.pad_ref, s32[512,1]{1,0:T(8,128)S(1)} %copy.68.column_ref, s32[1,512]{1,0:T(1,128)S(1)} %copy-done.82, bf16[512,1024]{1,0:T(8,128)(2,1)S(1)} %copy-done.24, ...), custom_call_target="tpu_custom_call" | custom-call | flops 1 | bytes 1 | tf_op jit(solution)/shard_map/pallas_call | solution.py:510
  489.5 6.1 shard_map.394
  498.7 6.8 %fusion.42 = f32[1024,1024]{1,0:T(8,128)} fusion(bf16[1024,1024]{1,0:T(8,128)(2,1)} %copy-done.16, bf16[1024,1024]{1,0:T(8,128)(2,1)} %bitcast.190), kind=kOutput, calls=%fused_computation.119 | convolution fusion | flops 2147483648 | bytes 8388608 | tf_op jit(solution)/shard_map/dot_general | solution.py:382
  505.6 2.6 fusion.41
  508.2 2.6 shard_map.395
  511.9 3.0 fusion.40
  515.7 2.7 add_add_fusion
  518.4 7.0 %shard_map.396 = (bf16[128,4224]{1,0:T(8,128)(2,1)}, bf16[128,4224]{1,0:T(8,128)(2,1)}, bf16[128,4224]{1,0:T(8,128)(2,1)}, bf16[128,4224]{1,0:T(8,128)(2,1)}) custom-call(bf16[1024,512]{1,0:T(8,128)(2,1)S(1)} %shard_map.375.refs_0_, bf16[1024,512]{1,0:T(8,128)(2,1)S(1)} %shard_map.372.refs_1_.refs_2_.refs_3_, ...), custom_call_target="tpu_custom_call" | custom-call | flops 1 | bytes 1 | tf_op jit(solution)/shard_map/pallas_call | solution.py:240
  527.0 4.5 convolution_add_fusion
  541.5 19.0 %collective-permute-done.60.refs_1_ = bf16[128,4224]{1,0:T(8,128)(2,1)S(1)} collective-permute-done((bf16[128,4224]{1,0:T(8,128)(2,1)}, bf16[128,4224]{1,0:T(8,128)(2,1)S(1)}, u32[]{:S(2)}, u32[]{:S(2)}) %collective-permute-start.60) | collective-permute-done | bytes 1081376 | tf_op jit(solution)/shard_map/ppermute | solution.py:51
  562.1 2.6 shard_map.400
  570.2 8.2 %collective-permute-done.62.refs_1_ = bf16[64,4224]{1,0:T(8,128)(2,1)S(1)} collective-permute-done((bf16[64,4224]{1,0:T(8,128)(2,1)S(1)}, bf16[64,4224]{1,0:T(8,128)(2,1)S(1)}, u32[]{:S(2)}, u32[]{:S(2)}) %collective-permute-start.62) | collective-permute-done | bytes 540704 | tf_op jit(solution)/shard_map/ppermute | solution.py:51
  580.1 8.1 %collective-permute-done.66.refs_2_ = bf16[32,4224]{1,0:T(8,128)(2,1)S(1)} collective-permute-done((bf16[32,4224]{1,0:T(8,128)(2,1)S(1)}, bf16[32,4224]{1,0:T(8,128)(2,1)S(1)}, u32[]{:S(2)}, u32[]{:S(2)}) %collective-permute-start.66) | collective-permute-done | bytes 270368 | tf_op jit(solution)/shard_map/ppermute | solution.py:51
  588.2 4.5 collective-permute-done.67.refs_3_
  594.2 3.1 collective-permute-start.69
  598.4 5.2 collective-permute-done.68.refs_1_
  603.6 11.1 %collective-permute-done.69.refs_2_ = bf16[32,4224]{1,0:T(8,128)(2,1)S(1)} collective-permute-done((bf16[32,4224]{1,0:T(8,128)(2,1)S(1)}, bf16[32,4224]{1,0:T(8,128)(2,1)S(1)}, u32[]{:S(2)}, u32[]{:S(2)}) %collective-permute-start.69) | collective-permute-done | bytes 270368 | tf_op jit(solution)/shard_map/ppermute | solution.py:51
  614.7 4.3 collective-permute-done.70.refs_3_
  (437 shorter events, 149.0 us)
Async XLA Ops:
  0.7 32.8 %collective-permute-start = (bf16[256,1024]{1,0:T(8,128)(2,1)}, bf16[256,1024]{1,0:T(8,128)(2,1)S(1)}, u32[]{:S(2)}, u32[]{:S(2)}) collective-permute-start(bf16[256,1024]{1,0:T(8,128)(2,1)} %refs_0_.6), channel_id=1, source_target_pairs={{0,2},{1,3},{2,0},{3,1},{4,6},{5,7},{6,4},{7,5},{8,10},{9,11},{10,... | collective-permute-start | bytes 1572872 | tf_op jit(solution)/shard_map/ppermute | solution.py:51
  6.7 11.1 %collective-permute-start.2 = (bf16[32,4224]{1,0:T(8,128)(2,1)}, bf16[32,4224]{1,0:T(8,128)(2,1)S(1)}, u32[]{:S(2)}, u32[]{:S(2)}) collective-permute-start(bf16[32,4224]{1,0:T(8,128)(2,1)} %shard_map.357.refs_0_), channel_id=1, source_target_pairs={{0,8},{1,9},{2,10},{3,11},{4,12},{5,13},{6,14},{7,15},{8,0},{9,1},... | collective-permute-start | bytes 811016 | tf_op jit(solution)/shard_map/ppermute | solution.py:51
  7.1 21.4 %collective-permute-start.3 = (bf16[32,4224]{1,0:T(8,128)(2,1)}, bf16[32,4224]{1,0:T(8,128)(2,1)S(1)}, u32[]{:S(2)}, u32[]{:S(2)}) collective-permute-start(bf16[32,4224]{1,0:T(8,128)(2,1)} %shard_map.357.refs_0_), channel_id=1, source_target_pairs={{0,16},{1,17},{2,18},{3,19},{4,20},{5,21},{6,22},{7,23},{8,24},{9,... | collective-permute-start | bytes 811016 | tf_op jit(solution)/shard_map/ppermute | solution.py:51
  9.7 23.7 %collective-permute-start.4 = (bf16[32,4224]{1,0:T(8,128)(2,1)}, bf16[32,4224]{1,0:T(8,128)(2,1)S(1)}, u32[]{:S(2)}, u32[]{:S(2)}) collective-permute-start(bf16[32,4224]{1,0:T(8,128)(2,1)} %shard_map.357.refs_0_), channel_id=1, source_target_pairs={{0,24},{1,25},{2,26},{3,27},{4,28},{5,29},{6,30},{7,31},{8,16},{9,... | collective-permute-start | bytes 811016 | tf_op jit(solution)/shard_map/ppermute | solution.py:51
  33.6 17.4 %collective-permute-start.6 = (bf16[2,256,1024]{2,1,0:T(8,128)(2,1)S(1)}, bf16[2,256,1024]{2,1,0:T(8,128)(2,1)S(1)}, u32[]{:S(2)}, u32[]{:S(2)}) collective-permute-start(bf16[2,256,1024]{2,1,0:T(8,128)(2,1)S(1)} %shard_map.361.refs_0_), channel_id=1, source_target_pairs={{0,1},{1,0},{2,3},{3,2},{4,5},{5,4},{6,7},{7,6},{8,9},{9,8},{10,11... | collective-permute-start | bytes 3145736 | tf_op jit(solution)/shard_map/ppermute | solution.py:51
  37.5 13.5 %collective-permute-start.5 = (bf16[2,32,4224]{2,1,0:T(8,128)(2,1)S(1)}, bf16[2,32,4224]{2,1,0:T(8,128)(2,1)S(1)}, u32[]{:S(2)}, u32[]{:S(2)}) collective-permute-start(bf16[2,32,4224]{2,1,0:T(8,128)(2,1)S(1)} %get-tuple-element.201.refs_0_), channel_id=1, source_target_pairs={{0,4},{1,5},{2,6},{3,7},{4,0},{5,1},{6,2},{7,3},{8,12},{9,13},{10,... | collective-permute-start | bytes 1622024 | tf_op jit(solution)/shard_map/ppermute | solution.py:51
  39.0 13.2 %collective-permute-start.8 = (bf16[2,32,4224]{2,1,0:T(8,128)(2,1)S(1)}, bf16[2,32,4224]{2,1,0:T(8,128)(2,1)S(1)}, u32[]{:S(2)}, u32[]{:S(2)}) collective-permute-start(bf16[2,32,4224]{2,1,0:T(8,128)(2,1)S(1)} %get-tuple-element.205.refs_2_), channel_id=1, source_target_pairs={{0,2},{1,3},{2,0},{3,1},{4,6},{5,7},{6,4},{7,5},{8,10},{9,11},{10,... | collective-permute-start | bytes 1622024 | tf_op jit(solution)/shard_map/ppermute | solution.py:51
  52.5 27.6 %collective-permute-start.9 = (bf16[2,2,32,4224]{3,2,1,0:T(8,128)(2,1)S(1)}, bf16[2,2,32,4224]{3,2,1,0:T(8,128)(2,1)}, u32[]{:S(2)}, u32[]{:S(2)}) collective-permute-start(bf16[2,2,32,4224]{3,2,1,0:T(8,128)(2,1)S(1)} %get-tuple-element.207.refs_0_), channel_id=1, source_target_pairs={{0,2},{1,3},{2,0},{3,1},{4,6},{5,7},{6,4},{7,5},{8,10},{9,11},{10,... | collective-permute-start | bytes 3244040 | tf_op jit(solution)/shard_map/ppermute | solution.py:51
  53.1 27.1 %collective-permute-start.15 = (bf16[2,2,32,4224]{3,2,1,0:T(8,128)(2,1)S(1)}, bf16[2,2,32,4224]{3,2,1,0:T(8,128)(2,1)}, u32[]{:S(2)}, u32[]{:S(2)}) collective-permute-start(bf16[2,2,32,4224]{3,2,1,0:T(8,128)(2,1)S(1)} %get-tuple-element.209.refs_4_), channel_id=1, source_target_pairs={{0,4},{1,5},{2,6},{3,7},{4,0},{5,1},{6,2},{7,3},{8,12},{9,13},{10,... | collective-permute-start | bytes 3244040 | tf_op jit(solution)/shard_map/ppermute | solution.py:51
  54.3 9.2 %collective-permute-start.10 = (bf16[32,4096]{1,0:T(8,128)(2,1)S(1)}, bf16[32,4096]{1,0:T(8,128)(2,1)S(1)}, u32[]{:S(2)}, u32[]{:S(2)}) collective-permute-start(bf16[32,4096]{1,0:T(8,128)(2,1)S(1)} %copy-done.46), channel_id=1, source_target_pairs={{0,8},{1,9},{2,10},{3,11},{4,12},{5,13},{6,14},{7,15},{8,0},{9,1},... | collective-permute-start | bytes 786440 | tf_op jit(solution)/shard_map/ppermute | solution.py:51
  54.3 19.9 %collective-permute-start.11 = (bf16[32,4096]{1,0:T(8,128)(2,1)S(1)}, bf16[32,4096]{1,0:T(8,128)(2,1)S(1)}, u32[]{:S(2)}, u32[]{:S(2)}) collective-permute-start(bf16[32,4096]{1,0:T(8,128)(2,1)S(1)} %copy-done.46), channel_id=1, source_target_pairs={{0,16},{1,17},{2,18},{3,19},{4,20},{5,21},{6,22},{7,23},{8,24},{9,... | collective-permute-start | bytes 786440 | tf_op jit(solution)/shard_map/ppermute | solution.py:51
  57.3 21.1 %collective-permute-start.12 = (bf16[32,4096]{1,0:T(8,128)(2,1)S(1)}, bf16[32,4096]{1,0:T(8,128)(2,1)S(1)}, u32[]{:S(2)}, u32[]{:S(2)}) collective-permute-start(bf16[32,4096]{1,0:T(8,128)(2,1)S(1)} %copy-done.46), channel_id=1, source_target_pairs={{0,24},{1,25},{2,26},{3,27},{4,28},{5,29},{6,30},{7,31},{8,16},{9,... | collective-permute-start | bytes 786440 | tf_op jit(solution)/shard_map/ppermute | solution.py:51
  63.6 17.8 %collective-permute-start.13 = (bf16[2,2,32,4224]{3,2,1,0:T(8,128)(2,1)S(1)}, bf16[2,2,32,4224]{3,2,1,0:T(8,128)(2,1)}, u32[]{:S(2)}, u32[]{:S(2)}) collective-permute-start(bf16[2,2,32,4224]{3,2,1,0:T(8,128)(2,1)S(1)} %get-tuple-element.207.refs_0_), channel_id=1, source_target_pairs={{0,1},{1,0},{2,3},{3,2},{4,5},{5,4},{6,7},{7,6},{8,9},{9,8},{10,11... | collective-permute-start | bytes 3244040 | tf_op jit(solution)/shard_map/ppermute | solution.py:51
  74.2 8.7 %collective-permute-start.16 = (bf16[2,2,32,4224]{3,2,1,0:T(8,128)(2,1)S(1)}, bf16[2,2,32,4224]{3,2,1,0:T(8,128)(2,1)}, u32[]{:S(2)}, u32[]{:S(2)}) collective-permute-start(bf16[2,2,32,4224]{3,2,1,0:T(8,128)(2,1)S(1)} %get-tuple-element.209.refs_4_), channel_id=1, source_target_pairs={{0,1},{1,0},{2,3},{3,2},{4,5},{5,4},{6,7},{7,6},{8,9},{9,8},{10,11... | collective-permute-start | bytes 3244040 | tf_op jit(solution)/shard_map/ppermute | solution.py:51
  80.8 20.9 %collective-permute-start.18 = (bf16[2,32,4096]{2,1,0:T(8,128)(2,1)}, bf16[2,32,4096]{2,1,0:T(8,128)(2,1)S(1)}, u32[]{:S(2)}, u32[]{:S(2)}) collective-permute-start(bf16[2,32,4096]{2,1,0:T(8,128)(2,1)} %copy-done.57), channel_id=1, source_target_pairs={{0,4},{1,5},{2,6},{3,7},{4,0},{5,1},{6,2},{7,3},{8,12},{9,13},{10,... | collective-permute-start | bytes 1572872 | tf_op jit(solution)/shard_map/ppermute | solution.py:51
  81.4 20.3 %collective-permute-start.19 = (bf16[2,32,4096]{2,1,0:T(8,128)(2,1)}, bf16[2,32,4096]{2,1,0:T(8,128)(2,1)S(1)}, u32[]{:S(2)}, u32[]{:S(2)}) collective-permute-start(bf16[2,32,4096]{2,1,0:T(8,128)(2,1)} %copy-done.59), channel_id=1, source_target_pairs={{0,2},{1,3},{2,0},{3,1},{4,6},{5,7},{6,4},{7,5},{8,10},{9,11},{10,... | collective-permute-start | bytes 1572872 | tf_op jit(solution)/shard_map/ppermute | solution.py:51
  103.2 55.4 %collective-permute-start.20 = (bf16[2,2,32,4096]{3,2,1,0:T(8,128)(2,1)}, bf16[2,2,32,4096]{3,2,1,0:T(8,128)(2,1)}, u32[]{:S(2)}, u32[]{:S(2)}) collective-permute-start(bf16[2,2,32,4096]{3,2,1,0:T(8,128)(2,1)} %get-tuple-element.225.refs_0_), channel_id=1, source_target_pairs={{0,2},{1,3},{2,0},{3,1},{4,6},{5,7},{6,4},{7,5},{8,10},{9,11},{10,... | collective-permute-start | bytes 3145736 | tf_op jit(solution)/shard_map/ppermute | solution.py:51
  104.8 53.8 %collective-permute-start.21 = (bf16[2,2,32,4096]{3,2,1,0:T(8,128)(2,1)}, bf16[2,2,32,4096]{3,2,1,0:T(8,128)(2,1)}, u32[]{:S(2)}, u32[]{:S(2)}) collective-permute-start(bf16[2,2,32,4096]{3,2,1,0:T(8,128)(2,1)} %get-tuple-element.226.refs_4_), channel_id=1, source_target_pairs={{0,4},{1,5},{2,6},{3,7},{4,0},{5,1},{6,2},{7,3},{8,12},{9,13},{10,... | collective-permute-start | bytes 3145736 | tf_op jit(solution)/shard_map/ppermute | solution.py:51
  105.3 31.0 %collective-permute-start.26 = (bf16[32,8192]{1,0:T(8,128)(2,1)}, bf16[32,8192]{1,0:T(8,128)(2,1)}, u32[]{:S(2)}, u32[]{:S(2)}) collective-permute-start(bf16[32,8192]{1,0:T(8,128)(2,1)} %shard_map.359.refs_0_), channel_id=1, source_target_pairs={{0,8},{1,9},{2,10},{3,11},{4,12},{5,13},{6,14},{7,15},{8,0},{9,1},... | collective-permute-start | bytes 1572872 | tf_op jit(solution)/shard_map/ppermute | solution.py:51
  105.3 38.2 %collective-permute-start.27 = (bf16[32,8192]{1,0:T(8,128)(2,1)}, bf16[32,8192]{1,0:T(8,128)(2,1)}, u32[]{:S(2)}, u32[]{:S(2)}) collective-permute-start(bf16[32,8192]{1,0:T(8,128)(2,1)} %shard_map.359.refs_0_), channel_id=1, source_target_pairs={{0,16},{1,17},{2,18},{3,19},{4,20},{5,21},{6,22},{7,23},{8,24},{9,... | collective-permute-start | bytes 1572872 | tf_op jit(solution)/shard_map/ppermute | solution.py:51
  108.4 45.6 %collective-permute-start.28 = (bf16[32,8192]{1,0:T(8,128)(2,1)}, bf16[32,8192]{1,0:T(8,128)(2,1)}, u32[]{:S(2)}, u32[]{:S(2)}) collective-permute-start(bf16[32,8192]{1,0:T(8,128)(2,1)} %shard_map.359.refs_0_), channel_id=1, source_target_pairs={{0,24},{1,25},{2,26},{3,27},{4,28},{5,29},{6,30},{7,31},{8,16},{9,... | collective-permute-start | bytes 1572872 | tf_op jit(solution)/shard_map/ppermute | solution.py:51
  136.4 28.8 %collective-permute-start.22 = (bf16[2,2,32,4096]{3,2,1,0:T(8,128)(2,1)}, bf16[2,2,32,4096]{3,2,1,0:T(8,128)(2,1)}, u32[]{:S(2)}, u32[]{:S(2)}) collective-permute-start(bf16[2,2,32,4096]{3,2,1,0:T(8,128)(2,1)} %get-tuple-element.225.refs_0_), channel_id=1, source_target_pairs={{0,1},{1,0},{2,3},{3,2},{4,5},{5,4},{6,7},{7,6},{8,9},{9,8},{10,11... | collective-permute-start | bytes 3145736 | tf_op jit(solution)/shard_map/ppermute | solution.py:51
  143.5 22.9 %collective-permute-start.24 = (bf16[2,2,32,4096]{3,2,1,0:T(8,128)(2,1)}, bf16[2,2,32,4096]{3,2,1,0:T(8,128)(2,1)}, u32[]{:S(2)}, u32[]{:S(2)}) collective-permute-start(bf16[2,2,32,4096]{3,2,1,0:T(8,128)(2,1)} %get-tuple-element.226.refs_4_), channel_id=1, source_target_pairs={{0,1},{1,0},{2,3},{3,2},{4,5},{5,4},{6,7},{7,6},{8,9},{9,8},{10,11... | collective-permute-start | bytes 3145736 | tf_op jit(solution)/shard_map/ppermute | solution.py:51
  158.6 7.8 %collective-permute-start.23 = (bf16[2,2,32,4096]{3,2,1,0:T(8,128)(2,1)}, bf16[2,2,32,4096]{3,2,1,0:T(8,128)(2,1)S(1)}, u32[]{:S(2)}, u32[]{:S(2)}) collective-permute-start(bf16[2,2,32,4096]{3,2,1,0:T(8,128)(2,1)} %collective-permute-done.20.refs_1_), channel_id=1, source_target_pairs={{0,1},{1,0},{2,3},{3,2},{4,5},{5,4},{6,7},{7,6},{8,9},{9,8},{10,11... | collective-permute-start | bytes 3145736 | tf_op jit(solution)/shard_map/ppermute | solution.py:51
  159.2 27.9 %collective-permute-start.29 = (bf16[2,32,8192]{2,1,0:T(8,128)(2,1)}, bf16[2,32,8192]{2,1,0:T(8,128)(2,1)S(1)}, u32[]{:S(2)}, u32[]{:S(2)}) collective-permute-start(bf16[2,32,8192]{2,1,0:T(8,128)(2,1)} %copy-done.51), channel_id=1, source_target_pairs={{0,4},{1,5},{2,6},{3,7},{4,0},{5,1},{6,2},{7,3},{8,12},{9,13},{10,... | collective-permute-start | bytes 3145736 | tf_op jit(solution)/shard_map/ppermute | solution.py:51
  165.9 24.9 %collective-permute-start.30 = (bf16[2,32,8192]{2,1,0:T(8,128)(2,1)S(1)}, bf16[2,32,8192]{2,1,0:T(8,128)(2,1)S(1)}, u32[]{:S(2)}, u32[]{:S(2)}) collective-permute-start(bf16[2,32,8192]{2,1,0:T(8,128)(2,1)S(1)} %copy-done.54), channel_id=1, source_target_pairs={{0,2},{1,3},{2,0},{3,1},{4,6},{5,7},{6,4},{7,5},{8,10},{9,11},{10,... | collective-permute-start | bytes 3145736 | tf_op jit(solution)/shard_map/ppermute | solution.py:51
  193.2 48.1 %collective-permute-start.31 = (bf16[2,2,32,8192]{3,2,1,0:T(8,128)(2,1)}, bf16[2,2,32,8192]{3,2,1,0:T(8,128)(2,1)}, u32[]{:S(2)}, u32[]{:S(2)}) collective-permute-start(bf16[2,2,32,8192]{3,2,1,0:T(8,128)(2,1)} %get-tuple-element.247.refs_0_), channel_id=1, source_target_pairs={{0,2},{1,3},{2,0},{3,1},{4,6},{5,7},{6,4},{7,5},{8,10},{9,11},{10,... | collective-permute-start | bytes 6291464 | tf_op jit(solution)/shard_map/ppermute | solution.py:51
  193.7 47.7 %collective-permute-start.34 = (bf16[2,2,32,8192]{3,2,1,0:T(8,128)(2,1)}, bf16[2,2,32,8192]{3,2,1,0:T(8,128)(2,1)}, u32[]{:S(2)}, u32[]{:S(2)}) collective-permute-start(bf16[2,2,32,8192]{3,2,1,0:T(8,128)(2,1)} %get-tuple-element.248.refs_4_), channel_id=1, source_target_pairs={{0,4},{1,5},{2,6},{3,7},{4,0},{5,1},{6,2},{7,3},{8,12},{9,13},{10,... | collective-permute-start | bytes 6291464 | tf_op jit(solution)/shard_map/ppermute | solution.py:51
  233.3 8.5 %collective-permute-start.32 = (bf16[2,2,32,8192]{3,2,1,0:T(8,128)(2,1)S(1)}, bf16[2,2,32,8192]{3,2,1,0:T(8,128)(2,1)S(1)}, u32[]{:S(2)}, u32[]{:S(2)}) collective-permute-start(bf16[2,2,32,8192]{3,2,1,0:T(8,128)(2,1)S(1)} %copy-done.33), channel_id=1, source_target_pairs={{0,1},{1,0},{2,3},{3,2},{4,5},{5,4},{6,7},{7,6},{8,9},{9,8},{10,11... | collective-permute-start | bytes 6291464 | tf_op jit(solution)/shard_map/ppermute | solution.py:51
  241.2 9.1 %collective-permute-start.33 = (bf16[2,2,32,8192]{3,2,1,0:T(8,128)(2,1)}, bf16[2,2,32,8192]{3,2,1,0:T(8,128)(2,1)S(1)}, u32[]{:S(2)}, u32[]{:S(2)}) collective-permute-start(bf16[2,2,32,8192]{3,2,1,0:T(8,128)(2,1)} %collective-permute-done.31.refs_1_), channel_id=1, source_target_pairs={{0,1},{1,0},{2,3},{3,2},{4,5},{5,4},{6,7},{7,6},{8,9},{9,8},{10,11... | collective-permute-start | bytes 6291464 | tf_op jit(solution)/shard_map/ppermute | solution.py:51
  241.5 10.2 %collective-permute-start.36 = (bf16[2,2,32,8192]{3,2,1,0:T(8,128)(2,1)}, bf16[2,2,32,8192]{3,2,1,0:T(8,128)(2,1)}, u32[]{:S(2)}, u32[]{:S(2)}) collective-permute-start(bf16[2,2,32,8192]{3,2,1,0:T(8,128)(2,1)} %collective-permute-done.34.refs_5_), channel_id=1, source_target_pairs={{0,1},{1,0},{2,3},{3,2},{4,5},{5,4},{6,7},{7,6},{8,9},{9,8},{10,11... | collective-permute-start | bytes 6291464 | tf_op jit(solution)/shard_map/ppermute | solution.py:51
  297.7 11.8 %collective-permute-start.37 = (bf16[2048,1024]{1,0:T(8,128)(2,1)S(1)}, bf16[2048,1024]{1,0:T(8,128)(2,1)}, u32[]{:S(2)}, u32[]{:S(2)}) collective-permute-start(bf16[2048,1024]{1,0:T(8,128)(2,1)S(1)} %shard_map.380), channel_id=1, source_target_pairs={{0,1},{1,0},{2,3},{3,2},{4,5},{5,4},{6,7},{7,6},{8,9},{9,8},{10,11... | collective-permute-start | bytes 12582920 | tf_op jit(solution)/shard_map/ppermute | solution.py:51
  319.7 14.8 %collective-permute-start.38 = (bf16[512,4096]{1,0:T(8,128)(2,1)S(1)}, bf16[512,4096]{1,0:T(8,128)(2,1)}, u32[]{:S(2)}, u32[]{:S(2)}) collective-permute-start(bf16[512,4096]{1,0:T(8,128)(2,1)S(1)} %shard_map.382), channel_id=1, source_target_pairs={{0,1},{1,0},{2,3},{3,2},{4,5},{5,4},{6,7},{7,6},{8,9},{9,8},{10,11... | collective-permute-start | bytes 12582920 | tf_op jit(solution)/shard_map/ppermute | solution.py:51
  320.0 28.8 %collective-permute-start.39 = (bf16[512,1024]{1,0:T(8,128)(2,1)S(1)}, bf16[512,1024]{1,0:T(8,128)(2,1)S(1)}, u32[]{:S(2)}, u32[]{:S(2)}) collective-permute-start(bf16[512,1024]{1,0:T(8,128)(2,1)S(1)} %get-tuple-element.258), channel_id=1, source_target_pairs={{0,4},{1,5},{2,6},{3,7},{4,0},{5,1},{6,2},{7,3},{8,12},{9,13},{10,... | collective-permute-start | bytes 3145736 | tf_op jit(solution)/shard_map/ppermute | solution.py:51
  321.5 27.3 %collective-permute-start.40 = (bf16[512,1024]{1,0:T(8,128)(2,1)S(1)}, bf16[512,1024]{1,0:T(8,128)(2,1)}, u32[]{:S(2)}, u32[]{:S(2)}) collective-permute-start(bf16[512,1024]{1,0:T(8,128)(2,1)S(1)} %get-tuple-element.260), channel_id=1, source_target_pairs={{0,2},{1,3},{2,0},{3,1},{4,6},{5,7},{6,4},{7,5},{8,10},{9,11},{10,... | collective-permute-start | bytes 3145736 | tf_op jit(solution)/shard_map/ppermute | solution.py:51
  352.9 52.9 %collective-permute-start.41 = (bf16[128,4096]{1,0:T(8,128)(2,1)}, bf16[128,4096]{1,0:T(8,128)(2,1)}, u32[]{:S(2)}, u32[]{:S(2)}) collective-permute-start(bf16[128,4096]{1,0:T(8,128)(2,1)} %get-tuple-element.280), channel_id=1, source_target_pairs={{0,4},{1,5},{2,6},{3,7},{4,0},{5,1},{6,2},{7,3},{8,12},{9,13},{10,... | collective-permute-start | bytes 3145736 | tf_op jit(solution)/shard_map/ppermute | solution.py:51
  353.4 52.4 %collective-permute-start.44 = (bf16[128,4096]{1,0:T(8,128)(2,1)}, bf16[128,4096]{1,0:T(8,128)(2,1)}, u32[]{:S(2)}, u32[]{:S(2)}) collective-permute-start(bf16[128,4096]{1,0:T(8,128)(2,1)} %get-tuple-element.289), channel_id=1, source_target_pairs={{0,2},{1,3},{2,0},{3,1},{4,6},{5,7},{6,4},{7,5},{8,10},{9,11},{10,... | collective-permute-start | bytes 3145736 | tf_op jit(solution)/shard_map/ppermute | solution.py:51
  353.9 51.9 %collective-permute-start.42 = (bf16[256,1024]{1,0:T(8,128)(2,1)}, bf16[256,1024]{1,0:T(8,128)(2,1)}, u32[]{:S(2)}, u32[]{:S(2)}) collective-permute-start(bf16[256,1024]{1,0:T(8,128)(2,1)} %get-tuple-element.272), channel_id=1, source_target_pairs={{0,2},{1,3},{2,0},{3,1},{4,6},{5,7},{6,4},{7,5},{8,10},{9,11},{10,... | collective-permute-start | bytes 1572872 | tf_op jit(solution)/shard_map/ppermute | solution.py:51
  355.4 50.4 %collective-permute-start.43 = (bf16[256,1024]{1,0:T(8,128)(2,1)}, bf16[256,1024]{1,0:T(8,128)(2,1)}, u32[]{:S(2)}, u32[]{:S(2)}) collective-permute-start(bf16[256,1024]{1,0:T(8,128)(2,1)} %get-tuple-element.274), channel_id=1, source_target_pairs={{0,4},{1,5},{2,6},{3,7},{4,0},{5,1},{6,2},{7,3},{8,12},{9,13},{10,... | collective-permute-start | bytes 1572872 | tf_op jit(solution)/shard_map/ppermute | solution.py:51
  405.8 15.5 %collective-permute-start.45 = (bf16[512,4224]{1,0:T(8,128)(2,1)}, bf16[512,4224]{1,0:T(8,128)(2,1)}, u32[]{:S(2)}, u32[]{:S(2)}) collective-permute-start(bf16[512,4224]{1,0:T(8,128)(2,1)} %shard_map.387), channel_id=1, source_target_pairs={{0,1},{1,0},{2,3},{3,2},{4,5},{5,4},{6,7},{7,6},{8,9},{9,8},{10,11... | collective-permute-start | bytes 12976136 | tf_op jit(solution)/shard_map/ppermute | solution.py:51
  410.2 21.4 %collective-permute-start.46 = (bf16[64,4096]{1,0:T(8,128)(2,1)S(1)}, bf16[64,4096]{1,0:T(8,128)(2,1)S(1)}, u32[]{:S(2)}, u32[]{:S(2)}) collective-permute-start(bf16[64,4096]{1,0:T(8,128)(2,1)S(1)} %get-tuple-element.292), channel_id=1, source_target_pairs={{0,2},{1,3},{2,0},{3,1},{4,6},{5,7},{6,4},{7,5},{8,10},{9,11},{10,... | collective-permute-start | bytes 1572872 | tf_op jit(solution)/shard_map/ppermute | solution.py:51
  410.9 20.7 %collective-permute-start.47 = (bf16[64,4096]{1,0:T(8,128)(2,1)S(1)}, bf16[64,4096]{1,0:T(8,128)(2,1)S(1)}, u32[]{:S(2)}, u32[]{:S(2)}) collective-permute-start(bf16[64,4096]{1,0:T(8,128)(2,1)S(1)} %get-tuple-element.294), channel_id=1, source_target_pairs={{0,4},{1,5},{2,6},{3,7},{4,0},{5,1},{6,2},{7,3},{8,12},{9,13},{10,... | collective-permute-start | bytes 1572872 | tf_op jit(solution)/shard_map/ppermute | solution.py:51
  432.9 64.8 %collective-permute-start.51 = (bf16[128,4224]{1,0:T(8,128)(2,1)}, bf16[128,4224]{1,0:T(8,128)(2,1)S(1)}, u32[]{:S(2)}, u32[]{:S(2)}) collective-permute-start(bf16[128,4224]{1,0:T(8,128)(2,1)} %get-tuple-element.313), channel_id=1, source_target_pairs={{0,4},{1,5},{2,6},{3,7},{4,0},{5,1},{6,2},{7,3},{8,12},{9,13},{10,... | collective-permute-start | bytes 3244040 | tf_op jit(solution)/shard_map/ppermute | solution.py:51
  434.5 64.2 %collective-permute-start.52 = (bf16[128,4224]{1,0:T(8,128)(2,1)}, bf16[128,4224]{1,0:T(8,128)(2,1)}, u32[]{:S(2)}, u32[]{:S(2)}) collective-permute-start(bf16[128,4224]{1,0:T(8,128)(2,1)} %get-tuple-element.316), channel_id=1, source_target_pairs={{0,2},{1,3},{2,0},{3,1},{4,6},{5,7},{6,4},{7,5},{8,10},{9,11},{10,... | collective-permute-start | bytes 3244040 | tf_op jit(solution)/shard_map/ppermute | solution.py:51
  435.9 9.9 %collective-permute-start.48 = (bf16[128,1024]{1,0:T(8,128)(2,1)S(1)}, bf16[128,1024]{1,0:T(8,128)(2,1)S(1)}, u32[]{:S(2)}, u32[]{:S(2)}) collective-permute-start(bf16[128,1024]{1,0:T(8,128)(2,1)S(1)} %get-tuple-element.284), channel_id=1, source_target_pairs={{0,8},{1,9},{2,10},{3,11},{4,12},{5,13},{6,14},{7,15},{8,0},{9,1},... | collective-permute-start | bytes 786440 | tf_op jit(solution)/shard_map/ppermute | solution.py:51
  435.9 21.1 %collective-permute-start.49 = (bf16[128,1024]{1,0:T(8,128)(2,1)S(1)}, bf16[128,1024]{1,0:T(8,128)(2,1)S(1)}, u32[]{:S(2)}, u32[]{:S(2)}) collective-permute-start(bf16[128,1024]{1,0:T(8,128)(2,1)S(1)} %get-tuple-element.285), channel_id=1, source_target_pairs={{0,16},{1,17},{2,18},{3,19},{4,20},{5,21},{6,22},{7,23},{8,24},{9,... | collective-permute-start | bytes 786440 | tf_op jit(solution)/shard_map/ppermute | solution.py:51
  439.1 22.4 %collective-permute-start.50 = (bf16[128,1024]{1,0:T(8,128)(2,1)S(1)}, bf16[128,1024]{1,0:T(8,128)(2,1)S(1)}, u32[]{:S(2)}, u32[]{:S(2)}) collective-permute-start(bf16[128,1024]{1,0:T(8,128)(2,1)S(1)} %get-tuple-element.286), channel_id=1, source_target_pairs={{0,24},{1,25},{2,26},{3,27},{4,28},{5,29},{6,30},{7,31},{8,16},{9,... | collective-permute-start | bytes 786440 | tf_op jit(solution)/shard_map/ppermute | solution.py:51
  462.1 33.5 %collective-permute-start.54 = (bf16[32,4096]{1,0:T(8,128)(2,1)S(1)}, bf16[32,4096]{1,0:T(8,128)(2,1)S(1)}, u32[]{:S(2)}, u32[]{:S(2)}) collective-permute-start(bf16[32,4096]{1,0:T(8,128)(2,1)S(1)} %get-tuple-element.323), channel_id=1, source_target_pairs={{0,8},{1,9},{2,10},{3,11},{4,12},{5,13},{6,14},{7,15},{8,0},{9,1},... | collective-permute-start | bytes 786440 | tf_op jit(solution)/shard_map/ppermute | solution.py:51
  462.1 34.2 %collective-permute-start.55 = (bf16[32,4096]{1,0:T(8,128)(2,1)S(1)}, bf16[32,4096]{1,0:T(8,128)(2,1)S(1)}, u32[]{:S(2)}, u32[]{:S(2)}) collective-permute-start(bf16[32,4096]{1,0:T(8,128)(2,1)S(1)} %get-tuple-element.324), channel_id=1, source_target_pairs={{0,16},{1,17},{2,18},{3,19},{4,20},{5,21},{6,22},{7,23},{8,24},{9,... | collective-permute-start | bytes 786440 | tf_op jit(solution)/shard_map/ppermute | solution.py:51
  465.3 31.7 %collective-permute-start.56 = (bf16[32,4096]{1,0:T(8,128)(2,1)S(1)}, bf16[32,4096]{1,0:T(8,128)(2,1)S(1)}, u32[]{:S(2)}, u32[]{:S(2)}) collective-permute-start(bf16[32,4096]{1,0:T(8,128)(2,1)S(1)} %get-tuple-element.325), channel_id=1, source_target_pairs={{0,24},{1,25},{2,26},{3,27},{4,28},{5,29},{6,30},{7,31},{8,16},{9,... | collective-permute-start | bytes 786440 | tf_op jit(solution)/shard_map/ppermute | solution.py:51
  498.7 19.6 %collective-permute-start.57 = (bf16[512,4224]{1,0:T(8,128)(2,1)}, bf16[512,4224]{1,0:T(8,128)(2,1)}, u32[]{:S(2)}, u32[]{:S(2)}) collective-permute-start(bf16[512,4224]{1,0:T(8,128)(2,1)} %shard_map.394), channel_id=1, source_target_pairs={{0,1},{1,0},{2,3},{3,2},{4,5},{5,4},{6,7},{7,6},{8,9},{9,8},{10,11... | collective-permute-start | bytes 12976136 | tf_op jit(solution)/shard_map/ppermute | solution.py:51
  510.8 14.7 %collective-permute-start.53 = (bf16[64,4224]{1,0:T(8,128)(2,1)S(1)}, bf16[64,4224]{1,0:T(8,128)(2,1)S(1)}, u32[]{:S(2)}, u32[]{:S(2)}) collective-permute-start(bf16[64,4224]{1,0:T(8,128)(2,1)S(1)} %get-tuple-element.319), channel_id=1, source_target_pairs={{0,2},{1,3},{2,0},{3,1},{4,6},{5,7},{6,4},{7,5},{8,10},{9,11},{10,... | collective-permute-start | bytes 1622024 | tf_op jit(solution)/shard_map/ppermute | solution.py:51
  511.5 14.4 %collective-permute-start.58 = (bf16[64,4224]{1,0:T(8,128)(2,1)S(1)}, bf16[64,4224]{1,0:T(8,128)(2,1)S(1)}, u32[]{:S(2)}, u32[]{:S(2)}) collective-permute-start(bf16[64,4224]{1,0:T(8,128)(2,1)S(1)} %get-tuple-element.321), channel_id=1, source_target_pairs={{0,4},{1,5},{2,6},{3,7},{4,0},{5,1},{6,2},{7,3},{8,12},{9,13},{10,... | collective-permute-start | bytes 1622024 | tf_op jit(solution)/shard_map/ppermute | solution.py:51
  534.1 26.5 %collective-permute-start.60 = (bf16[128,4224]{1,0:T(8,128)(2,1)}, bf16[128,4224]{1,0:T(8,128)(2,1)S(1)}, u32[]{:S(2)}, u32[]{:S(2)}) collective-permute-start(bf16[128,4224]{1,0:T(8,128)(2,1)} %get-tuple-element.340), channel_id=1, source_target_pairs={{0,4},{1,5},{2,6},{3,7},{4,0},{5,1},{6,2},{7,3},{8,12},{9,13},{10,... | collective-permute-start | bytes 3244040 | tf_op jit(solution)/shard_map/ppermute | solution.py:51
  535.8 26.3 %collective-permute-start.61 = (bf16[128,4224]{1,0:T(8,128)(2,1)}, bf16[128,4224]{1,0:T(8,128)(2,1)}, u32[]{:S(2)}, u32[]{:S(2)}) collective-permute-start(bf16[128,4224]{1,0:T(8,128)(2,1)} %get-tuple-element.344), channel_id=1, source_target_pairs={{0,2},{1,3},{2,0},{3,1},{4,6},{5,7},{6,4},{7,5},{8,10},{9,11},{10,... | collective-permute-start | bytes 3244040 | tf_op jit(solution)/shard_map/ppermute | solution.py:51
  564.7 13.7 %collective-permute-start.62 = (bf16[64,4224]{1,0:T(8,128)(2,1)S(1)}, bf16[64,4224]{1,0:T(8,128)(2,1)S(1)}, u32[]{:S(2)}, u32[]{:S(2)}) collective-permute-start(bf16[64,4224]{1,0:T(8,128)(2,1)S(1)} %get-tuple-element.346), channel_id=1, source_target_pairs={{0,2},{1,3},{2,0},{3,1},{4,6},{5,7},{6,4},{7,5},{8,10},{9,11},{10,... | collective-permute-start | bytes 1622024 | tf_op jit(solution)/shard_map/ppermute | solution.py:51
  566.2 13.3 %collective-permute-start.63 = (bf16[64,4224]{1,0:T(8,128)(2,1)S(1)}, bf16[64,4224]{1,0:T(8,128)(2,1)S(1)}, u32[]{:S(2)}, u32[]{:S(2)}) collective-permute-start(bf16[64,4224]{1,0:T(8,128)(2,1)S(1)} %get-tuple-element.347), channel_id=1, source_target_pairs={{0,4},{1,5},{2,6},{3,7},{4,0},{5,1},{6,2},{7,3},{8,12},{9,13},{10,... | collective-permute-start | bytes 1622024 | tf_op jit(solution)/shard_map/ppermute | solution.py:51
  566.7 13.4 %collective-permute-start.65 = (bf16[32,4224]{1,0:T(8,128)(2,1)S(1)}, bf16[32,4224]{1,0:T(8,128)(2,1)S(1)}, u32[]{:S(2)}, u32[]{:S(2)}) collective-permute-start(bf16[32,4224]{1,0:T(8,128)(2,1)S(1)} %copy-done.88), channel_id=1, source_target_pairs={{0,8},{1,9},{2,10},{3,11},{4,12},{5,13},{6,14},{7,15},{8,0},{9,1},... | collective-permute-start | bytes 811016 | tf_op jit(solution)/shard_map/ppermute | solution.py:51
  567.7 20.5 %collective-permute-start.66 = (bf16[32,4224]{1,0:T(8,128)(2,1)S(1)}, bf16[32,4224]{1,0:T(8,128)(2,1)S(1)}, u32[]{:S(2)}, u32[]{:S(2)}) collective-permute-start(bf16[32,4224]{1,0:T(8,128)(2,1)S(1)} %copy-done.86), channel_id=1, source_target_pairs={{0,16},{1,17},{2,18},{3,19},{4,20},{5,21},{6,22},{7,23},{8,24},{9,... | collective-permute-start | bytes 811016 | tf_op jit(solution)/shard_map/ppermute | solution.py:51
  569.7 23.0 %collective-permute-start.67 = (bf16[32,4224]{1,0:T(8,128)(2,1)S(1)}, bf16[32,4224]{1,0:T(8,128)(2,1)S(1)}, u32[]{:S(2)}, u32[]{:S(2)}) collective-permute-start(bf16[32,4224]{1,0:T(8,128)(2,1)S(1)} %copy-done.84), channel_id=1, source_target_pairs={{0,24},{1,25},{2,26},{3,27},{4,28},{5,29},{6,30},{7,31},{8,16},{9,... | collective-permute-start | bytes 811016 | tf_op jit(solution)/shard_map/ppermute | solution.py:51
  579.5 41.0 %collective-permute-start.64 = (bf16[256,1024]{1,0:T(8,128)(2,1)S(1)}, bf16[256,1024]{1,0:T(8,128)(2,1)S(1)}, u32[]{:S(2)}, u32[]{:S(2)}) collective-permute-start(bf16[256,1024]{1,0:T(8,128)(2,1)S(1)} %dynamic-slice_bitcast_fusion), channel_id=1, source_target_pairs={{0,2},{1,3},{2,0},{3,1},{4,6},{5,7},{6,4},{7,5},{8,10},{9,11},{10,... | collective-permute-start | bytes 1572872 | tf_op jit(solution)/shard_map/ppermute | solution.py:51
  594.1 9.5 %collective-permute-start.68 = (bf16[32,4224]{1,0:T(8,128)(2,1)S(1)}, bf16[32,4224]{1,0:T(8,128)(2,1)S(1)}, u32[]{:S(2)}, u32[]{:S(2)}) collective-permute-start(bf16[32,4224]{1,0:T(8,128)(2,1)S(1)} %get-tuple-element.357), channel_id=1, source_target_pairs={{0,8},{1,9},{2,10},{3,11},{4,12},{5,13},{6,14},{7,15},{8,0},{9,1},... | collective-permute-start | bytes 811016 | tf_op jit(solution)/shard_map/ppermute | solution.py:51
  594.2 20.5 %collective-permute-start.69 = (bf16[32,4224]{1,0:T(8,128)(2,1)S(1)}, bf16[32,4224]{1,0:T(8,128)(2,1)S(1)}, u32[]{:S(2)}, u32[]{:S(2)}) collective-permute-start(bf16[32,4224]{1,0:T(8,128)(2,1)S(1)} %get-tuple-element.358), channel_id=1, source_target_pairs={{0,16},{1,17},{2,18},{3,19},{4,20},{5,21},{6,22},{7,23},{8,24},{9,... | collective-permute-start | bytes 811016 | tf_op jit(solution)/shard_map/ppermute | solution.py:51
  597.3 21.7 %collective-permute-start.70 = (bf16[32,4224]{1,0:T(8,128)(2,1)S(1)}, bf16[32,4224]{1,0:T(8,128)(2,1)S(1)}, u32[]{:S(2)}, u32[]{:S(2)}) collective-permute-start(bf16[32,4224]{1,0:T(8,128)(2,1)S(1)} %get-tuple-element.359), channel_id=1, source_target_pairs={{0,24},{1,25},{2,26},{3,27},{4,28},{5,29},{6,30},{7,31},{8,16},{9,... | collective-permute-start | bytes 811016 | tf_op jit(solution)/shard_map/ppermute | solution.py:51
  (120 other events, 954.0 us)

commit v3 on v2

--- a/solution.py
+++ b/solution.py
@@ -400,9 +400,8 @@
 
 
 PAIR = 2 * HD
-BLOCK = 128
+BLOCK = 256
 DIMS_NT = (((1,), (1,)), ((), ()))
-DIMS_TN = (((0,), (0,)), ((), ()))
 
 
 def head_of(array, which, scale=None):
@@ -412,40 +411,56 @@
     return (out if scale is None else out * scale).astype(BF)
 
 
-def probabilities(q, k, bias):
-    scores = lax.dot_general(q, k, DIMS_NT, preferred_element_type=F32) + bias
-    exponent = jnp.exp(scores - jnp.max(scores, axis=-1, keepdims=True))
-    return exponent * (1.0 / jnp.sum(exponent, axis=-1, keepdims=True))
-
-
-def pair_forward(q, k, v, bias):
-    lane = lax.broadcasted_iota(jnp.int32, q.shape, 1)
-    outs = []
-    for which in range(2):
-        probs = probabilities(head_of(q, which, SCORE_SCALE), k, bias)
-        outs.append(matmul(probs.astype(BF), v))
-    return jnp.where(lane < HD, outs[0], outs[1]).astype(BF)
-
-
-def pair_backward(q, k, v, grad, bias):
-    gq, gk, gv = 0.0, 0.0, 0.0
-    for which in range(2):
-        q_one = head_of(q, which, SCORE_SCALE)
-        g_one = head_of(grad, which)
-        probs = probabilities(q_one, k, bias)
-        dprob = lax.dot_general(g_one, v, DIMS_NT, preferred_element_type=F32)
-        delta = jnp.sum(probs * dprob, axis=-1, keepdims=True)
-        dscore = (probs * (dprob - delta)).astype(BF)
-        gq = gq + matmul(dscore, head_of(k, which, SCORE_SCALE))
-        gk = gk + lax.dot_general(dscore, q_one, DIMS_TN, preferred_element_type=F32)
-        gv = gv + lax.dot_general(probs.astype(BF), g_one, DIMS_TN, preferred_element_type=F32)
-    return gq, gk, gv
+def across(left, right):
+    return lax.dot_general(left, right, DIMS_NT, preferred_element_type=F32)
+
+
+def pair_forward(q, k, v_t, bias):
+    probs, sums = [], []
+    for n in range(2):
+        scores = across(k, head_of(q, n, SCORE_SCALE)) + bias
+        peak = jnp.max(scores, axis=0, keepdims=True)
+        exponent = jnp.exp(scores - peak)
+        total = jnp.sum(exponent, axis=0, keepdims=True)
+        probs.append((exponent * (1.0 / total)).astype(BF))
+        sums.append(peak + jnp.log(total))
+    outs = [matmul(v_t[n * HD : (n + 1) * HD, :], probs[n]) for n in range(2)]
+    return jnp.concatenate(outs, axis=0).T.astype(BF), sums
+
+
+TILE = 128
+
+
+def pair_backward(tiles, keys, bias_ref, sums_ref, q, k, v, out, grad, probs_ref, dscores_ref):
+    length = q.shape[0]
+    q_one = [head_of(q, n, SCORE_SCALE) for n in range(2)]
+    g_one = [head_of(grad, n) for n in range(2)]
+    both = (grad.astype(F32) * out.astype(F32)).T
+    delta = [jnp.sum(both[n * HD : (n + 1) * HD, :], axis=0, keepdims=True) for n in range(2)]
+    for key, query in tiles:
+        down, over = slice(key, key + TILE), slice(query, query + BLOCK)
+        for n in range(2):
+            scores = across(k[down, :], q_one[n][over, :]) + bias_ref[down, over]
+            probs = jnp.exp(scores - sums_ref[0, n : n + 1, over])
+            dprob = across(v[down, :], g_one[n][over, :])
+            at = slice(n * length + query, n * length + query + BLOCK)
+            probs_ref[down, at] = probs.astype(BF)
+            dscores_ref[down, at] = (probs * (dprob - delta[n][:, over])).astype(BF)
+    k_t = k.T
+    gq = [
+        matmul(k_t[n * HD : (n + 1) * HD, :], dscores_ref[:keys, n * length : (n + 1) * length])
+        for n in range(2)
+    ]
+    gq = jnp.concatenate(gq, axis=0).T * SCORE_SCALE
+    gk = matmul(dscores_ref[:keys, :], jnp.concatenate(q_one, axis=0))
+    gv = matmul(probs_ref[:keys, :], jnp.concatenate(g_one, axis=0))
+    return gq.astype(BF), gk.astype(BF), gv.astype(BF)
 
 
 def self_bias(column, row, pad):
     length = column.shape[0]
-    at_q = lax.broadcasted_iota(jnp.int32, (length, length), 0)
-    at_k = lax.broadcasted_iota(jnp.int32, (length, length), 1)
+    at_k = lax.broadcasted_iota(jnp.int32, (length, length), 0)
+    at_q = lax.broadcasted_iota(jnp.int32, (length, length), 1)
     live = (column == row) & (at_q >= at_k) & ((at_k < length - pad) | (at_q == at_k))
     return jnp.where(live, 0.0, MASKED)
 
@@ -454,6 +469,10 @@
     return pl.BlockSpec((array.shape[0], PAIR), lambda n: (0, n))
 
 
+def sums_spec(length):
+    return pl.BlockSpec((1, 8, length), lambda n: (n, 0, 0))
+
+
 def whole_spec(array):
     return pl.BlockSpec(array.shape, lambda n: (0,) * array.ndim)
 
@@ -461,62 +480,77 @@
 def self_forward(pad, column, row, q, k, v):
     length, width = q.shape
 
-    def kernel(pad_ref, column_ref, row_ref, q_ref, k_ref, v_ref, out_ref, bias_ref):
+    def kernel(pad_ref, column_ref, row_ref, q_ref, k_ref, v_ref, out_ref, sums_ref, bias_ref):
         @pl.when(pl.program_id(0) == 0)
         def _():
             bias_ref[...] = self_bias(column_ref[...], row_ref[...], pad_ref[0])
 
+        v_t = v_ref[...].T
         for start in range(0, length, BLOCK):
-            mine, seen = pl.ds(start, BLOCK), pl.ds(0, start + BLOCK)
-            out_ref[mine, :] = pair_forward(
-                q_ref[mine, :], k_ref[seen, :], v_ref[seen, :], bias_ref[mine, seen]
+            mine, seen = slice(start, start + BLOCK), slice(0, start + BLOCK)
+            out_ref[mine, :], sums = pair_forward(
+                q_ref[mine, :], k_ref[seen, :], v_t[:, seen], bias_ref[seen, mine]
             )
+            for n in range(2):
+                sums_ref[0, n : n + 1, mine] = sums[n]
 
     return call(
         kernel,
         grid=(width // PAIR,),
-        out_shape=jax.ShapeDtypeStruct(q.shape, BF),
+        out_shape=[
+            jax.ShapeDtypeStruct(q.shape, BF),
+            jax.ShapeDtypeStruct((width // PAIR, 8, length), F32),
+        ],
         in_specs=[pl.BlockSpec(memory_space=pltpu.SMEM), whole_spec(column), whole_spec(row)]
         + [pair_spec(q)] * 3,
-        out_specs=pair_spec(q),
+        out_specs=[pair_spec(q), sums_spec(length)],
         scratch_shapes=[pltpu.VMEM((length, length), F32)],
         compiler_params=pltpu.CompilerParams(vmem_limit_bytes=40 * 2**20),
     )(pad, column, row, q, k, v)
 
 
-def self_backward(pad, column, row, q, k, v, grad):
+def self_backward(pad, column, row, sums, q, k, v, out, grad):
     length, width = q.shape
-
-    def kernel(pad_ref, column_ref, row_ref, q_ref, k_ref, v_ref, g_ref, gq_ref, gk_ref, gv_ref, bias_ref, k_sum, v_sum):
+    tiles = [
+        (key, query)
+        for query in range(0, length, BLOCK)
+        for key in range(0, query + BLOCK, TILE)
+    ]
+
+    def kernel(pad_ref, column_ref, row_ref, sums_ref, *refs):
+        q_ref, k_ref, v_ref, o_ref, g_ref, gq_ref, gk_ref, gv_ref, bias_ref, probs_ref, ds_ref = refs
+
         @pl.when(pl.program_id(0) == 0)
         def _():
             bias_ref[...] = self_bias(column_ref[...], row_ref[...], pad_ref[0])
-
-        for start in reversed(range(0, length, BLOCK)):
-            mine, seen = pl.ds(start, BLOCK), pl.ds(0, start + BLOCK)
-            gq, gk, gv = pair_backward(
-                q_ref[mine, :], k_ref[seen, :], v_ref[seen, :], g_ref[mine, :], bias_ref[mine, seen]
-            )
-            gq_ref[mine, :] = gq.astype(BF)
-            if start + BLOCK == length:
-                k_sum[...] = gk
-                v_sum[...] = gv
-            else:
-                k_sum[seen, :] += gk
-                v_sum[seen, :] += gv
-        gk_ref[...] = k_sum[...].astype(BF)
-        gv_ref[...] = v_sum[...].astype(BF)
+            probs_ref[...] = jnp.zeros_like(probs_ref)
+            ds_ref[...] = jnp.zeros_like(ds_ref)
+
+        gq_ref[...], gk_ref[...], gv_ref[...] = pair_backward(
+            tiles,
+            length,
+            bias_ref,
+            sums_ref,
+            q_ref[...],
+            k_ref[...],
+            v_ref[...],
+            o_ref[...],
+            g_ref[...],
+            probs_ref,
+            ds_ref,
+        )
 
     return call(
         kernel,
         grid=(width // PAIR,),
         out_shape=[jax.ShapeDtypeStruct(q.shape, BF)] * 3,
-        in_specs=[pl.BlockSpec(memory_space=pltpu.SMEM), whole_spec(column), whole_spec(row)]
-        + [pair_spec(q)] * 4,
+        in_specs=[SCALARS, whole_spec(column), whole_spec(row), sums_spec(length)]
+        + [pair_spec(q)] * 5,
         out_specs=[pair_spec(q)] * 3,
-        scratch_shapes=[pltpu.VMEM((length, length), F32)] + [pltpu.VMEM((length, PAIR), F32)] * 2,
-        compiler_params=pltpu.CompilerParams(vmem_limit_bytes=40 * 2**20),
-    )(pad, column, row, q, k, v, grad)
+        scratch_shapes=[pltpu.VMEM((length, length), F32)]
+        + [pltpu.VMEM((length, 2 * length), BF)] * 2,
+        compiler_params=params(),
+    )(pad, column, row, sums, q, k, v, out, grad)
 
 
 def windows(total):
@@ -533,7 +567,7 @@
     for size in windows(total):
         start = jnp.clip(low // 16 * 16, 0, total - size)
         starts.append(start)
-        rows.append(lax.dynamic_slice(ids, (start,), (size,)).reshape(1, size))
+        rows.append(lax.dynamic_slice(ids, (start,), (size,)).reshape(size, 1))
         choice = choice + (high - start > size).astype(jnp.int32)
     return jnp.stack([choice] + starts), rows
 
@@ -551,64 +585,76 @@
 
     def kernel(window_ref, column_ref, *refs):
         row_refs = refs[: len(rows)]
-        q_ref, k_ref, v_ref, out_ref, bias_ref = refs[len(rows) :]
+        q_ref, k_ref, v_ref, out_ref, sums_ref, bias_ref = refs[len(rows) :]
 
         def run(n, size, seen):
             @pl.when(pl.program_id(0) == 0)
             def _():
-                bias_ref[:, :size] = jnp.where(column_ref[...] == row_refs[n][...], 0.0, MASKED)
-
+                bias_ref[:size, :] = jnp.where(row_refs[n][...] == column_ref[...], 0.0, MASKED)
+
+            v_t = v_ref[seen, :].T
             for start in range(0, length, BLOCK):
-                mine = pl.ds(start, BLOCK)
-                out_ref[mine, :] = pair_forward(
-                    q_ref[mine, :], k_ref[seen, :], v_ref[seen, :], bias_ref[mine, :size]
+                mine = slice(start, start + BLOCK)
+                out_ref[mine, :], sums = pair_forward(
+                    q_ref[mine, :], k_ref[seen, :], v_t, bias_ref[:size, mine]
                 )
+                for m in range(2):
+                    sums_ref[0, m : m + 1, mine] = sums[m]
 
         on_window(window_ref, total, run)
 
     return call(
         kernel,
         grid=(width // PAIR,),
-        out_shape=jax.ShapeDtypeStruct(q.shape, BF),
+        out_shape=[
+            jax.ShapeDtypeStruct(q.shape, BF),
+            jax.ShapeDtypeStruct((width // PAIR, 8, length), F32),
+        ],
         in_specs=[pl.BlockSpec(memory_space=pltpu.SMEM), whole_spec(column)]
         + [whole_spec(row) for row in rows]
         + [pair_spec(q), pair_spec(k), pair_spec(v)],
-        out_specs=pair_spec(q),
-        scratch_shapes=[pltpu.VMEM((length, total), F32)],
+        out_specs=[pair_spec(q), sums_spec(length)],
+        scratch_shapes=[pltpu.VMEM((total, length), F32)],
         compiler_params=pltpu.CompilerParams(vmem_limit_bytes=40 * 2**20),
     )(window, column, *rows, q, k, v)
 
 
-def cross_backward(window, column, rows, q, k, v, grad):
+def cross_backward(window, row, ids, sums, q, k, v, out, grad):
     length, width = q.shape
     total = k.shape[0]
 
-    def kernel(window_ref, column_ref, *refs):
-        row_refs = refs[: len(rows)]
-        q_ref, k_ref, v_ref, g_ref, gq_ref, gk_ref, gv_ref, bias_ref, k_sum, v_sum = refs[len(rows) :]
+    def kernel(window_ref, row_ref, sums_ref, *refs):
+        id_refs = refs[: len(ids)]
+        q_ref, k_ref, v_ref, o_ref, g_ref, gq_ref, gk_ref, gv_ref, bias_ref, probs_ref, ds_ref = refs[
+            len(ids) :
+        ]
 
         def run(n, size, seen):
             @pl.when(pl.program_id(0) == 0)
             def _():
-                bias_ref[:, :size] = jnp.where(column_ref[...] == row_refs[n][...], 0.0, MASKED)
+                bias_ref[:size, :] = jnp.where(id_refs[n][...] == row_ref[...], 0.0, MASKED)
 
             if size < total:
                 gk_ref[...] = jnp.zeros_like(gk_ref)
                 gv_ref[...] = jnp.zeros_like(gv_ref)
-            for start in range(0, length, BLOCK):
-                mine = pl.ds(start, BLOCK)
-                gq, gk, gv = pair_backward(
-                    q_ref[mine, :], k_ref[seen, :], v_ref[seen, :], g_ref[mine, :], bias_ref[mine, :size]
-                )
-                gq_ref[mine, :] = gq.astype(BF)
-                if start == 0:
-                    k_sum[:size, :] = gk
-                    v_sum[:size, :] = gv
-                else:
-                    k_sum[:size, :] += gk
-                    v_sum[:size, :] += gv
-            gk_ref[seen, :] = k_sum[:size, :].astype(BF)
-            gv_ref[seen, :] = v_sum[:size, :].astype(BF)
+            tiles = [
+                (key, query)
+                for query in range(0, length, BLOCK)
+                for key in range(0, size, TILE)
+            ]
+            gq_ref[...], gk_ref[seen, :], gv_ref[seen, :] = pair_backward(
+                tiles,
+                size,
+                bias_ref,
+                sums_ref,
+                q_ref[...],
+                k_ref[seen, :],
+                v_ref[seen, :],
+                o_ref[...],
+                g_ref[...],
+                probs_ref,
+                ds_ref,
+            )
 
         on_window(window_ref, total, run)
 
@@ -616,13 +662,14 @@
         kernel,
         grid=(width // PAIR,),
         out_shape=[jax.ShapeDtypeStruct(a.shape, BF) for a in (q, k, v)],
-        in_specs=[pl.BlockSpec(memory_space=pltpu.SMEM), whole_spec(column)]
-        + [whole_spec(row) for row in rows]
-        + [pair_spec(q), pair_spec(k), pair_spec(v), pair_spec(q)],
+        in_specs=[SCALARS, whole_spec(row), sums_spec(length)]
+        + [whole_spec(a) for a in ids]
+        + [pair_spec(q), pair_spec(k), pair_spec(v), pair_spec(q), pair_spec(q)],
         out_specs=[pair_spec(q), pair_spec(k), pair_spec(v)],
-        scratch_shapes=[pltpu.VMEM((length, total), F32)] + [pltpu.VMEM((total, PAIR), F32)] * 2,
-        compiler_params=pltpu.CompilerParams(vmem_limit_bytes=40 * 2**20),
-    )(window, column, *rows, q, k, v, grad)
+        scratch_shapes=[pltpu.VMEM((total, length), F32)]
+        + [pltpu.VMEM((total, 2 * length), BF)] * 2,
+        compiler_params=params(),
+    )(window, row, sums, *ids, q, k, v, out, grad)
 
 
 def body(
@@ -690,9 +737,9 @@
 
     vectors = [norm1_gain, norm1_bias, norm2_gain, norm2_bias, norm3_gain, norm3_bias]
     vectors = jnp.pad(jnp.stack(vectors, axis=1).astype(BF), ((0, 0), (0, 122)))
-    self_piece = side_by_side([self_query, self_key, self_value, self_output, vectors])
+    self_piece = side_by_side([self_query, self_key, self_value, self_output])
     self_z = gather_z(self_piece)
-    cross_piece = side_by_side([cross_query, cross_key, cross_value, cross_output])
+    cross_piece = side_by_side([cross_query, cross_key, cross_value, cross_output, vectors])
     many = ffn_down.shape[0] // own_rows
     ffn_piece = side_by_side(
         [ffn_up] + [ffn_down[n * own_rows : (n + 1) * own_rows] for n in range(many)]
@@ -750,16 +797,14 @@
             )
     ids_all = ids_all.reshape(-1)
 
-    w_sq, w_sk, w_sv, w_so, vectors = assemble(
+    w_sq, w_sk, w_sv, w_so = assemble(
         grid,
         positions,
         self_a,
         self_b,
-        [(n * width, width, n, 0) for n in range(4)] + [(4 * width, 128, 4, 0)],
-        [(own_rows, width)] * 4 + [(own_rows, 128)],
-    )
-    vectors = vectors[:, :6].T.astype(F32)
-    gain1, bias1, gain2, bias2, gain3, bias3 = [vectors[n] for n in range(6)]
+        [(n * width, width, n, 0) for n in range(4)],
+        [(own_rows, width)] * 4,
+    )
 
     segment = dec_segment.reshape(-1)
     column, row = segment.reshape(-1, 1), segment.reshape(1, -1)
@@ -769,29 +814,31 @@
     q = matmul(hidden, w_sq).astype(BF)
     k = matmul(hidden, w_sk).astype(BF)
     v = matmul(hidden, w_sv).astype(BF)
-    cross_pair = cross_ag.second(q, k, v)
-    self_att = self_forward(pad_length, column, row, after(q, *cross_pair), k, v)
+    cross_pair = cross_ag.second(w_sq)
+    self_att, self_sums = self_forward(pad_length, column, row, after(q, *cross_pair, *rows), k, v)
     ffn_pair = stacked(ffn_z, self_att)
     cross_a, cross_b = cross_ag.cores(self_att)
     cross_got = cross_a[0][1:] + cross_b[0][1:]
     ffn_ag.first(hold(ffn_pair, *cross_got))
-    first, normal1, scale1 = norm_forward(
-        ALPHA_RES * hidden.astype(F32) + matmul(after(self_att, *cross_got), w_so), gain1, bias1
-    )
-    first_low = first.astype(BF)
-    w_cq, w_ck, w_cv, w_co = assemble(
+    w_cq, w_ck, w_cv, w_co, vectors = assemble(
         grid,
         positions,
         cross_a,
         cross_b,
-        [(n * width, width, n, 0) for n in range(4)],
-        [(own_rows, width)] * 4,
-    )
+        [(n * width, width, n, 0) for n in range(4)] + [(4 * width, 128, 4, 0)],
+        [(own_rows, width)] * 4 + [(own_rows, 128)],
+    )
+    vectors = vectors[:, :6].T.astype(F32)
+    gain1, bias1, gain2, bias2, gain3, bias3 = [vectors[n] for n in range(6)]
+    first, normal1, scale1 = norm_forward(
+        ALPHA_RES * hidden.astype(F32) + matmul(after(self_att, *cross_got), w_so), gain1, bias1
+    )
+    first_low = first.astype(BF)
     cq = matmul(first_low, w_cq).astype(BF)
     mk = matmul(mem_all, w_ck).astype(BF)
     mv = matmul(mem_all, w_cv).astype(BF)
     ffn_pair = ffn_ag.second(cq, mk, mv)
-    cross_att = cross_forward(window, column, rows, after(cq, *ffn_pair), mk, mv)
+    cross_att, cross_sums = cross_forward(window, row, rows, after(cq, *ffn_pair), mk, mv)
     second, normal2, scale2 = norm_forward(
         ALPHA_RES * first + matmul(cross_att, w_co), gain2, bias2
     )
@@ -849,7 +896,15 @@
 
     cross_norms = spread([g_gain2, g_bias2, g_gain3, g_bias3])
     grad_cq, grad_mk, grad_mv = cross_backward(
-        window, column, rows, cq, mk, mv, after(grad_catt, *down_kept, cross_norms[0])
+        window,
+        row,
+        rows,
+        cross_sums,
+        cq,
+        mk,
+        mv,
+        cross_att,
+        after(grad_catt, *down_kept, cross_norms[0]),
     )
     cross = Reduction(
         grid,
@@ -872,12 +927,20 @@
     cross_kept = cross.keep()
     up.wait(*cross_kept)
     up_kept = up.add_second()
-    cross.hold(*up_kept)
+    cross.hold(*up_kept, *down.got_a)
     cross.first()
     up.a = [after(a, *down.got_a) for a in up.a]
     up.last()
     grad_q, grad_k, grad_v = self_backward(
-        pad_length, column, row, q, k, v, after(grad_satt, *cross_kept, *up_kept, *down.got_a)
+        pad_length,
+        column,
+        row,
+        self_sums,
+        q,
+        k,
+        v,
+        self_att,
+        after(grad_satt, *cross_kept, *up_kept, *down.got_a),
     )
     own = Reduction(
         grid,
@@ -888,12 +951,7 @@
     cross.wait(own.away)
     cross_kept = cross.add_first()
     cross.second()
-    grad_in = (
-        ALPHA_RES * grad_res
-        + outer_right(after(grad_q, own.away, *cross_kept), w_sq)
-        + outer_right(grad_k, w_sk)
-        + outer_right(grad_v, w_sv)
-    )
+    grad_in = ALPHA_RES * grad_res + outer_right(after(grad_q, own.away, *cross_kept), w_sq)
     own.wait(grad_in)
     own_kept = own.keep()
     own.hold(*cross.got_a, *cross.got_b)
@@ -901,21 +959,24 @@
     cross.wait(*own_kept)
     cross_kept = cross.add_second()
     cross.last()
-    grad_mem = outer_right(after(grad_mk, *cross_kept), w_ck) + outer_right(grad_mv, w_cv)
+    grad_in = grad_in + outer_right(after(grad_k, *own_kept), w_sk) + outer_right(grad_v, w_sv)
+    grad_mem = outer_right(after(grad_mk, *own_kept), w_ck) + outer_right(grad_mv, w_cv)
     grad_mem = grad_mem.reshape(ny, 2, mem_rows, width)
     mem_own = [lax.dynamic_index_in_dim(grad_mem, n ^ here["c"], 1, keepdims=False) for n in range(2)]
-    mem_own = mem_own[0] + grid.exchange(mem_own[1].astype(BF), "c", 1).astype(F32)
-    mem_own = [lax.dynamic_index_in_dim(mem_own, n ^ here["y"], 0, keepdims=False) for n in range(ny)]
+    mem_away = mem_own[1].astype(BF)
     (out_down,) = down.finish([width])
     (out_up,) = up.finish([ffn])
-    own.wait(out_down, out_up, *mem_own)
+    own.wait(out_down, out_up, mem_away, mem_own[0], grad_in, *cross.got_a)
+    own_got = own.got_a + own.got_b
     own_kept = own.add_first()
     own.second()
+    mem_own = mem_own[0] + grid.exchange(after(mem_away, *own_got), "c", 1).astype(F32)
+    mem_own = [lax.dynamic_index_in_dim(mem_own, n ^ here["y"], 0, keepdims=False) for n in range(ny)]
+    mem_away = [a.astype(BF) for a in mem_own[1:]]
     out_mem = mem_own[0]
-    mem_own = [after(a, *own.got_a, *own.got_b) for a in mem_own]
     for n in range(1, ny):
-        out_mem = out_mem + grid.exchange(mem_own[n].astype(BF), "y", n).astype(F32)
-    own.wait(*cross.got_a)
+        got = grid.exchange(after(mem_away[n - 1], *own.got_a, *own.got_b), "y", n)
+        out_mem = out_mem + got.astype(F32)
     out_co, out_cq, out_ck, out_cv, late = cross.finish([width] * 4 + [128])
     own.wait(out_co)
     own.add_second()

time: 632 us -> 548 us (0.87)
  Pallas kernels: 224 us -> 182 us
  waiting for transfers between devices: 168 us -> 130 us
  matrix products: 98.3 us -> 89.8 us
    ppermute x71, waiting for transfers between devices: 168 us -> 130 us  [exchange(): return lax.ppermute(array, BOTH, pairs)]
    pallas_call x2, Pallas kernels: 49.6 us -> 24.4 us  [the longest x1 13.8 us: cross_forward(): call(kernel, grid=(width // PAIR,), out_shape=[jax.ShapeDtypeStruct(q.sha...]
    pallas_call x1, Pallas kernels: 29.7 us -> 17.2 us  [cross_backward(): call(kernel, grid=(width // PAIR,), out_shape=[jax.ShapeDtypeStruct(a.sha...]
    pallas_call x1, Pallas kernels: 22.8 us -> 13.7 us  [self_backward(): call(kernel, grid=(width // PAIR,), out_shape=[jax.ShapeDtypeStruct(q.sha...]
    unnamed x229 -> x221, local copies, waits for them, and re-layouts: 38.4 us -> 30.2 us
    dot_general x10, matrix products: 46.2 us -> 39.7 us  [matmul(): return jnp.dot(left, right, preferred_element_type=F32)]
  transfers between devices with their start and end apart: 71 -> 71, of which waited for: 31 -> 27; matrix products, arithmetic and copies ran while one was open for 16% -> 18% of each run, Pallas kernels for 29% -> 26%
where the time goes in v3:
time: 548 us; the launch traced here: 538 us
  Pallas kernels  182 us (33%)
  waiting for transfers between devices  130 us (24%)
  matrix products  89.8 us (16%)
  starting transfers between devices  64.7 us (12%)
  local copies, waits for them, and re-layouts  39.4 us (7%)
  other arithmetic  24.1 us (4%)
  between operations  7.87 us (1%)
    ppermute x71, waiting for transfers between devices, exchange(): return lax.ppermute(array, BOTH, pairs)  130 us
    ppermute x71, starting transfers between devices, exchange(): return lax.ppermute(array, BOTH, pairs)  64.7 us
    pallas_call x8, Pallas kernels, products(): call(kernel, grid=(steps,), out_shape=[jax.ShapeDtypeStruct((size, width)...  52.4 us
    dot_general x10, matrix products, outer_right(): lax.dot_general(left, right, (((1,), (1,)), ((), ())), preferred_element_...  50.1 us
    dot_general x10, matrix products, matmul(): return jnp.dot(left, right, preferred_element_type=F32)  39.7 us
    unnamed x221, local copies, waits for them, and re-layouts  30.2 us
    pallas_call x3, Pallas kernels, assemble(): call(kernel, out_shape=[jax.ShapeDtypeStruct((len(blocks),) + shape, BF)...  29.5 us
    pallas_call x1, Pallas kernels, cross_backward(): call(kernel, grid=(width // PAIR,), out_shape=[jax.ShapeDtypeStruct(a.sha...  17.2 us
  transfers between devices with their start and end apart: 71, of which 27 were waited for; matrix products, arithmetic and copies ran while one was open for 18% of the time, Pallas kernels for 26%

profile of v3, /device:TPU:8, one launch (start us, length us, event | category | flops | bytes accessed | tf_op | source)
XLA Modules:
  0.0 538.2 jit_solution(14039289286319344877)
XLA Ops:
  2.4 3.0 collective-permute-start.3
  15.4 8.4 %collective-permute-done.3.refs_2_ = bf16[32,4096]{1,0:T(8,128)(2,1)S(1)} collective-permute-done((bf16[32,4096]{1,0:T(8,128)(2,1)}, bf16[32,4096]{1,0:T(8,128)(2,1)S(1)}, u32[]{:S(2)}, u32[]{:S(2)}) %collective-permute-start.3) | collective-permute-done | bytes 262176 | tf_op jit(solution)/shard_map/ppermute | solution.py:51
  23.7 5.0 collective-permute-done.4.refs_3_
  37.0 8.9 %collective-permute-done.5.refs_1_ = bf16[2,32,4096]{2,1,0:T(8,128)(2,1)S(1)} collective-permute-done((bf16[2,32,4096]{2,1,0:T(8,128)(2,1)S(1)}, bf16[2,32,4096]{2,1,0:T(8,128)(2,1)S(1)}, u32[]{:S(2)}, u32[]{:S(2)}) %collective-permute-start.5) | collective-permute-done | bytes 524320 | tf_op jit(solution)/shard_map/ppermute | solution.py:51
  50.2 3.0 collective-permute-start.11
  53.2 5.9 %collective-permute-done.10.refs_1_ = bf16[32,4224]{1,0:T(8,128)(2,1)S(1)} collective-permute-done((bf16[32,4224]{1,0:T(8,128)(2,1)S(1)}, bf16[32,4224]{1,0:T(8,128)(2,1)S(1)}, u32[]{:S(2)}, u32[]{:S(2)}) %collective-permute-start.10) | collective-permute-done | bytes 270368 | tf_op jit(solution)/shard_map/ppermute | solution.py:51
  61.1 10.0 %collective-permute-done.11.refs_2_ = bf16[32,4224]{1,0:T(8,128)(2,1)S(1)} collective-permute-done((bf16[32,4224]{1,0:T(8,128)(2,1)S(1)}, bf16[32,4224]{1,0:T(8,128)(2,1)S(1)}, u32[]{:S(2)}, u32[]{:S(2)}) %collective-permute-start.11) | collective-permute-done | bytes 270368 | tf_op jit(solution)/shard_map/ppermute | solution.py:51
  71.1 6.6 %collective-permute-done.12.refs_3_ = bf16[32,4224]{1,0:T(8,128)(2,1)S(1)} collective-permute-done((bf16[32,4224]{1,0:T(8,128)(2,1)S(1)}, bf16[32,4224]{1,0:T(8,128)(2,1)S(1)}, u32[]{:S(2)}, u32[]{:S(2)}) %collective-permute-start.12) | collective-permute-done | bytes 270368 | tf_op jit(solution)/shard_map/ppermute | solution.py:51
  88.2 2.9 collective-permute-start.27
  92.9 7.7 %shard_map.364 = (bf16[32,32,1024]{2,1,0:T(8,128)(2,1)}, bf16[32,32,1024]{2,1,0:T(8,128)(2,1)}, bf16[32,32,1024]{2,1,0:T(8,128)(2,1)}, bf16[32,32,1024]{2,1,0:T(8,128)(2,1)}) custom-call(s32[32]{0:T(128)S(1)} %stack.230.where, bf16[2,2,32,4096]{3,2,1,0:T(8,128)(2,1)S(1)} %get-tuple-element.211.refs_0_, ...), custom_call_target="tpu_custom_call" | custom-call | flops 1 | bytes 1 | tf_op jit(solution)/shard_map/pallas_call | solution.py:164
  105.2 2.9 fusion.15.q_ref.refs_0_
  111.4 10.5 %shard_map.366 = (bf16[512,1024]{1,0:T(8,128)(2,1)S(1)}, f32[8,8,512]{2,1,0:T(8,128)S(1)}) custom-call(s32[1]{0:T(128)S(6)} %copy.95.pad_ref, s32[512,1]{1,0:T(8,128)S(1)} %copy.74.column_ref, s32[1,512]{1,0:T(1,128)S(1)} %copy-done.79, bf16[512,1024]{1,0:T(8,128)(2,1)S(1)} %fusion.15.q_ref.refs_0_, bf16[512,1024]{1,0:T(8,128)(2,1)S(1)} %fusion.16.k_ref.refs_1_, ...), custom_call_target="tpu_custom_call" | custom-call | flops 1 | bytes 1 | tf_op jit(solution)/shard_map/pallas_call | solution.py:497
  122.6 4.3 collective-permute-done.20.refs_1_
  129.6 7.1 %collective-permute-done.28.refs_3_ = bf16[32,8192]{1,0:T(8,128)(2,1)S(1)} collective-permute-done((bf16[32,8192]{1,0:T(8,128)(2,1)}, bf16[32,8192]{1,0:T(8,128)(2,1)S(1)}, u32[]{:S(2)}, u32[]{:S(2)}) %collective-permute-start.28) | collective-permute-done | bytes 524320 | tf_op jit(solution)/shard_map/ppermute | solution.py:51
  136.7 2.0 shard_map.368
  140.1 3.0 fusion.38
  145.0 8.6 %shard_map.367 = (bf16[32,32,1024]{2,1,0:T(8,128)(2,1)}, bf16[32,32,1024]{2,1,0:T(8,128)(2,1)}, bf16[32,32,1024]{2,1,0:T(8,128)(2,1)}, bf16[32,32,1024]{2,1,0:T(8,128)(2,1)}, bf16[32,32,128]{2,1,0:T(8,128)(2,1)S(1)}) custom-call(s32[32]{0:T(128)S(1)} %stack.230.where, bf16[2,2,32,4224]{3,2,1,0:T(8,128)(2,1)S(1)} %get-tuple-element.227.refs_0_, ...), custom_call_target="tpu_custom_call" | custom-call | flops 1 | bytes 1 | tf_op jit(solution)/shard_map/pallas_call | solution.py:164
  153.9 2.1 fusion.13.left_ref
  156.1 2.2 convolution_convert_fusion.7.refs_3_
  158.3 3.8 convolution_convert_fusion.1.refs_4_
  162.1 3.7 convolution_convert_fusion.refs_5_
  167.0 4.0 shard_map.370
  182.9 13.8 %shard_map.371 = (bf16[512,1024]{1,0:T(8,128)(2,1)S(1)}, f32[8,8,512]{2,1,0:T(8,128)S(1)}) custom-call(s32[4]{0:T(128)S(1)} %pad_add_fusion.1.window_ref, s32[1,512]{1,0:T(1,128)S(1)} %copy-done.79, s32[512,1]{1,0:T(8,128)S(1)} %copy-done.29, s32[640,1]{1,0:T(8,128)S(1)} %copy.77.refs_1_, s32[1024,1]{1,0:T(8,128)S(1)} %copy-done.12, ...), custom_call_target="tpu_custom_call" | custom-call | flops 1 | bytes 1 | tf_op jit(solution)/shard_map/pallas_call | solution.py:606
  203.4 12.6 %collective-permute-done.31.refs_1_ = bf16[2,2,32,8192]{3,2,1,0:T(8,128)(2,1)} collective-permute-done((bf16[2,2,32,8192]{3,2,1,0:T(8,128)(2,1)}, bf16[2,2,32,8192]{3,2,1,0:T(8,128)(2,1)}, u32[]{:S(2)}, u32[]{:S(2)}) %collective-permute-start.31) | collective-permute-done | bytes 2097184 | tf_op jit(solution)/shard_map/ppermute | solution.py:51
  223.5 13.1 %shard_map.378 = (bf16[32,32,4096]{2,1,0:T(8,128)(2,1)}, bf16[32,128,1024]{2,1,0:T(8,128)(2,1)}) custom-call(s32[32]{0:T(128)S(1)} %stack.230.where, bf16[2,2,32,8192]{3,2,1,0:T(8,128)(2,1)S(1)} %copy-done.33, bf16[2,2,32,8192]{3,2,1,0:T(8,128)(2,1)} %collective-permute-done.31.refs_1_, bf16[2,2,32,8192]{3,2,1,0:T(8,128)(2,1)} %copy-done.91, ...), custom_call_target="tpu_custom_call" | custom-call | flops 1 | bytes 1 | tf_op jit(solution)/shard_map/pallas_call | solution.py:164
  236.7 10.2 %multiply_convert_fusion = (bf16[512,4096]{1,0:T(8,128)(2,1)}, f32[512,4096]{1,0:T(8,128)}) fusion(bf16[512,1024]{1,0:T(8,128)(2,1)S(1)} %fusion.14.left_ref, bf16[1024,4096]{1,0:T(8,128)(2,1)} %bitcast.181), kind=kOutput, calls=%fused_computation.7 | convolution fusion | flops 4305453056 | bytes 22020096 | tf_op jit(solution)/shard_map/dot_general | solution.py:378
  246.9 3.6 shard_map.379.refs_0_
  250.5 10.0 %fusion.40 = (f32[512]{0:T(512)S(1)}, f32[512,1024]{1,0:T(8,128)S(1)}) fusion(bf16[512,4096]{1,0:T(8,128)(2,1)} %get-tuple-element.420.left_ref, bf16[4096,1024]{1,0:T(8,128)(2,1)} %bitcast.183, f32[1024]{0:T(1024)S(1)} %bitcast.172, f32[1024]{0:T(1024)S(1)} %bitcast.158, f32[512]{0:T(512)S(1)} %add_rsqrt_fusion.1, ...), kind=kOutput, calls=%fused_computation.118 | convolution fusion | flops 4298636800 | bytes 16791552 | tf_op jit(solution)/shard_map/dot_general | solution.py:378
  265.3 4.5 shard_map.380
  270.0 11.5 %fusion.5.refs_1_ = bf16[512,4096]{1,0:T(8,128)(2,1)} fusion(f32[512,4096]{1,0:T(8,128)} %get-tuple-element.421, bf16[512,1024]{1,0:T(8,128)(2,1)S(1)} %get-tuple-element.261.refs_1_, bf16[4096,1024]{1,0:T(8,128)(2,1)} %bitcast.184), kind=kOutput, calls=%fused_computation.6 | convolution fusion | flops 4315938816 | bytes 22020096 | tf_op jit(solution)/shard_map/dot_general | solution.py:382
  281.4 2.1 copy-done.88
  283.5 5.1 shard_map.381
  288.6 5.1 shard_map.382
  296.5 11.4 %multiply_add_fusion.2 = f32[512,1024]{1,0:T(8,128)} fusion(bf16[512,4096]{1,0:T(8,128)(2,1)} %fusion.5.refs_1_, bf16[1024,4096]{1,0:T(8,128)(2,1)} %bitcast.182, f32[512]{0:T(512)S(1)} %broadcast_multiply_fusion.4, f32[512]{0:T(512)S(1)} %add_rsqrt_fusion, f32[512,1024]{1,0:T(8,128)} %copy-done.80, f32[512]{0:T(512)S(1)} %broadcast_multiply_fusion.6, ...), kind=kOutput, calls=%fused_computation.30 | convolution fusion | flops 4300210176 | bytes 17838080 | tf_op jit(solution)/shard_map/dot_general | solution.py:382
  307.9 6.7 %shard_map.383 = (bf16[128,4096]{1,0:T(8,128)(2,1)S(1)}, bf16[128,4096]{1,0:T(8,128)(2,1)}, bf16[128,4096]{1,0:T(8,128)(2,1)S(1)}, bf16[128,4096]{1,0:T(8,128)(2,1)}) custom-call(bf16[1024,512]{1,0:T(8,128)(2,1)S(1)} %shard_map.374.refs_0_, bf16[512,4096]{1,0:T(8,128)(2,1)} %fusion.5.refs_1_, bf16[512,4096]{1,0:T(8,128)(2,1)} %collective-permute-done.38.refs_2_), custom_call_target="tpu_custom_call" | custom-call | flops 1 | bytes 1 | tf_op jit(solution)/shard_map/pallas_call | solution.py:240
  314.7 3.3 multiply_reduce_fusion.2
  320.1 2.3 convolution_convert_fusion.6.refs_7_
  322.4 2.5 shard_map.384
  339.4 17.2 %shard_map.386 = (bf16[512,1024]{1,0:T(8,128)(2,1)S(1)}, bf16[1024,1024]{1,0:T(8,128)(2,1)}, bf16[1024,1024]{1,0:T(8,128)(2,1)}) custom-call(s32[4]{0:T(128)S(1)} %pad_add_fusion.1.window_ref, s32[1,512]{1,0:T(1,128)S(1)} %copy-done.79, f32[8,8,512]{2,1,0:T(8,128)S(1)} %copy-done.76, s32[512,1]{1,0:T(8,128)S(1)} %copy-done.30, s32[640,1]{1,0:T(8,128)S(1)} %copy.77.refs_1_, ...), custom_call_target="tpu_custom_call" | custom-call | flops 1 | bytes 1 | tf_op jit(solution)/shard_map/pallas_call | solution.py:661
  356.6 8.4 %shard_map.387 = bf16[512,4224]{1,0:T(8,128)(2,1)} custom-call(bf16[1024,512]{1,0:T(8,128)(2,1)S(1)} %copy-done.3, bf16[1024,512]{1,0:T(8,128)(2,1)S(1)} %shard_map.376.refs_1_, bf16[1024,1024]{1,0:T(8,128)(2,1)} %copy-done, bf16[1024,1024]{1,0:T(8,128)(2,1)} %copy-done, bf16[1024,128]{1,0:T(8,128)(2,1)S(1)} %shard_map.385.refs_4_, ...), custom_call_target="tpu_custom_call" | custom-call | flops 1 | bytes 1 | tf_op jit(solution)/shard_map/pallas_call | solution.py:240
  365.2 2.1 shard_map.388
  368.1 2.9 collective-permute-start.49
  371.0 2.8 shard_map.389
  375.6 4.3 multiply_reduce_fusion
  383.3 3.9 convolution_convert_fusion.5.refs_4_
  387.1 9.3 %shard_map.391 = (bf16[128,4224]{1,0:T(8,128)(2,1)S(1)}, bf16[128,4224]{1,0:T(8,128)(2,1)}, bf16[128,4224]{1,0:T(8,128)(2,1)}, bf16[128,4224]{1,0:T(8,128)(2,1)}) custom-call(bf16[1024,512]{1,0:T(8,128)(2,1)S(1)} %copy-done.3, bf16[1024,512]{1,0:T(8,128)(2,1)S(1)} %shard_map.376.refs_1_, bf16[1024,1024]{1,0:T(8,128)(2,1)} %copy-done, ...), custom_call_target="tpu_custom_call" | custom-call | flops 1 | bytes 1 | tf_op jit(solution)/shard_map/pallas_call | solution.py:240
  404.3 13.7 %shard_map.393 = (bf16[512,1024]{1,0:T(8,128)(2,1)S(1)}, bf16[512,1024]{1,0:T(8,128)(2,1)S(1)}, bf16[512,1024]{1,0:T(8,128)(2,1)S(1)}) custom-call(s32[1]{0:T(128)S(6)} %copy.95.pad_ref, s32[512,1]{1,0:T(8,128)S(1)} %copy-done.32, s32[1,512]{1,0:T(1,128)S(1)} %copy-done.79, f32[8,8,512]{2,1,0:T(8,128)S(1)} %copy-done.78, bf16[512,1024]{1,0:T(8,128)(2,1)S(1)} %copy-done.21, ...), custom_call_target="tpu_custom_call" | custom-call | flops 1 | bytes 1 | tf_op jit(solution)/shard_map/pallas_call | solution.py:543
  419.1 6.2 %shard_map.394 = bf16[512,4224]{1,0:T(8,128)(2,1)} custom-call(bf16[1024,512]{1,0:T(8,128)(2,1)S(1)} %shard_map.375.refs_0_, bf16[1024,512]{1,0:T(8,128)(2,1)S(1)} %shard_map.372.refs_1_.refs_2_.refs_3_, bf16[1024,512]{1,0:T(8,128)(2,1)S(1)} %shard_map.372.refs_1_.refs_2_.refs_3_, bf16[1024,512]{1,0:T(8,128)(2,1)S(1)} %shard_map.372.refs_1_.refs_2_.refs_3_, ...), custom_call_target="tpu_custom_call" | custom-call | flops 1 | bytes 1 | tf_op jit(solution)/shard_map/pallas_call | solution.py:240
  428.6 6.8 %fusion.42 = f32[1024,1024]{1,0:T(8,128)} fusion(bf16[1024,1024]{1,0:T(8,128)(2,1)} %get-tuple-element.285.refs_8_, bf16[1024,1024]{1,0:T(8,128)(2,1)} %bitcast.193), kind=kOutput, calls=%fused_computation.120 | convolution fusion | flops 2147483648 | bytes 8388608 | tf_op jit(solution)/shard_map/dot_general | solution.py:382
  437.3 2.8 shard_map.395
  443.2 7.0 %shard_map.396 = (bf16[128,4224]{1,0:T(8,128)(2,1)}, bf16[128,4224]{1,0:T(8,128)(2,1)}, bf16[128,4224]{1,0:T(8,128)(2,1)}, bf16[128,4224]{1,0:T(8,128)(2,1)}) custom-call(bf16[1024,512]{1,0:T(8,128)(2,1)S(1)} %shard_map.375.refs_0_, bf16[1024,512]{1,0:T(8,128)(2,1)S(1)} %shard_map.372.refs_1_.refs_2_.refs_3_, ...), custom_call_target="tpu_custom_call" | custom-call | flops 1 | bytes 1 | tf_op jit(solution)/shard_map/pallas_call | solution.py:240
  451.5 3.3 collective-permute-done.57.refs_1_
  457.8 2.6 add_add_fusion
  464.6 4.7 convolution_add_fusion
  472.1 10.3 %collective-permute-done.61.refs_2_ = bf16[32,4224]{1,0:T(8,128)(2,1)S(1)} collective-permute-done((bf16[32,4224]{1,0:T(8,128)(2,1)S(1)}, bf16[32,4224]{1,0:T(8,128)(2,1)S(1)}, u32[]{:S(2)}, u32[]{:S(2)}) %collective-permute-start.61) | collective-permute-done | bytes 270368 | tf_op jit(solution)/shard_map/ppermute | solution.py:51
  482.4 4.5 collective-permute-done.62.refs_3_
  488.0 3.3 shard_map.400
  492.7 2.2 convert_add_fusion
  495.9 9.4 %collective-permute-done.65.refs_1_ = bf16[64,4224]{1,0:T(8,128)(2,1)S(1)} collective-permute-done((bf16[64,4224]{1,0:T(8,128)(2,1)}, bf16[64,4224]{1,0:T(8,128)(2,1)S(1)}, u32[]{:S(2)}, u32[]{:S(2)}) %collective-permute-start.65) | collective-permute-done | bytes 540704 | tf_op jit(solution)/shard_map/ppermute | solution.py:51
  508.6 2.9 collective-permute-start.69
  512.8 5.2 collective-permute-done.68.refs_1_
  518.0 11.3 %collective-permute-done.69.refs_2_ = bf16[32,4224]{1,0:T(8,128)(2,1)S(1)} collective-permute-done((bf16[32,4224]{1,0:T(8,128)(2,1)S(1)}, bf16[32,4224]{1,0:T(8,128)(2,1)S(1)}, u32[]{:S(2)}, u32[]{:S(2)}) %collective-permute-start.69) | collective-permute-done | bytes 270368 | tf_op jit(solution)/shard_map/ppermute | solution.py:51
  529.3 4.4 collective-permute-done.70.refs_3_
  535.2 2.5 bitcast_add_fusion
  (432 shorter events, 142.5 us)
Async XLA Ops:
  2.4 13.0 %collective-permute-start.2 = (bf16[32,4096]{1,0:T(8,128)(2,1)}, bf16[32,4096]{1,0:T(8,128)(2,1)S(1)}, u32[]{:S(2)}, u32[]{:S(2)}) collective-permute-start(bf16[32,4096]{1,0:T(8,128)(2,1)} %shard_map.357.refs_0_), channel_id=1, source_target_pairs={{0,8},{1,9},{2,10},{3,11},{4,12},{5,13},{6,14},{7,15},{8,0},{9,1},... | collective-permute-start | bytes 786440 | tf_op jit(solution)/shard_map/ppermute | solution.py:51
  2.4 21.3 %collective-permute-start.3 = (bf16[32,4096]{1,0:T(8,128)(2,1)}, bf16[32,4096]{1,0:T(8,128)(2,1)S(1)}, u32[]{:S(2)}, u32[]{:S(2)}) collective-permute-start(bf16[32,4096]{1,0:T(8,128)(2,1)} %shard_map.357.refs_0_), channel_id=1, source_target_pairs={{0,16},{1,17},{2,18},{3,19},{4,20},{5,21},{6,22},{7,23},{8,24},{9,... | collective-permute-start | bytes 786440 | tf_op jit(solution)/shard_map/ppermute | solution.py:51
  5.4 23.3 %collective-permute-start.4 = (bf16[32,4096]{1,0:T(8,128)(2,1)}, bf16[32,4096]{1,0:T(8,128)(2,1)S(1)}, u32[]{:S(2)}, u32[]{:S(2)}) collective-permute-start(bf16[32,4096]{1,0:T(8,128)(2,1)} %shard_map.357.refs_0_), channel_id=1, source_target_pairs={{0,24},{1,25},{2,26},{3,27},{4,28},{5,29},{6,30},{7,31},{8,16},{9,... | collective-permute-start | bytes 786440 | tf_op jit(solution)/shard_map/ppermute | solution.py:51
  5.9 22.9 %collective-permute-start = (bf16[256,1024]{1,0:T(8,128)(2,1)}, bf16[256,1024]{1,0:T(8,128)(2,1)S(1)}, u32[]{:S(2)}, u32[]{:S(2)}) collective-permute-start(bf16[256,1024]{1,0:T(8,128)(2,1)} %refs_0_.6), channel_id=1, source_target_pairs={{0,2},{1,3},{2,0},{3,1},{4,6},{5,7},{6,4},{7,5},{8,10},{9,11},{10,... | collective-permute-start | bytes 1572872 | tf_op jit(solution)/shard_map/ppermute | solution.py:51
  28.9 17.0 %collective-permute-start.6 = (bf16[2,256,1024]{2,1,0:T(8,128)(2,1)S(1)}, bf16[2,256,1024]{2,1,0:T(8,128)(2,1)S(1)}, u32[]{:S(2)}, u32[]{:S(2)}) collective-permute-start(bf16[2,256,1024]{2,1,0:T(8,128)(2,1)S(1)} %shard_map.361.refs_0_), channel_id=1, source_target_pairs={{0,1},{1,0},{2,3},{3,2},{4,5},{5,4},{6,7},{7,6},{8,9},{9,8},{10,11... | collective-permute-start | bytes 3145736 | tf_op jit(solution)/shard_map/ppermute | solution.py:51
  32.7 13.2 %collective-permute-start.5 = (bf16[2,32,4096]{2,1,0:T(8,128)(2,1)S(1)}, bf16[2,32,4096]{2,1,0:T(8,128)(2,1)S(1)}, u32[]{:S(2)}, u32[]{:S(2)}) collective-permute-start(bf16[2,32,4096]{2,1,0:T(8,128)(2,1)S(1)} %get-tuple-element.205.refs_0_), channel_id=1, source_target_pairs={{0,4},{1,5},{2,6},{3,7},{4,0},{5,1},{6,2},{7,3},{8,12},{9,13},{10,... | collective-permute-start | bytes 1572872 | tf_op jit(solution)/shard_map/ppermute | solution.py:51
  34.3 12.8 %collective-permute-start.8 = (bf16[2,32,4096]{2,1,0:T(8,128)(2,1)S(1)}, bf16[2,32,4096]{2,1,0:T(8,128)(2,1)S(1)}, u32[]{:S(2)}, u32[]{:S(2)}) collective-permute-start(bf16[2,32,4096]{2,1,0:T(8,128)(2,1)S(1)} %get-tuple-element.209.refs_2_), channel_id=1, source_target_pairs={{0,2},{1,3},{2,0},{3,1},{4,6},{5,7},{6,4},{7,5},{8,10},{9,11},{10,... | collective-permute-start | bytes 1572872 | tf_op jit(solution)/shard_map/ppermute | solution.py:51
  47.3 31.5 %collective-permute-start.9 = (bf16[2,2,32,4096]{3,2,1,0:T(8,128)(2,1)S(1)}, bf16[2,2,32,4096]{3,2,1,0:T(8,128)(2,1)}, u32[]{:S(2)}, u32[]{:S(2)}) collective-permute-start(bf16[2,2,32,4096]{3,2,1,0:T(8,128)(2,1)S(1)} %get-tuple-element.211.refs_0_), channel_id=1, source_target_pairs={{0,2},{1,3},{2,0},{3,1},{4,6},{5,7},{6,4},{7,5},{8,10},{9,11},{10,... | collective-permute-start | bytes 3145736 | tf_op jit(solution)/shard_map/ppermute | solution.py:51
  48.9 30.0 %collective-permute-start.15 = (bf16[2,2,32,4096]{3,2,1,0:T(8,128)(2,1)S(1)}, bf16[2,2,32,4096]{3,2,1,0:T(8,128)(2,1)}, u32[]{:S(2)}, u32[]{:S(2)}) collective-permute-start(bf16[2,2,32,4096]{3,2,1,0:T(8,128)(2,1)S(1)} %get-tuple-element.213.refs_4_), channel_id=1, source_target_pairs={{0,4},{1,5},{2,6},{3,7},{4,0},{5,1},{6,2},{7,3},{8,12},{9,13},{10,... | collective-permute-start | bytes 3145736 | tf_op jit(solution)/shard_map/ppermute | solution.py:51
  50.2 30.1 %collective-permute-start.13 = (bf16[2,2,32,4096]{3,2,1,0:T(8,128)(2,1)S(1)}, bf16[2,2,32,4096]{3,2,1,0:T(8,128)(2,1)S(1)}, u32[]{:S(2)}, u32[]{:S(2)}) collective-permute-start(bf16[2,2,32,4096]{3,2,1,0:T(8,128)(2,1)S(1)} %get-tuple-element.211.refs_0_), channel_id=1, source_target_pairs={{0,1},{1,0},{2,3},{3,2},{4,5},{5,4},{6,7},{7,6},{8,9},{9,8},{10,11... | collective-permute-start | bytes 3145736 | tf_op jit(solution)/shard_map/ppermute | solution.py:51
  50.2 20.9 %collective-permute-start.11 = (bf16[32,4224]{1,0:T(8,128)(2,1)S(1)}, bf16[32,4224]{1,0:T(8,128)(2,1)S(1)}, u32[]{:S(2)}, u32[]{:S(2)}) collective-permute-start(bf16[32,4224]{1,0:T(8,128)(2,1)S(1)} %copy-done.34), channel_id=1, source_target_pairs={{0,16},{1,17},{2,18},{3,19},{4,20},{5,21},{6,22},{7,23},{8,24},{9,... | collective-permute-start | bytes 811016 | tf_op jit(solution)/shard_map/ppermute | solution.py:51
  59.0 18.7 %collective-permute-start.12 = (bf16[32,4224]{1,0:T(8,128)(2,1)S(1)}, bf16[32,4224]{1,0:T(8,128)(2,1)S(1)}, u32[]{:S(2)}, u32[]{:S(2)}) collective-permute-start(bf16[32,4224]{1,0:T(8,128)(2,1)S(1)} %copy-done.34), channel_id=1, source_target_pairs={{0,24},{1,25},{2,26},{3,27},{4,28},{5,29},{6,30},{7,31},{8,16},{9,... | collective-permute-start | bytes 811016 | tf_op jit(solution)/shard_map/ppermute | solution.py:51
  71.1 17.0 %collective-permute-start.16 = (bf16[2,2,32,4096]{3,2,1,0:T(8,128)(2,1)S(1)}, bf16[2,2,32,4096]{3,2,1,0:T(8,128)(2,1)}, u32[]{:S(2)}, u32[]{:S(2)}) collective-permute-start(bf16[2,2,32,4096]{3,2,1,0:T(8,128)(2,1)S(1)} %get-tuple-element.213.refs_4_), channel_id=1, source_target_pairs={{0,1},{1,0},{2,3},{3,2},{4,5},{5,4},{6,7},{7,6},{8,9},{9,8},{10,11... | collective-permute-start | bytes 3145736 | tf_op jit(solution)/shard_map/ppermute | solution.py:51
  78.9 12.2 %collective-permute-start.17 = (bf16[2,2,32,4096]{3,2,1,0:T(8,128)(2,1)}, bf16[2,2,32,4096]{3,2,1,0:T(8,128)(2,1)}, u32[]{:S(2)}, u32[]{:S(2)}) collective-permute-start(bf16[2,2,32,4096]{3,2,1,0:T(8,128)(2,1)} %collective-permute-done.15.refs_5_), channel_id=1, source_target_pairs={{0,1},{1,0},{2,3},{3,2},{4,5},{5,4},{6,7},{7,6},{8,9},{9,8},{10,11... | collective-permute-start | bytes 3145736 | tf_op jit(solution)/shard_map/ppermute | solution.py:51
  79.4 21.3 %collective-permute-start.18 = (bf16[2,32,4224]{2,1,0:T(8,128)(2,1)}, bf16[2,32,4224]{2,1,0:T(8,128)(2,1)}, u32[]{:S(2)}, u32[]{:S(2)}) collective-permute-start(bf16[2,32,4224]{2,1,0:T(8,128)(2,1)} %get-tuple-element.223.refs_0_), channel_id=1, source_target_pairs={{0,4},{1,5},{2,6},{3,7},{4,0},{5,1},{6,2},{7,3},{8,12},{9,13},{10,... | collective-permute-start | bytes 1622024 | tf_op jit(solution)/shard_map/ppermute | solution.py:51
  81.2 19.5 %collective-permute-start.19 = (bf16[2,32,4224]{2,1,0:T(8,128)(2,1)}, bf16[2,32,4224]{2,1,0:T(8,128)(2,1)}, u32[]{:S(2)}, u32[]{:S(2)}) collective-permute-start(bf16[2,32,4224]{2,1,0:T(8,128)(2,1)} %get-tuple-element.225.refs_2_), channel_id=1, source_target_pairs={{0,2},{1,3},{2,0},{3,1},{4,6},{5,7},{6,4},{7,5},{8,10},{9,11},{10,... | collective-permute-start | bytes 1622024 | tf_op jit(solution)/shard_map/ppermute | solution.py:51
  88.1 40.0 %collective-permute-start.26 = (bf16[32,8192]{1,0:T(8,128)(2,1)}, bf16[32,8192]{1,0:T(8,128)(2,1)S(1)}, u32[]{:S(2)}, u32[]{:S(2)}) collective-permute-start(bf16[32,8192]{1,0:T(8,128)(2,1)} %shard_map.359.refs_0_), channel_id=1, source_target_pairs={{0,8},{1,9},{2,10},{3,11},{4,12},{5,13},{6,14},{7,15},{8,0},{9,1},... | collective-permute-start | bytes 1572872 | tf_op jit(solution)/shard_map/ppermute | solution.py:51
  88.2 40.4 %collective-permute-start.27 = (bf16[32,8192]{1,0:T(8,128)(2,1)}, bf16[32,8192]{1,0:T(8,128)(2,1)S(1)}, u32[]{:S(2)}, u32[]{:S(2)}) collective-permute-start(bf16[32,8192]{1,0:T(8,128)(2,1)} %shard_map.359.refs_0_), channel_id=1, source_target_pairs={{0,16},{1,17},{2,18},{3,19},{4,20},{5,21},{6,22},{7,23},{8,24},{9,... | collective-permute-start | bytes 1572872 | tf_op jit(solution)/shard_map/ppermute | solution.py:51
  91.1 45.6 %collective-permute-start.28 = (bf16[32,8192]{1,0:T(8,128)(2,1)}, bf16[32,8192]{1,0:T(8,128)(2,1)S(1)}, u32[]{:S(2)}, u32[]{:S(2)}) collective-permute-start(bf16[32,8192]{1,0:T(8,128)(2,1)} %shard_map.359.refs_0_), channel_id=1, source_target_pairs={{0,24},{1,25},{2,26},{3,27},{4,28},{5,29},{6,30},{7,31},{8,16},{9,... | collective-permute-start | bytes 1572872 | tf_op jit(solution)/shard_map/ppermute | solution.py:51
  102.4 24.5 %collective-permute-start.20 = (bf16[2,2,32,4224]{3,2,1,0:T(8,128)(2,1)S(1)}, bf16[2,2,32,4224]{3,2,1,0:T(8,128)(2,1)S(1)}, u32[]{:S(2)}, u32[]{:S(2)}) collective-permute-start(bf16[2,2,32,4224]{3,2,1,0:T(8,128)(2,1)S(1)} %get-tuple-element.227.refs_0_), channel_id=1, source_target_pairs={{0,2},{1,3},{2,0},{3,1},{4,6},{5,7},{6,4},{7,5},{8,10},{9,11},{10,... | collective-permute-start | bytes 3244040 | tf_op jit(solution)/shard_map/ppermute | solution.py:51
  104.0 24.2 %collective-permute-start.21 = (bf16[2,2,32,4224]{3,2,1,0:T(8,128)(2,1)S(1)}, bf16[2,2,32,4224]{3,2,1,0:T(8,128)(2,1)S(1)}, u32[]{:S(2)}, u32[]{:S(2)}) collective-permute-start(bf16[2,2,32,4224]{3,2,1,0:T(8,128)(2,1)S(1)} %get-tuple-element.228.refs_4_), channel_id=1, source_target_pairs={{0,4},{1,5},{2,6},{3,7},{4,0},{5,1},{6,2},{7,3},{8,12},{9,13},{10,... | collective-permute-start | bytes 3244040 | tf_op jit(solution)/shard_map/ppermute | solution.py:51
  126.9 16.5 %collective-permute-start.22 = (bf16[2,2,32,4224]{3,2,1,0:T(8,128)(2,1)S(1)}, bf16[2,2,32,4224]{3,2,1,0:T(8,128)(2,1)S(1)}, u32[]{:S(2)}, u32[]{:S(2)}) collective-permute-start(bf16[2,2,32,4224]{3,2,1,0:T(8,128)(2,1)S(1)} %get-tuple-element.227.refs_0_), channel_id=1, source_target_pairs={{0,1},{1,0},{2,3},{3,2},{4,5},{5,4},{6,7},{7,6},{8,9},{9,8},{10,11... | collective-permute-start | bytes 3244040 | tf_op jit(solution)/shard_map/ppermute | solution.py:51
  128.1 16.9 %collective-permute-start.24 = (bf16[2,2,32,4224]{3,2,1,0:T(8,128)(2,1)S(1)}, bf16[2,2,32,4224]{3,2,1,0:T(8,128)(2,1)}, u32[]{:S(2)}, u32[]{:S(2)}) collective-permute-start(bf16[2,2,32,4224]{3,2,1,0:T(8,128)(2,1)S(1)} %get-tuple-element.228.refs_4_), channel_id=1, source_target_pairs={{0,1},{1,0},{2,3},{3,2},{4,5},{5,4},{6,7},{7,6},{8,9},{9,8},{10,11... | collective-permute-start | bytes 3244040 | tf_op jit(solution)/shard_map/ppermute | solution.py:51
  128.2 16.9 %collective-permute-start.23 = (bf16[2,2,32,4224]{3,2,1,0:T(8,128)(2,1)S(1)}, bf16[2,2,32,4224]{3,2,1,0:T(8,128)(2,1)S(1)}, u32[]{:S(2)}, u32[]{:S(2)}) collective-permute-start(bf16[2,2,32,4224]{3,2,1,0:T(8,128)(2,1)S(1)} %collective-permute-done.20.refs_1_), channel_id=1, source_target_pairs={{0,1},{1,0},{2,3},{3,2},{4,5},{5,4},{6,7},{7,6},{8,9},{9,8},{10,11... | collective-permute-start | bytes 3244040 | tf_op jit(solution)/shard_map/ppermute | solution.py:51
  128.7 16.4 %collective-permute-start.25 = (bf16[2,2,32,4224]{3,2,1,0:T(8,128)(2,1)S(1)}, bf16[2,2,32,4224]{3,2,1,0:T(8,128)(2,1)}, u32[]{:S(2)}, u32[]{:S(2)}) collective-permute-start(bf16[2,2,32,4224]{3,2,1,0:T(8,128)(2,1)S(1)} %collective-permute-done.21.refs_5_), channel_id=1, source_target_pairs={{0,1},{1,0},{2,3},{3,2},{4,5},{5,4},{6,7},{7,6},{8,9},{9,8},{10,11... | collective-permute-start | bytes 3244040 | tf_op jit(solution)/shard_map/ppermute | solution.py:51
  138.8 27.0 %collective-permute-start.29 = (bf16[2,32,8192]{2,1,0:T(8,128)(2,1)S(1)}, bf16[2,32,8192]{2,1,0:T(8,128)(2,1)}, u32[]{:S(2)}, u32[]{:S(2)}) collective-permute-start(bf16[2,32,8192]{2,1,0:T(8,128)(2,1)S(1)} %get-tuple-element.245.refs_0_), channel_id=1, source_target_pairs={{0,4},{1,5},{2,6},{3,7},{4,0},{5,1},{6,2},{7,3},{8,12},{9,13},{10,... | collective-permute-start | bytes 3145736 | tf_op jit(solution)/shard_map/ppermute | solution.py:51
  143.4 23.5 %collective-permute-start.30 = (bf16[2,32,8192]{2,1,0:T(8,128)(2,1)}, bf16[2,32,8192]{2,1,0:T(8,128)(2,1)}, u32[]{:S(2)}, u32[]{:S(2)}) collective-permute-start(bf16[2,32,8192]{2,1,0:T(8,128)(2,1)} %get-tuple-element.250.refs_2_), channel_id=1, source_target_pairs={{0,2},{1,3},{2,0},{3,1},{4,6},{5,7},{6,4},{7,5},{8,10},{9,11},{10,... | collective-permute-start | bytes 3145736 | tf_op jit(solution)/shard_map/ppermute | solution.py:51
  170.9 45.1 %collective-permute-start.31 = (bf16[2,2,32,8192]{3,2,1,0:T(8,128)(2,1)}, bf16[2,2,32,8192]{3,2,1,0:T(8,128)(2,1)}, u32[]{:S(2)}, u32[]{:S(2)}) collective-permute-start(bf16[2,2,32,8192]{3,2,1,0:T(8,128)(2,1)} %get-tuple-element.252.refs_0_), channel_id=1, source_target_pairs={{0,2},{1,3},{2,0},{3,1},{4,6},{5,7},{6,4},{7,5},{8,10},{9,11},{10,... | collective-permute-start | bytes 6291464 | tf_op jit(solution)/shard_map/ppermute | solution.py:51
  172.5 44.7 %collective-permute-start.34 = (bf16[2,2,32,8192]{3,2,1,0:T(8,128)(2,1)}, bf16[2,2,32,8192]{3,2,1,0:T(8,128)(2,1)}, u32[]{:S(2)}, u32[]{:S(2)}) collective-permute-start(bf16[2,2,32,8192]{3,2,1,0:T(8,128)(2,1)} %get-tuple-element.253.refs_4_), channel_id=1, source_target_pairs={{0,4},{1,5},{2,6},{3,7},{4,0},{5,1},{6,2},{7,3},{8,12},{9,13},{10,... | collective-permute-start | bytes 6291464 | tf_op jit(solution)/shard_map/ppermute | solution.py:51
  181.6 35.6 %collective-permute-start.32 = (bf16[2,2,32,8192]{3,2,1,0:T(8,128)(2,1)}, bf16[2,2,32,8192]{3,2,1,0:T(8,128)(2,1)S(1)}, u32[]{:S(2)}, u32[]{:S(2)}) collective-permute-start(bf16[2,2,32,8192]{3,2,1,0:T(8,128)(2,1)} %get-tuple-element.252.refs_0_), channel_id=1, source_target_pairs={{0,1},{1,0},{2,3},{3,2},{4,5},{5,4},{6,7},{7,6},{8,9},{9,8},{10,11... | collective-permute-start | bytes 6291464 | tf_op jit(solution)/shard_map/ppermute | solution.py:51
  202.5 14.8 %collective-permute-start.35 = (bf16[2,2,32,8192]{3,2,1,0:T(8,128)(2,1)S(1)}, bf16[2,2,32,8192]{3,2,1,0:T(8,128)(2,1)S(1)}, u32[]{:S(2)}, u32[]{:S(2)}) collective-permute-start(bf16[2,2,32,8192]{3,2,1,0:T(8,128)(2,1)S(1)} %copy-done.90), channel_id=1, source_target_pairs={{0,1},{1,0},{2,3},{3,2},{4,5},{5,4},{6,7},{7,6},{8,9},{9,8},{10,11... | collective-permute-start | bytes 6291464 | tf_op jit(solution)/shard_map/ppermute | solution.py:51
  269.8 11.7 %collective-permute-start.37 = (bf16[2048,1024]{1,0:T(8,128)(2,1)S(1)}, bf16[2048,1024]{1,0:T(8,128)(2,1)S(1)}, u32[]{:S(2)}, u32[]{:S(2)}) collective-permute-start(bf16[2048,1024]{1,0:T(8,128)(2,1)S(1)} %shard_map.380), channel_id=1, source_target_pairs={{0,1},{1,0},{2,3},{3,2},{4,5},{5,4},{6,7},{7,6},{8,9},{9,8},{10,11... | collective-permute-start | bytes 12582920 | tf_op jit(solution)/shard_map/ppermute | solution.py:51
  293.7 14.2 %collective-permute-start.38 = (bf16[512,4096]{1,0:T(8,128)(2,1)S(1)}, bf16[512,4096]{1,0:T(8,128)(2,1)}, u32[]{:S(2)}, u32[]{:S(2)}) collective-permute-start(bf16[512,4096]{1,0:T(8,128)(2,1)S(1)} %shard_map.382), channel_id=1, source_target_pairs={{0,1},{1,0},{2,3},{3,2},{4,5},{5,4},{6,7},{7,6},{8,9},{9,8},{10,11... | collective-permute-start | bytes 12582920 | tf_op jit(solution)/shard_map/ppermute | solution.py:51
  294.2 28.2 %collective-permute-start.39 = (bf16[512,1024]{1,0:T(8,128)(2,1)S(1)}, bf16[512,1024]{1,0:T(8,128)(2,1)S(1)}, u32[]{:S(2)}, u32[]{:S(2)}) collective-permute-start(bf16[512,1024]{1,0:T(8,128)(2,1)S(1)} %get-tuple-element.264), channel_id=1, source_target_pairs={{0,4},{1,5},{2,6},{3,7},{4,0},{5,1},{6,2},{7,3},{8,12},{9,13},{10,... | collective-permute-start | bytes 3145736 | tf_op jit(solution)/shard_map/ppermute | solution.py:51
  295.0 27.4 %collective-permute-start.40 = (bf16[512,1024]{1,0:T(8,128)(2,1)S(1)}, bf16[512,1024]{1,0:T(8,128)(2,1)}, u32[]{:S(2)}, u32[]{:S(2)}) collective-permute-start(bf16[512,1024]{1,0:T(8,128)(2,1)S(1)} %get-tuple-element.266), channel_id=1, source_target_pairs={{0,2},{1,3},{2,0},{3,1},{4,6},{5,7},{6,4},{7,5},{8,10},{9,11},{10,... | collective-permute-start | bytes 3145736 | tf_op jit(solution)/shard_map/ppermute | solution.py:51
  326.5 38.5 %collective-permute-start.41 = (bf16[128,4096]{1,0:T(8,128)(2,1)}, bf16[128,4096]{1,0:T(8,128)(2,1)}, u32[]{:S(2)}, u32[]{:S(2)}) collective-permute-start(bf16[128,4096]{1,0:T(8,128)(2,1)} %get-tuple-element.287), channel_id=1, source_target_pairs={{0,4},{1,5},{2,6},{3,7},{4,0},{5,1},{6,2},{7,3},{8,12},{9,13},{10,... | collective-permute-start | bytes 3145736 | tf_op jit(solution)/shard_map/ppermute | solution.py:51
  327.8 37.3 %collective-permute-start.44 = (bf16[128,4096]{1,0:T(8,128)(2,1)}, bf16[128,4096]{1,0:T(8,128)(2,1)}, u32[]{:S(2)}, u32[]{:S(2)}) collective-permute-start(bf16[128,4096]{1,0:T(8,128)(2,1)} %get-tuple-element.296), channel_id=1, source_target_pairs={{0,2},{1,3},{2,0},{3,1},{4,6},{5,7},{6,4},{7,5},{8,10},{9,11},{10,... | collective-permute-start | bytes 3145736 | tf_op jit(solution)/shard_map/ppermute | solution.py:51
  328.3 36.8 %collective-permute-start.42 = (bf16[256,1024]{1,0:T(8,128)(2,1)}, bf16[256,1024]{1,0:T(8,128)(2,1)}, u32[]{:S(2)}, u32[]{:S(2)}) collective-permute-start(bf16[256,1024]{1,0:T(8,128)(2,1)} %get-tuple-element.279), channel_id=1, source_target_pairs={{0,2},{1,3},{2,0},{3,1},{4,6},{5,7},{6,4},{7,5},{8,10},{9,11},{10,... | collective-permute-start | bytes 1572872 | tf_op jit(solution)/shard_map/ppermute | solution.py:51
  329.8 35.2 %collective-permute-start.43 = (bf16[256,1024]{1,0:T(8,128)(2,1)}, bf16[256,1024]{1,0:T(8,128)(2,1)}, u32[]{:S(2)}, u32[]{:S(2)}) collective-permute-start(bf16[256,1024]{1,0:T(8,128)(2,1)} %get-tuple-element.281), channel_id=1, source_target_pairs={{0,4},{1,5},{2,6},{3,7},{4,0},{5,1},{6,2},{7,3},{8,12},{9,13},{10,... | collective-permute-start | bytes 1572872 | tf_op jit(solution)/shard_map/ppermute | solution.py:51
  365.1 17.5 %collective-permute-start.45 = (bf16[512,4224]{1,0:T(8,128)(2,1)}, bf16[512,4224]{1,0:T(8,128)(2,1)}, u32[]{:S(2)}, u32[]{:S(2)}) collective-permute-start(bf16[512,4224]{1,0:T(8,128)(2,1)} %shard_map.387), channel_id=1, source_target_pairs={{0,1},{1,0},{2,3},{3,2},{4,5},{5,4},{6,7},{7,6},{8,9},{9,8},{10,11... | collective-permute-start | bytes 12976136 | tf_op jit(solution)/shard_map/ppermute | solution.py:51
  368.0 29.7 %collective-permute-start.48 = (bf16[128,1024]{1,0:T(8,128)(2,1)}, bf16[128,1024]{1,0:T(8,128)(2,1)S(1)}, u32[]{:S(2)}, u32[]{:S(2)}) collective-permute-start(bf16[128,1024]{1,0:T(8,128)(2,1)} %get-tuple-element.291), channel_id=1, source_target_pairs={{0,8},{1,9},{2,10},{3,11},{4,12},{5,13},{6,14},{7,15},{8,0},{9,1},... | collective-permute-start | bytes 786440 | tf_op jit(solution)/shard_map/ppermute | solution.py:51
  368.1 29.7 %collective-permute-start.49 = (bf16[128,1024]{1,0:T(8,128)(2,1)S(1)}, bf16[128,1024]{1,0:T(8,128)(2,1)S(1)}, u32[]{:S(2)}, u32[]{:S(2)}) collective-permute-start(bf16[128,1024]{1,0:T(8,128)(2,1)S(1)} %get-tuple-element.292), channel_id=1, source_target_pairs={{0,16},{1,17},{2,18},{3,19},{4,20},{5,21},{6,22},{7,23},{8,24},{9,... | collective-permute-start | bytes 786440 | tf_op jit(solution)/shard_map/ppermute | solution.py:51
  373.8 22.7 %collective-permute-start.46 = (bf16[64,4096]{1,0:T(8,128)(2,1)}, bf16[64,4096]{1,0:T(8,128)(2,1)S(1)}, u32[]{:S(2)}, u32[]{:S(2)}) collective-permute-start(bf16[64,4096]{1,0:T(8,128)(2,1)} %get-tuple-element.299), channel_id=1, source_target_pairs={{0,2},{1,3},{2,0},{3,1},{4,6},{5,7},{6,4},{7,5},{8,10},{9,11},{10,... | collective-permute-start | bytes 1572872 | tf_op jit(solution)/shard_map/ppermute | solution.py:51
  374.3 22.2 %collective-permute-start.47 = (bf16[64,4096]{1,0:T(8,128)(2,1)S(1)}, bf16[64,4096]{1,0:T(8,128)(2,1)S(1)}, u32[]{:S(2)}, u32[]{:S(2)}) collective-permute-start(bf16[64,4096]{1,0:T(8,128)(2,1)S(1)} %get-tuple-element.301), channel_id=1, source_target_pairs={{0,4},{1,5},{2,6},{3,7},{4,0},{5,1},{6,2},{7,3},{8,12},{9,13},{10,... | collective-permute-start | bytes 1572872 | tf_op jit(solution)/shard_map/ppermute | solution.py:51
  382.6 15.2 %collective-permute-start.50 = (bf16[128,1024]{1,0:T(8,128)(2,1)S(1)}, bf16[128,1024]{1,0:T(8,128)(2,1)S(1)}, u32[]{:S(2)}, u32[]{:S(2)}) collective-permute-start(bf16[128,1024]{1,0:T(8,128)(2,1)S(1)} %get-tuple-element.293), channel_id=1, source_target_pairs={{0,24},{1,25},{2,26},{3,27},{4,28},{5,29},{6,30},{7,31},{8,16},{9,... | collective-permute-start | bytes 786440 | tf_op jit(solution)/shard_map/ppermute | solution.py:51
  398.5 28.9 %collective-permute-start.51 = (bf16[128,4224]{1,0:T(8,128)(2,1)}, bf16[128,4224]{1,0:T(8,128)(2,1)S(1)}, u32[]{:S(2)}, u32[]{:S(2)}) collective-permute-start(bf16[128,4224]{1,0:T(8,128)(2,1)} %get-tuple-element.321), channel_id=1, source_target_pairs={{0,4},{1,5},{2,6},{3,7},{4,0},{5,1},{6,2},{7,3},{8,12},{9,13},{10,... | collective-permute-start | bytes 3244040 | tf_op jit(solution)/shard_map/ppermute | solution.py:51
  399.2 29.2 %collective-permute-start.52 = (bf16[128,4224]{1,0:T(8,128)(2,1)}, bf16[128,4224]{1,0:T(8,128)(2,1)}, u32[]{:S(2)}, u32[]{:S(2)}) collective-permute-start(bf16[128,4224]{1,0:T(8,128)(2,1)} %get-tuple-element.324), channel_id=1, source_target_pairs={{0,2},{1,3},{2,0},{3,1},{4,6},{5,7},{6,4},{7,5},{8,10},{9,11},{10,... | collective-permute-start | bytes 3244040 | tf_op jit(solution)/shard_map/ppermute | solution.py:51
  400.8 24.5 %collective-permute-start.53 = (bf16[32,4096]{1,0:T(8,128)(2,1)S(1)}, bf16[32,4096]{1,0:T(8,128)(2,1)S(1)}, u32[]{:S(2)}, u32[]{:S(2)}) collective-permute-start(bf16[32,4096]{1,0:T(8,128)(2,1)S(1)} %get-tuple-element.331), channel_id=1, source_target_pairs={{0,8},{1,9},{2,10},{3,11},{4,12},{5,13},{6,14},{7,15},{8,0},{9,1},... | collective-permute-start | bytes 786440 | tf_op jit(solution)/shard_map/ppermute | solution.py:51
  401.7 24.3 %collective-permute-start.54 = (bf16[32,4096]{1,0:T(8,128)(2,1)S(1)}, bf16[32,4096]{1,0:T(8,128)(2,1)S(1)}, u32[]{:S(2)}, u32[]{:S(2)}) collective-permute-start(bf16[32,4096]{1,0:T(8,128)(2,1)S(1)} %get-tuple-element.332), channel_id=1, source_target_pairs={{0,16},{1,17},{2,18},{3,19},{4,20},{5,21},{6,22},{7,23},{8,24},{9,... | collective-permute-start | bytes 786440 | tf_op jit(solution)/shard_map/ppermute | solution.py:51
  403.7 23.0 %collective-permute-start.55 = (bf16[32,4096]{1,0:T(8,128)(2,1)S(1)}, bf16[32,4096]{1,0:T(8,128)(2,1)S(1)}, u32[]{:S(2)}, u32[]{:S(2)}) collective-permute-start(bf16[32,4096]{1,0:T(8,128)(2,1)S(1)} %get-tuple-element.333), channel_id=1, source_target_pairs={{0,24},{1,25},{2,26},{3,27},{4,28},{5,29},{6,30},{7,31},{8,16},{9,... | collective-permute-start | bytes 786440 | tf_op jit(solution)/shard_map/ppermute | solution.py:51
  428.5 14.7 %collective-permute-start.56 = (bf16[512,4224]{1,0:T(8,128)(2,1)}, bf16[512,4224]{1,0:T(8,128)(2,1)}, u32[]{:S(2)}, u32[]{:S(2)}) collective-permute-start(bf16[512,4224]{1,0:T(8,128)(2,1)} %shard_map.394), channel_id=1, source_target_pairs={{0,1},{1,0},{2,3},{3,2},{4,5},{5,4},{6,7},{7,6},{8,9},{9,8},{10,11... | collective-permute-start | bytes 12976136 | tf_op jit(solution)/shard_map/ppermute | solution.py:51
  440.0 14.7 %collective-permute-start.57 = (bf16[64,4224]{1,0:T(8,128)(2,1)S(1)}, bf16[64,4224]{1,0:T(8,128)(2,1)S(1)}, u32[]{:S(2)}, u32[]{:S(2)}) collective-permute-start(bf16[64,4224]{1,0:T(8,128)(2,1)S(1)} %get-tuple-element.327), channel_id=1, source_target_pairs={{0,2},{1,3},{2,0},{3,1},{4,6},{5,7},{6,4},{7,5},{8,10},{9,11},{10,... | collective-permute-start | bytes 1622024 | tf_op jit(solution)/shard_map/ppermute | solution.py:51
  440.5 14.4 %collective-permute-start.58 = (bf16[64,4224]{1,0:T(8,128)(2,1)S(1)}, bf16[64,4224]{1,0:T(8,128)(2,1)S(1)}, u32[]{:S(2)}, u32[]{:S(2)}) collective-permute-start(bf16[64,4224]{1,0:T(8,128)(2,1)S(1)} %get-tuple-element.329), channel_id=1, source_target_pairs={{0,4},{1,5},{2,6},{3,7},{4,0},{5,1},{6,2},{7,3},{8,12},{9,13},{10,... | collective-permute-start | bytes 1622024 | tf_op jit(solution)/shard_map/ppermute | solution.py:51
  454.9 32.1 %collective-permute-start.59 = (bf16[128,4224]{1,0:T(8,128)(2,1)}, bf16[128,4224]{1,0:T(8,128)(2,1)S(1)}, u32[]{:S(2)}, u32[]{:S(2)}) collective-permute-start(bf16[128,4224]{1,0:T(8,128)(2,1)} %get-tuple-element.342), channel_id=1, source_target_pairs={{0,4},{1,5},{2,6},{3,7},{4,0},{5,1},{6,2},{7,3},{8,12},{9,13},{10,... | collective-permute-start | bytes 3244040 | tf_op jit(solution)/shard_map/ppermute | solution.py:51
  456.2 30.8 %collective-permute-start.63 = (bf16[128,4224]{1,0:T(8,128)(2,1)}, bf16[128,4224]{1,0:T(8,128)(2,1)S(1)}, u32[]{:S(2)}, u32[]{:S(2)}) collective-permute-start(bf16[128,4224]{1,0:T(8,128)(2,1)} %get-tuple-element.350), channel_id=1, source_target_pairs={{0,2},{1,3},{2,0},{3,1},{4,6},{5,7},{6,4},{7,5},{8,10},{9,11},{10,... | collective-permute-start | bytes 3244040 | tf_op jit(solution)/shard_map/ppermute | solution.py:51
  461.0 11.1 %collective-permute-start.60 = (bf16[32,4224]{1,0:T(8,128)(2,1)S(1)}, bf16[32,4224]{1,0:T(8,128)(2,1)S(1)}, u32[]{:S(2)}, u32[]{:S(2)}) collective-permute-start(bf16[32,4224]{1,0:T(8,128)(2,1)S(1)} %get-tuple-element.346), channel_id=1, source_target_pairs={{0,8},{1,9},{2,10},{3,11},{4,12},{5,13},{6,14},{7,15},{8,0},{9,1},... | collective-permute-start | bytes 811016 | tf_op jit(solution)/shard_map/ppermute | solution.py:51
  462.8 19.6 %collective-permute-start.61 = (bf16[32,4224]{1,0:T(8,128)(2,1)S(1)}, bf16[32,4224]{1,0:T(8,128)(2,1)S(1)}, u32[]{:S(2)}, u32[]{:S(2)}) collective-permute-start(bf16[32,4224]{1,0:T(8,128)(2,1)S(1)} %get-tuple-element.347), channel_id=1, source_target_pairs={{0,16},{1,17},{2,18},{3,19},{4,20},{5,21},{6,22},{7,23},{8,24},{9,... | collective-permute-start | bytes 811016 | tf_op jit(solution)/shard_map/ppermute | solution.py:51
  463.9 23.1 %collective-permute-start.62 = (bf16[32,4224]{1,0:T(8,128)(2,1)S(1)}, bf16[32,4224]{1,0:T(8,128)(2,1)S(1)}, u32[]{:S(2)}, u32[]{:S(2)}) collective-permute-start(bf16[32,4224]{1,0:T(8,128)(2,1)S(1)} %get-tuple-element.348), channel_id=1, source_target_pairs={{0,24},{1,25},{2,26},{3,27},{4,28},{5,29},{6,30},{7,31},{8,16},{9,... | collective-permute-start | bytes 811016 | tf_op jit(solution)/shard_map/ppermute | solution.py:51
  491.3 14.0 %collective-permute-start.65 = (bf16[64,4224]{1,0:T(8,128)(2,1)}, bf16[64,4224]{1,0:T(8,128)(2,1)S(1)}, u32[]{:S(2)}, u32[]{:S(2)}) collective-permute-start(bf16[64,4224]{1,0:T(8,128)(2,1)} %get-tuple-element.355), channel_id=1, source_target_pairs={{0,2},{1,3},{2,0},{3,1},{4,6},{5,7},{6,4},{7,5},{8,10},{9,11},{10,... | collective-permute-start | bytes 1622024 | tf_op jit(solution)/shard_map/ppermute | solution.py:51
  491.9 13.7 %collective-permute-start.66 = (bf16[64,4224]{1,0:T(8,128)(2,1)}, bf16[64,4224]{1,0:T(8,128)(2,1)S(1)}, u32[]{:S(2)}, u32[]{:S(2)}) collective-permute-start(bf16[64,4224]{1,0:T(8,128)(2,1)} %get-tuple-element.356), channel_id=1, source_target_pairs={{0,4},{1,5},{2,6},{3,7},{4,0},{5,1},{6,2},{7,3},{8,12},{9,13},{10,... | collective-permute-start | bytes 1622024 | tf_op jit(solution)/shard_map/ppermute | solution.py:51
  505.7 29.6 %collective-permute-start.67 = (bf16[256,1024]{1,0:T(8,128)(2,1)}, bf16[256,1024]{1,0:T(8,128)(2,1)}, u32[]{:S(2)}, u32[]{:S(2)}) collective-permute-start(bf16[256,1024]{1,0:T(8,128)(2,1)} %fusion.19), channel_id=1, source_target_pairs={{0,2},{1,3},{2,0},{3,1},{4,6},{5,7},{6,4},{7,5},{8,10},{9,11},{10,... | collective-permute-start | bytes 1572872 | tf_op jit(solution)/shard_map/ppermute | solution.py:51
  508.5 9.5 %collective-permute-start.68 = (bf16[32,4224]{1,0:T(8,128)(2,1)S(1)}, bf16[32,4224]{1,0:T(8,128)(2,1)S(1)}, u32[]{:S(2)}, u32[]{:S(2)}) collective-permute-start(bf16[32,4224]{1,0:T(8,128)(2,1)S(1)} %get-tuple-element.365), channel_id=1, source_target_pairs={{0,8},{1,9},{2,10},{3,11},{4,12},{5,13},{6,14},{7,15},{8,0},{9,1},... | collective-permute-start | bytes 811016 | tf_op jit(solution)/shard_map/ppermute | solution.py:51
  508.6 20.7 %collective-permute-start.69 = (bf16[32,4224]{1,0:T(8,128)(2,1)S(1)}, bf16[32,4224]{1,0:T(8,128)(2,1)S(1)}, u32[]{:S(2)}, u32[]{:S(2)}) collective-permute-start(bf16[32,4224]{1,0:T(8,128)(2,1)S(1)} %get-tuple-element.366), channel_id=1, source_target_pairs={{0,16},{1,17},{2,18},{3,19},{4,20},{5,21},{6,22},{7,23},{8,24},{9,... | collective-permute-start | bytes 811016 | tf_op jit(solution)/shard_map/ppermute | solution.py:51
  511.5 22.2 %collective-permute-start.70 = (bf16[32,4224]{1,0:T(8,128)(2,1)S(1)}, bf16[32,4224]{1,0:T(8,128)(2,1)S(1)}, u32[]{:S(2)}, u32[]{:S(2)}) collective-permute-start(bf16[32,4224]{1,0:T(8,128)(2,1)S(1)} %get-tuple-element.367), channel_id=1, source_target_pairs={{0,24},{1,25},{2,26},{3,27},{4,28},{5,29},{6,30},{7,31},{8,16},{9,... | collective-permute-start | bytes 811016 | tf_op jit(solution)/shard_map/ppermute | solution.py:51
  (116 other events, 863.8 us)

commit v4 on v3

--- a/solution.py
+++ b/solution.py
@@ -79,7 +79,7 @@
 call = functools.partial(pl.pallas_call, cost_estimate=SHORT)
 
 
-def params(mib=48):
+def params(mib=16):
     return pltpu.CompilerParams(vmem_limit_bytes=mib * 2**20)
 
 
@@ -167,7 +167,7 @@
         in_specs=[SCALARS] + [ANYWHERE] * len(arrays),
         out_specs=[pl.BlockSpec(memory_space=pltpu.VMEM)] * len(shapes),
         scratch_shapes=[pltpu.SemaphoreType.DMA((len(parts) * len(blocks),))],
-        compiler_params=params(),
+        compiler_params=params(4 + len(blocks) * sum(m * n for m, n in shapes) // 2**19),
     )(positions, *arrays)
     return [a.reshape(-1, a.shape[2]) for a in out]
 
@@ -293,6 +293,135 @@
     return split
 
 
+def ffn_fits(grid, ffn):
+    return ffn // grid.total % 128 == 0
+
+
+def ffn_layer(grid, positions, part_a, part_b, second, cotangent, gain, bias):
+    tokens, width = second.shape
+    blocks = grid.blocks()
+    count = len(blocks)
+    nx, ny, nz = (grid.size[name] for name in "xyz")
+    arrays = [a for part in part_a + part_b for a in part]
+    rows = arrays[0].shape[2]
+    ffn = arrays[0].shape[3] // 2
+    each = ffn // count
+    many = each // rows
+    group = max(1, 512 // each)
+    chunk = group * each
+    piece = 64
+
+    def kernel(where, second_ref, cot_ref, gain_ref, bias_ref, *refs):
+        sources = refs[: len(arrays)]
+        out_ref, low_ref, second_grad, act_t, pre_grad, g_gain, g_bias = refs[len(arrays) : len(arrays) + 7]
+        up, down, slope, total, pre, act, low, sems = refs[len(arrays) + 7 :]
+
+        def source(n):
+            z, x, y, c = blocks[n]
+            if z < nz // 2:
+                return sources[c * ny + y].at[x, z]
+            return sources[2 * ny + c * nx + x].at[y, z - nz // 2]
+
+        up_copies, down_copies = [], []
+        for n in range(count):
+            at = pl.multiple_of(where[n] * rows, rows)
+            up_copies.append(
+                pltpu.make_async_copy(
+                    source(n).at[:, pl.ds(0, ffn)], up.at[pl.ds(at, rows), :], sems.at[n]
+                )
+            )
+        for n in range(count):
+            for m in range(many):
+                down_copies.append(
+                    pltpu.make_async_copy(
+                        source(n).at[:, pl.ds(ffn + m * width, width)],
+                        down.at[pl.ds(n * each + m * rows, rows), :],
+                        sems.at[count + n * many + m],
+                    )
+                )
+        for copy in up_copies + down_copies:
+            copy.start()
+        low[...] = second_ref[...].astype(BF)
+        for copy in up_copies:
+            copy.wait()
+
+        def units(n):
+            return pl.ds(pl.multiple_of(where[n] * each, each), each)
+
+        for g in range(count // group):
+            mine = slice(g * chunk, (g + 1) * chunk)
+            slot = g % 2
+            here = [up[:, units(g * group + n)] for n in range(group)]
+            pre[slot] = matmul(low[...], jnp.concatenate(here, axis=1))
+            for start in range(0, tokens, piece):
+                some = slice(start, start + piece)
+                x = pre[slot, some, :]
+                erf = 1.0 + lax.erf(x * (0.5**0.5))
+                act[slot, some, :] = (0.5 * x * erf).astype(BF)
+                slope[some, mine] = (
+                    0.5 * erf + x * jnp.exp(-0.5 * x * x) * 0.3989422804014327
+                ).astype(BF)
+            act_t[mine, :] = act[slot].T
+            for copy in down_copies[g * group * many : (g + 1) * group * many]:
+                copy.wait()
+            value = matmul(act[slot], down[mine, :])
+            if g == 0:
+                total[...] = value
+            else:
+                total[...] += value
+
+        gains, biases = 0.0, 0.0
+        for start in range(0, tokens, piece):
+            some = slice(start, start + piece)
+            value, normal, scale = norm_forward(
+                ALPHA_RES * second_ref[some, :] + total[some, :], gain_ref[...], bias_ref[...]
+            )
+            out_ref[some, :] = value.astype(BF)
+            grad, one, two = norm_backward(cot_ref[some, :].astype(F32), normal, scale, gain_ref[...])
+            gains, biases = gains + one.reshape(1, -1), biases + two.reshape(1, -1)
+            total[some, :] = grad
+            low_ref[some, :] = grad.astype(BF)
+        g_gain[...] = gains
+        g_bias[...] = biases
+
+        for g in range(count // group):
+            mine = slice(g * chunk, (g + 1) * chunk)
+            value = (across(low_ref[...], down[mine, :]) * slope[:, mine].astype(F32)).astype(BF)
+            for n in range(group):
+                pre_grad[:, units(g * group + n)] = value[:, n * each : (n + 1) * each]
+        for start in range(0, width, 256):
+            some = slice(start, start + 256)
+            second_grad[:, some] = ALPHA_RES * total[:, some] + across(pre_grad[...], up[some, :])
+
+    vmem = pl.BlockSpec(memory_space=pltpu.VMEM)
+    shapes = [
+        ((tokens, width), BF),
+        ((tokens, width), BF),
+        ((tokens, width), F32),
+        ((ffn, tokens), BF),
+        ((tokens, ffn), BF),
+        ((1, width), F32),
+        ((1, width), F32),
+    ]
+    return call(
+        kernel,
+        out_shape=[jax.ShapeDtypeStruct(shape, dtype) for shape, dtype in shapes],
+        in_specs=[SCALARS] + [vmem] * 4 + [ANYWHERE] * len(arrays),
+        out_specs=[vmem] * len(shapes),
+        scratch_shapes=[
+            pltpu.VMEM((width, ffn), BF),
+            pltpu.VMEM((ffn, width), BF),
+            pltpu.VMEM((tokens, ffn), BF),
+            pltpu.VMEM((tokens, width), F32),
+            pltpu.VMEM((2, tokens, chunk), F32),
+            pltpu.VMEM((2, tokens, chunk), BF),
+            pltpu.VMEM((tokens, width), BF),
+            pltpu.SemaphoreType.DMA((count * (1 + many),)),
+        ],
+        compiler_params=params(60),
+    )(positions, second, cotangent, gain.reshape(1, -1), bias.reshape(1, -1), *arrays)
+
+
 class Reduction:
     def __init__(self, grid, pairs):
         self.grid = grid
@@ -429,6 +558,8 @@
 
 
 TILE = 128
+FORWARD = 40
+BACKWARD = 40
 
 
 def pair_backward(tiles, keys, bias_ref, sums_ref, q, k, v, out, grad, probs_ref, dscores_ref):
@@ -505,7 +636,7 @@
         + [pair_spec(q)] * 3,
         out_specs=[pair_spec(q), sums_spec(length)],
         scratch_shapes=[pltpu.VMEM((length, length), F32)],
-        compiler_params=pltpu.CompilerParams(vmem_limit_bytes=40 * 2**20),
+        compiler_params=params(FORWARD),
     )(pad, column, row, q, k, v)
 
 
@@ -549,7 +680,7 @@
         out_specs=[pair_spec(q)] * 3,
         scratch_shapes=[pltpu.VMEM((length, length), F32)]
         + [pltpu.VMEM((length, 2 * length), BF)] * 2,
-        compiler_params=params(),
+        compiler_params=params(BACKWARD),
     )(pad, column, row, sums, q, k, v, out, grad)
 
 
@@ -615,7 +746,7 @@
         + [pair_spec(q), pair_spec(k), pair_spec(v)],
         out_specs=[pair_spec(q), sums_spec(length)],
         scratch_shapes=[pltpu.VMEM((total, length), F32)],
-        compiler_params=pltpu.CompilerParams(vmem_limit_bytes=40 * 2**20),
+        compiler_params=params(FORWARD),
     )(window, column, *rows, q, k, v)
 
 
@@ -668,7 +799,7 @@
         out_specs=[pair_spec(q), pair_spec(k), pair_spec(v)],
         scratch_shapes=[pltpu.VMEM((total, length), F32)]
         + [pltpu.VMEM((total, 2 * length), BF)] * 2,
-        compiler_params=params(),
+        compiler_params=params(BACKWARD),
     )(window, row, sums, *ids, q, k, v, out, grad)
 
 
@@ -808,15 +939,15 @@
 
     segment = dec_segment.reshape(-1)
     column, row = segment.reshape(-1, 1), segment.reshape(1, -1)
-    window, rows = choose_window(segment, ids_all)
     hidden_t = turn(grid, positions, hidden)
     mem_t = turn(grid, positions, mem_all)
     q = matmul(hidden, w_sq).astype(BF)
     k = matmul(hidden, w_sk).astype(BF)
     v = matmul(hidden, w_sv).astype(BF)
     cross_pair = cross_ag.second(w_sq)
-    self_att, self_sums = self_forward(pad_length, column, row, after(q, *cross_pair, *rows), k, v)
+    self_att, self_sums = self_forward(pad_length, column, row, after(q, *cross_pair), k, v)
     ffn_pair = stacked(ffn_z, self_att)
+    window, rows = choose_window(segment, after(ids_all, *ffn_pair))
     cross_a, cross_b = cross_ag.cores(self_att)
     cross_got = cross_a[0][1:] + cross_b[0][1:]
     ffn_ag.first(hold(ffn_pair, *cross_got))
@@ -849,45 +980,52 @@
     cross_att_t = turn(grid, positions, cross_att)
     turned = (hidden_t, mem_t, second_t, self_att_t, first_t, cross_att_t)
     ffn_a, ffn_b = ffn_ag.cores(*turned)
-    w_up, w_down = assemble(
-        grid,
-        positions,
-        ffn_a,
-        ffn_b,
-        [(0, ffn, 0, 0)] + [(ffn + n * width, width, 1, n * own_rows) for n in range(many)],
-        [(own_rows, ffn), (own_rows * many, width)],
-    )
-    pre = matmul(second_low, w_up)
-    erf = 1.0 + lax.erf(pre * (0.5**0.5))
-    act = (0.5 * pre * erf).astype(BF)
-    slope = 0.5 * erf + pre * jnp.exp(-0.5 * pre * pre) * 0.3989422804014327
-    third, normal3, scale3 = norm_forward(ALPHA_RES * second + matmul(act, w_down), gain3, bias3)
-
-    grad_third, g_gain3, g_bias3 = norm_backward(cotangent.astype(F32), normal3, scale3, gain3)
-    third_low = grad_third.astype(BF)
-    down = Reduction(grid, [(turn(grid, positions, act), third_low)])
+    if ffn_fits(grid, ffn):
+        out, third_low, grad_second, act_t, grad_pre, g_gain3, g_bias3 = ffn_layer(
+            grid, positions, ffn_a, ffn_b, second, cotangent, gain3, bias3
+        )
+        g_gain3, g_bias3 = g_gain3.reshape(-1), g_bias3.reshape(-1)
+    else:
+        w_up, w_down = assemble(
+            grid,
+            positions,
+            ffn_a,
+            ffn_b,
+            [(0, ffn, 0, 0)] + [(ffn + n * width, width, 1, n * own_rows) for n in range(many)],
+            [(own_rows, ffn), (own_rows * many, width)],
+        )
+        pre = matmul(second_low, w_up)
+        erf = 1.0 + lax.erf(pre * (0.5**0.5))
+        act = (0.5 * pre * erf).astype(BF)
+        slope = 0.5 * erf + pre * jnp.exp(-0.5 * pre * pre) * 0.3989422804014327
+        third, normal3, scale3 = norm_forward(
+            ALPHA_RES * second + matmul(act, w_down), gain3, bias3
+        )
+        out = third.astype(BF)
+        grad_third, g_gain3, g_bias3 = norm_backward(
+            cotangent.astype(F32), normal3, scale3, gain3
+        )
+        third_low = grad_third.astype(BF)
+        act_t = turn(grid, positions, act)
+        grad_pre = (slope * outer_right(third_low, w_down)).astype(BF)
+        grad_second = ALPHA_RES * grad_third + outer_right(grad_pre, w_up)
+
+    down = Reduction(grid, [(act_t, third_low)])
     down.start()
     down.cores()
-    grad_pre = (slope * outer_right(after(third_low, down.away), w_down)).astype(BF)
-    down.wait(grad_pre)
-    down_kept = down.keep()
-    down.first()
-    up = Reduction(grid, [(second_t, after(grad_pre, *down_kept))])
+    up = Reduction(grid, [(second_t, after(grad_pre, down.away))])
     up.start()
     up.cores()
-    grad_second = ALPHA_RES * grad_third + outer_right(after(grad_pre, up.away), w_up)
-    up.wait(grad_second)
-    up_kept = up.keep()
     grad_mid, g_gain2, g_bias2 = norm_backward(
-        after(grad_second, *up_kept), normal2, scale2, gain2
+        after(grad_second, up.away), normal2, scale2, gain2
     )
     mid_low = grad_mid.astype(BF)
     grad_catt = outer_right(mid_low, w_co).astype(BF)
     down.wait(grad_catt)
-    down_kept = down.add_first()
-    down.second()
-    up.hold(*down_kept)
-    up.first()
+    down_kept = down.keep()
+    down.first()
+    up.wait(*down_kept)
+    up_kept = up.keep()
     unit = jnp.eye(128, dtype=BF)
 
     def spread(vectors):
@@ -904,33 +1042,30 @@
         mk,
         mv,
         cross_att,
-        after(grad_catt, *down_kept, cross_norms[0]),
+        after(grad_catt, *up_kept, cross_norms[0]),
     )
+    down.wait(grad_cq)
+    down_kept = down.add_first()
+    down.second()
+    up.hold(*down_kept)
+    up.first()
     cross = Reduction(
         grid,
-        [(cross_att_t, mid_low), (first_t, grad_cq), (mem_t, grad_mk), (mem_t, grad_mv), cross_norms],
+        [
+            (cross_att_t, mid_low),
+            (first_t, after(grad_cq, *down_kept)),
+            (mem_t, grad_mk),
+            (mem_t, grad_mv),
+            cross_norms,
+        ],
     )
     cross.start()
-    cross.cores(*down.got_a, *down.got_b, *up.got_a, *up.got_b)
-    down.wait(cross.away)
-    down_kept = down.add_second()
-    down.last()
-    up.wait(*down_kept)
-    up_kept = up.add_first()
-    up.second()
-    grad_first = ALPHA_RES * grad_mid + outer_right(after(grad_cq, cross.away, *up_kept), w_cq)
+    cross.cores(*down.got_a, *down.got_b)
+    grad_first = ALPHA_RES * grad_mid + outer_right(after(grad_cq, cross.away), w_cq)
     grad_res, g_gain1, g_bias1 = norm_backward(grad_first, normal1, scale1, gain1)
     res_low = grad_res.astype(BF)
     grad_satt = outer_right(res_low, w_so).astype(BF)
     own_norms = spread([g_gain1, g_bias1])
-    cross.wait(grad_satt, own_norms[0])
-    cross_kept = cross.keep()
-    up.wait(*cross_kept)
-    up_kept = up.add_second()
-    cross.hold(*up_kept, *down.got_a)
-    cross.first()
-    up.a = [after(a, *down.got_a) for a in up.a]
-    up.last()
     grad_q, grad_k, grad_v = self_backward(
         pad_length,
         column,
@@ -940,24 +1075,45 @@
         k,
         v,
         self_att,
-        after(grad_satt, *cross_kept, *up_kept, *down.got_a),
+        after(grad_satt, own_norms[0]),
     )
+    down.wait(grad_q)
+    down_kept = down.add_second()
+    down.last()
+    up.wait(*down_kept)
+    up_kept = up.add_first()
+    up.second()
+    cross.wait(*up_kept)
+    cross_kept = cross.keep()
+    cross.hold(*up.got_a, *up.got_b)
+    cross.first()
     own = Reduction(
         grid,
-        [(self_att_t, res_low), (hidden_t, grad_q), (hidden_t, grad_k), (hidden_t, grad_v), own_norms],
+        [
+            (self_att_t, res_low),
+            (hidden_t, after(grad_q, *cross_kept)),
+            (hidden_t, grad_k),
+            (hidden_t, grad_v),
+            own_norms,
+        ],
     )
     own.start()
-    own.cores(*cross.got_a, *cross.got_b, *up.got_a)
-    cross.wait(own.away)
+    own.cores(*up.got_a, *up.got_b, *down.got_a)
+    grad_in = ALPHA_RES * grad_res + outer_right(after(grad_q, own.away), w_sq)
+    up.wait(grad_in)
+    up_kept = up.add_second()
+    up.a = [after(a, *down.got_a) for a in up.a]
+    up.last()
+    own.wait(grad_in, *up_kept)
+    own_kept = own.keep()
+    cross.wait(*up_kept, *own_kept)
     cross_kept = cross.add_first()
     cross.second()
-    grad_in = ALPHA_RES * grad_res + outer_right(after(grad_q, own.away, *cross_kept), w_sq)
-    own.wait(grad_in)
-    own_kept = own.keep()
     own.hold(*cross.got_a, *cross.got_b)
     own.first()
     cross.wait(*own_kept)
     cross_kept = cross.add_second()
+    cross.a = [after(a, *up.got_a) for a in cross.a]
     cross.last()
     grad_in = grad_in + outer_right(after(grad_k, *own_kept), w_sk) + outer_right(grad_v, w_sv)
     grad_mem = outer_right(after(grad_mk, *own_kept), w_ck) + outer_right(grad_mv, w_cv)
@@ -984,7 +1140,7 @@
     out_so, out_sq, out_sk, out_sv, last = own.finish([width] * 4 + [128])
     norms = [last[:, 0], last[:, 1]] + [late[:, n] for n in range(4)]
     return (
-        third.astype(BF),
+        out,
         grad_in,
         out_mem,
         out_sq,

time: 548 us -> 515 us (0.940)
  matrix products: 89.8 us -> 34.1 us
  waiting for transfers between devices: 130 us -> 151 us
  local copies, waits for them, and re-layouts: 39.4 us -> 47.2 us
  other arithmetic: 24.1 us -> 17.7 us
    pallas_call x0 -> x1, Pallas kernels: none -> 34.4 us  [ffn_layer(): call(kernel, out_shape=[jax.ShapeDtypeStruct(shape, dtype) for shape, dty...]
    dot_general x10 -> x8, matrix products: 50.1 us -> 17.9 us  [outer_right(): lax.dot_general(left, right, (((1,), (1,)), ((), ())), preferred_element_...]
    dot_general x10 -> x8, matrix products: 39.7 us -> 16.2 us  [matmul(): return jnp.dot(left, right, preferred_element_type=F32)]
    ppermute x71, waiting for transfers between devices: 130 us -> 151 us  [exchange(): return lax.ppermute(array, BOTH, pairs)]
    pallas_call x3 -> x2, Pallas kernels: 29.5 us -> 10.9 us  [assemble(): call(kernel, out_shape=[jax.ShapeDtypeStruct((len(blocks),) + shape, BF)...]
    pallas_call x8, Pallas kernels: 52.4 us -> 39.2 us  [products(): call(kernel, grid=(steps,), out_shape=[jax.ShapeDtypeStruct((size, width)...]
    unnamed x221 -> x264, local copies, waits for them, and re-layouts: 30.2 us -> 37.4 us
  transfers between devices with their start and end apart: 71 -> 71, of which waited for: 27 -> 35; matrix products, arithmetic and copies ran while one was open for 18% -> 12% of each run, Pallas kernels for 26% -> 26%
where the time goes in v4:
time: 515 us; the launch traced here: 506 us
  Pallas kernels  179 us (35%)
  waiting for transfers between devices  151 us (29%)
  starting transfers between devices  68.4 us (13%)
  local copies, waits for them, and re-layouts  47.2 us (9%)
  matrix products  34.1 us (7%)
  other arithmetic  17.7 us (3%)
  between operations  7.77 us (2%)
    ppermute x71, waiting for transfers between devices, exchange(): return lax.ppermute(array, BOTH, pairs)  151 us
    ppermute x71, starting transfers between devices, exchange(): return lax.ppermute(array, BOTH, pairs)  68.4 us
    pallas_call x8, Pallas kernels, products(): call(kernel, grid=(steps,), out_shape=[jax.ShapeDtypeStruct((size, width)...  39.2 us
    unnamed x264, local copies, waits for them, and re-layouts  37.4 us
    pallas_call x1, Pallas kernels, ffn_layer(): call(kernel, out_shape=[jax.ShapeDtypeStruct(shape, dtype) for shape, dty...  34.4 us
    dot_general x8, matrix products, outer_right(): lax.dot_general(left, right, (((1,), (1,)), ((), ())), preferred_element_...  17.9 us
    pallas_call x1, Pallas kernels, cross_backward(): call(kernel, grid=(width // PAIR,), out_shape=[jax.ShapeDtypeStruct(a.sha...  17.5 us
    dot_general x8, matrix products, matmul(): return jnp.dot(left, right, preferred_element_type=F32)  16.2 us
  transfers between devices with their start and end apart: 71, of which 35 were waited for; matrix products, arithmetic and copies ran while one was open for 12% of the time, Pallas kernels for 26%

profile of v4, /device:TPU:8, one launch (start us, length us, event | category | flops | bytes accessed | tf_op | source)
XLA Modules:
  0.0 505.6 jit_solution(13828553882245883137)
XLA Ops:
  15.2 7.6 %collective-permute-done.4.refs_3_ = bf16[32,4096]{1,0:T(8,128)(2,1)S(1)} collective-permute-done((bf16[32,4096]{1,0:T(8,128)(2,1)}, bf16[32,4096]{1,0:T(8,128)(2,1)S(1)}, u32[]{:S(2)}, u32[]{:S(2)}) %collective-permute-start.4) | collective-permute-done | bytes 262176 | tf_op jit(solution)/shard_map/ppermute | solution.py:51
  22.9 3.8 collective-permute-done.3.refs_2_
  28.5 2.0 collective-permute-done.1
  34.9 8.9 %collective-permute-done.8.refs_3_ = bf16[2,32,4096]{2,1,0:T(8,128)(2,1)S(1)} collective-permute-done((bf16[2,32,4096]{2,1,0:T(8,128)(2,1)S(1)}, bf16[2,32,4096]{2,1,0:T(8,128)(2,1)S(1)}, u32[]{:S(2)}, u32[]{:S(2)}) %collective-permute-start.8) | collective-permute-done | bytes 524320 | tf_op jit(solution)/shard_map/ppermute | solution.py:51
  49.6 4.2 collective-permute-start.11
  53.7 15.9 %collective-permute-done.12.refs_3_ = bf16[32,4224]{1,0:T(8,128)(2,1)S(1)} collective-permute-done((bf16[32,4224]{1,0:T(8,128)(2,1)S(1)}, bf16[32,4224]{1,0:T(8,128)(2,1)S(1)}, u32[]{:S(2)}, u32[]{:S(2)}) %collective-permute-start.12) | collective-permute-done | bytes 270368 | tf_op jit(solution)/shard_map/ppermute | solution.py:51
  70.9 5.2 %collective-permute-done.10.refs_1_ = bf16[32,4224]{1,0:T(8,128)(2,1)S(1)} collective-permute-done((bf16[32,4224]{1,0:T(8,128)(2,1)S(1)}, bf16[32,4224]{1,0:T(8,128)(2,1)S(1)}, u32[]{:S(2)}, u32[]{:S(2)}) %collective-permute-start.10) | collective-permute-done | bytes 270368 | tf_op jit(solution)/shard_map/ppermute | solution.py:51
  80.3 2.9 collective-permute-start.27
  84.6 4.7 shard_map.364
  100.5 10.5 %shard_map.366 = (bf16[512,1024]{1,0:T(8,128)(2,1)S(1)}, f32[8,8,512]{2,1,0:T(8,128)S(1)}) custom-call(s32[1]{0:T(128)S(6)} %copy.95.pad_ref, s32[512,1]{1,0:T(8,128)S(1)} %copy.75.column_ref, s32[1,512]{1,0:T(1,128)S(1)} %copy-done.98, bf16[512,1024]{1,0:T(8,128)(2,1)S(1)} %fusion.1.q_ref.refs_0_, bf16[512,1024]{1,0:T(8,128)(2,1)S(1)} %fusion.2.k_ref.refs_1_, ...), custom_call_target="tpu_custom_call" | custom-call | flops 1 | bytes 1 | tf_op jit(solution)/shard_map/pallas_call | solution.py:628
  111.7 6.8 %collective-permute-done.21.refs_5_ = bf16[2,2,32,4224]{3,2,1,0:T(8,128)(2,1)S(1)} collective-permute-done((bf16[2,2,32,4224]{3,2,1,0:T(8,128)(2,1)S(1)}, bf16[2,2,32,4224]{3,2,1,0:T(8,128)(2,1)S(1)}, u32[]{:S(2)}, u32[]{:S(2)}) %collective-permute-start.21) | collective-permute-done | bytes 1081376 | tf_op jit(solution)/shard_map/ppermute | solution.py:51
  120.0 5.1 %collective-permute-done.27.refs_2_ = bf16[32,8192]{1,0:T(8,128)(2,1)} collective-permute-done((bf16[32,8192]{1,0:T(8,128)(2,1)}, bf16[32,8192]{1,0:T(8,128)(2,1)}, u32[]{:S(2)}, u32[]{:S(2)}) %collective-permute-start.27) | collective-permute-done | bytes 524320 | tf_op jit(solution)/shard_map/ppermute | solution.py:51
  126.0 3.3 shard_map.368
  134.2 6.2 %shard_map.367 = (bf16[32,32,1024]{2,1,0:T(8,128)(2,1)S(1)}, bf16[32,32,1024]{2,1,0:T(8,128)(2,1)S(1)}, bf16[32,32,1024]{2,1,0:T(8,128)(2,1)S(1)}, bf16[32,32,10...) custom-call(s32[32]{0:T(128)S(1)} %stack.222.where, bf16[2,2,32,4224]{3,2,1,0:T(8,128)(2,1)S(1)} %get-tuple-element.237.refs_0_, ...), custom_call_target="tpu_custom_call" | custom-call | flops 1 | bytes 1 | tf_op jit(solution)/shard_map/pallas_call | solution.py:164
  146.7 2.0 fusion.left_ref
  148.8 2.2 convolution_convert_fusion.7.refs_3_
  151.0 3.7 convolution_convert_fusion.refs_5_
  154.7 3.7 convolution_convert_fusion.1.refs_4_
  158.5 4.0 shard_map.370
  170.7 1.9 select_reduce_fusion.1
  188.1 13.5 %shard_map.371 = (bf16[512,1024]{1,0:T(8,128)(2,1)S(1)}, f32[8,8,512]{2,1,0:T(8,128)S(1)}) custom-call(s32[4]{0:T(128)S(1)} %pad_add_fusion.1.window_ref, s32[1,512]{1,0:T(1,128)S(1)} %copy-done.98, s32[512,1]{1,0:T(8,128)S(1)} %copy-done.54, s32[640,1]{1,0:T(8,128)S(1)} %reshape.145.refs_1_, s32[1024,1]{1,0:T(8,128)S(1)} %copy-done.26, ...), custom_call_target="tpu_custom_call" | custom-call | flops 1 | bytes 1 | tf_op jit(solution)/shard_map/pallas_call | solution.py:737
  211.2 3.6 collective-permute-done.36.refs_7_
  214.8 3.0 collective-permute-done.33.refs_3_
  217.8 34.4 %shard_map.378 = (bf16[512,1024]{1,0:T(8,128)(2,1)}, bf16[512,1024]{1,0:T(8,128)(2,1)}, f32[512,1024]{1,0:T(8,128)}, bf16[4096,512]{1,0:T(8,128)(2,1)}, bf16[512...) custom-call(s32[32]{0:T(128)} %copy-done.96, f32[512,1024]{1,0:T(8,128)} %get-tuple-element.418.second_ref, ...), custom_call_target="tpu_custom_call" | custom-call | flops 1 | bytes 1 | tf_op jit(solution)/shard_map/pallas_call | solution.py:406
  252.3 2.2 copy-done.1
  255.7 3.3 shard_map.379
  259.2 3.4 shard_map.380
  264.0 2.0 fusion.18
  266.0 2.3 convolution_convert_fusion.6.refs_7_
  268.9 4.1 shard_map.381
  276.3 4.7 shard_map.382
  281.0 17.5 %shard_map.384 = (bf16[512,1024]{1,0:T(8,128)(2,1)S(1)}, bf16[1024,1024]{1,0:T(8,128)(2,1)S(1)}, bf16[1024,1024]{1,0:T(8,128)(2,1)S(1)}) custom-call(s32[4]{0:T(128)S(1)} %pad_add_fusion.1.window_ref, s32[1,512]{1,0:T(1,128)S(1)} %copy-done.98, f32[8,8,512]{2,1,0:T(8,128)S(1)} %get-tuple-element.277.sums_ref, s32[512,1]{1,0:T(8,128)S(1)} %copy-done.55, ...), custom_call_target="tpu_custom_call" | custom-call | flops 1 | bytes 1 | tf_op jit(solution)/shard_map/pallas_call | solution.py:792
  298.8 3.4 shard_map.385
  304.9 5.6 %shard_map.386 = bf16[512,4224]{1,0:T(8,128)(2,1)} custom-call(bf16[1024,512]{1,0:T(8,128)(2,1)S(1)} %copy-done.9, bf16[1024,512]{1,0:T(8,128)(2,1)S(1)} %copy-done.7, bf16[1024,1024]{1,0:T(8,128)(2,1)S(1)} %shard_map.373.refs_2_.refs_3_, bf16[1024,1024]{1,0:T(8,128)(2,1)S(1)} %shard_map.373.refs_2_.refs_3_, bf16[1024,128]{1,0:T(8,128)(2,1)S(1)} %copy-done.51, ...), custom_call_target="tpu_custom_call" | custom-call | flops 1 | bytes 1 | tf_op jit(solution)/shard_map/pallas_call | solution.py:240
  310.5 4.4 collective-permute-done.42.refs_3_
  316.9 2.0 multiply_reduce_fusion
  321.0 2.0 fusion.17
  325.6 13.5 %shard_map.388 = (bf16[512,1024]{1,0:T(8,128)(2,1)S(1)}, bf16[512,1024]{1,0:T(8,128)(2,1)S(1)}, bf16[512,1024]{1,0:T(8,128)(2,1)S(1)}) custom-call(s32[1]{0:T(128)S(6)} %copy.95.pad_ref, s32[512,1]{1,0:T(8,128)S(1)} %copy-done.57, s32[1,512]{1,0:T(1,128)S(1)} %copy-done.98, f32[8,8,512]{2,1,0:T(8,128)S(1)} %copy-done.95, bf16[512,1024]{1,0:T(8,128)(2,1)S(1)} %copy-done.40, ...), custom_call_target="tpu_custom_call" | custom-call | flops 1 | bytes 1 | tf_op jit(solution)/shard_map/pallas_call | solution.py:674
  344.7 1.9 shard_map.390
  349.9 3.7 collective-permute-start.48
  355.1 7.3 %shard_map.391 = (bf16[128,4224]{1,0:T(8,128)(2,1)S(1)}, bf16[128,4224]{1,0:T(8,128)(2,1)}, bf16[128,4224]{1,0:T(8,128)(2,1)S(1)}, bf16[128,4224]{1,0:T(8,128)(2,1)}) custom-call(bf16[1024,512]{1,0:T(8,128)(2,1)S(1)} %copy-done.9, bf16[1024,512]{1,0:T(8,128)(2,1)S(1)} %copy-done.7, bf16[1024,1024]{1,0:T(8,128)(2,1)S(1)} %shard_map.373.refs_2_.refs_3_, ...), custom_call_target="tpu_custom_call" | custom-call | flops 1 | bytes 1 | tf_op jit(solution)/shard_map/pallas_call | solution.py:240
  362.6 4.9 shard_map.392
  368.1 3.5 collective-permute-done.49.refs_2_
  372.4 4.7 collective-permute-done.50.refs_3_
  381.7 3.7 multiply_add_fusion
  387.1 2.4 collective-permute-start.57
  389.6 5.9 %shard_map.394 = (bf16[128,4224]{1,0:T(8,128)(2,1)S(1)}, bf16[128,4224]{1,0:T(8,128)(2,1)S(1)}, bf16[128,4224]{1,0:T(8,128)(2,1)S(1)}, bf16[128,4224]{1,0:T(8,128)(2,1)S(1)}) custom-call(bf16[1024,512]{1,0:T(8,128)(2,1)S(1)} %copy-done.5, bf16[1024,512]{1,0:T(8,128)(2,1)S(1)} %shard_map.372.refs_1_.refs_2_.refs_3_, ...), custom_call_target="tpu_custom_call" | custom-call | flops 1 | bytes 1 | tf_op jit(solution)/shard_map/pallas_call | solution.py:240
  395.5 10.3 %collective-permute-done.53.refs_3_ = bf16[128,4224]{1,0:T(8,128)(2,1)S(1)} collective-permute-done((bf16[128,4224]{1,0:T(8,128)(2,1)}, bf16[128,4224]{1,0:T(8,128)(2,1)S(1)}, u32[]{:S(2)}, u32[]{:S(2)}) %collective-permute-start.53) | collective-permute-done | bytes 1081376 | tf_op jit(solution)/shard_map/ppermute | solution.py:51
  407.0 2.7 shard_map.395
  411.6 2.4 fusion.27
  417.2 6.5 %collective-permute-done.55.refs_3_ = bf16[64,4224]{1,0:T(8,128)(2,1)S(1)} collective-permute-done((bf16[64,4224]{1,0:T(8,128)(2,1)S(1)}, bf16[64,4224]{1,0:T(8,128)(2,1)S(1)}, u32[]{:S(2)}, u32[]{:S(2)}) %collective-permute-start.55) | collective-permute-done | bytes 540704 | tf_op jit(solution)/shard_map/ppermute | solution.py:51
  425.9 2.6 add_add_fusion
  428.6 2.4 convolution_add_fusion
  432.7 2.4 collective-permute-start.60
  436.3 12.3 %collective-permute-done.62.refs_3_ = bf16[32,4224]{1,0:T(8,128)(2,1)S(1)} collective-permute-done((bf16[32,4224]{1,0:T(8,128)(2,1)S(1)}, bf16[32,4224]{1,0:T(8,128)(2,1)S(1)}, u32[]{:S(2)}, u32[]{:S(2)}) %collective-permute-start.62) | collective-permute-done | bytes 270368 | tf_op jit(solution)/shard_map/ppermute | solution.py:51
  448.6 3.8 collective-permute-done.61.refs_2_
  452.5 2.2 shard_map.399
  457.4 2.2 convert_add_fusion
  460.6 8.9 %collective-permute-done.66.refs_3_ = bf16[64,4224]{1,0:T(8,128)(2,1)S(1)} collective-permute-done((bf16[64,4224]{1,0:T(8,128)(2,1)}, bf16[64,4224]{1,0:T(8,128)(2,1)S(1)}, u32[]{:S(2)}, u32[]{:S(2)}) %collective-permute-start.66) | collective-permute-done | bytes 540704 | tf_op jit(solution)/shard_map/ppermute | solution.py:51
  473.4 3.5 collective-permute-start.68
  479.2 7.1 %collective-permute-done.68.refs_1_ = bf16[32,4224]{1,0:T(8,128)(2,1)S(1)} collective-permute-done((bf16[32,4224]{1,0:T(8,128)(2,1)S(1)}, bf16[32,4224]{1,0:T(8,128)(2,1)S(1)}, u32[]{:S(2)}, u32[]{:S(2)}) %collective-permute-start.68) | collective-permute-done | bytes 270368 | tf_op jit(solution)/shard_map/ppermute | solution.py:51
  486.3 9.2 %collective-permute-done.69.refs_2_ = bf16[32,4224]{1,0:T(8,128)(2,1)S(1)} collective-permute-done((bf16[32,4224]{1,0:T(8,128)(2,1)S(1)}, bf16[32,4224]{1,0:T(8,128)(2,1)S(1)}, u32[]{:S(2)}, u32[]{:S(2)}) %collective-permute-start.69) | collective-permute-done | bytes 270368 | tf_op jit(solution)/shard_map/ppermute | solution.py:51
  495.5 5.8 %collective-permute-done.70.refs_3_ = bf16[32,4224]{1,0:T(8,128)(2,1)S(1)} collective-permute-done((bf16[32,4224]{1,0:T(8,128)(2,1)S(1)}, bf16[32,4224]{1,0:T(8,128)(2,1)S(1)}, u32[]{:S(2)}, u32[]{:S(2)}) %collective-permute-start.70) | collective-permute-done | bytes 270368 | tf_op jit(solution)/shard_map/ppermute | solution.py:51
  502.8 2.5 bitcast_add_fusion
  (461 shorter events, 143.0 us)
Async XLA Ops:
  2.4 20.5 %collective-permute-start.4 = (bf16[32,4096]{1,0:T(8,128)(2,1)}, bf16[32,4096]{1,0:T(8,128)(2,1)S(1)}, u32[]{:S(2)}, u32[]{:S(2)}) collective-permute-start(bf16[32,4096]{1,0:T(8,128)(2,1)} %shard_map.357.refs_0_), channel_id=1, source_target_pairs={{0,24},{1,25},{2,26},{3,27},{4,28},{5,29},{6,30},{7,31},{8,16},{9,... | collective-permute-start | bytes 786440 | tf_op jit(solution)/shard_map/ppermute | solution.py:51
  4.0 22.7 %collective-permute-start.3 = (bf16[32,4096]{1,0:T(8,128)(2,1)}, bf16[32,4096]{1,0:T(8,128)(2,1)S(1)}, u32[]{:S(2)}, u32[]{:S(2)}) collective-permute-start(bf16[32,4096]{1,0:T(8,128)(2,1)} %shard_map.357.refs_0_), channel_id=1, source_target_pairs={{0,16},{1,17},{2,18},{3,19},{4,20},{5,21},{6,22},{7,23},{8,24},{9,... | collective-permute-start | bytes 786440 | tf_op jit(solution)/shard_map/ppermute | solution.py:51
  5.1 21.7 %collective-permute-start.2 = (bf16[32,4096]{1,0:T(8,128)(2,1)}, bf16[32,4096]{1,0:T(8,128)(2,1)S(1)}, u32[]{:S(2)}, u32[]{:S(2)}) collective-permute-start(bf16[32,4096]{1,0:T(8,128)(2,1)} %shard_map.357.refs_0_), channel_id=1, source_target_pairs={{0,8},{1,9},{2,10},{3,11},{4,12},{5,13},{6,14},{7,15},{8,0},{9,1},... | collective-permute-start | bytes 786440 | tf_op jit(solution)/shard_map/ppermute | solution.py:51
  6.5 20.3 %collective-permute-start = (bf16[256,1024]{1,0:T(8,128)(2,1)}, bf16[256,1024]{1,0:T(8,128)(2,1)S(1)}, u32[]{:S(2)}, u32[]{:S(2)}) collective-permute-start(bf16[256,1024]{1,0:T(8,128)(2,1)} %refs_0_.6), channel_id=1, source_target_pairs={{0,2},{1,3},{2,0},{3,1},{4,6},{5,7},{6,4},{7,5},{8,10},{9,11},{10,... | collective-permute-start | bytes 1572872 | tf_op jit(solution)/shard_map/ppermute | solution.py:51
  26.9 17.0 %collective-permute-start.6 = (bf16[2,256,1024]{2,1,0:T(8,128)(2,1)S(1)}, bf16[2,256,1024]{2,1,0:T(8,128)(2,1)S(1)}, u32[]{:S(2)}, u32[]{:S(2)}) collective-permute-start(bf16[2,256,1024]{2,1,0:T(8,128)(2,1)S(1)} %shard_map.361.refs_0_), channel_id=1, source_target_pairs={{0,1},{1,0},{2,3},{3,2},{4,5},{5,4},{6,7},{7,6},{8,9},{9,8},{10,11... | collective-permute-start | bytes 3145736 | tf_op jit(solution)/shard_map/ppermute | solution.py:51
  30.7 13.2 %collective-permute-start.8 = (bf16[2,32,4096]{2,1,0:T(8,128)(2,1)S(1)}, bf16[2,32,4096]{2,1,0:T(8,128)(2,1)S(1)}, u32[]{:S(2)}, u32[]{:S(2)}) collective-permute-start(bf16[2,32,4096]{2,1,0:T(8,128)(2,1)S(1)} %get-tuple-element.219.refs_2_), channel_id=1, source_target_pairs={{0,2},{1,3},{2,0},{3,1},{4,6},{5,7},{6,4},{7,5},{8,10},{9,11},{10,... | collective-permute-start | bytes 1572872 | tf_op jit(solution)/shard_map/ppermute | solution.py:51
  32.3 12.8 %collective-permute-start.5 = (bf16[2,32,4096]{2,1,0:T(8,128)(2,1)S(1)}, bf16[2,32,4096]{2,1,0:T(8,128)(2,1)S(1)}, u32[]{:S(2)}, u32[]{:S(2)}) collective-permute-start(bf16[2,32,4096]{2,1,0:T(8,128)(2,1)S(1)} %get-tuple-element.215.refs_0_), channel_id=1, source_target_pairs={{0,4},{1,5},{2,6},{3,7},{4,0},{5,1},{6,2},{7,3},{8,12},{9,13},{10,... | collective-permute-start | bytes 1572872 | tf_op jit(solution)/shard_map/ppermute | solution.py:51
  46.3 30.0 %collective-permute-start.15 = (bf16[2,2,32,4096]{3,2,1,0:T(8,128)(2,1)}, bf16[2,2,32,4096]{3,2,1,0:T(8,128)(2,1)}, u32[]{:S(2)}, u32[]{:S(2)}) collective-permute-start(bf16[2,2,32,4096]{3,2,1,0:T(8,128)(2,1)} %get-tuple-element.223.refs_4_), channel_id=1, source_target_pairs={{0,4},{1,5},{2,6},{3,7},{4,0},{5,1},{6,2},{7,3},{8,12},{9,13},{10,... | collective-permute-start | bytes 3145736 | tf_op jit(solution)/shard_map/ppermute | solution.py:51
  47.8 28.5 %collective-permute-start.9 = (bf16[2,2,32,4096]{3,2,1,0:T(8,128)(2,1)S(1)}, bf16[2,2,32,4096]{3,2,1,0:T(8,128)(2,1)}, u32[]{:S(2)}, u32[]{:S(2)}) collective-permute-start(bf16[2,2,32,4096]{3,2,1,0:T(8,128)(2,1)S(1)} %get-tuple-element.221.refs_0_), channel_id=1, source_target_pairs={{0,2},{1,3},{2,0},{3,1},{4,6},{5,7},{6,4},{7,5},{8,10},{9,11},{10,... | collective-permute-start | bytes 3145736 | tf_op jit(solution)/shard_map/ppermute | solution.py:51
  49.1 20.5 %collective-permute-start.12 = (bf16[32,4224]{1,0:T(8,128)(2,1)S(1)}, bf16[32,4224]{1,0:T(8,128)(2,1)S(1)}, u32[]{:S(2)}, u32[]{:S(2)}) collective-permute-start(bf16[32,4224]{1,0:T(8,128)(2,1)S(1)} %copy-done.60), channel_id=1, source_target_pairs={{0,24},{1,25},{2,26},{3,27},{4,28},{5,29},{6,30},{7,31},{8,16},{9,... | collective-permute-start | bytes 811016 | tf_op jit(solution)/shard_map/ppermute | solution.py:51
  49.6 27.8 %collective-permute-start.13 = (bf16[2,2,32,4096]{3,2,1,0:T(8,128)(2,1)S(1)}, bf16[2,2,32,4096]{3,2,1,0:T(8,128)(2,1)S(1)}, u32[]{:S(2)}, u32[]{:S(2)}) collective-permute-start(bf16[2,2,32,4096]{3,2,1,0:T(8,128)(2,1)S(1)} %get-tuple-element.221.refs_0_), channel_id=1, source_target_pairs={{0,1},{1,0},{2,3},{3,2},{4,5},{5,4},{6,7},{7,6},{8,9},{9,8},{10,11... | collective-permute-start | bytes 3145736 | tf_op jit(solution)/shard_map/ppermute | solution.py:51
  49.6 21.4 %collective-permute-start.11 = (bf16[32,4224]{1,0:T(8,128)(2,1)S(1)}, bf16[32,4224]{1,0:T(8,128)(2,1)S(1)}, u32[]{:S(2)}, u32[]{:S(2)}) collective-permute-start(bf16[32,4224]{1,0:T(8,128)(2,1)S(1)} %copy-done.60), channel_id=1, source_target_pairs={{0,16},{1,17},{2,18},{3,19},{4,20},{5,21},{6,22},{7,23},{8,24},{9,... | collective-permute-start | bytes 811016 | tf_op jit(solution)/shard_map/ppermute | solution.py:51
  70.9 8.9 %collective-permute-start.16 = (bf16[2,2,32,4096]{3,2,1,0:T(8,128)(2,1)}, bf16[2,2,32,4096]{3,2,1,0:T(8,128)(2,1)}, u32[]{:S(2)}, u32[]{:S(2)}) collective-permute-start(bf16[2,2,32,4096]{3,2,1,0:T(8,128)(2,1)} %get-tuple-element.223.refs_4_), channel_id=1, source_target_pairs={{0,1},{1,0},{2,3},{3,2},{4,5},{5,4},{6,7},{7,6},{8,9},{9,8},{10,11... | collective-permute-start | bytes 3145736 | tf_op jit(solution)/shard_map/ppermute | solution.py:51
  76.4 6.8 %collective-permute-start.14 = (bf16[2,2,32,4096]{3,2,1,0:T(8,128)(2,1)}, bf16[2,2,32,4096]{3,2,1,0:T(8,128)(2,1)}, u32[]{:S(2)}, u32[]{:S(2)}) collective-permute-start(bf16[2,2,32,4096]{3,2,1,0:T(8,128)(2,1)} %collective-permute-done.9.refs_1_), channel_id=1, source_target_pairs={{0,1},{1,0},{2,3},{3,2},{4,5},{5,4},{6,7},{7,6},{8,9},{9,8},{10,11... | collective-permute-start | bytes 3145736 | tf_op jit(solution)/shard_map/ppermute | solution.py:51
  76.9 14.4 %collective-permute-start.19 = (bf16[2,32,4224]{2,1,0:T(8,128)(2,1)S(1)}, bf16[2,32,4224]{2,1,0:T(8,128)(2,1)}, u32[]{:S(2)}, u32[]{:S(2)}) collective-permute-start(bf16[2,32,4224]{2,1,0:T(8,128)(2,1)S(1)} %get-tuple-element.235.refs_2_), channel_id=1, source_target_pairs={{0,2},{1,3},{2,0},{3,1},{4,6},{5,7},{6,4},{7,5},{8,10},{9,11},{10,... | collective-permute-start | bytes 1622024 | tf_op jit(solution)/shard_map/ppermute | solution.py:51
  78.4 14.1 %collective-permute-start.18 = (bf16[2,32,4224]{2,1,0:T(8,128)(2,1)S(1)}, bf16[2,32,4224]{2,1,0:T(8,128)(2,1)}, u32[]{:S(2)}, u32[]{:S(2)}) collective-permute-start(bf16[2,32,4224]{2,1,0:T(8,128)(2,1)S(1)} %get-tuple-element.233.refs_0_), channel_id=1, source_target_pairs={{0,4},{1,5},{2,6},{3,7},{4,0},{5,1},{6,2},{7,3},{8,12},{9,13},{10,... | collective-permute-start | bytes 1622024 | tf_op jit(solution)/shard_map/ppermute | solution.py:51
  79.9 39.7 %collective-permute-start.28 = (bf16[32,8192]{1,0:T(8,128)(2,1)}, bf16[32,8192]{1,0:T(8,128)(2,1)}, u32[]{:S(2)}, u32[]{:S(2)}) collective-permute-start(bf16[32,8192]{1,0:T(8,128)(2,1)} %shard_map.359.refs_0_), channel_id=1, source_target_pairs={{0,24},{1,25},{2,26},{3,27},{4,28},{5,29},{6,30},{7,31},{8,16},{9,... | collective-permute-start | bytes 1572872 | tf_op jit(solution)/shard_map/ppermute | solution.py:51
  80.3 44.9 %collective-permute-start.27 = (bf16[32,8192]{1,0:T(8,128)(2,1)}, bf16[32,8192]{1,0:T(8,128)(2,1)}, u32[]{:S(2)}, u32[]{:S(2)}) collective-permute-start(bf16[32,8192]{1,0:T(8,128)(2,1)} %shard_map.359.refs_0_), channel_id=1, source_target_pairs={{0,16},{1,17},{2,18},{3,19},{4,20},{5,21},{6,22},{7,23},{8,24},{9,... | collective-permute-start | bytes 1572872 | tf_op jit(solution)/shard_map/ppermute | solution.py:51
  83.2 42.8 %collective-permute-start.26 = (bf16[32,8192]{1,0:T(8,128)(2,1)}, bf16[32,8192]{1,0:T(8,128)(2,1)}, u32[]{:S(2)}, u32[]{:S(2)}) collective-permute-start(bf16[32,8192]{1,0:T(8,128)(2,1)} %shard_map.359.refs_0_), channel_id=1, source_target_pairs={{0,8},{1,9},{2,10},{3,11},{4,12},{5,13},{6,14},{7,15},{8,0},{9,1},... | collective-permute-start | bytes 1572872 | tf_op jit(solution)/shard_map/ppermute | solution.py:51
  93.8 24.8 %collective-permute-start.21 = (bf16[2,2,32,4224]{3,2,1,0:T(8,128)(2,1)S(1)}, bf16[2,2,32,4224]{3,2,1,0:T(8,128)(2,1)S(1)}, u32[]{:S(2)}, u32[]{:S(2)}) collective-permute-start(bf16[2,2,32,4224]{3,2,1,0:T(8,128)(2,1)S(1)} %get-tuple-element.238.refs_4_), channel_id=1, source_target_pairs={{0,4},{1,5},{2,6},{3,7},{4,0},{5,1},{6,2},{7,3},{8,12},{9,13},{10,... | collective-permute-start | bytes 3244040 | tf_op jit(solution)/shard_map/ppermute | solution.py:51
  95.1 24.4 %collective-permute-start.20 = (bf16[2,2,32,4224]{3,2,1,0:T(8,128)(2,1)S(1)}, bf16[2,2,32,4224]{3,2,1,0:T(8,128)(2,1)S(1)}, u32[]{:S(2)}, u32[]{:S(2)}) collective-permute-start(bf16[2,2,32,4224]{3,2,1,0:T(8,128)(2,1)S(1)} %get-tuple-element.237.refs_0_), channel_id=1, source_target_pairs={{0,2},{1,3},{2,0},{3,1},{4,6},{5,7},{6,4},{7,5},{8,10},{9,11},{10,... | collective-permute-start | bytes 3244040 | tf_op jit(solution)/shard_map/ppermute | solution.py:51
  118.5 14.1 %collective-permute-start.22 = (bf16[2,2,32,4224]{3,2,1,0:T(8,128)(2,1)S(1)}, bf16[2,2,32,4224]{3,2,1,0:T(8,128)(2,1)S(1)}, u32[]{:S(2)}, u32[]{:S(2)}) collective-permute-start(bf16[2,2,32,4224]{3,2,1,0:T(8,128)(2,1)S(1)} %get-tuple-element.237.refs_0_), channel_id=1, source_target_pairs={{0,1},{1,0},{2,3},{3,2},{4,5},{5,4},{6,7},{7,6},{8,9},{9,8},{10,11... | collective-permute-start | bytes 3244040 | tf_op jit(solution)/shard_map/ppermute | solution.py:51
  119.5 14.6 %collective-permute-start.24 = (bf16[2,2,32,4224]{3,2,1,0:T(8,128)(2,1)S(1)}, bf16[2,2,32,4224]{3,2,1,0:T(8,128)(2,1)S(1)}, u32[]{:S(2)}, u32[]{:S(2)}) collective-permute-start(bf16[2,2,32,4224]{3,2,1,0:T(8,128)(2,1)S(1)} %get-tuple-element.238.refs_4_), channel_id=1, source_target_pairs={{0,1},{1,0},{2,3},{3,2},{4,5},{5,4},{6,7},{7,6},{8,9},{9,8},{10,11... | collective-permute-start | bytes 3244040 | tf_op jit(solution)/shard_map/ppermute | solution.py:51
  119.5 14.6 %collective-permute-start.25 = (bf16[2,2,32,4224]{3,2,1,0:T(8,128)(2,1)S(1)}, bf16[2,2,32,4224]{3,2,1,0:T(8,128)(2,1)S(1)}, u32[]{:S(2)}, u32[]{:S(2)}) collective-permute-start(bf16[2,2,32,4224]{3,2,1,0:T(8,128)(2,1)S(1)} %collective-permute-done.21.refs_5_), channel_id=1, source_target_pairs={{0,1},{1,0},{2,3},{3,2},{4,5},{5,4},{6,7},{7,6},{8,9},{9,8},{10,11... | collective-permute-start | bytes 3244040 | tf_op jit(solution)/shard_map/ppermute | solution.py:51
  125.2 9.0 %collective-permute-start.23 = (bf16[2,2,32,4224]{3,2,1,0:T(8,128)(2,1)S(1)}, bf16[2,2,32,4224]{3,2,1,0:T(8,128)(2,1)S(1)}, u32[]{:S(2)}, u32[]{:S(2)}) collective-permute-start(bf16[2,2,32,4224]{3,2,1,0:T(8,128)(2,1)S(1)} %collective-permute-done.20.refs_1_), channel_id=1, source_target_pairs={{0,1},{1,0},{2,3},{3,2},{4,5},{5,4},{6,7},{7,6},{8,9},{9,8},{10,11... | collective-permute-start | bytes 3244040 | tf_op jit(solution)/shard_map/ppermute | solution.py:51
  129.4 29.1 %collective-permute-start.30 = (bf16[2,32,8192]{2,1,0:T(8,128)(2,1)}, bf16[2,32,8192]{2,1,0:T(8,128)(2,1)}, u32[]{:S(2)}, u32[]{:S(2)}) collective-permute-start(bf16[2,32,8192]{2,1,0:T(8,128)(2,1)} %get-tuple-element.261.refs_2_), channel_id=1, source_target_pairs={{0,2},{1,3},{2,0},{3,1},{4,6},{5,7},{6,4},{7,5},{8,10},{9,11},{10,... | collective-permute-start | bytes 3145736 | tf_op jit(solution)/shard_map/ppermute | solution.py:51
  132.6 25.9 %collective-permute-start.29 = (bf16[2,32,8192]{2,1,0:T(8,128)(2,1)S(1)}, bf16[2,32,8192]{2,1,0:T(8,128)(2,1)}, u32[]{:S(2)}, u32[]{:S(2)}) collective-permute-start(bf16[2,32,8192]{2,1,0:T(8,128)(2,1)S(1)} %get-tuple-element.257.refs_0_), channel_id=1, source_target_pairs={{0,4},{1,5},{2,6},{3,7},{4,0},{5,1},{6,2},{7,3},{8,12},{9,13},{10,... | collective-permute-start | bytes 3145736 | tf_op jit(solution)/shard_map/ppermute | solution.py:51
  162.5 47.9 %collective-permute-start.34 = (bf16[2,2,32,8192]{3,2,1,0:T(8,128)(2,1)}, bf16[2,2,32,8192]{3,2,1,0:T(8,128)(2,1)}, u32[]{:S(2)}, u32[]{:S(2)}) collective-permute-start(bf16[2,2,32,8192]{3,2,1,0:T(8,128)(2,1)} %get-tuple-element.264.refs_4_), channel_id=1, source_target_pairs={{0,4},{1,5},{2,6},{3,7},{4,0},{5,1},{6,2},{7,3},{8,12},{9,13},{10,... | collective-permute-start | bytes 6291464 | tf_op jit(solution)/shard_map/ppermute | solution.py:51
  163.6 47.6 %collective-permute-start.31 = (bf16[2,2,32,8192]{3,2,1,0:T(8,128)(2,1)}, bf16[2,2,32,8192]{3,2,1,0:T(8,128)(2,1)}, u32[]{:S(2)}, u32[]{:S(2)}) collective-permute-start(bf16[2,2,32,8192]{3,2,1,0:T(8,128)(2,1)} %get-tuple-element.263.refs_0_), channel_id=1, source_target_pairs={{0,2},{1,3},{2,0},{3,1},{4,6},{5,7},{6,4},{7,5},{8,10},{9,11},{10,... | collective-permute-start | bytes 6291464 | tf_op jit(solution)/shard_map/ppermute | solution.py:51
  182.8 28.4 %collective-permute-start.32 = (bf16[2,2,32,8192]{3,2,1,0:T(8,128)(2,1)}, bf16[2,2,32,8192]{3,2,1,0:T(8,128)(2,1)}, u32[]{:S(2)}, u32[]{:S(2)}) collective-permute-start(bf16[2,2,32,8192]{3,2,1,0:T(8,128)(2,1)} %get-tuple-element.263.refs_0_), channel_id=1, source_target_pairs={{0,1},{1,0},{2,3},{3,2},{4,5},{5,4},{6,7},{7,6},{8,9},{9,8},{10,11... | collective-permute-start | bytes 6291464 | tf_op jit(solution)/shard_map/ppermute | solution.py:51
  182.8 28.4 %collective-permute-start.35 = (bf16[2,2,32,8192]{3,2,1,0:T(8,128)(2,1)}, bf16[2,2,32,8192]{3,2,1,0:T(8,128)(2,1)}, u32[]{:S(2)}, u32[]{:S(2)}) collective-permute-start(bf16[2,2,32,8192]{3,2,1,0:T(8,128)(2,1)} %get-tuple-element.264.refs_4_), channel_id=1, source_target_pairs={{0,1},{1,0},{2,3},{3,2},{4,5},{5,4},{6,7},{7,6},{8,9},{9,8},{10,11... | collective-permute-start | bytes 6291464 | tf_op jit(solution)/shard_map/ppermute | solution.py:51
  259.0 9.3 %collective-permute-start.38 = (bf16[2048,1024]{1,0:T(8,128)(2,1)S(1)}, bf16[2048,1024]{1,0:T(8,128)(2,1)S(1)}, u32[]{:S(2)}, u32[]{:S(2)}) collective-permute-start(bf16[2048,1024]{1,0:T(8,128)(2,1)S(1)} %shard_map.379), channel_id=1, source_target_pairs={{0,1},{1,0},{2,3},{3,2},{4,5},{5,4},{6,7},{7,6},{8,9},{9,8},{10,11... | collective-permute-start | bytes 12582920 | tf_op jit(solution)/shard_map/ppermute | solution.py:51
  262.6 13.6 %collective-permute-start.37 = (bf16[512,4096]{1,0:T(8,128)(2,1)S(1)}, bf16[512,4096]{1,0:T(8,128)(2,1)S(1)}, u32[]{:S(2)}, u32[]{:S(2)}) collective-permute-start(bf16[512,4096]{1,0:T(8,128)(2,1)S(1)} %shard_map.380), channel_id=1, source_target_pairs={{0,1},{1,0},{2,3},{3,2},{4,5},{5,4},{6,7},{7,6},{8,9},{9,8},{10,11... | collective-permute-start | bytes 12582920 | tf_op jit(solution)/shard_map/ppermute | solution.py:51
  273.0 25.5 %collective-permute-start.40 = (bf16[512,1024]{1,0:T(8,128)(2,1)}, bf16[512,1024]{1,0:T(8,128)(2,1)S(1)}, u32[]{:S(2)}, u32[]{:S(2)}) collective-permute-start(bf16[512,1024]{1,0:T(8,128)(2,1)} %get-tuple-element.282), channel_id=1, source_target_pairs={{0,2},{1,3},{2,0},{3,1},{4,6},{5,7},{6,4},{7,5},{8,10},{9,11},{10,... | collective-permute-start | bytes 3145736 | tf_op jit(solution)/shard_map/ppermute | solution.py:51
  273.6 25.2 %collective-permute-start.39 = (bf16[512,1024]{1,0:T(8,128)(2,1)}, bf16[512,1024]{1,0:T(8,128)(2,1)}, u32[]{:S(2)}, u32[]{:S(2)}) collective-permute-start(bf16[512,1024]{1,0:T(8,128)(2,1)} %get-tuple-element.280), channel_id=1, source_target_pairs={{0,4},{1,5},{2,6},{3,7},{4,0},{5,1},{6,2},{7,3},{8,12},{9,13},{10,... | collective-permute-start | bytes 3145736 | tf_op jit(solution)/shard_map/ppermute | solution.py:51
  302.2 12.7 %collective-permute-start.42 = (bf16[256,1024]{1,0:T(8,128)(2,1)S(1)}, bf16[256,1024]{1,0:T(8,128)(2,1)S(1)}, u32[]{:S(2)}, u32[]{:S(2)}) collective-permute-start(bf16[256,1024]{1,0:T(8,128)(2,1)S(1)} %get-tuple-element.297), channel_id=1, source_target_pairs={{0,4},{1,5},{2,6},{3,7},{4,0},{5,1},{6,2},{7,3},{8,12},{9,13},{10,... | collective-permute-start | bytes 1572872 | tf_op jit(solution)/shard_map/ppermute | solution.py:51
  303.3 12.2 %collective-permute-start.41 = (bf16[256,1024]{1,0:T(8,128)(2,1)S(1)}, bf16[256,1024]{1,0:T(8,128)(2,1)S(1)}, u32[]{:S(2)}, u32[]{:S(2)}) collective-permute-start(bf16[256,1024]{1,0:T(8,128)(2,1)S(1)} %get-tuple-element.295), channel_id=1, source_target_pairs={{0,2},{1,3},{2,0},{3,1},{4,6},{5,7},{6,4},{7,5},{8,10},{9,11},{10,... | collective-permute-start | bytes 1572872 | tf_op jit(solution)/shard_map/ppermute | solution.py:51
  315.5 38.2 %collective-permute-start.43 = (bf16[512,4224]{1,0:T(8,128)(2,1)}, bf16[512,4224]{1,0:T(8,128)(2,1)}, u32[]{:S(2)}, u32[]{:S(2)}) collective-permute-start(bf16[512,4224]{1,0:T(8,128)(2,1)} %shard_map.386), channel_id=1, source_target_pairs={{0,1},{1,0},{2,3},{3,2},{4,5},{5,4},{6,7},{7,6},{8,9},{9,8},{10,11... | collective-permute-start | bytes 12976136 | tf_op jit(solution)/shard_map/ppermute | solution.py:51
  315.5 28.6 %collective-permute-start.45 = (bf16[128,4096]{1,0:T(8,128)(2,1)}, bf16[128,4096]{1,0:T(8,128)(2,1)}, u32[]{:S(2)}, u32[]{:S(2)}) collective-permute-start(bf16[128,4096]{1,0:T(8,128)(2,1)} %get-tuple-element.316), channel_id=1, source_target_pairs={{0,2},{1,3},{2,0},{3,1},{4,6},{5,7},{6,4},{7,5},{8,10},{9,11},{10,... | collective-permute-start | bytes 3145736 | tf_op jit(solution)/shard_map/ppermute | solution.py:51
  319.0 25.7 %collective-permute-start.44 = (bf16[128,4096]{1,0:T(8,128)(2,1)}, bf16[128,4096]{1,0:T(8,128)(2,1)}, u32[]{:S(2)}, u32[]{:S(2)}) collective-permute-start(bf16[128,4096]{1,0:T(8,128)(2,1)} %get-tuple-element.307), channel_id=1, source_target_pairs={{0,4},{1,5},{2,6},{3,7},{4,0},{5,1},{6,2},{7,3},{8,12},{9,13},{10,... | collective-permute-start | bytes 3145736 | tf_op jit(solution)/shard_map/ppermute | solution.py:51
  348.2 29.6 %collective-permute-start.46 = (bf16[64,4096]{1,0:T(8,128)(2,1)S(1)}, bf16[64,4096]{1,0:T(8,128)(2,1)S(1)}, u32[]{:S(2)}, u32[]{:S(2)}) collective-permute-start(bf16[64,4096]{1,0:T(8,128)(2,1)S(1)} %get-tuple-element.319), channel_id=1, source_target_pairs={{0,2},{1,3},{2,0},{3,1},{4,6},{5,7},{6,4},{7,5},{8,10},{9,11},{10,... | collective-permute-start | bytes 1572872 | tf_op jit(solution)/shard_map/ppermute | solution.py:51
  348.8 29.8 %collective-permute-start.47 = (bf16[64,4096]{1,0:T(8,128)(2,1)S(1)}, bf16[64,4096]{1,0:T(8,128)(2,1)S(1)}, u32[]{:S(2)}, u32[]{:S(2)}) collective-permute-start(bf16[64,4096]{1,0:T(8,128)(2,1)S(1)} %get-tuple-element.321), channel_id=1, source_target_pairs={{0,4},{1,5},{2,6},{3,7},{4,0},{5,1},{6,2},{7,3},{8,12},{9,13},{10,... | collective-permute-start | bytes 1572872 | tf_op jit(solution)/shard_map/ppermute | solution.py:51
  349.9 17.5 %collective-permute-start.48 = (bf16[128,1024]{1,0:T(8,128)(2,1)S(1)}, bf16[128,1024]{1,0:T(8,128)(2,1)S(1)}, u32[]{:S(2)}, u32[]{:S(2)}) collective-permute-start(bf16[128,1024]{1,0:T(8,128)(2,1)S(1)} %get-tuple-element.311), channel_id=1, source_target_pairs={{0,8},{1,9},{2,10},{3,11},{4,12},{5,13},{6,14},{7,15},{8,0},{9,1},... | collective-permute-start | bytes 786440 | tf_op jit(solution)/shard_map/ppermute | solution.py:51
  353.7 18.0 %collective-permute-start.49 = (bf16[128,1024]{1,0:T(8,128)(2,1)S(1)}, bf16[128,1024]{1,0:T(8,128)(2,1)S(1)}, u32[]{:S(2)}, u32[]{:S(2)}) collective-permute-start(bf16[128,1024]{1,0:T(8,128)(2,1)S(1)} %get-tuple-element.312), channel_id=1, source_target_pairs={{0,16},{1,17},{2,18},{3,19},{4,20},{5,21},{6,22},{7,23},{8,24},{9,... | collective-permute-start | bytes 786440 | tf_op jit(solution)/shard_map/ppermute | solution.py:51
  353.7 23.4 %collective-permute-start.50 = (bf16[128,1024]{1,0:T(8,128)(2,1)S(1)}, bf16[128,1024]{1,0:T(8,128)(2,1)S(1)}, u32[]{:S(2)}, u32[]{:S(2)}) collective-permute-start(bf16[128,1024]{1,0:T(8,128)(2,1)S(1)} %get-tuple-element.313), channel_id=1, source_target_pairs={{0,24},{1,25},{2,26},{3,27},{4,28},{5,29},{6,30},{7,31},{8,16},{9,... | collective-permute-start | bytes 786440 | tf_op jit(solution)/shard_map/ppermute | solution.py:51
  379.4 7.8 %collective-permute-start.51 = (bf16[512,4224]{1,0:T(8,128)(2,1)}, bf16[512,4224]{1,0:T(8,128)(2,1)}, u32[]{:S(2)}, u32[]{:S(2)}) collective-permute-start(bf16[512,4224]{1,0:T(8,128)(2,1)} %shard_map.392), channel_id=1, source_target_pairs={{0,1},{1,0},{2,3},{3,2},{4,5},{5,4},{6,7},{7,6},{8,9},{9,8},{10,11... | collective-permute-start | bytes 12976136 | tf_op jit(solution)/shard_map/ppermute | solution.py:51
  379.4 26.5 %collective-permute-start.53 = (bf16[128,4224]{1,0:T(8,128)(2,1)}, bf16[128,4224]{1,0:T(8,128)(2,1)S(1)}, u32[]{:S(2)}, u32[]{:S(2)}) collective-permute-start(bf16[128,4224]{1,0:T(8,128)(2,1)} %get-tuple-element.349), channel_id=1, source_target_pairs={{0,2},{1,3},{2,0},{3,1},{4,6},{5,7},{6,4},{7,5},{8,10},{9,11},{10,... | collective-permute-start | bytes 3244040 | tf_op jit(solution)/shard_map/ppermute | solution.py:51
  380.7 26.3 %collective-permute-start.52 = (bf16[128,4224]{1,0:T(8,128)(2,1)}, bf16[128,4224]{1,0:T(8,128)(2,1)}, u32[]{:S(2)}, u32[]{:S(2)}) collective-permute-start(bf16[128,4224]{1,0:T(8,128)(2,1)} %get-tuple-element.346), channel_id=1, source_target_pairs={{0,4},{1,5},{2,6},{3,7},{4,0},{5,1},{6,2},{7,3},{8,12},{9,13},{10,... | collective-permute-start | bytes 3244040 | tf_op jit(solution)/shard_map/ppermute | solution.py:51
  386.0 29.0 %collective-permute-start.59 = (bf16[32,4096]{1,0:T(8,128)(2,1)S(1)}, bf16[32,4096]{1,0:T(8,128)(2,1)S(1)}, u32[]{:S(2)}, u32[]{:S(2)}) collective-permute-start(bf16[32,4096]{1,0:T(8,128)(2,1)S(1)} %get-tuple-element.357), channel_id=1, source_target_pairs={{0,24},{1,25},{2,26},{3,27},{4,28},{5,29},{6,30},{7,31},{8,16},{9,... | collective-permute-start | bytes 786440 | tf_op jit(solution)/shard_map/ppermute | solution.py:51
  386.6 28.4 %collective-permute-start.58 = (bf16[32,4096]{1,0:T(8,128)(2,1)S(1)}, bf16[32,4096]{1,0:T(8,128)(2,1)S(1)}, u32[]{:S(2)}, u32[]{:S(2)}) collective-permute-start(bf16[32,4096]{1,0:T(8,128)(2,1)S(1)} %get-tuple-element.356), channel_id=1, source_target_pairs={{0,16},{1,17},{2,18},{3,19},{4,20},{5,21},{6,22},{7,23},{8,24},{9,... | collective-permute-start | bytes 786440 | tf_op jit(solution)/shard_map/ppermute | solution.py:51
  387.1 27.9 %collective-permute-start.57 = (bf16[32,4096]{1,0:T(8,128)(2,1)S(1)}, bf16[32,4096]{1,0:T(8,128)(2,1)S(1)}, u32[]{:S(2)}, u32[]{:S(2)}) collective-permute-start(bf16[32,4096]{1,0:T(8,128)(2,1)S(1)} %get-tuple-element.355), channel_id=1, source_target_pairs={{0,8},{1,9},{2,10},{3,11},{4,12},{5,13},{6,14},{7,15},{8,0},{9,1},... | collective-permute-start | bytes 786440 | tf_op jit(solution)/shard_map/ppermute | solution.py:51
  409.7 14.0 %collective-permute-start.55 = (bf16[64,4224]{1,0:T(8,128)(2,1)S(1)}, bf16[64,4224]{1,0:T(8,128)(2,1)S(1)}, u32[]{:S(2)}, u32[]{:S(2)}) collective-permute-start(bf16[64,4224]{1,0:T(8,128)(2,1)S(1)} %get-tuple-element.352), channel_id=1, source_target_pairs={{0,4},{1,5},{2,6},{3,7},{4,0},{5,1},{6,2},{7,3},{8,12},{9,13},{10,... | collective-permute-start | bytes 1622024 | tf_op jit(solution)/shard_map/ppermute | solution.py:51
  410.8 13.7 %collective-permute-start.54 = (bf16[64,4224]{1,0:T(8,128)(2,1)S(1)}, bf16[64,4224]{1,0:T(8,128)(2,1)S(1)}, u32[]{:S(2)}, u32[]{:S(2)}) collective-permute-start(bf16[64,4224]{1,0:T(8,128)(2,1)S(1)} %get-tuple-element.351), channel_id=1, source_target_pairs={{0,2},{1,3},{2,0},{3,1},{4,6},{5,7},{6,4},{7,5},{8,10},{9,11},{10,... | collective-permute-start | bytes 1622024 | tf_op jit(solution)/shard_map/ppermute | solution.py:51
  424.4 28.0 %collective-permute-start.63 = (bf16[128,4224]{1,0:T(8,128)(2,1)S(1)}, bf16[128,4224]{1,0:T(8,128)(2,1)S(1)}, u32[]{:S(2)}, u32[]{:S(2)}) collective-permute-start(bf16[128,4224]{1,0:T(8,128)(2,1)S(1)} %get-tuple-element.369), channel_id=1, source_target_pairs={{0,2},{1,3},{2,0},{3,1},{4,6},{5,7},{6,4},{7,5},{8,10},{9,11},{10,... | collective-permute-start | bytes 3244040 | tf_op jit(solution)/shard_map/ppermute | solution.py:51
  424.8 27.6 %collective-permute-start.56 = (bf16[128,4224]{1,0:T(8,128)(2,1)S(1)}, bf16[128,4224]{1,0:T(8,128)(2,1)S(1)}, u32[]{:S(2)}, u32[]{:S(2)}) collective-permute-start(bf16[128,4224]{1,0:T(8,128)(2,1)S(1)} %get-tuple-element.353), channel_id=1, source_target_pairs={{0,4},{1,5},{2,6},{3,7},{4,0},{5,1},{6,2},{7,3},{8,12},{9,13},{10,... | collective-permute-start | bytes 3244040 | tf_op jit(solution)/shard_map/ppermute | solution.py:51
  431.6 17.0 %collective-permute-start.62 = (bf16[32,4224]{1,0:T(8,128)(2,1)S(1)}, bf16[32,4224]{1,0:T(8,128)(2,1)S(1)}, u32[]{:S(2)}, u32[]{:S(2)}) collective-permute-start(bf16[32,4224]{1,0:T(8,128)(2,1)S(1)} %get-tuple-element.367), channel_id=1, source_target_pairs={{0,24},{1,25},{2,26},{3,27},{4,28},{5,29},{6,30},{7,31},{8,16},{9,... | collective-permute-start | bytes 811016 | tf_op jit(solution)/shard_map/ppermute | solution.py:51
  432.2 20.2 %collective-permute-start.61 = (bf16[32,4224]{1,0:T(8,128)(2,1)S(1)}, bf16[32,4224]{1,0:T(8,128)(2,1)S(1)}, u32[]{:S(2)}, u32[]{:S(2)}) collective-permute-start(bf16[32,4224]{1,0:T(8,128)(2,1)S(1)} %get-tuple-element.365), channel_id=1, source_target_pairs={{0,16},{1,17},{2,18},{3,19},{4,20},{5,21},{6,22},{7,23},{8,24},{9,... | collective-permute-start | bytes 811016 | tf_op jit(solution)/shard_map/ppermute | solution.py:51
  432.7 19.7 %collective-permute-start.60 = (bf16[32,4224]{1,0:T(8,128)(2,1)S(1)}, bf16[32,4224]{1,0:T(8,128)(2,1)S(1)}, u32[]{:S(2)}, u32[]{:S(2)}) collective-permute-start(bf16[32,4224]{1,0:T(8,128)(2,1)S(1)} %get-tuple-element.363), channel_id=1, source_target_pairs={{0,8},{1,9},{2,10},{3,11},{4,12},{5,13},{6,14},{7,15},{8,0},{9,1},... | collective-permute-start | bytes 811016 | tf_op jit(solution)/shard_map/ppermute | solution.py:51
  454.7 14.9 %collective-permute-start.66 = (bf16[64,4224]{1,0:T(8,128)(2,1)}, bf16[64,4224]{1,0:T(8,128)(2,1)S(1)}, u32[]{:S(2)}, u32[]{:S(2)}) collective-permute-start(bf16[64,4224]{1,0:T(8,128)(2,1)} %get-tuple-element.375), channel_id=1, source_target_pairs={{0,4},{1,5},{2,6},{3,7},{4,0},{5,1},{6,2},{7,3},{8,12},{9,13},{10,... | collective-permute-start | bytes 1622024 | tf_op jit(solution)/shard_map/ppermute | solution.py:51
  455.6 14.6 %collective-permute-start.65 = (bf16[64,4224]{1,0:T(8,128)(2,1)}, bf16[64,4224]{1,0:T(8,128)(2,1)S(1)}, u32[]{:S(2)}, u32[]{:S(2)}) collective-permute-start(bf16[64,4224]{1,0:T(8,128)(2,1)} %get-tuple-element.374), channel_id=1, source_target_pairs={{0,2},{1,3},{2,0},{3,1},{4,6},{5,7},{6,4},{7,5},{8,10},{9,11},{10,... | collective-permute-start | bytes 1622024 | tf_op jit(solution)/shard_map/ppermute | solution.py:51
  470.2 32.6 %collective-permute-start.67 = (bf16[256,1024]{1,0:T(8,128)(2,1)}, bf16[256,1024]{1,0:T(8,128)(2,1)}, u32[]{:S(2)}, u32[]{:S(2)}) collective-permute-start(bf16[256,1024]{1,0:T(8,128)(2,1)} %fusion.5), channel_id=1, source_target_pairs={{0,2},{1,3},{2,0},{3,1},{4,6},{5,7},{6,4},{7,5},{8,10},{9,11},{10,... | collective-permute-start | bytes 1572872 | tf_op jit(solution)/shard_map/ppermute | solution.py:51
  473.4 12.8 %collective-permute-start.68 = (bf16[32,4224]{1,0:T(8,128)(2,1)S(1)}, bf16[32,4224]{1,0:T(8,128)(2,1)S(1)}, u32[]{:S(2)}, u32[]{:S(2)}) collective-permute-start(bf16[32,4224]{1,0:T(8,128)(2,1)S(1)} %get-tuple-element.385), channel_id=1, source_target_pairs={{0,8},{1,9},{2,10},{3,11},{4,12},{5,13},{6,14},{7,15},{8,0},{9,1},... | collective-permute-start | bytes 811016 | tf_op jit(solution)/shard_map/ppermute | solution.py:51
  476.9 18.6 %collective-permute-start.69 = (bf16[32,4224]{1,0:T(8,128)(2,1)S(1)}, bf16[32,4224]{1,0:T(8,128)(2,1)S(1)}, u32[]{:S(2)}, u32[]{:S(2)}) collective-permute-start(bf16[32,4224]{1,0:T(8,128)(2,1)S(1)} %get-tuple-element.386), channel_id=1, source_target_pairs={{0,16},{1,17},{2,18},{3,19},{4,20},{5,21},{6,22},{7,23},{8,24},{9,... | collective-permute-start | bytes 811016 | tf_op jit(solution)/shard_map/ppermute | solution.py:51
  476.9 24.4 %collective-permute-start.70 = (bf16[32,4224]{1,0:T(8,128)(2,1)S(1)}, bf16[32,4224]{1,0:T(8,128)(2,1)S(1)}, u32[]{:S(2)}, u32[]{:S(2)}) collective-permute-start(bf16[32,4224]{1,0:T(8,128)(2,1)S(1)} %get-tuple-element.387), channel_id=1, source_target_pairs={{0,24},{1,25},{2,26},{3,27},{4,28},{5,29},{6,30},{7,31},{8,16},{9,... | collective-permute-start | bytes 811016 | tf_op jit(solution)/shard_map/ppermute | solution.py:51
  (138 other events, 1189.8 us)

commit v5 on v4

--- a/solution.py
+++ b/solution.py
@@ -309,7 +309,7 @@
     many = each // rows
     group = max(1, 512 // each)
     chunk = group * each
-    piece = 64
+    piece = 256
 
     def kernel(where, second_ref, cot_ref, gain_ref, bias_ref, *refs):
         sources = refs[: len(arrays)]
@@ -339,11 +339,13 @@
                         sems.at[count + n * many + m],
                     )
                 )
-        for copy in up_copies + down_copies:
+        for copy in up_copies:
             copy.start()
         low[...] = second_ref[...].astype(BF)
         for copy in up_copies:
             copy.wait()
+        for copy in down_copies:
+            copy.start()
 
         def units(n):
             return pl.ds(pl.multiple_of(where[n] * each, each), each)

time: 515 us -> 515 us (level)
  no operation moved by 1% of the time
where the time goes in v5:
time: 515 us; the launch traced here: 506 us
  Pallas kernels  179 us (35%)
  waiting for transfers between devices  152 us (30%)
  starting transfers between devices  68 us (13%)
  local copies, waits for them, and re-layouts  47.2 us (9%)
  matrix products  34.1 us (7%)
  other arithmetic  17.7 us (3%)
  between operations  7.77 us (2%)
    ppermute x71, waiting for transfers between devices, exchange(): return lax.ppermute(array, BOTH, pairs)  152 us
    ppermute x71, starting transfers between devices, exchange(): return lax.ppermute(array, BOTH, pairs)  68 us
    pallas_call x8, Pallas kernels, products(): call(kernel, grid=(steps,), out_shape=[jax.ShapeDtypeStruct((size, width)...  39.3 us
    unnamed x264, local copies, waits for them, and re-layouts  37.4 us
    pallas_call x1, Pallas kernels, ffn_layer(): call(kernel, out_shape=[jax.ShapeDtypeStruct(shape, dtype) for shape, dty...  34.9 us
    dot_general x8, matrix products, outer_right(): lax.dot_general(left, right, (((1,), (1,)), ((), ())), preferred_element_...  17.9 us
    pallas_call x1, Pallas kernels, cross_backward(): call(kernel, grid=(width // PAIR,), out_shape=[jax.ShapeDtypeStruct(a.sha...  17.5 us
    dot_general x8, matrix products, matmul(): return jnp.dot(left, right, preferred_element_type=F32)  16.2 us
  transfers between devices with their start and end apart: 71, of which 35 were waited for; matrix products, arithmetic and copies ran while one was open for 12% of the time, Pallas kernels for 26%

profile of v5, /device:TPU:8, one launch (start us, length us, event | category | flops | bytes accessed | tf_op | source)
XLA Modules:
  0.0 505.9 jit_solution(13076741828450745166)
XLA Ops:
  15.2 7.6 %collective-permute-done.4.refs_3_ = bf16[32,4096]{1,0:T(8,128)(2,1)S(1)} collective-permute-done((bf16[32,4096]{1,0:T(8,128)(2,1)}, bf16[32,4096]{1,0:T(8,128)(2,1)S(1)}, u32[]{:S(2)}, u32[]{:S(2)}) %collective-permute-start.4) | collective-permute-done | bytes 262176 | tf_op jit(solution)/shard_map/ppermute | solution.py:51
  22.9 3.8 collective-permute-done.3.refs_2_
  28.5 2.0 collective-permute-done.1
  34.9 8.9 %collective-permute-done.8.refs_3_ = bf16[2,32,4096]{2,1,0:T(8,128)(2,1)S(1)} collective-permute-done((bf16[2,32,4096]{2,1,0:T(8,128)(2,1)S(1)}, bf16[2,32,4096]{2,1,0:T(8,128)(2,1)S(1)}, u32[]{:S(2)}, u32[]{:S(2)}) %collective-permute-start.8) | collective-permute-done | bytes 524320 | tf_op jit(solution)/shard_map/ppermute | solution.py:51
  49.6 4.2 collective-permute-start.11
  53.7 15.9 %collective-permute-done.12.refs_3_ = bf16[32,4224]{1,0:T(8,128)(2,1)S(1)} collective-permute-done((bf16[32,4224]{1,0:T(8,128)(2,1)S(1)}, bf16[32,4224]{1,0:T(8,128)(2,1)S(1)}, u32[]{:S(2)}, u32[]{:S(2)}) %collective-permute-start.12) | collective-permute-done | bytes 270368 | tf_op jit(solution)/shard_map/ppermute | solution.py:51
  70.9 5.2 %collective-permute-done.10.refs_1_ = bf16[32,4224]{1,0:T(8,128)(2,1)S(1)} collective-permute-done((bf16[32,4224]{1,0:T(8,128)(2,1)S(1)}, bf16[32,4224]{1,0:T(8,128)(2,1)S(1)}, u32[]{:S(2)}, u32[]{:S(2)}) %collective-permute-start.10) | collective-permute-done | bytes 270368 | tf_op jit(solution)/shard_map/ppermute | solution.py:51
  80.3 2.9 collective-permute-start.27
  84.6 4.7 shard_map.364
  100.5 10.5 %shard_map.366 = (bf16[512,1024]{1,0:T(8,128)(2,1)S(1)}, f32[8,8,512]{2,1,0:T(8,128)S(1)}) custom-call(s32[1]{0:T(128)S(6)} %copy.95.pad_ref, s32[512,1]{1,0:T(8,128)S(1)} %copy.75.column_ref, s32[1,512]{1,0:T(1,128)S(1)} %copy-done.98, bf16[512,1024]{1,0:T(8,128)(2,1)S(1)} %fusion.1.q_ref.refs_0_, bf16[512,1024]{1,0:T(8,128)(2,1)S(1)} %fusion.2.k_ref.refs_1_, ...), custom_call_target="tpu_custom_call" | custom-call | flops 1 | bytes 1 | tf_op jit(solution)/shard_map/pallas_call | solution.py:630
  111.7 6.8 %collective-permute-done.21.refs_5_ = bf16[2,2,32,4224]{3,2,1,0:T(8,128)(2,1)S(1)} collective-permute-done((bf16[2,2,32,4224]{3,2,1,0:T(8,128)(2,1)S(1)}, bf16[2,2,32,4224]{3,2,1,0:T(8,128)(2,1)S(1)}, u32[]{:S(2)}, u32[]{:S(2)}) %collective-permute-start.21) | collective-permute-done | bytes 1081376 | tf_op jit(solution)/shard_map/ppermute | solution.py:51
  120.0 5.1 %collective-permute-done.27.refs_2_ = bf16[32,8192]{1,0:T(8,128)(2,1)} collective-permute-done((bf16[32,8192]{1,0:T(8,128)(2,1)}, bf16[32,8192]{1,0:T(8,128)(2,1)}, u32[]{:S(2)}, u32[]{:S(2)}) %collective-permute-start.27) | collective-permute-done | bytes 524320 | tf_op jit(solution)/shard_map/ppermute | solution.py:51
  126.0 3.3 shard_map.368
  134.2 6.2 %shard_map.367 = (bf16[32,32,1024]{2,1,0:T(8,128)(2,1)S(1)}, bf16[32,32,1024]{2,1,0:T(8,128)(2,1)S(1)}, bf16[32,32,1024]{2,1,0:T(8,128)(2,1)S(1)}, bf16[32,32,10...) custom-call(s32[32]{0:T(128)S(1)} %stack.222.where, bf16[2,2,32,4224]{3,2,1,0:T(8,128)(2,1)S(1)} %get-tuple-element.237.refs_0_, ...), custom_call_target="tpu_custom_call" | custom-call | flops 1 | bytes 1 | tf_op jit(solution)/shard_map/pallas_call | solution.py:164
  146.7 2.0 fusion.left_ref
  148.8 2.2 convolution_convert_fusion.7.refs_3_
  151.0 3.7 convolution_convert_fusion.refs_5_
  154.7 3.7 convolution_convert_fusion.1.refs_4_
  158.5 4.0 shard_map.370
  170.7 1.9 select_reduce_fusion.1
  188.1 13.5 %shard_map.371 = (bf16[512,1024]{1,0:T(8,128)(2,1)S(1)}, f32[8,8,512]{2,1,0:T(8,128)S(1)}) custom-call(s32[4]{0:T(128)S(1)} %pad_add_fusion.1.window_ref, s32[1,512]{1,0:T(1,128)S(1)} %copy-done.98, s32[512,1]{1,0:T(8,128)S(1)} %copy-done.54, s32[640,1]{1,0:T(8,128)S(1)} %reshape.145.refs_1_, s32[1024,1]{1,0:T(8,128)S(1)} %copy-done.26, ...), custom_call_target="tpu_custom_call" | custom-call | flops 1 | bytes 1 | tf_op jit(solution)/shard_map/pallas_call | solution.py:739
  211.2 3.6 collective-permute-done.36.refs_7_
  214.8 3.0 collective-permute-done.33.refs_3_
  217.8 34.9 %shard_map.378 = (bf16[512,1024]{1,0:T(8,128)(2,1)}, bf16[512,1024]{1,0:T(8,128)(2,1)}, f32[512,1024]{1,0:T(8,128)}, bf16[4096,512]{1,0:T(8,128)(2,1)}, bf16[512...) custom-call(s32[32]{0:T(128)} %copy-done.96, f32[512,1024]{1,0:T(8,128)} %get-tuple-element.418.second_ref, ...), custom_call_target="tpu_custom_call" | custom-call | flops 1 | bytes 1 | tf_op jit(solution)/shard_map/pallas_call | solution.py:408
  252.7 2.2 copy-done.1
  256.1 3.3 shard_map.379
  259.7 3.4 shard_map.380
  264.5 2.0 fusion.18
  266.5 2.3 convolution_convert_fusion.6.refs_7_
  269.4 4.1 shard_map.381
  276.7 4.7 shard_map.382
  281.4 17.5 %shard_map.384 = (bf16[512,1024]{1,0:T(8,128)(2,1)S(1)}, bf16[1024,1024]{1,0:T(8,128)(2,1)S(1)}, bf16[1024,1024]{1,0:T(8,128)(2,1)S(1)}) custom-call(s32[4]{0:T(128)S(1)} %pad_add_fusion.1.window_ref, s32[1,512]{1,0:T(1,128)S(1)} %copy-done.98, f32[8,8,512]{2,1,0:T(8,128)S(1)} %get-tuple-element.277.sums_ref, s32[512,1]{1,0:T(8,128)S(1)} %copy-done.55, ...), custom_call_target="tpu_custom_call" | custom-call | flops 1 | bytes 1 | tf_op jit(solution)/shard_map/pallas_call | solution.py:794
  299.3 3.4 shard_map.385
  305.4 5.6 %shard_map.386 = bf16[512,4224]{1,0:T(8,128)(2,1)} custom-call(bf16[1024,512]{1,0:T(8,128)(2,1)S(1)} %copy-done.9, bf16[1024,512]{1,0:T(8,128)(2,1)S(1)} %copy-done.7, bf16[1024,1024]{1,0:T(8,128)(2,1)S(1)} %shard_map.373.refs_2_.refs_3_, bf16[1024,1024]{1,0:T(8,128)(2,1)S(1)} %shard_map.373.refs_2_.refs_3_, bf16[1024,128]{1,0:T(8,128)(2,1)S(1)} %copy-done.51, ...), custom_call_target="tpu_custom_call" | custom-call | flops 1 | bytes 1 | tf_op jit(solution)/shard_map/pallas_call | solution.py:240
  311.0 4.5 collective-permute-done.42.refs_3_
  317.4 2.0 multiply_reduce_fusion
  321.4 2.0 fusion.17
  326.1 13.5 %shard_map.388 = (bf16[512,1024]{1,0:T(8,128)(2,1)S(1)}, bf16[512,1024]{1,0:T(8,128)(2,1)S(1)}, bf16[512,1024]{1,0:T(8,128)(2,1)S(1)}) custom-call(s32[1]{0:T(128)S(6)} %copy.95.pad_ref, s32[512,1]{1,0:T(8,128)S(1)} %copy-done.57, s32[1,512]{1,0:T(1,128)S(1)} %copy-done.98, f32[8,8,512]{2,1,0:T(8,128)S(1)} %copy-done.95, bf16[512,1024]{1,0:T(8,128)(2,1)S(1)} %copy-done.40, ...), custom_call_target="tpu_custom_call" | custom-call | flops 1 | bytes 1 | tf_op jit(solution)/shard_map/pallas_call | solution.py:676
  345.1 1.9 shard_map.390
  350.5 3.4 collective-permute-start.48
  355.4 7.3 %shard_map.391 = (bf16[128,4224]{1,0:T(8,128)(2,1)S(1)}, bf16[128,4224]{1,0:T(8,128)(2,1)}, bf16[128,4224]{1,0:T(8,128)(2,1)S(1)}, bf16[128,4224]{1,0:T(8,128)(2,1)}) custom-call(bf16[1024,512]{1,0:T(8,128)(2,1)S(1)} %copy-done.9, bf16[1024,512]{1,0:T(8,128)(2,1)S(1)} %copy-done.7, bf16[1024,1024]{1,0:T(8,128)(2,1)S(1)} %shard_map.373.refs_2_.refs_3_, ...), custom_call_target="tpu_custom_call" | custom-call | flops 1 | bytes 1 | tf_op jit(solution)/shard_map/pallas_call | solution.py:240
  362.8 4.9 shard_map.392
  368.4 3.5 collective-permute-done.49.refs_2_
  372.7 4.7 collective-permute-done.50.refs_3_
  382.2 3.7 multiply_add_fusion
  387.6 2.4 collective-permute-start.57
  390.0 5.9 %shard_map.394 = (bf16[128,4224]{1,0:T(8,128)(2,1)S(1)}, bf16[128,4224]{1,0:T(8,128)(2,1)S(1)}, bf16[128,4224]{1,0:T(8,128)(2,1)S(1)}, bf16[128,4224]{1,0:T(8,128)(2,1)S(1)}) custom-call(bf16[1024,512]{1,0:T(8,128)(2,1)S(1)} %copy-done.5, bf16[1024,512]{1,0:T(8,128)(2,1)S(1)} %shard_map.372.refs_1_.refs_2_.refs_3_, ...), custom_call_target="tpu_custom_call" | custom-call | flops 1 | bytes 1 | tf_op jit(solution)/shard_map/pallas_call | solution.py:240
  396.0 10.2 %collective-permute-done.53.refs_3_ = bf16[128,4224]{1,0:T(8,128)(2,1)S(1)} collective-permute-done((bf16[128,4224]{1,0:T(8,128)(2,1)}, bf16[128,4224]{1,0:T(8,128)(2,1)S(1)}, u32[]{:S(2)}, u32[]{:S(2)}) %collective-permute-start.53) | collective-permute-done | bytes 1081376 | tf_op jit(solution)/shard_map/ppermute | solution.py:51
  407.5 2.7 shard_map.395
  411.9 2.4 fusion.27
  417.5 6.6 %collective-permute-done.55.refs_3_ = bf16[64,4224]{1,0:T(8,128)(2,1)S(1)} collective-permute-done((bf16[64,4224]{1,0:T(8,128)(2,1)S(1)}, bf16[64,4224]{1,0:T(8,128)(2,1)S(1)}, u32[]{:S(2)}, u32[]{:S(2)}) %collective-permute-start.55) | collective-permute-done | bytes 540704 | tf_op jit(solution)/shard_map/ppermute | solution.py:51
  426.4 2.6 add_add_fusion
  429.0 2.4 convolution_add_fusion
  433.1 2.4 collective-permute-start.60
  436.7 12.3 %collective-permute-done.62.refs_3_ = bf16[32,4224]{1,0:T(8,128)(2,1)S(1)} collective-permute-done((bf16[32,4224]{1,0:T(8,128)(2,1)S(1)}, bf16[32,4224]{1,0:T(8,128)(2,1)S(1)}, u32[]{:S(2)}, u32[]{:S(2)}) %collective-permute-start.62) | collective-permute-done | bytes 270368 | tf_op jit(solution)/shard_map/ppermute | solution.py:51
  449.0 3.8 collective-permute-done.61.refs_2_
  452.8 2.2 shard_map.399
  457.7 2.2 convert_add_fusion
  460.9 9.0 %collective-permute-done.66.refs_3_ = bf16[64,4224]{1,0:T(8,128)(2,1)S(1)} collective-permute-done((bf16[64,4224]{1,0:T(8,128)(2,1)}, bf16[64,4224]{1,0:T(8,128)(2,1)S(1)}, u32[]{:S(2)}, u32[]{:S(2)}) %collective-permute-start.66) | collective-permute-done | bytes 540704 | tf_op jit(solution)/shard_map/ppermute | solution.py:51
  473.7 3.5 collective-permute-start.68
  479.4 7.1 %collective-permute-done.68.refs_1_ = bf16[32,4224]{1,0:T(8,128)(2,1)S(1)} collective-permute-done((bf16[32,4224]{1,0:T(8,128)(2,1)S(1)}, bf16[32,4224]{1,0:T(8,128)(2,1)S(1)}, u32[]{:S(2)}, u32[]{:S(2)}) %collective-permute-start.68) | collective-permute-done | bytes 270368 | tf_op jit(solution)/shard_map/ppermute | solution.py:51
  486.5 9.2 %collective-permute-done.69.refs_2_ = bf16[32,4224]{1,0:T(8,128)(2,1)S(1)} collective-permute-done((bf16[32,4224]{1,0:T(8,128)(2,1)S(1)}, bf16[32,4224]{1,0:T(8,128)(2,1)S(1)}, u32[]{:S(2)}, u32[]{:S(2)}) %collective-permute-start.69) | collective-permute-done | bytes 270368 | tf_op jit(solution)/shard_map/ppermute | solution.py:51
  495.8 5.8 %collective-permute-done.70.refs_3_ = bf16[32,4224]{1,0:T(8,128)(2,1)S(1)} collective-permute-done((bf16[32,4224]{1,0:T(8,128)(2,1)S(1)}, bf16[32,4224]{1,0:T(8,128)(2,1)S(1)}, u32[]{:S(2)}, u32[]{:S(2)}) %collective-permute-start.70) | collective-permute-done | bytes 270368 | tf_op jit(solution)/shard_map/ppermute | solution.py:51
  503.1 2.5 bitcast_add_fusion
  (461 shorter events, 143.1 us)
Async XLA Ops:
  2.4 20.5 %collective-permute-start.4 = (bf16[32,4096]{1,0:T(8,128)(2,1)}, bf16[32,4096]{1,0:T(8,128)(2,1)S(1)}, u32[]{:S(2)}, u32[]{:S(2)}) collective-permute-start(bf16[32,4096]{1,0:T(8,128)(2,1)} %shard_map.357.refs_0_), channel_id=1, source_target_pairs={{0,24},{1,25},{2,26},{3,27},{4,28},{5,29},{6,30},{7,31},{8,16},{9,... | collective-permute-start | bytes 786440 | tf_op jit(solution)/shard_map/ppermute | solution.py:51
  4.0 22.7 %collective-permute-start.3 = (bf16[32,4096]{1,0:T(8,128)(2,1)}, bf16[32,4096]{1,0:T(8,128)(2,1)S(1)}, u32[]{:S(2)}, u32[]{:S(2)}) collective-permute-start(bf16[32,4096]{1,0:T(8,128)(2,1)} %shard_map.357.refs_0_), channel_id=1, source_target_pairs={{0,16},{1,17},{2,18},{3,19},{4,20},{5,21},{6,22},{7,23},{8,24},{9,... | collective-permute-start | bytes 786440 | tf_op jit(solution)/shard_map/ppermute | solution.py:51
  5.1 21.7 %collective-permute-start.2 = (bf16[32,4096]{1,0:T(8,128)(2,1)}, bf16[32,4096]{1,0:T(8,128)(2,1)S(1)}, u32[]{:S(2)}, u32[]{:S(2)}) collective-permute-start(bf16[32,4096]{1,0:T(8,128)(2,1)} %shard_map.357.refs_0_), channel_id=1, source_target_pairs={{0,8},{1,9},{2,10},{3,11},{4,12},{5,13},{6,14},{7,15},{8,0},{9,1},... | collective-permute-start | bytes 786440 | tf_op jit(solution)/shard_map/ppermute | solution.py:51
  6.5 20.3 %collective-permute-start = (bf16[256,1024]{1,0:T(8,128)(2,1)}, bf16[256,1024]{1,0:T(8,128)(2,1)S(1)}, u32[]{:S(2)}, u32[]{:S(2)}) collective-permute-start(bf16[256,1024]{1,0:T(8,128)(2,1)} %refs_0_.6), channel_id=1, source_target_pairs={{0,2},{1,3},{2,0},{3,1},{4,6},{5,7},{6,4},{7,5},{8,10},{9,11},{10,... | collective-permute-start | bytes 1572872 | tf_op jit(solution)/shard_map/ppermute | solution.py:51
  26.9 17.0 %collective-permute-start.6 = (bf16[2,256,1024]{2,1,0:T(8,128)(2,1)S(1)}, bf16[2,256,1024]{2,1,0:T(8,128)(2,1)S(1)}, u32[]{:S(2)}, u32[]{:S(2)}) collective-permute-start(bf16[2,256,1024]{2,1,0:T(8,128)(2,1)S(1)} %shard_map.361.refs_0_), channel_id=1, source_target_pairs={{0,1},{1,0},{2,3},{3,2},{4,5},{5,4},{6,7},{7,6},{8,9},{9,8},{10,11... | collective-permute-start | bytes 3145736 | tf_op jit(solution)/shard_map/ppermute | solution.py:51
  30.7 13.2 %collective-permute-start.8 = (bf16[2,32,4096]{2,1,0:T(8,128)(2,1)S(1)}, bf16[2,32,4096]{2,1,0:T(8,128)(2,1)S(1)}, u32[]{:S(2)}, u32[]{:S(2)}) collective-permute-start(bf16[2,32,4096]{2,1,0:T(8,128)(2,1)S(1)} %get-tuple-element.219.refs_2_), channel_id=1, source_target_pairs={{0,2},{1,3},{2,0},{3,1},{4,6},{5,7},{6,4},{7,5},{8,10},{9,11},{10,... | collective-permute-start | bytes 1572872 | tf_op jit(solution)/shard_map/ppermute | solution.py:51
  32.3 12.8 %collective-permute-start.5 = (bf16[2,32,4096]{2,1,0:T(8,128)(2,1)S(1)}, bf16[2,32,4096]{2,1,0:T(8,128)(2,1)S(1)}, u32[]{:S(2)}, u32[]{:S(2)}) collective-permute-start(bf16[2,32,4096]{2,1,0:T(8,128)(2,1)S(1)} %get-tuple-element.215.refs_0_), channel_id=1, source_target_pairs={{0,4},{1,5},{2,6},{3,7},{4,0},{5,1},{6,2},{7,3},{8,12},{9,13},{10,... | collective-permute-start | bytes 1572872 | tf_op jit(solution)/shard_map/ppermute | solution.py:51
  46.3 30.0 %collective-permute-start.15 = (bf16[2,2,32,4096]{3,2,1,0:T(8,128)(2,1)}, bf16[2,2,32,4096]{3,2,1,0:T(8,128)(2,1)}, u32[]{:S(2)}, u32[]{:S(2)}) collective-permute-start(bf16[2,2,32,4096]{3,2,1,0:T(8,128)(2,1)} %get-tuple-element.223.refs_4_), channel_id=1, source_target_pairs={{0,4},{1,5},{2,6},{3,7},{4,0},{5,1},{6,2},{7,3},{8,12},{9,13},{10,... | collective-permute-start | bytes 3145736 | tf_op jit(solution)/shard_map/ppermute | solution.py:51
  47.8 28.5 %collective-permute-start.9 = (bf16[2,2,32,4096]{3,2,1,0:T(8,128)(2,1)S(1)}, bf16[2,2,32,4096]{3,2,1,0:T(8,128)(2,1)}, u32[]{:S(2)}, u32[]{:S(2)}) collective-permute-start(bf16[2,2,32,4096]{3,2,1,0:T(8,128)(2,1)S(1)} %get-tuple-element.221.refs_0_), channel_id=1, source_target_pairs={{0,2},{1,3},{2,0},{3,1},{4,6},{5,7},{6,4},{7,5},{8,10},{9,11},{10,... | collective-permute-start | bytes 3145736 | tf_op jit(solution)/shard_map/ppermute | solution.py:51
  49.1 20.5 %collective-permute-start.12 = (bf16[32,4224]{1,0:T(8,128)(2,1)S(1)}, bf16[32,4224]{1,0:T(8,128)(2,1)S(1)}, u32[]{:S(2)}, u32[]{:S(2)}) collective-permute-start(bf16[32,4224]{1,0:T(8,128)(2,1)S(1)} %copy-done.60), channel_id=1, source_target_pairs={{0,24},{1,25},{2,26},{3,27},{4,28},{5,29},{6,30},{7,31},{8,16},{9,... | collective-permute-start | bytes 811016 | tf_op jit(solution)/shard_map/ppermute | solution.py:51
  49.6 27.8 %collective-permute-start.13 = (bf16[2,2,32,4096]{3,2,1,0:T(8,128)(2,1)S(1)}, bf16[2,2,32,4096]{3,2,1,0:T(8,128)(2,1)S(1)}, u32[]{:S(2)}, u32[]{:S(2)}) collective-permute-start(bf16[2,2,32,4096]{3,2,1,0:T(8,128)(2,1)S(1)} %get-tuple-element.221.refs_0_), channel_id=1, source_target_pairs={{0,1},{1,0},{2,3},{3,2},{4,5},{5,4},{6,7},{7,6},{8,9},{9,8},{10,11... | collective-permute-start | bytes 3145736 | tf_op jit(solution)/shard_map/ppermute | solution.py:51
  49.6 21.4 %collective-permute-start.11 = (bf16[32,4224]{1,0:T(8,128)(2,1)S(1)}, bf16[32,4224]{1,0:T(8,128)(2,1)S(1)}, u32[]{:S(2)}, u32[]{:S(2)}) collective-permute-start(bf16[32,4224]{1,0:T(8,128)(2,1)S(1)} %copy-done.60), channel_id=1, source_target_pairs={{0,16},{1,17},{2,18},{3,19},{4,20},{5,21},{6,22},{7,23},{8,24},{9,... | collective-permute-start | bytes 811016 | tf_op jit(solution)/shard_map/ppermute | solution.py:51
  70.9 8.9 %collective-permute-start.16 = (bf16[2,2,32,4096]{3,2,1,0:T(8,128)(2,1)}, bf16[2,2,32,4096]{3,2,1,0:T(8,128)(2,1)}, u32[]{:S(2)}, u32[]{:S(2)}) collective-permute-start(bf16[2,2,32,4096]{3,2,1,0:T(8,128)(2,1)} %get-tuple-element.223.refs_4_), channel_id=1, source_target_pairs={{0,1},{1,0},{2,3},{3,2},{4,5},{5,4},{6,7},{7,6},{8,9},{9,8},{10,11... | collective-permute-start | bytes 3145736 | tf_op jit(solution)/shard_map/ppermute | solution.py:51
  76.4 6.8 %collective-permute-start.14 = (bf16[2,2,32,4096]{3,2,1,0:T(8,128)(2,1)}, bf16[2,2,32,4096]{3,2,1,0:T(8,128)(2,1)}, u32[]{:S(2)}, u32[]{:S(2)}) collective-permute-start(bf16[2,2,32,4096]{3,2,1,0:T(8,128)(2,1)} %collective-permute-done.9.refs_1_), channel_id=1, source_target_pairs={{0,1},{1,0},{2,3},{3,2},{4,5},{5,4},{6,7},{7,6},{8,9},{9,8},{10,11... | collective-permute-start | bytes 3145736 | tf_op jit(solution)/shard_map/ppermute | solution.py:51
  76.9 14.4 %collective-permute-start.19 = (bf16[2,32,4224]{2,1,0:T(8,128)(2,1)S(1)}, bf16[2,32,4224]{2,1,0:T(8,128)(2,1)}, u32[]{:S(2)}, u32[]{:S(2)}) collective-permute-start(bf16[2,32,4224]{2,1,0:T(8,128)(2,1)S(1)} %get-tuple-element.235.refs_2_), channel_id=1, source_target_pairs={{0,2},{1,3},{2,0},{3,1},{4,6},{5,7},{6,4},{7,5},{8,10},{9,11},{10,... | collective-permute-start | bytes 1622024 | tf_op jit(solution)/shard_map/ppermute | solution.py:51
  78.4 14.1 %collective-permute-start.18 = (bf16[2,32,4224]{2,1,0:T(8,128)(2,1)S(1)}, bf16[2,32,4224]{2,1,0:T(8,128)(2,1)}, u32[]{:S(2)}, u32[]{:S(2)}) collective-permute-start(bf16[2,32,4224]{2,1,0:T(8,128)(2,1)S(1)} %get-tuple-element.233.refs_0_), channel_id=1, source_target_pairs={{0,4},{1,5},{2,6},{3,7},{4,0},{5,1},{6,2},{7,3},{8,12},{9,13},{10,... | collective-permute-start | bytes 1622024 | tf_op jit(solution)/shard_map/ppermute | solution.py:51
  79.9 39.7 %collective-permute-start.28 = (bf16[32,8192]{1,0:T(8,128)(2,1)}, bf16[32,8192]{1,0:T(8,128)(2,1)}, u32[]{:S(2)}, u32[]{:S(2)}) collective-permute-start(bf16[32,8192]{1,0:T(8,128)(2,1)} %shard_map.359.refs_0_), channel_id=1, source_target_pairs={{0,24},{1,25},{2,26},{3,27},{4,28},{5,29},{6,30},{7,31},{8,16},{9,... | collective-permute-start | bytes 1572872 | tf_op jit(solution)/shard_map/ppermute | solution.py:51
  80.3 44.9 %collective-permute-start.27 = (bf16[32,8192]{1,0:T(8,128)(2,1)}, bf16[32,8192]{1,0:T(8,128)(2,1)}, u32[]{:S(2)}, u32[]{:S(2)}) collective-permute-start(bf16[32,8192]{1,0:T(8,128)(2,1)} %shard_map.359.refs_0_), channel_id=1, source_target_pairs={{0,16},{1,17},{2,18},{3,19},{4,20},{5,21},{6,22},{7,23},{8,24},{9,... | collective-permute-start | bytes 1572872 | tf_op jit(solution)/shard_map/ppermute | solution.py:51
  83.2 42.8 %collective-permute-start.26 = (bf16[32,8192]{1,0:T(8,128)(2,1)}, bf16[32,8192]{1,0:T(8,128)(2,1)}, u32[]{:S(2)}, u32[]{:S(2)}) collective-permute-start(bf16[32,8192]{1,0:T(8,128)(2,1)} %shard_map.359.refs_0_), channel_id=1, source_target_pairs={{0,8},{1,9},{2,10},{3,11},{4,12},{5,13},{6,14},{7,15},{8,0},{9,1},... | collective-permute-start | bytes 1572872 | tf_op jit(solution)/shard_map/ppermute | solution.py:51
  93.8 24.8 %collective-permute-start.21 = (bf16[2,2,32,4224]{3,2,1,0:T(8,128)(2,1)S(1)}, bf16[2,2,32,4224]{3,2,1,0:T(8,128)(2,1)S(1)}, u32[]{:S(2)}, u32[]{:S(2)}) collective-permute-start(bf16[2,2,32,4224]{3,2,1,0:T(8,128)(2,1)S(1)} %get-tuple-element.238.refs_4_), channel_id=1, source_target_pairs={{0,4},{1,5},{2,6},{3,7},{4,0},{5,1},{6,2},{7,3},{8,12},{9,13},{10,... | collective-permute-start | bytes 3244040 | tf_op jit(solution)/shard_map/ppermute | solution.py:51
  95.1 24.4 %collective-permute-start.20 = (bf16[2,2,32,4224]{3,2,1,0:T(8,128)(2,1)S(1)}, bf16[2,2,32,4224]{3,2,1,0:T(8,128)(2,1)S(1)}, u32[]{:S(2)}, u32[]{:S(2)}) collective-permute-start(bf16[2,2,32,4224]{3,2,1,0:T(8,128)(2,1)S(1)} %get-tuple-element.237.refs_0_), channel_id=1, source_target_pairs={{0,2},{1,3},{2,0},{3,1},{4,6},{5,7},{6,4},{7,5},{8,10},{9,11},{10,... | collective-permute-start | bytes 3244040 | tf_op jit(solution)/shard_map/ppermute | solution.py:51
  118.5 14.1 %collective-permute-start.22 = (bf16[2,2,32,4224]{3,2,1,0:T(8,128)(2,1)S(1)}, bf16[2,2,32,4224]{3,2,1,0:T(8,128)(2,1)S(1)}, u32[]{:S(2)}, u32[]{:S(2)}) collective-permute-start(bf16[2,2,32,4224]{3,2,1,0:T(8,128)(2,1)S(1)} %get-tuple-element.237.refs_0_), channel_id=1, source_target_pairs={{0,1},{1,0},{2,3},{3,2},{4,5},{5,4},{6,7},{7,6},{8,9},{9,8},{10,11... | collective-permute-start | bytes 3244040 | tf_op jit(solution)/shard_map/ppermute | solution.py:51
  119.5 14.6 %collective-permute-start.24 = (bf16[2,2,32,4224]{3,2,1,0:T(8,128)(2,1)S(1)}, bf16[2,2,32,4224]{3,2,1,0:T(8,128)(2,1)S(1)}, u32[]{:S(2)}, u32[]{:S(2)}) collective-permute-start(bf16[2,2,32,4224]{3,2,1,0:T(8,128)(2,1)S(1)} %get-tuple-element.238.refs_4_), channel_id=1, source_target_pairs={{0,1},{1,0},{2,3},{3,2},{4,5},{5,4},{6,7},{7,6},{8,9},{9,8},{10,11... | collective-permute-start | bytes 3244040 | tf_op jit(solution)/shard_map/ppermute | solution.py:51
  119.5 14.6 %collective-permute-start.25 = (bf16[2,2,32,4224]{3,2,1,0:T(8,128)(2,1)S(1)}, bf16[2,2,32,4224]{3,2,1,0:T(8,128)(2,1)S(1)}, u32[]{:S(2)}, u32[]{:S(2)}) collective-permute-start(bf16[2,2,32,4224]{3,2,1,0:T(8,128)(2,1)S(1)} %collective-permute-done.21.refs_5_), channel_id=1, source_target_pairs={{0,1},{1,0},{2,3},{3,2},{4,5},{5,4},{6,7},{7,6},{8,9},{9,8},{10,11... | collective-permute-start | bytes 3244040 | tf_op jit(solution)/shard_map/ppermute | solution.py:51
  125.2 9.0 %collective-permute-start.23 = (bf16[2,2,32,4224]{3,2,1,0:T(8,128)(2,1)S(1)}, bf16[2,2,32,4224]{3,2,1,0:T(8,128)(2,1)S(1)}, u32[]{:S(2)}, u32[]{:S(2)}) collective-permute-start(bf16[2,2,32,4224]{3,2,1,0:T(8,128)(2,1)S(1)} %collective-permute-done.20.refs_1_), channel_id=1, source_target_pairs={{0,1},{1,0},{2,3},{3,2},{4,5},{5,4},{6,7},{7,6},{8,9},{9,8},{10,11... | collective-permute-start | bytes 3244040 | tf_op jit(solution)/shard_map/ppermute | solution.py:51
  129.4 29.1 %collective-permute-start.30 = (bf16[2,32,8192]{2,1,0:T(8,128)(2,1)}, bf16[2,32,8192]{2,1,0:T(8,128)(2,1)}, u32[]{:S(2)}, u32[]{:S(2)}) collective-permute-start(bf16[2,32,8192]{2,1,0:T(8,128)(2,1)} %get-tuple-element.261.refs_2_), channel_id=1, source_target_pairs={{0,2},{1,3},{2,0},{3,1},{4,6},{5,7},{6,4},{7,5},{8,10},{9,11},{10,... | collective-permute-start | bytes 3145736 | tf_op jit(solution)/shard_map/ppermute | solution.py:51
  132.6 25.9 %collective-permute-start.29 = (bf16[2,32,8192]{2,1,0:T(8,128)(2,1)S(1)}, bf16[2,32,8192]{2,1,0:T(8,128)(2,1)}, u32[]{:S(2)}, u32[]{:S(2)}) collective-permute-start(bf16[2,32,8192]{2,1,0:T(8,128)(2,1)S(1)} %get-tuple-element.257.refs_0_), channel_id=1, source_target_pairs={{0,4},{1,5},{2,6},{3,7},{4,0},{5,1},{6,2},{7,3},{8,12},{9,13},{10,... | collective-permute-start | bytes 3145736 | tf_op jit(solution)/shard_map/ppermute | solution.py:51
  162.5 47.9 %collective-permute-start.34 = (bf16[2,2,32,8192]{3,2,1,0:T(8,128)(2,1)}, bf16[2,2,32,8192]{3,2,1,0:T(8,128)(2,1)}, u32[]{:S(2)}, u32[]{:S(2)}) collective-permute-start(bf16[2,2,32,8192]{3,2,1,0:T(8,128)(2,1)} %get-tuple-element.264.refs_4_), channel_id=1, source_target_pairs={{0,4},{1,5},{2,6},{3,7},{4,0},{5,1},{6,2},{7,3},{8,12},{9,13},{10,... | collective-permute-start | bytes 6291464 | tf_op jit(solution)/shard_map/ppermute | solution.py:51
  163.6 47.6 %collective-permute-start.31 = (bf16[2,2,32,8192]{3,2,1,0:T(8,128)(2,1)}, bf16[2,2,32,8192]{3,2,1,0:T(8,128)(2,1)}, u32[]{:S(2)}, u32[]{:S(2)}) collective-permute-start(bf16[2,2,32,8192]{3,2,1,0:T(8,128)(2,1)} %get-tuple-element.263.refs_0_), channel_id=1, source_target_pairs={{0,2},{1,3},{2,0},{3,1},{4,6},{5,7},{6,4},{7,5},{8,10},{9,11},{10,... | collective-permute-start | bytes 6291464 | tf_op jit(solution)/shard_map/ppermute | solution.py:51
  182.8 28.4 %collective-permute-start.32 = (bf16[2,2,32,8192]{3,2,1,0:T(8,128)(2,1)}, bf16[2,2,32,8192]{3,2,1,0:T(8,128)(2,1)}, u32[]{:S(2)}, u32[]{:S(2)}) collective-permute-start(bf16[2,2,32,8192]{3,2,1,0:T(8,128)(2,1)} %get-tuple-element.263.refs_0_), channel_id=1, source_target_pairs={{0,1},{1,0},{2,3},{3,2},{4,5},{5,4},{6,7},{7,6},{8,9},{9,8},{10,11... | collective-permute-start | bytes 6291464 | tf_op jit(solution)/shard_map/ppermute | solution.py:51
  182.8 28.4 %collective-permute-start.35 = (bf16[2,2,32,8192]{3,2,1,0:T(8,128)(2,1)}, bf16[2,2,32,8192]{3,2,1,0:T(8,128)(2,1)}, u32[]{:S(2)}, u32[]{:S(2)}) collective-permute-start(bf16[2,2,32,8192]{3,2,1,0:T(8,128)(2,1)} %get-tuple-element.264.refs_4_), channel_id=1, source_target_pairs={{0,1},{1,0},{2,3},{3,2},{4,5},{5,4},{6,7},{7,6},{8,9},{9,8},{10,11... | collective-permute-start | bytes 6291464 | tf_op jit(solution)/shard_map/ppermute | solution.py:51
  259.5 9.3 %collective-permute-start.38 = (bf16[2048,1024]{1,0:T(8,128)(2,1)S(1)}, bf16[2048,1024]{1,0:T(8,128)(2,1)S(1)}, u32[]{:S(2)}, u32[]{:S(2)}) collective-permute-start(bf16[2048,1024]{1,0:T(8,128)(2,1)S(1)} %shard_map.379), channel_id=1, source_target_pairs={{0,1},{1,0},{2,3},{3,2},{4,5},{5,4},{6,7},{7,6},{8,9},{9,8},{10,11... | collective-permute-start | bytes 12582920 | tf_op jit(solution)/shard_map/ppermute | solution.py:51
  263.1 13.6 %collective-permute-start.37 = (bf16[512,4096]{1,0:T(8,128)(2,1)S(1)}, bf16[512,4096]{1,0:T(8,128)(2,1)S(1)}, u32[]{:S(2)}, u32[]{:S(2)}) collective-permute-start(bf16[512,4096]{1,0:T(8,128)(2,1)S(1)} %shard_map.380), channel_id=1, source_target_pairs={{0,1},{1,0},{2,3},{3,2},{4,5},{5,4},{6,7},{7,6},{8,9},{9,8},{10,11... | collective-permute-start | bytes 12582920 | tf_op jit(solution)/shard_map/ppermute | solution.py:51
  273.5 25.5 %collective-permute-start.40 = (bf16[512,1024]{1,0:T(8,128)(2,1)}, bf16[512,1024]{1,0:T(8,128)(2,1)S(1)}, u32[]{:S(2)}, u32[]{:S(2)}) collective-permute-start(bf16[512,1024]{1,0:T(8,128)(2,1)} %get-tuple-element.282), channel_id=1, source_target_pairs={{0,2},{1,3},{2,0},{3,1},{4,6},{5,7},{6,4},{7,5},{8,10},{9,11},{10,... | collective-permute-start | bytes 3145736 | tf_op jit(solution)/shard_map/ppermute | solution.py:51
  274.0 25.2 %collective-permute-start.39 = (bf16[512,1024]{1,0:T(8,128)(2,1)}, bf16[512,1024]{1,0:T(8,128)(2,1)}, u32[]{:S(2)}, u32[]{:S(2)}) collective-permute-start(bf16[512,1024]{1,0:T(8,128)(2,1)} %get-tuple-element.280), channel_id=1, source_target_pairs={{0,4},{1,5},{2,6},{3,7},{4,0},{5,1},{6,2},{7,3},{8,12},{9,13},{10,... | collective-permute-start | bytes 3145736 | tf_op jit(solution)/shard_map/ppermute | solution.py:51
  302.7 12.8 %collective-permute-start.42 = (bf16[256,1024]{1,0:T(8,128)(2,1)S(1)}, bf16[256,1024]{1,0:T(8,128)(2,1)S(1)}, u32[]{:S(2)}, u32[]{:S(2)}) collective-permute-start(bf16[256,1024]{1,0:T(8,128)(2,1)S(1)} %get-tuple-element.297), channel_id=1, source_target_pairs={{0,4},{1,5},{2,6},{3,7},{4,0},{5,1},{6,2},{7,3},{8,12},{9,13},{10,... | collective-permute-start | bytes 1572872 | tf_op jit(solution)/shard_map/ppermute | solution.py:51
  303.7 12.4 %collective-permute-start.41 = (bf16[256,1024]{1,0:T(8,128)(2,1)S(1)}, bf16[256,1024]{1,0:T(8,128)(2,1)S(1)}, u32[]{:S(2)}, u32[]{:S(2)}) collective-permute-start(bf16[256,1024]{1,0:T(8,128)(2,1)S(1)} %get-tuple-element.295), channel_id=1, source_target_pairs={{0,2},{1,3},{2,0},{3,1},{4,6},{5,7},{6,4},{7,5},{8,10},{9,11},{10,... | collective-permute-start | bytes 1572872 | tf_op jit(solution)/shard_map/ppermute | solution.py:51
  316.1 37.8 %collective-permute-start.43 = (bf16[512,4224]{1,0:T(8,128)(2,1)}, bf16[512,4224]{1,0:T(8,128)(2,1)}, u32[]{:S(2)}, u32[]{:S(2)}) collective-permute-start(bf16[512,4224]{1,0:T(8,128)(2,1)} %shard_map.386), channel_id=1, source_target_pairs={{0,1},{1,0},{2,3},{3,2},{4,5},{5,4},{6,7},{7,6},{8,9},{9,8},{10,11... | collective-permute-start | bytes 12976136 | tf_op jit(solution)/shard_map/ppermute | solution.py:51
  316.1 28.5 %collective-permute-start.45 = (bf16[128,4096]{1,0:T(8,128)(2,1)}, bf16[128,4096]{1,0:T(8,128)(2,1)}, u32[]{:S(2)}, u32[]{:S(2)}) collective-permute-start(bf16[128,4096]{1,0:T(8,128)(2,1)} %get-tuple-element.316), channel_id=1, source_target_pairs={{0,2},{1,3},{2,0},{3,1},{4,6},{5,7},{6,4},{7,5},{8,10},{9,11},{10,... | collective-permute-start | bytes 3145736 | tf_op jit(solution)/shard_map/ppermute | solution.py:51
  319.5 25.7 %collective-permute-start.44 = (bf16[128,4096]{1,0:T(8,128)(2,1)}, bf16[128,4096]{1,0:T(8,128)(2,1)}, u32[]{:S(2)}, u32[]{:S(2)}) collective-permute-start(bf16[128,4096]{1,0:T(8,128)(2,1)} %get-tuple-element.307), channel_id=1, source_target_pairs={{0,4},{1,5},{2,6},{3,7},{4,0},{5,1},{6,2},{7,3},{8,12},{9,13},{10,... | collective-permute-start | bytes 3145736 | tf_op jit(solution)/shard_map/ppermute | solution.py:51
  348.7 29.4 %collective-permute-start.46 = (bf16[64,4096]{1,0:T(8,128)(2,1)S(1)}, bf16[64,4096]{1,0:T(8,128)(2,1)S(1)}, u32[]{:S(2)}, u32[]{:S(2)}) collective-permute-start(bf16[64,4096]{1,0:T(8,128)(2,1)S(1)} %get-tuple-element.319), channel_id=1, source_target_pairs={{0,2},{1,3},{2,0},{3,1},{4,6},{5,7},{6,4},{7,5},{8,10},{9,11},{10,... | collective-permute-start | bytes 1572872 | tf_op jit(solution)/shard_map/ppermute | solution.py:51
  349.4 29.4 %collective-permute-start.47 = (bf16[64,4096]{1,0:T(8,128)(2,1)S(1)}, bf16[64,4096]{1,0:T(8,128)(2,1)S(1)}, u32[]{:S(2)}, u32[]{:S(2)}) collective-permute-start(bf16[64,4096]{1,0:T(8,128)(2,1)S(1)} %get-tuple-element.321), channel_id=1, source_target_pairs={{0,4},{1,5},{2,6},{3,7},{4,0},{5,1},{6,2},{7,3},{8,12},{9,13},{10,... | collective-permute-start | bytes 1572872 | tf_op jit(solution)/shard_map/ppermute | solution.py:51
  350.5 17.2 %collective-permute-start.48 = (bf16[128,1024]{1,0:T(8,128)(2,1)S(1)}, bf16[128,1024]{1,0:T(8,128)(2,1)S(1)}, u32[]{:S(2)}, u32[]{:S(2)}) collective-permute-start(bf16[128,1024]{1,0:T(8,128)(2,1)S(1)} %get-tuple-element.311), channel_id=1, source_target_pairs={{0,8},{1,9},{2,10},{3,11},{4,12},{5,13},{6,14},{7,15},{8,0},{9,1},... | collective-permute-start | bytes 786440 | tf_op jit(solution)/shard_map/ppermute | solution.py:51
  353.9 18.0 %collective-permute-start.49 = (bf16[128,1024]{1,0:T(8,128)(2,1)S(1)}, bf16[128,1024]{1,0:T(8,128)(2,1)S(1)}, u32[]{:S(2)}, u32[]{:S(2)}) collective-permute-start(bf16[128,1024]{1,0:T(8,128)(2,1)S(1)} %get-tuple-element.312), channel_id=1, source_target_pairs={{0,16},{1,17},{2,18},{3,19},{4,20},{5,21},{6,22},{7,23},{8,24},{9,... | collective-permute-start | bytes 786440 | tf_op jit(solution)/shard_map/ppermute | solution.py:51
  354.0 23.4 %collective-permute-start.50 = (bf16[128,1024]{1,0:T(8,128)(2,1)S(1)}, bf16[128,1024]{1,0:T(8,128)(2,1)S(1)}, u32[]{:S(2)}, u32[]{:S(2)}) collective-permute-start(bf16[128,1024]{1,0:T(8,128)(2,1)S(1)} %get-tuple-element.313), channel_id=1, source_target_pairs={{0,24},{1,25},{2,26},{3,27},{4,28},{5,29},{6,30},{7,31},{8,16},{9,... | collective-permute-start | bytes 786440 | tf_op jit(solution)/shard_map/ppermute | solution.py:51
  379.6 7.9 %collective-permute-start.51 = (bf16[512,4224]{1,0:T(8,128)(2,1)}, bf16[512,4224]{1,0:T(8,128)(2,1)}, u32[]{:S(2)}, u32[]{:S(2)}) collective-permute-start(bf16[512,4224]{1,0:T(8,128)(2,1)} %shard_map.392), channel_id=1, source_target_pairs={{0,1},{1,0},{2,3},{3,2},{4,5},{5,4},{6,7},{7,6},{8,9},{9,8},{10,11... | collective-permute-start | bytes 12976136 | tf_op jit(solution)/shard_map/ppermute | solution.py:51
  379.6 26.5 %collective-permute-start.53 = (bf16[128,4224]{1,0:T(8,128)(2,1)}, bf16[128,4224]{1,0:T(8,128)(2,1)S(1)}, u32[]{:S(2)}, u32[]{:S(2)}) collective-permute-start(bf16[128,4224]{1,0:T(8,128)(2,1)} %get-tuple-element.349), channel_id=1, source_target_pairs={{0,2},{1,3},{2,0},{3,1},{4,6},{5,7},{6,4},{7,5},{8,10},{9,11},{10,... | collective-permute-start | bytes 3244040 | tf_op jit(solution)/shard_map/ppermute | solution.py:51
  381.2 26.3 %collective-permute-start.52 = (bf16[128,4224]{1,0:T(8,128)(2,1)}, bf16[128,4224]{1,0:T(8,128)(2,1)}, u32[]{:S(2)}, u32[]{:S(2)}) collective-permute-start(bf16[128,4224]{1,0:T(8,128)(2,1)} %get-tuple-element.346), channel_id=1, source_target_pairs={{0,4},{1,5},{2,6},{3,7},{4,0},{5,1},{6,2},{7,3},{8,12},{9,13},{10,... | collective-permute-start | bytes 3244040 | tf_op jit(solution)/shard_map/ppermute | solution.py:51
  386.4 28.8 %collective-permute-start.59 = (bf16[32,4096]{1,0:T(8,128)(2,1)S(1)}, bf16[32,4096]{1,0:T(8,128)(2,1)S(1)}, u32[]{:S(2)}, u32[]{:S(2)}) collective-permute-start(bf16[32,4096]{1,0:T(8,128)(2,1)S(1)} %get-tuple-element.357), channel_id=1, source_target_pairs={{0,24},{1,25},{2,26},{3,27},{4,28},{5,29},{6,30},{7,31},{8,16},{9,... | collective-permute-start | bytes 786440 | tf_op jit(solution)/shard_map/ppermute | solution.py:51
  387.0 28.2 %collective-permute-start.58 = (bf16[32,4096]{1,0:T(8,128)(2,1)S(1)}, bf16[32,4096]{1,0:T(8,128)(2,1)S(1)}, u32[]{:S(2)}, u32[]{:S(2)}) collective-permute-start(bf16[32,4096]{1,0:T(8,128)(2,1)S(1)} %get-tuple-element.356), channel_id=1, source_target_pairs={{0,16},{1,17},{2,18},{3,19},{4,20},{5,21},{6,22},{7,23},{8,24},{9,... | collective-permute-start | bytes 786440 | tf_op jit(solution)/shard_map/ppermute | solution.py:51
  387.6 27.7 %collective-permute-start.57 = (bf16[32,4096]{1,0:T(8,128)(2,1)S(1)}, bf16[32,4096]{1,0:T(8,128)(2,1)S(1)}, u32[]{:S(2)}, u32[]{:S(2)}) collective-permute-start(bf16[32,4096]{1,0:T(8,128)(2,1)S(1)} %get-tuple-element.355), channel_id=1, source_target_pairs={{0,8},{1,9},{2,10},{3,11},{4,12},{5,13},{6,14},{7,15},{8,0},{9,1},... | collective-permute-start | bytes 786440 | tf_op jit(solution)/shard_map/ppermute | solution.py:51
  410.2 13.9 %collective-permute-start.55 = (bf16[64,4224]{1,0:T(8,128)(2,1)S(1)}, bf16[64,4224]{1,0:T(8,128)(2,1)S(1)}, u32[]{:S(2)}, u32[]{:S(2)}) collective-permute-start(bf16[64,4224]{1,0:T(8,128)(2,1)S(1)} %get-tuple-element.352), channel_id=1, source_target_pairs={{0,4},{1,5},{2,6},{3,7},{4,0},{5,1},{6,2},{7,3},{8,12},{9,13},{10,... | collective-permute-start | bytes 1622024 | tf_op jit(solution)/shard_map/ppermute | solution.py:51
  411.2 13.6 %collective-permute-start.54 = (bf16[64,4224]{1,0:T(8,128)(2,1)S(1)}, bf16[64,4224]{1,0:T(8,128)(2,1)S(1)}, u32[]{:S(2)}, u32[]{:S(2)}) collective-permute-start(bf16[64,4224]{1,0:T(8,128)(2,1)S(1)} %get-tuple-element.351), channel_id=1, source_target_pairs={{0,2},{1,3},{2,0},{3,1},{4,6},{5,7},{6,4},{7,5},{8,10},{9,11},{10,... | collective-permute-start | bytes 1622024 | tf_op jit(solution)/shard_map/ppermute | solution.py:51
  424.8 28.0 %collective-permute-start.63 = (bf16[128,4224]{1,0:T(8,128)(2,1)S(1)}, bf16[128,4224]{1,0:T(8,128)(2,1)S(1)}, u32[]{:S(2)}, u32[]{:S(2)}) collective-permute-start(bf16[128,4224]{1,0:T(8,128)(2,1)S(1)} %get-tuple-element.369), channel_id=1, source_target_pairs={{0,2},{1,3},{2,0},{3,1},{4,6},{5,7},{6,4},{7,5},{8,10},{9,11},{10,... | collective-permute-start | bytes 3244040 | tf_op jit(solution)/shard_map/ppermute | solution.py:51
  425.3 27.5 %collective-permute-start.56 = (bf16[128,4224]{1,0:T(8,128)(2,1)S(1)}, bf16[128,4224]{1,0:T(8,128)(2,1)S(1)}, u32[]{:S(2)}, u32[]{:S(2)}) collective-permute-start(bf16[128,4224]{1,0:T(8,128)(2,1)S(1)} %get-tuple-element.353), channel_id=1, source_target_pairs={{0,4},{1,5},{2,6},{3,7},{4,0},{5,1},{6,2},{7,3},{8,12},{9,13},{10,... | collective-permute-start | bytes 3244040 | tf_op jit(solution)/shard_map/ppermute | solution.py:51
  432.0 16.9 %collective-permute-start.62 = (bf16[32,4224]{1,0:T(8,128)(2,1)S(1)}, bf16[32,4224]{1,0:T(8,128)(2,1)S(1)}, u32[]{:S(2)}, u32[]{:S(2)}) collective-permute-start(bf16[32,4224]{1,0:T(8,128)(2,1)S(1)} %get-tuple-element.367), channel_id=1, source_target_pairs={{0,24},{1,25},{2,26},{3,27},{4,28},{5,29},{6,30},{7,31},{8,16},{9,... | collective-permute-start | bytes 811016 | tf_op jit(solution)/shard_map/ppermute | solution.py:51
  432.6 20.1 %collective-permute-start.61 = (bf16[32,4224]{1,0:T(8,128)(2,1)S(1)}, bf16[32,4224]{1,0:T(8,128)(2,1)S(1)}, u32[]{:S(2)}, u32[]{:S(2)}) collective-permute-start(bf16[32,4224]{1,0:T(8,128)(2,1)S(1)} %get-tuple-element.365), channel_id=1, source_target_pairs={{0,16},{1,17},{2,18},{3,19},{4,20},{5,21},{6,22},{7,23},{8,24},{9,... | collective-permute-start | bytes 811016 | tf_op jit(solution)/shard_map/ppermute | solution.py:51
  433.1 19.6 %collective-permute-start.60 = (bf16[32,4224]{1,0:T(8,128)(2,1)S(1)}, bf16[32,4224]{1,0:T(8,128)(2,1)S(1)}, u32[]{:S(2)}, u32[]{:S(2)}) collective-permute-start(bf16[32,4224]{1,0:T(8,128)(2,1)S(1)} %get-tuple-element.363), channel_id=1, source_target_pairs={{0,8},{1,9},{2,10},{3,11},{4,12},{5,13},{6,14},{7,15},{8,0},{9,1},... | collective-permute-start | bytes 811016 | tf_op jit(solution)/shard_map/ppermute | solution.py:51
  455.0 14.9 %collective-permute-start.66 = (bf16[64,4224]{1,0:T(8,128)(2,1)}, bf16[64,4224]{1,0:T(8,128)(2,1)S(1)}, u32[]{:S(2)}, u32[]{:S(2)}) collective-permute-start(bf16[64,4224]{1,0:T(8,128)(2,1)} %get-tuple-element.375), channel_id=1, source_target_pairs={{0,4},{1,5},{2,6},{3,7},{4,0},{5,1},{6,2},{7,3},{8,12},{9,13},{10,... | collective-permute-start | bytes 1622024 | tf_op jit(solution)/shard_map/ppermute | solution.py:51
  455.9 14.6 %collective-permute-start.65 = (bf16[64,4224]{1,0:T(8,128)(2,1)}, bf16[64,4224]{1,0:T(8,128)(2,1)S(1)}, u32[]{:S(2)}, u32[]{:S(2)}) collective-permute-start(bf16[64,4224]{1,0:T(8,128)(2,1)} %get-tuple-element.374), channel_id=1, source_target_pairs={{0,2},{1,3},{2,0},{3,1},{4,6},{5,7},{6,4},{7,5},{8,10},{9,11},{10,... | collective-permute-start | bytes 1622024 | tf_op jit(solution)/shard_map/ppermute | solution.py:51
  470.5 32.6 %collective-permute-start.67 = (bf16[256,1024]{1,0:T(8,128)(2,1)}, bf16[256,1024]{1,0:T(8,128)(2,1)}, u32[]{:S(2)}, u32[]{:S(2)}) collective-permute-start(bf16[256,1024]{1,0:T(8,128)(2,1)} %fusion.5), channel_id=1, source_target_pairs={{0,2},{1,3},{2,0},{3,1},{4,6},{5,7},{6,4},{7,5},{8,10},{9,11},{10,... | collective-permute-start | bytes 1572872 | tf_op jit(solution)/shard_map/ppermute | solution.py:51
  473.7 12.8 %collective-permute-start.68 = (bf16[32,4224]{1,0:T(8,128)(2,1)S(1)}, bf16[32,4224]{1,0:T(8,128)(2,1)S(1)}, u32[]{:S(2)}, u32[]{:S(2)}) collective-permute-start(bf16[32,4224]{1,0:T(8,128)(2,1)S(1)} %get-tuple-element.385), channel_id=1, source_target_pairs={{0,8},{1,9},{2,10},{3,11},{4,12},{5,13},{6,14},{7,15},{8,0},{9,1},... | collective-permute-start | bytes 811016 | tf_op jit(solution)/shard_map/ppermute | solution.py:51
  477.2 18.6 %collective-permute-start.69 = (bf16[32,4224]{1,0:T(8,128)(2,1)S(1)}, bf16[32,4224]{1,0:T(8,128)(2,1)S(1)}, u32[]{:S(2)}, u32[]{:S(2)}) collective-permute-start(bf16[32,4224]{1,0:T(8,128)(2,1)S(1)} %get-tuple-element.386), channel_id=1, source_target_pairs={{0,16},{1,17},{2,18},{3,19},{4,20},{5,21},{6,22},{7,23},{8,24},{9,... | collective-permute-start | bytes 811016 | tf_op jit(solution)/shard_map/ppermute | solution.py:51
  477.2 24.4 %collective-permute-start.70 = (bf16[32,4224]{1,0:T(8,128)(2,1)S(1)}, bf16[32,4224]{1,0:T(8,128)(2,1)S(1)}, u32[]{:S(2)}, u32[]{:S(2)}) collective-permute-start(bf16[32,4224]{1,0:T(8,128)(2,1)S(1)} %get-tuple-element.387), channel_id=1, source_target_pairs={{0,24},{1,25},{2,26},{3,27},{4,28},{5,29},{6,30},{7,31},{8,16},{9,... | collective-permute-start | bytes 811016 | tf_op jit(solution)/shard_map/ppermute | solution.py:51
  (138 other events, 1188.6 us)
